TPU v7x, 32 devices: a whole 2x2x4 slice. The times are simulated.
32 devices in a mesh: dp: 4 (over x, core), expert: 8 (over z, y).
Axes of the slice: x: 2, y: 2, z: 4, core: 2. Of those that a mesh axis runs over, the one named last changes fastest.
Arguments:
- tokens: bfloat16 [8, 1536, 768], P('expert', 'dp'), may hold values from -6 to 6
- doc_lengths: int32 [8, 4, 4], P('expert', 'dp'), may hold values from 1 to 64, 128 in all within a row
- assign: int32 [8, 1536, 1], P('expert', 'dp'), may hold values from 0 to 7, as said below
- ln_gain: float32 [768, 4], replicated, may hold values from 0.5 to 1.5
- ln_bias: float32 [768, 4], replicated, may hold values from -1 to 1
- attn_in: bfloat16 [768, 2, 2304], replicated, may hold values from -0.21875 to 0.21875
- attn_out: bfloat16 [768, 2, 768], replicated, may hold values from -0.875 to 0.875
- ffn_in: bfloat16 [768, 3072], replicated, may hold values from -0.21875 to 0.21875
- ffn_out: bfloat16 [3072, 768], replicated, may hold values from -0.109375 to 0.109375
- router: bfloat16 [768, 8], replicated, may hold values from -0.14941406 to 0.14941406
- expert_in: bfloat16 [8, 768, 3072], P('expert'), may hold values from -0.21875 to 0.21875
- expert_out: bfloat16 [8, 3072, 768], P('expert'), may hold values from -0.21875 to 0.21875
- cotangent: bfloat16 [8, 1536, 768], P('expert', 'dp'), may hold values from -6 to 6
Outputs:
- output: bfloat16 [8, 1536, 768], P('expert', 'dp')
- balance: float32 [], replicated
- grad_tokens: bfloat16 [8, 1536, 768], P('expert', 'dp')
- grad_ln_gain: float32 [768, 4], P('dp')
- grad_ln_bias: float32 [768, 4], P('dp')
- grad_attn_in: float32 [768, 2, 2304], P('dp')
- grad_attn_out: float32 [768, 2, 768], P('dp')
- grad_ffn_in: float32 [768, 3072], P('dp')
- grad_ffn_out: float32 [3072, 768], P('dp')
- grad_router: float32 [768, 8], P('dp')
- grad_expert_in: float32 [8, 768, 3072], P('expert', 'dp')
- grad_expert_out: float32 [8, 3072, 768], P('expert', 'dp')
Inputs may be any that keep to these rules, and one draw needn't show every extreme that they name: `doc_lengths`: the 4 lengths of one device sum to 128. `assign`: every expert is named by some token.
All inputs are finite; a program needn't handle non-finite values.
Results may differ from a plain program's by a relative error of at most 0.022.
Values may be sent and summed in bfloat16 or wider, within the bound.
A program may use at most 320 MiB of HBM per device.

v0:
```python
import jax
import jax.numpy as jnp
from jax import lax
from jax.sharding import PartitionSpec as P

HEADS = 12
HEAD_DIM = 64
LONG_DEV = 256


epsilon = 1e-05
balance_weight = 0.01
masked_score = -1e30


def exact_gelu(values):
    return jax.nn.gelu(values, approximate=False)


def gelu_backward(hidden, upstream):
    _, pullback = jax.vjp(exact_gelu, hidden)
    return pullback(upstream)[0]


def norm_forward(stream, norm_gain, norm_shift):
    center = stream - jnp.mean(stream, axis=-1, keepdims=True)
    inverse = lax.rsqrt(jnp.mean(center * center, axis=-1, keepdims=True) + epsilon)
    unit_rows = center * inverse
    return (unit_rows * norm_gain + norm_shift, unit_rows, inverse)


def norm_backward(unit_rows, inverse, norm_gain, upstream):
    scaled = upstream * norm_gain
    inner = (
        scaled
        - jnp.mean(scaled, axis=-1, keepdims=True)
        - unit_rows * jnp.mean(scaled * unit_rows, axis=-1, keepdims=True)
    )
    return (inverse * inner, jnp.sum(upstream * unit_rows, axis=0), jnp.sum(upstream, axis=0))


def as_heads(flat_rows):
    return flat_rows.reshape(flat_rows.shape[0], HEADS, HEAD_DIM)


def block_scores(queries, key_rows, allowed):
    scores = jnp.einsum(
        "qhd,khd->qhk", queries, as_heads(key_rows), preferred_element_type=jnp.float32
    ) * HEAD_DIM ** (-0.5)
    return jnp.where(allowed[:, None, :], scores, masked_score)


def long_allowed(layout, first_row, row_count):
    is_long, position = layout
    key_place = first_row + jnp.arange(row_count, dtype=jnp.int32)
    return is_long[:, None] & (key_place[None, :] <= position[:, None])


def fold_block(running, queries, key_rows, value_rows, allowed):
    running_top, running_total, weighted = running
    scores = block_scores(queries, key_rows, allowed)
    new_top = jnp.maximum(running_top, jnp.max(scores, axis=-1))
    factor = jnp.exp(running_top - new_top)
    weights = jnp.where(allowed[:, None, :], jnp.exp(scores - new_top[..., None]), 0.0)
    running_total = running_total * factor + jnp.sum(weights, axis=-1)
    weighted = weighted * factor[..., None] + jnp.einsum(
        "qhk,khd->qhd",
        weights.astype(jnp.bfloat16),
        as_heads(value_rows),
        preferred_element_type=jnp.float32,
    )
    return (new_top, running_total, weighted)


def score_grads(queries, grad_heads, log_total, row_delta, block_keys, block_values, allowed):
    scores = block_scores(queries, block_keys, allowed)
    probs_block = jnp.where(allowed[:, None, :], jnp.exp(scores - log_total[..., None]), 0.0)
    grad_probs = jnp.einsum(
        "qhd,khd->qhk", grad_heads, as_heads(block_values), preferred_element_type=jnp.float32
    )
    grad_scores = (probs_block * (grad_probs - row_delta[..., None])).astype(jnp.bfloat16)
    return (probs_block.astype(jnp.bfloat16), grad_scores)


def attend_forward(normed_low, weight_in, layout, short_allowed):
    model_width = normed_low.shape[1]
    row_count = normed_low.shape[0]
    mixed = jnp.dot(normed_low, weight_in, preferred_element_type=jnp.float32).astype(jnp.bfloat16)
    queries = as_heads(mixed[:, :model_width])
    key_rows = mixed[:, model_width : 2 * model_width]
    value_rows = mixed[:, 2 * model_width :]
    running = (
        jnp.full((row_count, HEADS), masked_score, jnp.float32),
        jnp.zeros((row_count, HEADS), jnp.float32),
        jnp.zeros((row_count, HEADS, HEAD_DIM), jnp.float32),
    )
    running = fold_block(
        running, queries, key_rows[LONG_DEV:], value_rows[LONG_DEV:], short_allowed
    )
    long_keys = key_rows[:LONG_DEV]
    long_values = value_rows[:LONG_DEV]
    key_piece = (
        lax.all_gather(long_keys, "dp", axis=0, tiled=True),
        lax.all_gather(long_values, "dp", axis=0, tiled=True),
    )
    running = fold_block(
        running,
        queries,
        key_piece[0],
        key_piece[1],
        long_allowed(layout, jnp.int32(0), key_piece[0].shape[0]),
    )
    running_top, running_total, weighted = running
    context = (weighted / running_total[..., None]).reshape(row_count, model_width)
    return (mixed, context, running_top + jnp.log(running_total), None)


def attend_backward(mixed, context, log_total, gathered, grad_context, layout, short_allowed):
    model_width = context.shape[1]
    row_count = context.shape[0]
    queries = as_heads(mixed[:, :model_width])
    key_rows = mixed[:, model_width : 2 * model_width]
    value_rows = mixed[:, 2 * model_width :]
    grad_heads = as_heads(grad_context)
    row_delta = jnp.sum(grad_heads.astype(jnp.float32) * as_heads(context), axis=-1)
    head_scale = HEAD_DIM ** (-0.5)
    short_probs, short_scores = score_grads(
        queries,
        grad_heads,
        log_total,
        row_delta,
        key_rows[LONG_DEV:],
        value_rows[LONG_DEV:],
        short_allowed,
    )
    grad_query = (
        jnp.einsum(
            "qhk,khd->qhd",
            short_scores,
            as_heads(key_rows[LONG_DEV:]),
            preferred_element_type=jnp.float32,
        )
        * head_scale
    )
    short_count = row_count - LONG_DEV
    short_key_grad = (
        jnp.einsum("qhk,qhd->khd", short_scores, queries, preferred_element_type=jnp.float32)
        * head_scale
    ).reshape(short_count, model_width)
    short_value_grad = jnp.einsum(
        "qhk,qhd->khd", short_probs, grad_heads, preferred_element_type=jnp.float32
    ).reshape(short_count, model_width)
    gathered = (
        lax.all_gather(key_rows[:LONG_DEV], "dp", axis=0, tiled=True),
        lax.all_gather(value_rows[:LONG_DEV], "dp", axis=0, tiled=True),
    )
    long_count = gathered[0].shape[0]

    def visit(block_step, partial_state):
        query_sum, key_terms, value_terms = partial_state
        first_row = block_step * LONG_DEV
        block_keys = lax.dynamic_slice_in_dim(gathered[0], first_row, LONG_DEV, 0)
        block_values = lax.dynamic_slice_in_dim(gathered[1], first_row, LONG_DEV, 0)
        probs_low, grad_scores = score_grads(
            queries,
            grad_heads,
            log_total,
            row_delta,
            block_keys,
            block_values,
            long_allowed(layout, first_row, LONG_DEV),
        )
        more_query = (
            jnp.einsum(
                "qhk,khd->qhd",
                grad_scores,
                as_heads(block_keys),
                preferred_element_type=jnp.float32,
            )
            * head_scale
        )
        more_key = (
            jnp.einsum("qhk,qhd->khd", grad_scores, queries, preferred_element_type=jnp.float32)
            * head_scale
        ).reshape(LONG_DEV, model_width)
        more_value = jnp.einsum(
            "qhk,qhd->khd", probs_low, grad_heads, preferred_element_type=jnp.float32
        ).reshape(LONG_DEV, model_width)
        return (
            query_sum + more_query,
            lax.dynamic_update_slice_in_dim(key_terms, more_key, first_row, 0),
            lax.dynamic_update_slice_in_dim(value_terms, more_value, first_row, 0),
        )

    start_state = (
        grad_query,
        jnp.zeros((long_count, model_width), jnp.float32),
        jnp.zeros((long_count, model_width), jnp.float32),
    )
    grad_query, key_terms, value_terms = lax.fori_loop(
        0, long_count // LONG_DEV, visit, start_state
    )
    own_keys, own_values = (
        lax.psum_scatter(
            key_terms.astype(jnp.bfloat16), "dp", scatter_dimension=0, tiled=True
        ).astype(jnp.float32),
        lax.psum_scatter(
            value_terms.astype(jnp.bfloat16), "dp", scatter_dimension=0, tiled=True
        ).astype(jnp.float32),
    )
    grad_keys = jnp.concatenate([own_keys, short_key_grad], axis=0)
    grad_values = jnp.concatenate([own_values, short_value_grad], axis=0)
    return jnp.concatenate(
        [grad_query.reshape(row_count, model_width), grad_keys, grad_values], axis=1
    ).astype(jnp.bfloat16)


def attention_forward(stream, norm_gain, norm_shift, weight_in, weight_out, layout, short_allowed):
    normed, unit_rows, inverse = norm_forward(stream, norm_gain, norm_shift)
    normed_low = normed.astype(jnp.bfloat16)
    mixed, context, log_total, gathered = attend_forward(
        normed_low, weight_in, layout, short_allowed
    )
    context_low = context.astype(jnp.bfloat16)
    stream_next = stream + jnp.dot(context_low, weight_out, preferred_element_type=jnp.float32)
    return (
        stream_next,
        (unit_rows, inverse, normed_low, mixed, context, context_low, log_total, gathered),
    )


def attention_backward(
    upstream, kept_state, norm_gain, weight_in, weight_out, layout, short_allowed
):
    unit_rows, inverse, normed_low, mixed, context, context_low, log_total, gathered = kept_state
    upstream_low = upstream.astype(jnp.bfloat16)
    grad_out_weight = jnp.einsum(
        "td,te->de", context_low, upstream_low, preferred_element_type=jnp.float32
    )
    grad_context = jnp.einsum(
        "te,de->td", upstream_low, weight_out, preferred_element_type=jnp.float32
    ).astype(jnp.bfloat16)
    grad_mixed = attend_backward(
        mixed, context, log_total, gathered, grad_context, layout, short_allowed
    )
    grad_in_weight = jnp.einsum(
        "td,te->de", normed_low, grad_mixed, preferred_element_type=jnp.float32
    )
    grad_normed = jnp.einsum("te,de->td", grad_mixed, weight_in, preferred_element_type=jnp.float32)
    grad_stream, grad_gain, grad_shift = norm_backward(unit_rows, inverse, norm_gain, grad_normed)
    return (upstream + grad_stream, grad_in_weight, grad_out_weight, grad_gain, grad_shift)


def ffn_forward(stream, norm_gain, norm_shift, weight_in, weight_out):
    normed, unit_rows, inverse = norm_forward(stream, norm_gain, norm_shift)
    normed_low = normed.astype(jnp.bfloat16)
    hidden = jnp.dot(normed_low, weight_in, preferred_element_type=jnp.float32)
    active = exact_gelu(hidden).astype(jnp.bfloat16)
    stream_next = stream + jnp.dot(active, weight_out, preferred_element_type=jnp.float32)
    return (stream_next, (unit_rows, inverse, normed_low, hidden, active))


def ffn_backward(upstream, kept_state, norm_gain, weight_in, weight_out):
    unit_rows, inverse, normed_low, hidden, active = kept_state
    upstream_low = upstream.astype(jnp.bfloat16)
    grad_out_weight = jnp.einsum(
        "tf,td->fd", active, upstream_low, preferred_element_type=jnp.float32
    )
    grad_active = jnp.einsum(
        "td,fd->tf", upstream_low, weight_out, preferred_element_type=jnp.float32
    )
    grad_hidden = gelu_backward(hidden, grad_active).astype(jnp.bfloat16)
    grad_in_weight = jnp.einsum(
        "td,tf->df", normed_low, grad_hidden, preferred_element_type=jnp.float32
    )
    grad_normed = jnp.einsum(
        "tf,df->td", grad_hidden, weight_in, preferred_element_type=jnp.float32
    )
    grad_stream, grad_gain, grad_shift = norm_backward(unit_rows, inverse, norm_gain, grad_normed)
    return (upstream + grad_stream, grad_in_weight, grad_out_weight, grad_gain, grad_shift)


def mixture_forward(stream, norm_gain, norm_shift, router, expert_in, expert_out, assign_ids):
    normed, unit_rows, inverse = norm_forward(stream, norm_gain, norm_shift)
    normed_low = normed.astype(jnp.bfloat16)
    model_width = stream.shape[1]
    row_count = stream.shape[0]
    experts_all = router.shape[1]
    capacity = (5 * row_count + 4 * experts_all - 1) // (4 * experts_all)
    logits = jnp.dot(normed_low, router, preferred_element_type=jnp.float32)
    expert_numbers = jnp.arange(experts_all, dtype=jnp.int32)
    chosen_hot = (assign_ids[:, None] == expert_numbers[None, :]).astype(jnp.float32)
    gate_value = jax.nn.sigmoid(jnp.sum(logits * chosen_hot, axis=-1))
    counts, gate_sums = lax.psum(
        (jnp.sum(chosen_hot, axis=0), jnp.sum(gate_value[:, None] * chosen_hot, axis=0)),
        ("dp", "expert"),
    )
    tokens_all = row_count * lax.axis_size("dp") * lax.axis_size("expert")
    token_share = counts / tokens_all
    balance = experts_all * jnp.sum((token_share - 1.0 / experts_all) * (gate_sums / tokens_all))
    hot_count = (assign_ids[:, None] == expert_numbers[None, :]).astype(jnp.int32)
    before = jnp.cumsum(hot_count, axis=0) - hot_count
    slot_place = jnp.sum(before * hot_count, axis=-1)
    slot_index = jnp.where(slot_place < capacity, assign_ids * capacity + slot_place, -1)
    dispatch = (
        slot_index[:, None] == jnp.arange(experts_all * capacity, dtype=jnp.int32)[None, :]
    ).astype(jnp.bfloat16)
    outgoing = jnp.einsum(
        "tc,td->cd", dispatch, normed_low, preferred_element_type=jnp.float32
    ).astype(jnp.bfloat16)
    outgoing = outgoing.reshape(experts_all, capacity, model_width)
    incoming = lax.all_to_all(outgoing, "expert", split_axis=0, concat_axis=0, tiled=True)
    slot_count = incoming.shape[1]
    grouped = incoming.reshape(-1, expert_in.shape[0], slot_count, model_width)
    hidden = jnp.einsum("sjcd,jdf->sjcf", grouped, expert_in, preferred_element_type=jnp.float32)
    active = exact_gelu(hidden).astype(jnp.bfloat16)
    result = jnp.einsum(
        "sjcf,jfd->sjcd", active, expert_out, preferred_element_type=jnp.float32
    ).astype(jnp.bfloat16)
    homeward = lax.all_to_all(
        result.reshape(incoming.shape), "expert", split_axis=0, concat_axis=0, tiled=True
    )
    gathered = jnp.dot(
        dispatch,
        homeward.reshape(experts_all * capacity, model_width),
        preferred_element_type=jnp.float32,
    )
    stream_next = stream + gate_value[:, None] * gathered
    kept_state = (
        unit_rows,
        inverse,
        normed_low,
        gate_value,
        token_share,
        tokens_all,
        chosen_hot,
        dispatch,
        gathered,
        incoming,
    )
    return (stream_next, balance, kept_state)


def mixture_backward(upstream, kept_state, norm_gain, router, expert_in, expert_out):
    (
        unit_rows,
        inverse,
        normed_low,
        gate_value,
        token_share,
        tokens_all,
        chosen_hot,
        dispatch,
        gathered,
        arrived,
    ) = kept_state
    model_width = upstream.shape[1]
    experts_all = router.shape[1]
    grad_gate = jnp.sum(upstream * gathered, axis=-1)
    grad_return = (gate_value[:, None] * upstream).astype(jnp.bfloat16)
    outgoing = jnp.einsum(
        "tc,td->cd", dispatch, grad_return, preferred_element_type=jnp.float32
    ).astype(jnp.bfloat16)
    outgoing = outgoing.reshape(experts_all, -1, model_width)
    incoming = lax.all_to_all(outgoing, "expert", split_axis=0, concat_axis=0, tiled=True)
    slot_count = incoming.shape[1]
    grouped_grad = incoming.reshape(-1, expert_in.shape[0], slot_count, model_width)
    grouped_rows = arrived.reshape(-1, expert_in.shape[0], slot_count, model_width)
    hidden = jnp.einsum(
        "sjcd,jdf->sjcf", grouped_rows, expert_in, preferred_element_type=jnp.float32
    )
    active = exact_gelu(hidden).astype(jnp.bfloat16)
    grad_out_weight = jnp.einsum(
        "sjcf,sjcd->jfd", active, grouped_grad, preferred_element_type=jnp.float32
    )
    grad_active = jnp.einsum(
        "sjcd,jfd->sjcf", grouped_grad, expert_out, preferred_element_type=jnp.float32
    )
    grad_hidden = gelu_backward(hidden, grad_active).astype(jnp.bfloat16)
    grad_in_weight = jnp.einsum(
        "sjcd,sjcf->jdf", grouped_rows, grad_hidden, preferred_element_type=jnp.float32
    )
    grad_rows = jnp.einsum(
        "sjcf,jdf->sjcd", grad_hidden, expert_in, preferred_element_type=jnp.float32
    ).astype(jnp.bfloat16)
    homeward = lax.all_to_all(
        grad_rows.reshape(incoming.shape), "expert", split_axis=0, concat_axis=0, tiled=True
    )
    grad_normed = jnp.dot(
        dispatch, homeward.reshape(-1, model_width), preferred_element_type=jnp.float32
    )
    share_weight = balance_weight * experts_all * (token_share - 1.0 / experts_all) / tokens_all
    grad_gate = grad_gate + jnp.sum(chosen_hot * share_weight[None, :], axis=-1)
    grad_chosen = grad_gate * gate_value * (1.0 - gate_value)
    grad_logits = grad_chosen[:, None] * chosen_hot
    router_float = router.astype(jnp.float32)
    grad_router = jnp.einsum(
        "td,te->de", normed_low.astype(jnp.float32), grad_logits, precision=lax.Precision.HIGHEST
    )
    grad_normed = grad_normed + jnp.einsum(
        "te,de->td", grad_logits, router_float, precision=lax.Precision.HIGHEST
    )
    grad_stream, grad_gain, grad_shift = norm_backward(unit_rows, inverse, norm_gain, grad_normed)
    return (
        upstream + grad_stream,
        grad_in_weight,
        grad_out_weight,
        grad_router,
        grad_gain,
        grad_shift,
    )


def shards(
    tokens,
    doc_lengths,
    assign,
    ln_gain,
    ln_bias,
    attn_in,
    attn_out,
    ffn_in,
    ffn_out,
    router,
    expert_in,
    expert_out,
    cotangent,
):
    stream_first = tokens[0].astype(jnp.float32)
    row_count = stream_first.shape[0]
    row_index = jnp.arange(row_count, dtype=jnp.int32)
    is_long = row_index < LONG_DEV
    layout = (is_long, lax.axis_index("dp") * LONG_DEV + row_index)
    doc_ends = jnp.cumsum(doc_lengths[0, 0])
    short_place = jnp.arange(row_count - LONG_DEV, dtype=jnp.int32)
    short_ids = jnp.sum((short_place[:, None] >= doc_ends[None, :]).astype(jnp.int32), axis=-1)
    row_docs = jnp.concatenate([jnp.full((LONG_DEV,), -1, jnp.int32), short_ids])
    short_allowed = (row_docs[:, None] == short_ids[None, :]) & (
        short_place[None, :] + LONG_DEV <= row_index[:, None]
    )
    stream_one, kept_one = attention_forward(
        stream_first,
        ln_gain[:, 0],
        ln_bias[:, 0],
        attn_in[:, 0],
        attn_out[:, 0],
        layout,
        short_allowed,
    )
    stream_two, kept_two = ffn_forward(stream_one, ln_gain[:, 1], ln_bias[:, 1], ffn_in, ffn_out)
    stream_three, kept_three = attention_forward(
        stream_two,
        ln_gain[:, 2],
        ln_bias[:, 2],
        attn_in[:, 1],
        attn_out[:, 1],
        layout,
        short_allowed,
    )
    stream_four, balance, kept_four = mixture_forward(
        stream_three, ln_gain[:, 3], ln_bias[:, 3], router, expert_in, expert_out, assign[0, :, 0]
    )
    output = stream_four.astype(jnp.bfloat16)[None]
    upstream = cotangent[0].astype(jnp.float32)
    upstream, expert_in_grad, expert_out_grad, router_grad, gain_three, shift_three = (
        mixture_backward(upstream, kept_four, ln_gain[:, 3], router, expert_in, expert_out)
    )
    upstream, second_in_grad, second_out_grad, gain_two, shift_two = attention_backward(
        upstream, kept_three, ln_gain[:, 2], attn_in[:, 1], attn_out[:, 1], layout, short_allowed
    )
    upstream, ffn_in_grad, ffn_out_grad, gain_one, shift_one = ffn_backward(
        upstream, kept_two, ln_gain[:, 1], ffn_in, ffn_out
    )
    upstream, first_in_grad, first_out_grad, gain_zero, shift_zero = attention_backward(
        upstream, kept_one, ln_gain[:, 0], attn_in[:, 0], attn_out[:, 0], layout, short_allowed
    )
    grad_tokens = upstream.astype(jnp.bfloat16)[None]
    attn_in_grad = jnp.stack([first_in_grad, second_in_grad], axis=1)
    attn_out_grad = jnp.stack([first_out_grad, second_out_grad], axis=1)
    gain_grad = jnp.stack([gain_zero, gain_one, gain_two, gain_three], axis=1)
    shift_grad = jnp.stack([shift_zero, shift_one, shift_two, shift_three], axis=1)
    copied_grads = (
        attn_in_grad,
        attn_out_grad,
        ffn_in_grad,
        ffn_out_grad,
        router_grad,
        gain_grad,
        shift_grad,
    )
    ranks = lax.axis_size("dp") * lax.axis_size("expert")
    flat = [initial.reshape(ranks, -1) for initial in copied_grads]
    shares = (
        lax.psum_scatter(flat[0], ("dp", "expert"), scatter_dimension=0, tiled=True),
        lax.psum_scatter(flat[1], ("dp", "expert"), scatter_dimension=0, tiled=True),
        lax.psum_scatter(flat[2], ("dp", "expert"), scatter_dimension=0, tiled=True),
        lax.psum_scatter(flat[3], ("dp", "expert"), scatter_dimension=0, tiled=True),
        lax.psum_scatter(flat[4], ("dp", "expert"), scatter_dimension=0, tiled=True),
        lax.psum_scatter(flat[5], ("dp", "expert"), scatter_dimension=0, tiled=True),
        lax.psum_scatter(flat[6], ("dp", "expert"), scatter_dimension=0, tiled=True),
    )
    filled = (
        lax.all_gather(shares[0].astype(jnp.bfloat16), "expert", axis=0, tiled=True).astype(
            jnp.float32
        ),
        lax.all_gather(shares[1].astype(jnp.bfloat16), "expert", axis=0, tiled=True).astype(
            jnp.float32
        ),
        lax.all_gather(shares[2].astype(jnp.bfloat16), "expert", axis=0, tiled=True).astype(
            jnp.float32
        ),
        lax.all_gather(shares[3].astype(jnp.bfloat16), "expert", axis=0, tiled=True).astype(
            jnp.float32
        ),
        lax.all_gather(shares[4].astype(jnp.bfloat16), "expert", axis=0, tiled=True).astype(
            jnp.float32
        ),
        lax.all_gather(shares[5].astype(jnp.bfloat16), "expert", axis=0, tiled=True).astype(
            jnp.float32
        ),
        lax.all_gather(shares[6].astype(jnp.bfloat16), "expert", axis=0, tiled=True).astype(
            jnp.float32
        ),
    )
    summed = [
        collected.reshape((initial.shape[0] // lax.axis_size("dp"),) + initial.shape[1:])
        for initial, collected in zip(copied_grads, filled)
    ]
    expert_in_sum, expert_out_sum = (
        lax.psum_scatter(
            expert_in_grad.astype(jnp.bfloat16), "dp", scatter_dimension=1, tiled=True
        ).astype(jnp.float32),
        lax.psum_scatter(
            expert_out_grad.astype(jnp.bfloat16), "dp", scatter_dimension=1, tiled=True
        ).astype(jnp.float32),
    )
    return (
        output,
        balance,
        grad_tokens,
        summed[5],
        summed[6],
        summed[0],
        summed[1],
        summed[2],
        summed[3],
        summed[4],
        expert_in_sum,
        expert_out_sum,
    )


def solution(mesh):
    return jax.shard_map(
        shards,
        mesh=mesh,
        in_specs=(
            P("expert", "dp", None),
            P("expert", "dp", None),
            P("expert", "dp", None),
            P(),
            P(),
            P(),
            P(),
            P(),
            P(),
            P(),
            P("expert", None, None),
            P("expert", None, None),
            P("expert", "dp", None),
        ),
        out_specs=(
            P("expert", "dp", None),
            P(),
            P("expert", "dp", None),
            P("dp", None),
            P("dp", None),
            P("dp", None, None),
            P("dp", None, None),
            P("dp", None),
            P("dp", None),
            P("dp", None),
            P("expert", "dp", None),
            P("expert", "dp", None),
        ),
        check_vma=False,
    )
```

profile of v0, /device:TPU:0, one launch (start us, length us, event | category | flops | bytes accessed | tf_op | source)
XLA Modules:
  0.0 1507.9 jit_solution(13576753208155425966)
XLA Ops:
  9.9 14.9 fusion.248
  31.5 5.4 fusion.249
  41.0 10.8 all-gather.15.cloned.1.call-done
  51.8 2.8 copy.168
  54.6 11.1 fusion.36
  65.7 10.9 fusion.38
  79.3 10.3 fusion.106
  94.1 16.0 %multiply_convert_fusion = (bf16[384,3072]{1,0:T(8,128)(2,1)S(1)}, f32[384,3072]{1,0:T(8,128)}, f32[384,3072]{1,0:T(8,128)}) fusion(bf16[768,3072]{1,0:T(8,128)(2,1)} %param.24, f32[384,768]{1,0:T(8,128)S(1)} %get-tuple-element.725, f32[768]{0:T(1024)S(1)} %get-tuple-element.629, f32[768]{0:T(1024)S(1)} %get-tuple-element.745, ...), kind=kOutput, calls=%fused_computation.112 | convolution fusion | flops 1890091008 | bytes 17703936 | tf_op jit(solution)/shard_map/dot_general | solution.py:257
  121.2 14.0 all-gather.19.cloned.1.call-done
  137.8 11.1 fusion.37
  148.9 10.9 fusion.40
  159.9 2.6 copy.178
  162.5 9.8 fusion.109
  181.9 5.5 all-to-all-start
  190.0 2.7 convolution_convert_fusion.2
  194.8 13.3 all-to-all-done
  208.1 4.2 all-to-all-start.2
  212.4 5.1 fusion.73
  217.5 2.6 copy-done.31
  220.1 19.0 %fusion.127 = bf16[8,60,768]{2,1,0:T(8,128)(2,1)} fusion(bf16[1,3072,768]{2,1,0:T(8,128)(2,1)} %param.28, f32[8,60,3072]{2,1,0:T(8,128)S(1)} %fusion.73), kind=kOutput, calls=%fused_computation.195 | convolution fusion | flops 2361139200 | bytes 11354112 | tf_op jit(solution)/shard_map/sjcf,jfd->sjcd/dot_general | solution.py:317
  239.1 5.9 all-to-all-start.1
  245.0 18.3 %fusion.54 = bf16[8,1,60,3072]{3,2,0,1:T(8,128)(2,1)S(1)} fusion(f32[8,60,3072]{2,1,0:T(8,128)} %copy-done.31, bf16[8,60,768]{2,1,0:T(8,128)(2,1)} %all-to-all-done.2, bf16[1,3072,768]{2,1,0:T(8,128)(2,1)} %param.28), kind=kOutput, calls=%fused_computation.81 | convolution fusion | flops 2371092480 | bytes 14303232 | tf_op jit(solution)/shard_map/sjcd,jfd->sjcf/dot_general | solution.py:376
  265.0 5.9 fusion.122
  270.9 6.0 all-to-all-start.3
  277.6 40.7 %psum.14 = f32[8]{0:T(128)} all-reduce(f32[8]{0:T(128)} %convert_reduce_fusion.5), channel_id=1, replica_groups=mesh['dp'=4,'expert'=8] {'dp','expert'}, use_global_device_ids=true, to_apply=%region_23.24 | all-reduce | flops 8 | bytes 64 | tf_op jit(solution)/shard_map/psum | solution.py:294
  322.4 2.8 fusion.146
  330.3 3.1 multiply_reduce_fusion
  345.6 34.6 %while.36 = (s32[]{:T(128)}, f32[384,12,64]{0,2,1:T(8,128)S(1)}, bf16[1024,768]{0,1:T(8,128)(2,1)}, bf16[1024,768]{0,1:T(8,128)(2,1)S(1)}, bf16[1024,768]{0,1:T(...) while((s32[]{:T(128)}, f32[384,12,64]{0,2,1:T(8,128)S(1)}, ...), condition=%wide.region_33.34_spmd.clone, body=%wide.region_32.33_spmd.clone.sunk | while | flops 770311168 | bytes 33779688 | solution.py:200
  385.9 24.7 %reduce-scatter.9.cloned.1.call-done = bf16[256,768]{0,1:T(8,128)(2,1)} async-done(((bf16[1024,768]{0,1:T(8,128)(2,1)}), bf16[256,768]{0,1:T(8,128)(2,1)}) %reduce-scatter.9.cloned.1.call-update) | async-done | bytes 393232 | tf_op jit(solution)/shard_map/reduce_scatter | solution.py:207
  410.6 31.3 %reduce-scatter.7.cloned.1.call-done = bf16[256,768]{0,1:T(8,128)(2,1)} async-done(((bf16[1024,768]{0,1:T(8,128)(2,1)}), bf16[256,768]{0,1:T(8,128)(2,1)}) %reduce-scatter.7.cloned.1.call-update) | async-done | bytes 393232 | tf_op jit(solution)/shard_map/reduce_scatter | solution.py:204
  442.0 6.1 multiply_reduce_fusion.1
  448.7 6.2 add_convert_fusion
  456.4 2.9 multiply_reduce_fusion.2
  472.2 35.0 %while.37 = (s32[]{:T(128)}, f32[384,12,64]{0,2,1:T(8,128)S(1)}, bf16[1024,768]{0,1:T(8,128)(2,1)}, bf16[1024,768]{0,1:T(8,128)(2,1)}, bf16[1024,768]{0,1:T(8,12...) while((s32[]{:T(128)}, f32[384,12,64]{0,2,1:T(8,128)S(1)}, ...), condition=%wide.region_42.43_spmd.clone, body=%wide.region_41.42_spmd.clone.sunk | while | flops 770311168 | bytes 33853448 | solution.py:200
  508.3 7.0 fusion.80
  515.3 18.7 %fusion.81 = bf16[1,3072,768]{2,1,0:T(8,128)(2,1)} fusion(bf16[8,60,768]{2,1,0:T(8,128)(2,1)} %all-to-all-done.2, f32[8,60,3072]{2,1,0:T(8,128)} %copy-done.31), kind=kOutput, calls=%fused_computation.127 | convolution fusion | flops 2363129856 | bytes 11354112 | tf_op jit(solution)/shard_map/sjcf,sjcd->jfd/dot_general | solution.py:373
  537.3 3.6 convolution_bitcast_fusion.2
  545.4 3.3 fusion.170
  550.8 5.8 fusion.245
  556.7 5.1 fusion.200
  565.3 5.9 copy.196
  571.2 7.2 reshape.751
  578.4 8.6 reshape.754
  587.0 9.3 reshape.757
  596.4 6.5 convolution_bitcast_fusion
  603.1 7.1 fusion.137
  611.1 6.2 convolution_bitcast_fusion.1
  617.3 12.7 pad_maximum_fusion
  630.0 26.8 %copy.195 = f32[768,2,2304]{2,1,0:T(2,128)} copy(f32[768,2,2304]{2,0,1:T(8,128)} %pad_maximum_fusion) | data formatting | bytes 28311552 | tf_op jit(solution)/shard_map/stack | solution.py:478
  656.8 15.9 %reshape.748 = f32[32,110592]{1,0:T(8,128)} reshape(f32[768,2,2304]{2,1,0:T(2,128)} %copy.195) | data formatting | bytes 28311552 | tf_op jit(solution)/shard_map/reshape | solution.py:492
  672.8 604.5 %all-reduce.10 = (f32[8]{0:T(128)S(1)}, bf16[32,96]{1,0:T(8,128)(2,1)S(1)}, bf16[32,96]{1,0:T(8,128)(2,1)S(1)}, bf16[32,110592]{1,0:T(8,128)(2,1)}, bf16[32,3686...) all-reduce(f32[8]{0:T(128)S(1)} %copy-done.127, ...), channel_id=1, replica_groups=mesh['dp'=4,'expert'=8] {'dp','expert'}, use_global_device_ids=true, to_apply=%region_25.26 | all-reduce | flops 9449480 | bytes 56696896 | tf_op jit(solution)/shard_map/psum | solution.py:294
  1282.0 2.7 fusion.191
  1286.0 19.3 %all-gather.6 = bf16[8,1,192]{2,1,0:T(2,128)(2,1)S(1)} all-gather(bf16[1,1,192]{2,1,0:T(2,128)(2,1)S(1)} %fusion.224), channel_id=1, replica_groups=mesh['dp'=4,'expert'=8] {'expert'}, dimensions={0}, use_global_device_ids=true | all-gather | bytes 3456 | tf_op jit(solution)/shard_map/all_gather | solution.py:515
  1306.1 16.4 %all-gather = bf16[8,1,96]{2,1,0:T(2,128)(2,1)S(1)} all-gather(bf16[1,1,96]{2,1,0:T(2,128)(2,1)S(1)} %fusion.226), channel_id=1, replica_groups=mesh['dp'=4,'expert'=8] {'expert'}, dimensions={0}, use_global_device_ids=true | all-gather | bytes 1728 | tf_op jit(solution)/shard_map/all_gather | solution.py:518
  1323.3 18.1 %all-gather.1 = bf16[8,1,96]{2,1,0:T(2,128)(2,1)S(1)} all-gather(bf16[1,1,96]{2,1,0:T(2,128)(2,1)S(1)} %fusion.228), channel_id=1, replica_groups=mesh['dp'=4,'expert'=8] {'expert'}, dimensions={0}, use_global_device_ids=true | all-gather | bytes 1728 | tf_op jit(solution)/shard_map/all_gather | solution.py:521
  1342.2 36.1 %all-gather.3 = bf16[8,1,36864]{2,1,0:T(2,128)(2,1)S(1)} all-gather(bf16[1,1,36864]{2,1,0:T(2,128)(2,1)S(1)} %fusion.209), channel_id=1, replica_groups=mesh['dp'=4,'expert'=8] {'expert'}, dimensions={0}, use_global_device_ids=true | all-gather | bytes 663552 | tf_op jit(solution)/shard_map/all_gather | solution.py:506
  1378.4 3.5 convert_reduce_fusion.4
  1387.7 2.9 convert_element_type.302
  1390.6 2.8 convert_element_type.305
  1393.5 9.0 convert_reduce_fusion.2
  1404.4 8.6 convert_reduce_fusion.1
  1414.8 43.4 %all-gather.23.cloned.1.call-done = bf16[8,1,110592]{2,1,0:T(2,128)(2,1)} async-done(((bf16[1,1,110592]{2,1,0:T(2,128)(2,1)}), bf16[8,1,110592]{2,1,0:T(2,128)(2,1)}) %all-gather.23.cloned.1.call-update) | async-done | bytes 1769488 | tf_op jit(solution)/shard_map/all_gather | solution.py:503
  1458.2 37.1 %convert_reduce_fusion = f32[8,110592]{1,0:T(8,128)S(1)} fusion(bf16[8,1,110592]{2,1,0:T(2,128)(2,1)} %all-gather.23.cloned.1.call-done), kind=kLoop, calls=%fused_computation.132 | loop fusion | flops 884736 | bytes 5308416 | tf_op jit(solution)/shard_map/reshape | solution.py:526
  1495.3 4.8 reshape.769
  (587 shorter events, 193.1 us)
Async XLA Ops:
  7.2 180.3 %copy-start = (bf16[768,8]{0,1:T(8,128)(2,1)S(1)}, bf16[768,8]{0,1:T(8,128)(2,1)}, u32[]{:S(2)}) copy-start(bf16[768,8]{0,1:T(8,128)(2,1)} %param.26) | copy-start | bytes 36868
  7.2 44.6 %all-gather.15.cloned.1.call-start = ((), (), s32[]{:S(2)}) async-start(), calls=%async_computation.10 | async-start | bytes 1966080 | tf_op jit(solution)/shard_map/all_gather | solution.py:103
  8.5 17.2 %copy-start.91 = (f32[384]{0:T(512)}, f32[384]{0:T(512)S(1)}, u32[]{:S(2)}) copy-start(f32[384]{0:T(512)S(1)} %broadcast_multiply_fusion.11) | copy-start | bytes 4612
  9.9 15.8 %copy-start.115 = (f32[384]{0:T(512)}, f32[384]{0:T(512)S(1)}, u32[]{:S(2)}) copy-start(f32[384]{0:T(512)S(1)} %add_rsqrt_fusion.3) | copy-start | bytes 4612
  9.9 15.0 copy-start.107
  9.9 15.0 copy-start.108
  9.9 15.8 %copy-start.39 = (bf16[1,384,768]{2,1,0:T(8,128)(2,1)S(1)}, bf16[1,384,768]{2,1,0:T(8,128)(2,1)}, u32[]{:S(2)}) copy-start(bf16[1,384,768]{2,1,0:T(8,128)(2,1)} %param.17) | copy-start | bytes 1769476
  25.6 68.4 %copy-start.66 = (f32[768]{0:T(1024)}, f32[768]{0:T(1024)S(1)}, u32[]{:S(2)}) copy-start(f32[768]{0:T(1024)S(1)} %get-tuple-element.745) | copy-start | bytes 9220
  25.6 68.4 %copy-start.68 = (f32[768]{0:T(1024)}, f32[768]{0:T(1024)S(1)}, u32[]{:S(2)}) copy-start(f32[768]{0:T(1024)S(1)} %get-tuple-element.629) | copy-start | bytes 9220
  25.6 87.0 %copy-start.104 = (f32[768]{0:T(1024)}, f32[768]{0:T(1024)S(1)}, u32[]{:S(2)}) copy-start(f32[768]{0:T(1024)S(1)} %get-tuple-element.743) | copy-start | bytes 9220
  25.6 87.0 %copy-start.122 = (f32[768]{0:T(1024)}, f32[768]{0:T(1024)S(1)}, u32[]{:S(2)}) copy-start(f32[768]{0:T(1024)S(1)} %get-tuple-element.631) | copy-start | bytes 9220
  29.3 47.4 %all-gather.17.cloned.1.call-start = ((), (), s32[]{:S(2)}) async-start(), calls=%async_computation.11 | async-start | bytes 1966080 | tf_op jit(solution)/shard_map/all_gather | solution.py:104
  30.0 105.1 %all-gather.19.cloned.1.call-start = ((), (), s32[]{:S(2)}) async-start(), calls=%async_computation.12 | async-start | bytes 1966080 | tf_op jit(solution)/shard_map/all_gather | solution.py:103
  38.9 26.9 %copy-start.2 = (bf16[384,768]{0,1:T(8,128)(2,1)}, bf16[384,768]{0,1:T(8,128)(2,1)S(1)}, u32[]{:S(2)}) copy-start(bf16[384,768]{0,1:T(8,128)(2,1)S(1)} %copy.165) | copy-start | bytes 1769476
  39.0 51.7 %copy-start.47 = (pred[384,128]{0,1:T(8,128)(4,1)}, pred[384,128]{0,1:T(8,128)(4,1)S(1)}, u32[]{:S(2)}) copy-start(pred[384,128]{0,1:T(8,128)(4,1)S(1)} %fusion.208) | copy-start | bytes 147460
  39.3 40.0 %copy-start.24 = (pred[384,1024]{0,1:T(8,128)(4,1)}, pred[384,1024]{0,1:T(8,128)(4,1)S(1)}, u32[]{:S(2)}) copy-start(pred[384,1024]{0,1:T(8,128)(4,1)S(1)} %fusion.97) | copy-start | bytes 1179652
  41.0 49.7 %copy-start.6 = (f32[384,12,128]{0,2,1:T(8,128)}, f32[384,12,128]{0,2,1:T(8,128)S(1)}, u32[]{:S(2)}) copy-start(f32[384,12,128]{0,2,1:T(8,128)S(1)} %get-tuple-element.719) | copy-start | bytes 7077892
  79.3 11.4 copy-start.58
  92.3 17.7 %copy-start.64 = (bf16[384,12,64]{0,2,1:T(8,128)(2,1)}, bf16[384,12,64]{0,2,1:T(8,128)(2,1)S(1)}, u32[]{:S(2)}) copy-start(bf16[384,12,64]{0,2,1:T(8,128)(2,1)S(1)} %get-tuple-element.722) | copy-start | bytes 1769476
  93.0 17.1 %slice-start.3 = ((s8[4718592]{0:T(1024)(128)(4,1)}), s8[4194304]{0:T(1024)(128)(4,1)S(1)}, s32[]{:S(2)}) async-start(s8[4718592]{0:T(1024)(128)(4,1)} %bitcast.587), calls=%async_computation.26 | async-start | bytes 8388608
  93.0 19.6 %slice-start = ((s8[7077888]{0:T(1024)(128)(4,1)}), s8[4194304]{0:T(1024)(128)(4,1)S(1)}, s32[]{:S(2)}) async-start(s8[7077888]{0:T(1024)(128)(4,1)} %bitcast.557), calls=%async_computation.23 | async-start | bytes 8388608
  93.7 16.4 %copy-start.19 = (f32[384,768]{1,0:T(8,128)}, f32[384,768]{1,0:T(8,128)S(1)}, u32[]{:S(2)}) copy-start(f32[384,768]{1,0:T(8,128)S(1)} %get-tuple-element.725) | copy-start | bytes 3538948
  93.7 16.3 %copy-start.83 = (f32[384]{0:T(512)}, f32[384]{0:T(512)S(1)}, u32[]{:S(2)}) copy-start(f32[384]{0:T(512)S(1)} %broadcast_multiply_fusion.10) | copy-start | bytes 4612
  94.0 16.1 %copy-start.87 = (f32[384]{0:T(512)}, f32[384]{0:T(512)S(1)}, u32[]{:S(2)}) copy-start(f32[384]{0:T(512)S(1)} %add_rsqrt_fusion.2) | copy-start | bytes 4612
  94.1 16.1 %slice-start.4 = ((s8[4718592]{0:T(1024)(128)(4,1)}), s8[524288]{0:T(1024)(128)(4,1)S(1)}, s32[]{:S(2)}) async-start(s8[4718592]{0:T(1024)(128)(4,1)} %bitcast.587), calls=%async_computation.27 | async-start | bytes 1048576
  94.1 18.5 %slice-start.1 = ((s8[7077888]{0:T(1024)(128)(4,1)}), s8[2883584]{0:T(1024)(128)(4,1)S(1)}, s32[]{:S(2)}) async-start(s8[7077888]{0:T(1024)(128)(4,1)} %bitcast.557), calls=%async_computation.24 | async-start | bytes 5767168
  115.3 44.6 %all-gather.21.cloned.1.call-start = ((), (), s32[]{:S(2)}) async-start(), calls=%async_computation.13 | async-start | bytes 1966080 | tf_op jit(solution)/shard_map/all_gather | solution.py:104
  115.4 210.6 %copy-start.72 = (s32[384]{0:T(512)}, s32[384]{0:T(512)S(1)}, u32[]{:S(2)}) copy-start(s32[384]{0:T(512)S(1)} %reduce.7) | copy-start | bytes 4612
  119.4 29.5 %copy-start.4 = (bf16[384,768]{0,1:T(8,128)(2,1)}, bf16[384,768]{0,1:T(8,128)(2,1)S(1)}, u32[]{:S(2)}) copy-start(bf16[384,768]{0,1:T(8,128)(2,1)S(1)} %copy.174) | copy-start | bytes 1769476
  119.4 18.4 %copy-start.25 = (pred[384,1024]{0,1:T(8,128)(4,1)S(1)}, pred[384,1024]{0,1:T(8,128)(4,1)}, u32[]{:S(2)}) copy-start(pred[384,1024]{0,1:T(8,128)(4,1)} %copy-done.24) | copy-start | bytes 1179652
  121.2 220.1 %copy-start.8 = (f32[384,12,128]{0,2,1:T(8,128)}, f32[384,12,128]{0,2,1:T(8,128)S(1)}, u32[]{:S(2)}) copy-start(f32[384,12,128]{0,2,1:T(8,128)S(1)} %get-tuple-element.730) | copy-start | bytes 7077892
  162.5 10.9 copy-start.59
  181.9 26.2 %all-to-all-start = ((bf16[8,60,768]{2,1,0:T(8,128)(2,1)}), bf16[8,60,768]{2,1,0:T(8,128)(2,1)}, u32[]{:S(2)}, u32[]{:S(2)}) async-start(bf16[8,60,768]{2,1,0:T(8,128)(2,1)} %reshape.726), calls=%async_computation | async-start | bytes 1572864 | tf_op jit(solution)/shard_map/all_to_all | solution.py:312
  208.1 30.9 %all-to-all-start.2 = ((bf16[8,60,768]{2,1,0:T(8,128)(2,1)}), bf16[8,60,768]{2,1,0:T(8,128)(2,1)}, u32[]{:S(2)}, u32[]{:S(2)}) async-start(bf16[8,60,768]{2,1,0:T(8,128)(2,1)} %reshape.731), calls=%async_computation.2 | async-start | bytes 1572864 | tf_op jit(solution)/shard_map/all_to_all | solution.py:365
  239.1 31.8 %all-to-all-start.1 = ((bf16[8,60,768]{2,1,0:T(8,128)(2,1)}), bf16[8,60,768]{2,1,0:T(8,128)(2,1)}, u32[]{:S(2)}, u32[]{:S(2)}) async-start(bf16[8,60,768]{2,1,0:T(8,128)(2,1)} %fusion.127), calls=%async_computation.1 | async-start | bytes 1572864 | tf_op jit(solution)/shard_map/all_to_all | solution.py:320
  270.9 57.4 %all-to-all-start.3 = ((bf16[8,60,768]{2,1,0:T(8,128)(2,1)}), bf16[8,60,768]{2,1,0:T(8,128)(2,1)}, u32[]{:S(2)}, u32[]{:S(2)}) async-start(bf16[8,60,768]{2,1,0:T(8,128)(2,1)} %fusion.122), calls=%async_computation.3 | async-start | bytes 1572864 | tf_op jit(solution)/shard_map/all_to_all | solution.py:386
  276.9 133.7 %reduce-scatter.9.cloned.1.call-start = ((), (), s32[]{:S(2)}) async-start(), calls=%async_computation.15 | async-start | bytes 1966080 | tf_op jit(solution)/shard_map/reduce_scatter | solution.py:207
  381.4 60.6 %reduce-scatter.7.cloned.1.call-start = ((), (), s32[]{:S(2)}) async-start(), calls=%async_computation.14 | async-start | bytes 1966080 | tf_op jit(solution)/shard_map/reduce_scatter | solution.py:204
  381.9 60.0 %copy-start.14 = (f32[384,768]{1,0:T(8,128)S(1)}, f32[384,768]{1,0:T(8,128)}, u32[]{:S(2)}) copy-start(f32[384,768]{1,0:T(8,128)} %copy-done.12) | copy-start | bytes 3538948
  381.9 60.0 %copy-start.94 = (f32[384]{0:T(512)S(1)}, f32[384]{0:T(512)}, u32[]{:S(2)}) copy-start(f32[384]{0:T(512)} %copy-done.93) | copy-start | bytes 4612
  382.0 60.0 %copy-start.105 = (f32[768]{0:T(1024)S(1)}, f32[768]{0:T(1024)}, u32[]{:S(2)}) copy-start(f32[768]{0:T(1024)} %copy-done.104) | copy-start | bytes 9220
  382.0 60.0 %copy-start.119 = (f32[384]{0:T(512)S(1)}, f32[384]{0:T(512)}, u32[]{:S(2)}) copy-start(f32[384]{0:T(512)} %copy-done.118) | copy-start | bytes 4612
  382.0 220.9 %reduce-scatter.13.cloned.1.call-start = ((), (), s32[]{:S(2)}) async-start(), calls=%async_computation.17 | async-start | bytes 1966080 | tf_op jit(solution)/shard_map/reduce_scatter | solution.py:207
  383.0 59.0 %copy-start.61 = (bf16[384,12,64]{0,2,1:T(8,128)(2,1)S(1)}, bf16[384,12,64]{0,2,1:T(8,128)(2,1)}, u32[]{:S(2)}) copy-start(bf16[384,12,64]{0,2,1:T(8,128)(2,1)} %convert.44) | copy-start | bytes 1769476
  385.2 62.9 %copy-start.70 = (bf16[12,64,128]{2,1,0:T(8,128)(2,1)}, bf16[12,64,128]{2,1,0:T(8,128)(2,1)S(1)}, u32[]{:S(2)}) copy-start(bf16[12,64,128]{2,1,0:T(8,128)(2,1)S(1)} %fusion.165) | copy-start | bytes 589828
  385.9 62.2 %copy-start.133 = (bf16[12,64,128]{2,1,0:T(8,128)(2,1)}, bf16[12,64,128]{2,1,0:T(8,128)(2,1)S(1)}, u32[]{:S(2)}) copy-start(bf16[12,64,128]{2,1,0:T(8,128)(2,1)S(1)} %fusion.167) | copy-start | bytes 589828
  448.6 10.7 copy-start.22
  507.3 95.6 %reduce-scatter.11.cloned.1.call-start = ((), (), s32[]{:S(2)}) async-start(), calls=%async_computation.16 | async-start | bytes 1966080 | tf_op jit(solution)/shard_map/reduce_scatter | solution.py:204
  508.0 879.7 %reduce-scatter.15.cloned.1.call-start = ((), (), s32[]{:S(2)}) async-start(), calls=%async_computation.18 | async-start | bytes 5898240 | tf_op jit(solution)/shard_map/reduce_scatter | solution.py:530
  515.2 875.4 %reduce-scatter.17.cloned.1.call-start = ((), (), s32[]{:S(2)}) async-start(), calls=%async_computation.19 | async-start | bytes 5898240 | tf_op jit(solution)/shard_map/reduce_scatter | solution.py:533
  534.1 11.3 copy-start.34
  534.1 859.4 %all-gather.25.cloned.1.call-start = ((), (), s32[]{:S(2)}) async-start(), calls=%async_computation.21 | async-start | bytes 2654208 | tf_op jit(solution)/shard_map/all_gather | solution.py:509
  587.0 9.3 copy-start.95
  587.0 9.3 copy-start.106
  656.8 16.0 %copy-start.74 = (f32[32,192]{1,0:T(8,128)S(1)}, f32[32,192]{1,0:T(8,128)}, u32[]{:S(2)}) copy-start(f32[32,192]{1,0:T(8,128)} %reshape.760) | copy-start | bytes 73732
  656.8 16.0 %copy-start.127 = (f32[8]{0:T(128)S(1)}, f32[8]{0:T(128)}, u32[]{:S(2)}) copy-start(f32[8]{0:T(128)} %get-tuple-element.633) | copy-start | bytes 100
  1279.5 124.8 %all-gather.27.cloned.1.call-start = ((), (), s32[]{:S(2)}) async-start(), calls=%async_computation.22 | async-start | bytes 2654208 | tf_op jit(solution)/shard_map/all_gather | solution.py:512
  1281.9 176.3 %all-gather.23.cloned.1.call-start = ((), (), s32[]{:S(2)}) async-start(), calls=%async_computation.20 | async-start | bytes 3981312 | tf_op jit(solution)/shard_map/all_gather | solution.py:503
  1284.7 99.2 %copy-start.134 = (f32[8]{0:T(128)S(1)}, f32[8]{0:T(128)}, u32[]{:S(2)}) copy-start(f32[8]{0:T(128)} %psum.14) | copy-start | bytes 100
  1284.7 100.4 %copy-start.129 = (f32[384]{0:T(512)S(1)}, f32[384]{0:T(512)}, u32[]{:S(2)}) copy-start(f32[384]{0:T(512)} %get-tuple-element.615) | copy-start | bytes 4612
  1284.7 100.4 %copy-start.128 = (f32[384]{0:T(512)S(1)}, f32[384]{0:T(512)}, u32[]{:S(2)}) copy-start(f32[384]{0:T(512)} %get-tuple-element.616) | copy-start | bytes 4612
  1284.7 100.4 %copy-start.103 = (f32[768]{0:T(1024)S(1)}, f32[768]{0:T(1024)}, u32[]{:S(2)}) copy-start(f32[768]{0:T(1024)} %copy-done.100) | copy-start | bytes 9220
  1284.7 100.4 %copy-start.117 = (f32[384]{0:T(512)S(1)}, f32[384]{0:T(512)}, u32[]{:S(2)}) copy-start(f32[384]{0:T(512)} %copy-done.115) | copy-start | bytes 4612
  1458.2 41.9 %copy-start.1 = (bf16[768,8]{0,1:T(8,128)(2,1)S(1)}, bf16[768,8]{0,1:T(8,128)(2,1)}, u32[]{:S(2)}) copy-start(bf16[768,8]{0,1:T(8,128)(2,1)} %param.26) | copy-start | bytes 36868
  (109 other events, 449.3 us)
Sparse Core Ops, SparseCore 0:
  29.4 22.3 all-gather.14
  53.9 19.6 all-gather.16
  115.4 19.7 all-gather.18
  137.1 19.6 all-gather.20
  381.5 29.0 reduce-scatter.8
  413.7 28.1 reduce-scatter.6
  507.4 28.1 reduce-scatter.12
  538.9 28.1 reduce-scatter.10
  569.6 47.8 reduce-scatter.14
  620.0 47.7 reduce-scatter.16
  1279.6 51.2 all-gather.24
  1333.0 58.1 all-gather.26
  1393.9 64.2 all-gather.22
where the time goes:
time: 1520 us; the launch traced here: 1510 us
  blocking collectives  735 us (48%)
  matrix products  270 us (18%)
  local copies, waits for them, and re-layouts  199 us (13%)
  waiting for transfers between devices  140 us (9%)
  other arithmetic  123 us (8%)
  starting transfers between devices  22.3 us (1%)
  between operations  17.7 us (1%)
    psum x2, blocking collectives, mixture_forward(): lax.psum((jnp.sum(chosen_hot, axis=0), jnp.sum(gate_value[:, None] * chos...  645 us
    reshape x7, other arithmetic, shards(): collected.reshape((initial.shape[0] // lax.axis_size('dp'),) + initial.sh...  58.3 us
    all_gather x1, waiting for transfers between devices, shards(): lax.all_gather(shares[0].astype(jnp.bfloat16), 'expert', axis=0, tiled=True)  43.4 us
    reshape x7, local copies, waits for them, and re-layouts, shards(): flat = [initial.reshape(ranks, -1) for initial in copied_grads]  43.1 us
    all_gather x1, blocking collectives, shards(): lax.all_gather(shares[1].astype(jnp.bfloat16), 'expert', axis=0, tiled=True)  36.1 us
    dot_general x12, matrix products, block_scores(): jnp.einsum('qhd,khd->qhk', queries, as_heads(key_rows), preferred_element...  32.2 us
    reduce_scatter x2, waiting for transfers between devices, attend_backward(): lax.psum_scatter(key_terms.astype(jnp.bfloat16), 'dp', scatter_dimension=...  31.3 us
  transfers between devices with their start and end apart: 17, of which 6 were waited for; matrix products, arithmetic and copies ran while one was open for 23% of the time, Pallas kernels for 0%

commit v1 on v0

--- a/solution.py
+++ b/solution.py
@@ -1,8 +1,13 @@
+import functools
+
 import jax
 import jax.numpy as jnp
 from jax import lax
+from jax.experimental import pallas as pl
+from jax.experimental.pallas import tpu as pltpu
 from jax.sharding import PartitionSpec as P
 
+MESH = pl.DeviceIdType.MESH
 HEADS = 12
 HEAD_DIM = 64
 LONG_DEV = 256
@@ -11,6 +16,210 @@
 epsilon = 1e-05
 balance_weight = 0.01
 masked_score = -1e30
+
+
+def bit_of(index, level):
+    return (index // (1 << level)) % 2
+
+
+def flip(index, level):
+    return index + (1 << level) * (1 - 2 * bit_of(index, level))
+
+
+def partner_index(index, mask, levels):
+    total = 0
+    for level in range(levels):
+        own = bit_of(index, level)
+        total = total + (1 << level) * (1 - own if (mask >> level) & 1 else own)
+    return total
+
+
+def reduce_plan(n_dp, n_ex, rows):
+    dp_levels = n_dp.bit_length() - 1
+    ex_levels = n_ex.bit_length() - 1
+    halvings, piece = 0, rows
+    while halvings < ex_levels and piece % 32 == 0:
+        piece //= 2
+        halvings += 1
+    kinds = [("dp", b) for b in range(dp_levels)]
+    kinds += [("half", b) for b in range(halvings)]
+    kinds += [("both", b) for b in range(halvings, ex_levels)]
+    kinds += [("back", b) for b in reversed(range(halvings))]
+    return kinds, halvings, piece
+
+
+def grad_kernel(n_dp, n_ex, rows, kinds, halvings, firsts, chunks, fin_slots, *refs):
+    count, groups = len(kinds), len(firsts)
+    x_refs, dy_refs, out_ref = refs[:groups], refs[groups : 2 * groups], refs[2 * groups]
+    it = iter(refs[2 * groups + 1 :])
+    send_bufs = [next(it) if k[0] != "back" else None for k in kinds]
+    recv_bufs = [next(it) if k[0] != "back" else None for k in kinds]
+    keep_bufs = [next(it) if k[0] != "back" else None for k in kinds]
+    fin = next(it)
+    send_sems = [next(it) for _ in kinds]
+    recv_sems = [next(it) for _ in kinds]
+    t = pl.program_id(0)
+    d, e = lax.axis_index("dp"), lax.axis_index("expert")
+    dp_levels, ex_levels = n_dp.bit_length() - 1, n_ex.bit_length() - 1
+
+    def peer(kind, level):
+        return (flip(d, level), e) if kind == "dp" else (d, flip(e, level))
+
+    @pl.when(t == 0)
+    def _():
+        barrier = pltpu.get_barrier_semaphore()
+        for level in range(dp_levels):
+            pl.semaphore_signal(barrier, inc=1, device_id=peer("dp", level), device_id_type=MESH)
+        for level in range(ex_levels):
+            pl.semaphore_signal(barrier, inc=1, device_id=peer("ex", level), device_id_type=MESH)
+        pl.semaphore_wait(barrier, dp_levels + ex_levels)
+
+    def kept_rows(depth):
+        start = 0
+        for b in range(depth):
+            start = start + bit_of(e, b) * (rows >> (b + 1))
+        return start
+
+    def copy_of(s, c):
+        kind, level = kinds[s]
+        slot = lax.rem(c, 2)
+        if kind == "back":
+            span = rows >> (level + 1)
+            at = pl.ds(pl.multiple_of(kept_rows(level + 1), span), span)
+            src = fin.at[lax.rem(c, fin_slots), at]
+            dst = src
+        else:
+            src, dst = send_bufs[s].at[slot], recv_bufs[s].at[slot]
+        return pltpu.make_async_remote_copy(
+            src_ref=src,
+            dst_ref=dst,
+            send_sem=send_sems[s].at[slot],
+            recv_sem=recv_sems[s].at[slot],
+            device_id=peer(kind, level),
+            device_id_type=MESH,
+        )
+
+    def arrive(s, c):
+        kind, level = kinds[s]
+        copy_of(s, c).wait()
+        slot = lax.rem(c, 2)
+        if kind == "back":
+            return None
+        if kind == "dp":
+            n = recv_bufs[s].shape[1]
+            return [keep_bufs[s][slot, i] + recv_bufs[s][slot, i].astype(jnp.float32) for i in range(n)]
+        return [keep_bufs[s][slot] + recv_bufs[s][slot].astype(jnp.float32)]
+
+    def leave(s, c, values):
+        kind, level = kinds[s]
+        slot = lax.rem(c, 2)
+        if kind == "dp":
+            for i in range(len(values) // 2):
+                send_bufs[s][slot, i] = values[2 * i + 1].astype(jnp.bfloat16)
+        elif kind == "half":
+            (value,) = values
+            half = value.shape[0] // 2
+            own = bit_of(e, level)
+            top, low = value[:half], value[half:]
+            send_bufs[s][slot] = jnp.where(own == 0, low, top).astype(jnp.bfloat16)
+        elif kind == "both":
+            (value,) = values
+            send_bufs[s][slot] = value.astype(jnp.bfloat16)
+        elif values is not None:
+            (value,) = values
+            span = value.shape[0]
+            at = pl.ds(pl.multiple_of(kept_rows(halvings), span), span)
+            fin[lax.rem(c, fin_slots), at] = value.astype(jnp.bfloat16)
+        copy_of(s, c).start()
+        if kind == "dp":
+            for i in range(len(values) // 2):
+                keep_bufs[s][slot, i] = values[2 * i]
+        elif kind == "half":
+            keep_bufs[s][slot] = jnp.where(own == 0, top, low)
+        elif kind == "both":
+            keep_bufs[s][slot] = value.astype(jnp.bfloat16).astype(jnp.float32)
+
+    ends = list(firsts[1:]) + [chunks]
+    for s in reversed(range(count + 1)):
+        c = t - s
+        if s == 0:
+            for g in range(groups):
+
+                @pl.when((c >= firsts[g]) & (c < ends[g]))
+                def _(g=g):
+                    dy = dy_refs[g][...]
+                    slot = lax.rem(c, 2)
+
+                    def piece(mask):
+                        q = partner_index(d, mask, dp_levels)
+                        return jnp.dot(x_refs[g][q], dy, preferred_element_type=jnp.float32)
+
+                    for i in range(n_dp // 2):
+                        send_bufs[0][slot, i] = piece(2 * i + 1).astype(jnp.bfloat16)
+                    copy_of(0, c).start()
+                    for i in range(n_dp // 2):
+                        keep_bufs[0][slot, i] = piece(2 * i)
+
+        else:
+
+            @pl.when((c >= 0) & (c < chunks))
+            def _(s=s, c=c):
+                values = arrive(s - 1, c)
+                if s < count:
+                    leave(s, c, values)
+                elif kinds[s - 1][0] == "back":
+                    out_ref[...] = fin[lax.rem(c, fin_slots)]
+                else:
+                    out_ref[...] = values[0].astype(jnp.bfloat16)
+
+
+def reduce_grads(n_dp, n_ex, pairs, width):
+    _, _, rows, tokens = pairs[0][0].shape
+    sizes = [x.shape[1] * (dy.shape[1] // width) for x, dy in pairs]
+    firsts = [sum(sizes[:i]) for i in range(len(sizes))]
+    chunks = sum(sizes)
+    kinds, halvings, piece = reduce_plan(n_dp, n_ex, rows)
+    count = len(kinds)
+    fin_slots = max(1, halvings + 1)
+    shapes = []
+    for kind, level in kinds:
+        if kind == "dp":
+            shapes.append((n_dp >> (level + 1), rows, width))
+        elif kind == "half":
+            shapes.append((rows >> (level + 1), width))
+        elif kind == "both":
+            shapes.append((piece, width))
+    scratch = [pltpu.VMEM((2,) + s, jnp.bfloat16) for s in shapes] * 2
+    scratch += [pltpu.VMEM((2,) + s, jnp.float32) for s in shapes]
+    scratch += [pltpu.VMEM((fin_slots, rows, width), jnp.bfloat16)]
+    scratch += [pltpu.SemaphoreType.DMA((2,)) for _ in kinds] * 2
+    in_specs = []
+    for (x, dy), first, size in zip(pairs, firsts, sizes):
+        many = x.shape[1] > 1
+
+        def x_place(t, first=first, size=size, many=many):
+            return (0, jnp.clip(t - first, 0, size - 1) if many else 0, 0, 0)
+
+        in_specs.append(pl.BlockSpec((n_dp, None, rows, tokens), x_place))
+    for (x, dy), first, size in zip(pairs, firsts, sizes):
+        many = dy.shape[1] > width
+
+        def dy_place(t, first=first, size=size, many=many):
+            return (0, jnp.clip(t - first, 0, size - 1) if many else 0)
+
+        in_specs.append(pl.BlockSpec((tokens, width), dy_place))
+    return pl.pallas_call(
+        functools.partial(grad_kernel, n_dp, n_ex, rows, kinds, halvings, firsts, chunks, fin_slots),
+        grid=(chunks + count,),
+        out_shape=jax.ShapeDtypeStruct((chunks, rows, width), jnp.bfloat16),
+        in_specs=in_specs,
+        out_specs=pl.BlockSpec((None, rows, width), lambda t: (jnp.maximum(t - count, 0), 0, 0)),
+        scratch_shapes=scratch,
+        compiler_params=pltpu.CompilerParams(
+            collective_id=1, has_side_effects=True, vmem_limit_bytes=48 * 1024 * 1024
+        ),
+        name="dense_grads",
+    )(*[x for x, _ in pairs], *[dy for _, dy in pairs])
 
 
 def exact_gelu(values):
@@ -97,12 +306,8 @@
     running = fold_block(
         running, queries, key_rows[LONG_DEV:], value_rows[LONG_DEV:], short_allowed
     )
-    long_keys = key_rows[:LONG_DEV]
-    long_values = value_rows[:LONG_DEV]
-    key_piece = (
-        lax.all_gather(long_keys, "dp", axis=0, tiled=True),
-        lax.all_gather(long_values, "dp", axis=0, tiled=True),
-    )
+    both = lax.all_gather(mixed[:LONG_DEV, model_width:], "dp", axis=0, tiled=True)
+    key_piece = (both[:, :model_width], both[:, model_width:])
     running = fold_block(
         running,
         queries,
@@ -112,7 +317,7 @@
     )
     running_top, running_total, weighted = running
     context = (weighted / running_total[..., None]).reshape(row_count, model_width)
-    return (mixed, context, running_top + jnp.log(running_total), None)
+    return (mixed, context, running_top + jnp.log(running_total), key_piece)
 
 
 def attend_backward(mixed, context, log_total, gathered, grad_context, layout, short_allowed):
@@ -150,10 +355,6 @@
     short_value_grad = jnp.einsum(
         "qhk,qhd->khd", short_probs, grad_heads, preferred_element_type=jnp.float32
     ).reshape(short_count, model_width)
-    gathered = (
-        lax.all_gather(key_rows[:LONG_DEV], "dp", axis=0, tiled=True),
-        lax.all_gather(value_rows[:LONG_DEV], "dp", axis=0, tiled=True),
-    )
     long_count = gathered[0].shape[0]
 
     def visit(block_step, partial_state):
@@ -200,14 +401,10 @@
     grad_query, key_terms, value_terms = lax.fori_loop(
         0, long_count // LONG_DEV, visit, start_state
     )
-    own_keys, own_values = (
-        lax.psum_scatter(
-            key_terms.astype(jnp.bfloat16), "dp", scatter_dimension=0, tiled=True
-        ).astype(jnp.float32),
-        lax.psum_scatter(
-            value_terms.astype(jnp.bfloat16), "dp", scatter_dimension=0, tiled=True
-        ).astype(jnp.float32),
-    )
+    own = lax.psum_scatter(
+        jnp.concatenate([key_terms, value_terms], axis=1).astype(jnp.bfloat16), "dp", scatter_dimension=0, tiled=True
+    ).astype(jnp.float32)
+    own_keys, own_values = own[:, :model_width], own[:, model_width:]
     grad_keys = jnp.concatenate([own_keys, short_key_grad], axis=0)
     grad_values = jnp.concatenate([own_values, short_value_grad], axis=0)
     return jnp.concatenate(
@@ -234,21 +431,16 @@
 ):
     unit_rows, inverse, normed_low, mixed, context, context_low, log_total, gathered = kept_state
     upstream_low = upstream.astype(jnp.bfloat16)
-    grad_out_weight = jnp.einsum(
-        "td,te->de", context_low, upstream_low, preferred_element_type=jnp.float32
-    )
     grad_context = jnp.einsum(
         "te,de->td", upstream_low, weight_out, preferred_element_type=jnp.float32
     ).astype(jnp.bfloat16)
     grad_mixed = attend_backward(
         mixed, context, log_total, gathered, grad_context, layout, short_allowed
     )
-    grad_in_weight = jnp.einsum(
-        "td,te->de", normed_low, grad_mixed, preferred_element_type=jnp.float32
-    )
     grad_normed = jnp.einsum("te,de->td", grad_mixed, weight_in, preferred_element_type=jnp.float32)
     grad_stream, grad_gain, grad_shift = norm_backward(unit_rows, inverse, norm_gain, grad_normed)
-    return (upstream + grad_stream, grad_in_weight, grad_out_weight, grad_gain, grad_shift)
+    pairs = ((context_low, upstream_low), (normed_low, grad_mixed))
+    return (upstream + grad_stream, pairs, grad_gain, grad_shift)
 
 
 def ffn_forward(stream, norm_gain, norm_shift, weight_in, weight_out):
@@ -263,21 +455,16 @@
 def ffn_backward(upstream, kept_state, norm_gain, weight_in, weight_out):
     unit_rows, inverse, normed_low, hidden, active = kept_state
     upstream_low = upstream.astype(jnp.bfloat16)
-    grad_out_weight = jnp.einsum(
-        "tf,td->fd", active, upstream_low, preferred_element_type=jnp.float32
-    )
     grad_active = jnp.einsum(
         "td,fd->tf", upstream_low, weight_out, preferred_element_type=jnp.float32
     )
     grad_hidden = gelu_backward(hidden, grad_active).astype(jnp.bfloat16)
-    grad_in_weight = jnp.einsum(
-        "td,tf->df", normed_low, grad_hidden, preferred_element_type=jnp.float32
-    )
     grad_normed = jnp.einsum(
         "tf,df->td", grad_hidden, weight_in, preferred_element_type=jnp.float32
     )
     grad_stream, grad_gain, grad_shift = norm_backward(unit_rows, inverse, norm_gain, grad_normed)
-    return (upstream + grad_stream, grad_in_weight, grad_out_weight, grad_gain, grad_shift)
+    pairs = ((active, upstream_low), (normed_low, grad_hidden))
+    return (upstream + grad_stream, pairs, grad_gain, grad_shift)
 
 
 def mixture_forward(stream, norm_gain, norm_shift, router, expert_in, expert_out, assign_ids):
@@ -291,10 +478,8 @@
     expert_numbers = jnp.arange(experts_all, dtype=jnp.int32)
     chosen_hot = (assign_ids[:, None] == expert_numbers[None, :]).astype(jnp.float32)
     gate_value = jax.nn.sigmoid(jnp.sum(logits * chosen_hot, axis=-1))
-    counts, gate_sums = lax.psum(
-        (jnp.sum(chosen_hot, axis=0), jnp.sum(gate_value[:, None] * chosen_hot, axis=0)),
-        ("dp", "expert"),
-    )
+    counts = lax.psum(jnp.sum(chosen_hot, axis=0), ("dp", "expert"))
+    gate_sums = lax.psum(jnp.sum(gate_value[:, None] * chosen_hot, axis=0), ("dp", "expert"))
     tokens_all = row_count * lax.axis_size("dp") * lax.axis_size("expert")
     token_share = counts / tokens_all
     balance = experts_all * jnp.sum((token_share - 1.0 / experts_all) * (gate_sums / tokens_all))
@@ -465,66 +650,55 @@
     upstream, expert_in_grad, expert_out_grad, router_grad, gain_three, shift_three = (
         mixture_backward(upstream, kept_four, ln_gain[:, 3], router, expert_in, expert_out)
     )
-    upstream, second_in_grad, second_out_grad, gain_two, shift_two = attention_backward(
+    upstream, second_pairs, gain_two, shift_two = attention_backward(
         upstream, kept_three, ln_gain[:, 2], attn_in[:, 1], attn_out[:, 1], layout, short_allowed
     )
-    upstream, ffn_in_grad, ffn_out_grad, gain_one, shift_one = ffn_backward(
-        upstream, kept_two, ln_gain[:, 1], ffn_in, ffn_out
-    )
-    upstream, first_in_grad, first_out_grad, gain_zero, shift_zero = attention_backward(
+    upstream, dense_pairs, gain_one, shift_one = ffn_backward(upstream, kept_two, ln_gain[:, 1], ffn_in, ffn_out)
+    upstream, first_pairs, gain_zero, shift_zero = attention_backward(
         upstream, kept_one, ln_gain[:, 0], attn_in[:, 0], attn_out[:, 0], layout, short_allowed
     )
     grad_tokens = upstream.astype(jnp.bfloat16)[None]
-    attn_in_grad = jnp.stack([first_in_grad, second_in_grad], axis=1)
-    attn_out_grad = jnp.stack([first_out_grad, second_out_grad], axis=1)
-    gain_grad = jnp.stack([gain_zero, gain_one, gain_two, gain_three], axis=1)
-    shift_grad = jnp.stack([shift_zero, shift_one, shift_two, shift_three], axis=1)
-    copied_grads = (
-        attn_in_grad,
-        attn_out_grad,
-        ffn_in_grad,
-        ffn_out_grad,
-        router_grad,
-        gain_grad,
-        shift_grad,
-    )
-    ranks = lax.axis_size("dp") * lax.axis_size("expert")
-    flat = [initial.reshape(ranks, -1) for initial in copied_grads]
-    shares = (
-        lax.psum_scatter(flat[0], ("dp", "expert"), scatter_dimension=0, tiled=True),
-        lax.psum_scatter(flat[1], ("dp", "expert"), scatter_dimension=0, tiled=True),
-        lax.psum_scatter(flat[2], ("dp", "expert"), scatter_dimension=0, tiled=True),
-        lax.psum_scatter(flat[3], ("dp", "expert"), scatter_dimension=0, tiled=True),
-        lax.psum_scatter(flat[4], ("dp", "expert"), scatter_dimension=0, tiled=True),
-        lax.psum_scatter(flat[5], ("dp", "expert"), scatter_dimension=0, tiled=True),
-        lax.psum_scatter(flat[6], ("dp", "expert"), scatter_dimension=0, tiled=True),
-    )
-    filled = (
-        lax.all_gather(shares[0].astype(jnp.bfloat16), "expert", axis=0, tiled=True).astype(
-            jnp.float32
-        ),
-        lax.all_gather(shares[1].astype(jnp.bfloat16), "expert", axis=0, tiled=True).astype(
-            jnp.float32
-        ),
-        lax.all_gather(shares[2].astype(jnp.bfloat16), "expert", axis=0, tiled=True).astype(
-            jnp.float32
-        ),
-        lax.all_gather(shares[3].astype(jnp.bfloat16), "expert", axis=0, tiled=True).astype(
-            jnp.float32
-        ),
-        lax.all_gather(shares[4].astype(jnp.bfloat16), "expert", axis=0, tiled=True).astype(
-            jnp.float32
-        ),
-        lax.all_gather(shares[5].astype(jnp.bfloat16), "expert", axis=0, tiled=True).astype(
-            jnp.float32
-        ),
-        lax.all_gather(shares[6].astype(jnp.bfloat16), "expert", axis=0, tiled=True).astype(
-            jnp.float32
-        ),
-    )
+    n_dp, n_ex = lax.axis_size("dp"), lax.axis_size("expert")
+    model_width = tokens.shape[2]
+    rows = model_width // n_dp
+
+    def blocks_of(acts):
+        return acts.T.reshape(n_dp, -1, rows, row_count).astype(jnp.bfloat16)
+
+    pairs = [(blocks_of(x), dy) for x, dy in second_pairs + dense_pairs + first_pairs]
+    chunks = reduce_grads(n_dp, n_ex, pairs, model_width).astype(jnp.float32)
+
+    def wide(first, count):
+        return chunks[first : first + count].transpose(1, 0, 2).reshape(rows, count * model_width)
+
+    per_in = attn_in.shape[2] // model_width
+    per_ffn = ffn_in.shape[1] // model_width
+    at = 0
+    second_out = chunks[0]
+    second_in = wide(1, per_in)
+    at = 1 + per_in
+    ffn_out_sum = chunks[at : at + per_ffn].reshape(per_ffn * rows, model_width)
+    ffn_in_sum = wide(at + per_ffn, per_ffn)
+    at = at + 2 * per_ffn
+    first_out = chunks[at]
+    first_in = wide(at + 1, per_in)
+    small = jnp.concatenate(
+        [
+            jnp.stack([gain_zero, gain_one, gain_two, gain_three, shift_zero, shift_one, shift_two, shift_three], axis=0),
+            router_grad.T,
+        ],
+        axis=0,
+    )
+    small = lax.psum(small, ("dp", "expert"))
+    small = lax.dynamic_slice_in_dim(small, lax.axis_index("dp") * rows, rows, 1).T
     summed = [
-        collected.reshape((initial.shape[0] // lax.axis_size("dp"),) + initial.shape[1:])
-        for initial, collected in zip(copied_grads, filled)
+        jnp.stack([first_in, second_in], axis=1),
+        jnp.stack([first_out, second_out], axis=1),
+        ffn_in_sum,
+        ffn_out_sum,
+        small[:, 8:],
+        small[:, :4],
+        small[:, 4:8],
     ]
     expert_in_sum, expert_out_sum = (
         lax.psum_scatter(

time: 1520 us -> 916 us (0.60)
  blocking collectives: 735 us -> 80.1 us
  Pallas kernels: 0 us -> 144 us
  waiting for transfers between devices: 140 us -> 62.2 us
  other arithmetic: 123 us -> 84.2 us
  matrix products: 270 us -> 293 us
    psum x2, blocking collectives: 645 us -> 80.1 us  [the longest x1 40.5 us: mixture_forward(): counts = lax.psum(jnp.sum(chosen_hot, axis=0), ('dp', 'expert'))]
    pallas_call x0 -> x1, Pallas kernels: none -> 144 us  [reduce_grads(): pl.pallas_call(functools.partial(grad_kernel, n_dp, n_ex, rows, kinds, ha...]
    all_gather x4 -> x0, blocking collectives: 90 us -> none  [the longest x1 36.1 us: shards(): lax.all_gather(shares[1].astype(jnp.bfloat16), 'expert', axis=0, tiled=True)]
    reshape x7 -> x0, other arithmetic: 58.3 us -> none  [shards(): collected.reshape((initial.shape[0] // lax.axis_size('dp'),) + initial.sh...]
    reduce_scatter x4 -> x2, waiting for transfers between devices: 56 us -> 7.64 us  [attend_backward(): lax.psum_scatter(jnp.concatenate([key_terms, value_terms], axis=1).astype...]
    reshape x14 -> x7, local copies, waits for them, and re-layouts: 53.8 us -> 6.21 us  [the longest x2 1.97 us: attend_backward(): short_key_grad = (jnp.einsum('qhk,qhd->khd', short_scores, queries, prefe...]
    all_gather x7 -> x2, waiting for transfers between devices: 68.2 us -> 39 us  [attend_forward(): lax.all_gather(mixed[:LONG_DEV, model_width:], 'dp', axis=0, tiled=True)]
    dot_general x6 -> x0, matrix products: 28.1 us -> none  [the longest x2 12.7 us: attention_backward(): jnp.einsum('td,te->de', normed_low, grad_mixed, preferred_element_type=jn...]
  transfers between devices with their start and end apart: 17 -> 10, of which waited for: 6 -> 4; matrix products, arithmetic and copies ran while one was open for 23% -> 30% of each run, Pallas kernels for 0% -> 0%
where the time goes in v1:
time: 916 us; the launch traced here: 905 us
  matrix products  293 us (32%)
  local copies, waits for them, and re-layouts  201 us (22%)
  Pallas kernels  144 us (16%)
  other arithmetic  84.2 us (9%)
  blocking collectives  80.1 us (9%)
  waiting for transfers between devices  62.2 us (7%)
  starting transfers between devices  21.8 us (2%)
  between operations  18.1 us (2%)
    pallas_call x1, Pallas kernels, reduce_grads(): pl.pallas_call(functools.partial(grad_kernel, n_dp, n_ex, rows, kinds, ha...  144 us
    psum x1, blocking collectives, mixture_forward(): counts = lax.psum(jnp.sum(chosen_hot, axis=0), ('dp', 'expert'))  40.5 us
    psum x1, blocking collectives, mixture_forward(): lax.psum(jnp.sum(gate_value[:, None] * chosen_hot, axis=0), ('dp', 'exper...  39.6 us
    all_gather x2, waiting for transfers between devices, attend_forward(): lax.all_gather(mixed[:LONG_DEV, model_width:], 'dp', axis=0, tiled=True)  39 us
    dot_general x12, matrix products, block_scores(): jnp.einsum('qhd,khd->qhk', queries, as_heads(key_rows), preferred_element...  37 us
    dot_general x8, matrix products, visit(): jnp.einsum('qhk,qhd->khd', probs_low, grad_heads, preferred_element_type=...  36.3 us
    dynamic_update_slice x16, local copies, waits for them, and re-layouts, visit(): lax.dynamic_update_slice_in_dim(value_terms, more_value, first_row, 0)  31.7 us
    unnamed x255, local copies, waits for them, and re-layouts  23.7 us
  transfers between devices with their start and end apart: 10, of which 4 were waited for; matrix products, arithmetic and copies ran while one was open for 30% of the time, Pallas kernels for 0%

profile of v1, /device:TPU:0, one launch (start us, length us, event | category | flops | bytes accessed | tf_op | source)
XLA Modules:
  0.0 904.8 jit_solution(17698081026348164380)
XLA Ops:
  9.9 14.9 %fusion.248 = (bf16[768,1,2304]{2,1,0:T(2,128)(2,1)}, bf16[768,1,2304]{2,1,0:T(2,128)(2,1)S(1)}) fusion(bf16[768,2,2304]{2,1,0:T(2,128)(2,1)} %param.22), kind=kLoop, calls=%fused_computation.395 | loop fusion | bytes 14155776 | tf_op jit(solution)/shard_map/slice | solution.py:640
  34.1 9.5 %fusion.251 = (bf16[768,1,768]{2,1,0:T(2,128)(2,1)}, bf16[768,1,768]{2,1,0:T(2,128)(2,1)}) fusion(bf16[768,2,768]{2,1,0:T(2,128)(2,1)} %param.23), kind=kLoop, calls=%fused_computation.398 | loop fusion | bytes 4718592 | tf_op jit(solution)/shard_map/slice | solution.py:641
  43.5 16.6 %all-gather.3.cloned.1.call-done = bf16[1024,1536]{1,0:T(8,128)(2,1)} async-done(((bf16[256,1536]{1,0:T(8,128)(2,1)}), bf16[1024,1536]{1,0:T(8,128)(2,1)}) %all-gather.3.cloned.1.call-update) | async-done | bytes 3145744 | tf_op jit(solution)/shard_map/all_gather | solution.py:309
  60.2 3.7 fusion.250
  63.9 2.8 copy.151
  69.3 10.9 %fusion.36 = (f32[384,12]{0,1:T(8,128)S(1)}, f32[12,1024,384]{2,1,0:T(8,128)}) fusion(pred[384,1024]{0,1:T(8,128)(4,1)S(1)} %fusion.116, bf16[1024,12,64]{0,2,1:T(8,128)(2,1)} %bitcast.10, bf16[384,12,64]{0,2,1:T(8,128)(2,1)} %bitcast.6), kind=kOutput, calls=%fused_computation.58 | convolution fusion | flops 618130944 | bytes 21448704 | tf_op jit(solution)/shard_map/qhd,khd->qhk/dot_general | solution.py:256
  80.8 10.8 %fusion.38 = f32[384,12]{0,1:T(8,128)S(1)} fusion(f32[12,1024,384]{2,1,0:T(8,128)} %get-tuple-element.697, f32[384,12]{0,1:T(8,128)S(1)} %get-tuple-element.690, pred[384,1024]{0,1:T(8,128)(4,1)S(1)} %fusion.116), kind=kLoop, calls=%fused_computation.60 | loop fusion | flops 23588352 | bytes 19304448 | tf_op jit(solution)/shard_map/reduce_sum | solution.py:274
  91.7 10.0 %fusion.125 = f32[384,12,64]{0,2,1:T(8,128)S(1)} fusion(bf16[1024,12,64]{0,2,1:T(8,128)(2,1)} %bitcast.12, f32[12,1024,384]{2,1,0:T(8,128)} %get-tuple-element.697, f32[384,12]{0,1:T(8,128)S(1)} %get-tuple-element.690, pred[384,1024]{0,1:T(8,128)(4,1)S(1)} %fusion.116), kind=kOutput, calls=%fused_computation.197 | convolution fusion | flops 627572736 | bytes 22038528 | tf_op jit(solution)/shard_map/qhk,khd->qhd/dot_general | solution.py:275
  106.5 11.4 %fusion.66 = (f32[384,3072]{1,0:T(8,128)S(1)}, f32[384,3072]{1,0:T(8,128)S(1)}) fusion(bf16[768,3072]{1,0:T(8,128)(2,1)S(1)} %bitcast.666, f32[384,768]{1,0:T(8,128)S(1)} %get-tuple-element.701, f32[768]{0:T(1024)S(1)} %copy-done.93, f32[768]{0:T(1024)S(1)} %get-tuple-element.719, f32[384]{0:T(512)S(1)} %add_rsqrt_fusion.2, ...), kind=kOutput, calls=%fused_computation.99 | convolution fusion | flops 1886552064 | bytes 15344640 | tf_op jit(solution)/shard_map/dot_general | solution.py:449
  131.9 22.4 %all-gather.5.cloned.1.call-done = bf16[1024,1536]{1,0:T(8,128)(2,1)} async-done(((bf16[256,1536]{1,0:T(8,128)(2,1)}), bf16[1024,1536]{1,0:T(8,128)(2,1)}) %all-gather.5.cloned.1.call-update) | async-done | bytes 3145744 | tf_op jit(solution)/shard_map/all_gather | solution.py:309
  154.3 3.8 fusion.249
  160.7 10.8 %fusion.37 = (f32[384,12]{0,1:T(8,128)S(1)}, f32[12,1024,384]{2,1,0:T(8,128)}) fusion(pred[384,1024]{0,1:T(8,128)(4,1)S(1)} %fusion.116, bf16[1024,12,64]{0,2,1:T(8,128)(2,1)} %bitcast.22, bf16[384,12,64]{0,2,1:T(8,128)(2,1)S(1)} %bitcast.617), kind=kOutput, calls=%fused_computation.59 | convolution fusion | flops 618130944 | bytes 21448704 | tf_op jit(solution)/shard_map/qhd,khd->qhk/dot_general | solution.py:256
  174.3 10.8 %fusion.40 = f32[384,12]{0,1:T(8,128)S(1)} fusion(f32[12,1024,384]{2,1,0:T(8,128)} %get-tuple-element.709, f32[384,12]{0,1:T(8,128)S(1)} %get-tuple-element.687, pred[384,1024]{0,1:T(8,128)(4,1)S(1)} %fusion.116), kind=kLoop, calls=%fused_computation.62 | loop fusion | flops 23588352 | bytes 19304448 | tf_op jit(solution)/shard_map/reduce_sum | solution.py:274
  185.1 9.7 %fusion.128 = f32[384,12,64]{0,2,1:T(8,128)S(1)} fusion(bf16[1024,12,64]{0,2,1:T(8,128)(2,1)} %bitcast.24, f32[12,1024,384]{2,1,0:T(8,128)} %get-tuple-element.709, f32[384,12]{0,1:T(8,128)S(1)} %get-tuple-element.687, pred[384,1024]{0,1:T(8,128)(4,1)S(1)} %fusion.116), kind=kOutput, calls=%fused_computation.198 | convolution fusion | flops 627572736 | bytes 22038528 | tf_op jit(solution)/shard_map/qhk,khd->qhd/dot_general | solution.py:275
  200.9 5.5 all-to-all-start
  211.5 15.4 %all-to-all-done = bf16[8,60,768]{2,1,0:T(8,128)(2,1)S(1)} async-done(((bf16[8,60,768]{2,1,0:T(8,128)(2,1)}), bf16[8,60,768]{2,1,0:T(8,128)(2,1)S(1)}, u32[]{:S(2)}, u32[]{:S(2)}) %all-to-all-start) | async-done | bytes 737312 | tf_op jit(solution)/shard_map/all_to_all | solution.py:497
  226.9 4.2 all-to-all-start.2
  231.2 4.9 fusion.77
  238.7 19.0 %fusion.146 = bf16[8,60,768]{2,1,0:T(8,128)(2,1)} fusion(bf16[1,3072,768]{2,1,0:T(8,128)(2,1)} %param.28, f32[8,60,3072]{2,1,0:T(8,128)S(1)} %fusion.77), kind=kOutput, calls=%fused_computation.216 | convolution fusion | flops 2361139200 | bytes 11354112 | tf_op jit(solution)/shard_map/sjcf,jfd->sjcd/dot_general | solution.py:502
  257.7 5.9 all-to-all-start.1
  263.6 18.5 %fusion.54 = bf16[8,1,60,3072]{3,2,0,1:T(8,128)(2,1)S(1)} fusion(f32[8,60,3072]{2,1,0:T(8,128)} %copy-done.33, bf16[8,60,768]{2,1,0:T(8,128)(2,1)} %all-to-all-done.2, bf16[1,3072,768]{2,1,0:T(8,128)(2,1)} %param.28), kind=kOutput, calls=%fused_computation.81 | convolution fusion | flops 2371092480 | bytes 14303232 | tf_op jit(solution)/shard_map/sjcd,jfd->sjcf/dot_general | solution.py:561
  283.9 3.6 fusion.141
  287.4 6.0 all-to-all-start.3
  293.6 40.5 %psum.21 = f32[8]{0:T(128)S(1)} all-reduce(f32[8]{0:T(128)S(1)} %convert_reduce_fusion.1), channel_id=1, replica_groups=mesh['dp'=4,'expert'=8] {'dp','expert'}, use_global_device_ids=true, to_apply=%region_23.24 | all-reduce | flops 8 | bytes 64 | tf_op jit(solution)/shard_map/psum | solution.py:481
  335.8 2.9 fusion.166
  357.1 84.8 %while.36 = (s32[]{:T(128)}, f32[384,12,64]{0,2,1:T(8,128)}, bf16[1024,768]{1,0:T(8,128)(2,1)}, bf16[1024,768]{1,0:T(8,128)(2,1)}, bf16[1024,768]{0,1:T(8,128)(2...) while((s32[]{:T(128)}, f32[384,12,64]{0,2,1:T(8,128)}, ...), condition=%wide.region_33.34_spmd.clone, body=%wide.region_32.33_spmd.clone.sunk | while | flops 770311168 | bytes 51867628 | solution.py:401
  360.5 3.0 fusion.371
  367.0 4.5 fusion.373
  381.7 3.0 fusion.371
  388.2 4.5 fusion.373
  402.9 3.0 fusion.371
  409.5 4.5 fusion.373
  424.1 3.0 fusion.371
  430.7 4.5 fusion.373
  441.9 3.8 pad_maximum_fusion.1
  445.8 6.6 fusion.97
  452.5 18.9 %fusion.98 = bf16[1,3072,768]{2,1,0:T(8,128)(2,1)} fusion(bf16[8,60,768]{2,1,0:T(8,128)(2,1)} %all-to-all-done.2, f32[8,60,3072]{2,1,0:T(8,128)} %copy-done.33), kind=kOutput, calls=%fused_computation.145 | convolution fusion | flops 2363129856 | bytes 11354112 | tf_op jit(solution)/shard_map/sjcf,sjcd->jfd/dot_general | solution.py:558
  476.6 7.6 reduce-scatter.5.cloned.1.call-done
  485.7 5.1 fusion.150
  493.6 3.4 add_convert_fusion.refs_9_
  497.0 5.3 fusion.266
  518.1 90.3 %while.37 = (s32[]{:T(128)}, f32[384,12,64]{0,2,1:T(8,128)}, bf16[1024,768]{1,0:T(8,128)(2,1)}, bf16[1024,768]{1,0:T(8,128)(2,1)}, bf16[1024,768]{0,1:T(8,128)(2...) while((s32[]{:T(128)}, f32[384,12,64]{0,2,1:T(8,128)}, ...), condition=%wide.region_41.42_spmd.clone, body=%wide.region_40.41_spmd.clone.sunk | while | flops 770311168 | bytes 56340600 | solution.py:401
  529.2 4.6 fusion.387
  537.7 2.9 fusion.386
  552.0 4.5 fusion.387
  560.5 2.9 fusion.386
  574.5 4.6 fusion.387
  583.0 2.9 fusion.386
  597.0 4.5 fusion.387
  605.5 2.9 fusion.386
  608.4 3.8 pad_maximum_fusion.2
  612.3 12.3 %fusion.69 = bf16[3072,384]{0,1:T(8,128)(2,1)} fusion(f32[384,3072]{1,0:T(8,128)} %copy-done.23), kind=kLoop, calls=%fused_computation.102 | loop fusion | flops 76677120 | bytes 7077888 | tf_op jit(solution)/shard_map/convert_element_type | solution.py:450
  624.6 4.4 copy.187
  649.7 3.0 convert_element_type.259
  652.8 2.8 convert_element_type.262
  658.1 4.9 fusion.149
  668.7 144.2 %dense_grads.1 = bf16[16,192,768]{2,1,0:T(8,128)(2,1)} custom-call(bf16[4,1,192,384]{3,2,1,0:T(8,128)(2,1)S(1)} %bitcast.610, bf16[4,1,192,384]{3,2,1,0:T(8,128)(2,1)S(1)} %bitcast.612, bf16[4,4,192,384]{3,2,1,0:T(8,128)(2,1)} %bitcast.633, bf16[4,1,192,384]{3,2,1,0:T(8,128)(2,1)S(1)} %bitcast.611, bf16[4,1,192,384]{3,2,1,0:T(8,128)(2,1)S(1)} %bitcast.615, ...), custom_call_target="tpu_custom_call" | custom-call | tf_op jit(solution)/shard_map/dense_grads/pallas_call | solution.py:211
  812.9 3.4 convert_element_type.256
  824.8 39.6 %all-reduce.1 = (f32[8]{0:T(128)}, f32[16,768]{1,0:T(8,128)}) all-reduce(f32[8]{0:T(128)} %get-tuple-element.599, f32[16,768]{1,0:T(8,128)} %concatenate.47), channel_id=1, replica_groups=mesh['dp'=4,'expert'=8] {'dp','expert'}, use_global_device_ids=true, to_apply=%region_25.26 | all-reduce | flops 12296 | bytes 98368 | tf_op jit(solution)/shard_map/psum | solution.py:482
  871.2 4.2 stack_reshape.6
  875.4 4.1 copy.194
  879.5 4.2 stack_reshape.7
  885.9 4.5 copy.196
  893.5 2.9 fusion.200
  (574 shorter events, 262.3 us)
Async XLA Ops:
  7.2 199.2 %copy-start = (bf16[768,8]{0,1:T(8,128)(2,1)S(1)}, bf16[768,8]{0,1:T(8,128)(2,1)}, u32[]{:S(2)}) copy-start(bf16[768,8]{0,1:T(8,128)(2,1)} %param.26) | copy-start | bytes 36868
  7.2 53.0 %all-gather.3.cloned.1.call-start = ((), (), s32[]{:S(2)}) async-start(), calls=%async_computation.8 | async-start | bytes 3932160 | tf_op jit(solution)/shard_map/all_gather | solution.py:309
  8.5 17.1 %copy-start.74 = (f32[384]{0:T(512)}, f32[384]{0:T(512)S(1)}, u32[]{:S(2)}) copy-start(f32[384]{0:T(512)S(1)} %broadcast_multiply_fusion.11) | copy-start | bytes 4612
  9.9 15.7 %copy-start.82 = (f32[384]{0:T(512)}, f32[384]{0:T(512)S(1)}, u32[]{:S(2)}) copy-start(f32[384]{0:T(512)S(1)} %add_rsqrt_fusion.3) | copy-start | bytes 4612
  9.9 15.0 %copy-start.107 = (f32[768,4]{0,1:T(4,128)S(1)}, f32[768,4]{0,1:T(4,128)}, u32[]{:S(2)}) copy-start(f32[768,4]{0,1:T(4,128)} %param.21) | copy-start | bytes 36868
  9.9 15.0 %copy-start.108 = (f32[768,4]{0,1:T(4,128)S(1)}, f32[768,4]{0,1:T(4,128)}, u32[]{:S(2)}) copy-start(f32[768,4]{0,1:T(4,128)} %param.20) | copy-start | bytes 36868
  9.9 15.7 %copy-start.28 = (bf16[1,384,768]{2,1,0:T(8,128)(2,1)S(1)}, bf16[1,384,768]{2,1,0:T(8,128)(2,1)}, u32[]{:S(2)}) copy-start(bf16[1,384,768]{2,1,0:T(8,128)(2,1)} %param.17) | copy-start | bytes 1769476
  25.6 80.8 %copy-start.68 = (f32[768]{0:T(1024)}, f32[768]{0:T(1024)S(1)}, u32[]{:S(2)}) copy-start(f32[768]{0:T(1024)S(1)} %get-tuple-element.719) | copy-start | bytes 9220
  25.6 96.1 %copy-start.70 = (f32[768]{0:T(1024)}, f32[768]{0:T(1024)S(1)}, u32[]{:S(2)}) copy-start(f32[768]{0:T(1024)S(1)} %get-tuple-element.717) | copy-start | bytes 9220
  28.8 125.5 %all-gather.5.cloned.1.call-start = ((), (), s32[]{:S(2)}) async-start(), calls=%async_computation.9 | async-start | bytes 3932160 | tf_op jit(solution)/shard_map/all_gather | solution.py:309
  32.0 441.4 %copy-start.45 = (pred[384,128]{0,1:T(8,128)(4,1)}, pred[384,128]{0,1:T(8,128)(4,1)S(1)}, u32[]{:S(2)}) copy-start(pred[384,128]{0,1:T(8,128)(4,1)S(1)} %fusion.211) | copy-start | bytes 147460
  34.1 68.7 %copy-start.17 = (f32[384,12,128]{0,2,1:T(8,128)}, f32[384,12,128]{0,2,1:T(8,128)S(1)}, u32[]{:S(2)}) copy-start(f32[384,12,128]{0,2,1:T(8,128)S(1)} %get-tuple-element.695) | copy-start | bytes 7077892
  91.7 11.1 %copy-start.58 = (bf16[128,768]{0,1:T(8,128)(2,1)S(1)}, bf16[128,768]{0,1:T(8,128)(2,1)}, u32[]{:S(2)}) copy-start(bf16[128,768]{0,1:T(8,128)(2,1)} %copy.149) | copy-start | bytes 589828
  91.7 11.1 %copy-start.81 = (f32[384,12]{0,1:T(8,128)S(1)}, f32[384,12]{0,1:T(8,128)}, u32[]{:S(2)}) copy-start(f32[384,12]{0,1:T(8,128)} %get-tuple-element.689) | copy-start | bytes 55300
  104.5 13.4 %slice-start.8 = ((s8[4718592]{0:T(1024)(128)(4,1)}), s8[4194304]{0:T(1024)(128)(4,1)S(1)}, s32[]{:S(2)}) async-start(s8[4718592]{0:T(1024)(128)(4,1)} %bitcast.641), calls=%async_computation.22 | async-start | bytes 8388608
  104.5 17.2 %slice-start.4 = ((s8[7077888]{0:T(1024)(128)(4,1)}), s8[4194304]{0:T(1024)(128)(4,1)S(1)}, s32[]{:S(2)}) async-start(s8[7077888]{0:T(1024)(128)(4,1)} %bitcast.634), calls=%async_computation.18 | async-start | bytes 8388608
  106.1 11.8 %copy-start.21 = (f32[384,768]{1,0:T(8,128)}, f32[384,768]{1,0:T(8,128)S(1)}, u32[]{:S(2)}) copy-start(f32[384,768]{1,0:T(8,128)S(1)} %get-tuple-element.701) | copy-start | bytes 3538948
  106.1 11.7 %copy-start.77 = (f32[384]{0:T(512)}, f32[384]{0:T(512)S(1)}, u32[]{:S(2)}) copy-start(f32[384]{0:T(512)S(1)} %broadcast_multiply_fusion.10) | copy-start | bytes 4612
  106.4 11.5 %copy-start.87 = (f32[384]{0:T(512)}, f32[384]{0:T(512)S(1)}, u32[]{:S(2)}) copy-start(f32[384]{0:T(512)S(1)} %add_rsqrt_fusion.2) | copy-start | bytes 4612
  106.4 11.4 %slice-start.9 = ((s8[4718592]{0:T(1024)(128)(4,1)}), s8[524288]{0:T(1024)(128)(4,1)S(1)}, s32[]{:S(2)}) async-start(s8[4718592]{0:T(1024)(128)(4,1)} %bitcast.641), calls=%async_computation.23 | async-start | bytes 1048576
  106.4 15.3 %slice-start.5 = ((s8[7077888]{0:T(1024)(128)(4,1)}), s8[2883584]{0:T(1024)(128)(4,1)S(1)}, s32[]{:S(2)}) async-start(s8[7077888]{0:T(1024)(128)(4,1)} %bitcast.634), calls=%async_computation.19 | async-start | bytes 5767168
  121.4 75.6 %copy-start.15 = (f32[384,768]{1,0:T(8,128)}, f32[384,768]{1,0:T(8,128)S(1)}, u32[]{:S(2)}) copy-start(f32[384,768]{1,0:T(8,128)S(1)} %get-tuple-element.705) | copy-start | bytes 3538948
  125.6 213.1 %copy-start.63 = (s32[384]{0:T(512)}, s32[384]{0:T(512)S(1)}, u32[]{:S(2)}) copy-start(s32[384]{0:T(512)S(1)} %reduce.7) | copy-start | bytes 4612
  128.3 32.4 %copy-start.10 = (bf16[384,768]{0,1:T(8,128)(2,1)}, bf16[384,768]{0,1:T(8,128)(2,1)S(1)}, u32[]{:S(2)}) copy-start(bf16[384,768]{0,1:T(8,128)(2,1)S(1)} %copy.157) | copy-start | bytes 1769476
  129.8 28.3 %copy-start.53 = (bf16[128,768]{0,1:T(8,128)(2,1)}, bf16[128,768]{0,1:T(8,128)(2,1)S(1)}, u32[]{:S(2)}) copy-start(bf16[128,768]{0,1:T(8,128)(2,1)S(1)} %copy.156) | copy-start | bytes 589828
  185.1 9.7 %copy-start.19 = (f32[384,12,128]{0,2,1:T(8,128)S(1)}, f32[384,12,128]{0,2,1:T(8,128)}, u32[]{:S(2)}) copy-start(f32[384,12,128]{0,2,1:T(8,128)} %get-tuple-element.707) | copy-start | bytes 7077892
  199.1 27.8 %copy-start.35 = (bf16[384,768]{1,0:T(8,128)(2,1)}, bf16[384,768]{1,0:T(8,128)(2,1)S(1)}, u32[]{:S(2)}) copy-start(bf16[384,768]{1,0:T(8,128)(2,1)S(1)} %add_convert_fusion.2) | copy-start | bytes 1769476
  200.9 26.1 %all-to-all-start = ((bf16[8,60,768]{2,1,0:T(8,128)(2,1)}), bf16[8,60,768]{2,1,0:T(8,128)(2,1)S(1)}, u32[]{:S(2)}, u32[]{:S(2)}) async-start(bf16[8,60,768]{2,1,0:T(8,128)(2,1)} %reshape.687), calls=%async_computation | async-start | bytes 1572864 | tf_op jit(solution)/shard_map/all_to_all | solution.py:497
  226.9 9.1 %copy-start.42 = (bf16[8,60,768]{2,1,0:T(8,128)(2,1)}, bf16[8,60,768]{2,1,0:T(8,128)(2,1)S(1)}, u32[]{:S(2)}) copy-start(bf16[8,60,768]{2,1,0:T(8,128)(2,1)S(1)} %all-to-all-done) | copy-start | bytes 2211844
  226.9 30.8 %all-to-all-start.2 = ((bf16[8,60,768]{2,1,0:T(8,128)(2,1)}), bf16[8,60,768]{2,1,0:T(8,128)(2,1)}, u32[]{:S(2)}, u32[]{:S(2)}) async-start(bf16[8,60,768]{2,1,0:T(8,128)(2,1)} %reshape.692), calls=%async_computation.2 | async-start | bytes 1572864 | tf_op jit(solution)/shard_map/all_to_all | solution.py:550
  238.7 45.2 %slice-start.6 = ((s8[4718592]{0:T(1024)(128)(4,1)}), s8[524288]{0:T(1024)(128)(4,1)S(1)}, s32[]{:S(2)}) async-start(s8[4718592]{0:T(1024)(128)(4,1)} %bitcast.639), calls=%async_computation.20 | async-start | bytes 1048576
  257.7 29.7 %all-to-all-start.1 = ((bf16[8,60,768]{2,1,0:T(8,128)(2,1)}), bf16[8,60,768]{2,1,0:T(8,128)(2,1)S(1)}, u32[]{:S(2)}, u32[]{:S(2)}) async-start(bf16[8,60,768]{2,1,0:T(8,128)(2,1)} %fusion.146), calls=%async_computation.1 | async-start | bytes 1572864 | tf_op jit(solution)/shard_map/all_to_all | solution.py:505
  263.6 20.2 %slice-start.7 = ((s8[4718592]{0:T(1024)(128)(4,1)}), s8[4194304]{0:T(1024)(128)(4,1)S(1)}, s32[]{:S(2)}) async-start(s8[4718592]{0:T(1024)(128)(4,1)} %bitcast.639), calls=%async_computation.21 | async-start | bytes 8388608
  287.4 52.0 %all-to-all-start.3 = ((bf16[8,60,768]{2,1,0:T(8,128)(2,1)}), bf16[8,60,768]{2,1,0:T(8,128)(2,1)}, u32[]{:S(2)}, u32[]{:S(2)}) async-start(bf16[8,60,768]{2,1,0:T(8,128)(2,1)} %fusion.141), calls=%async_computation.3 | async-start | bytes 1572864 | tf_op jit(solution)/shard_map/all_to_all | solution.py:571
  293.4 190.8 %reduce-scatter.5.cloned.1.call-start = ((), (), s32[]{:S(2)}) async-start(), calls=%async_computation.10 | async-start | bytes 3932160 | tf_op jit(solution)/shard_map/reduce_scatter | solution.py:404
  335.8 8.5 copy-start.49
  445.8 203.9 %reduce-scatter.9.cloned.1.call-start = ((), (), s32[]{:S(2)}) async-start(), calls=%async_computation.12 | async-start | bytes 5898240 | tf_op jit(solution)/shard_map/reduce_scatter | solution.py:704
  452.5 200.3 %reduce-scatter.11.cloned.1.call-start = ((), (), s32[]{:S(2)}) async-start(), calls=%async_computation.13 | async-start | bytes 5898240 | tf_op jit(solution)/shard_map/reduce_scatter | solution.py:707
  471.5 184.1 %reduce-scatter.7.cloned.1.call-start = ((), (), s32[]{:S(2)}) async-start(), calls=%async_computation.11 | async-start | bytes 3932160 | tf_op jit(solution)/shard_map/reduce_scatter | solution.py:404
  476.1 14.8 %copy-start.59 = (bf16[128,768]{1,0:T(8,128)(2,1)}, bf16[128,768]{1,0:T(8,128)(2,1)S(1)}, u32[]{:S(2)}) copy-start(bf16[128,768]{1,0:T(8,128)(2,1)S(1)} %copy.171) | copy-start | bytes 589828
  476.5 14.4 %copy-start.47 = (bf16[384,768]{1,0:T(8,128)(2,1)}, bf16[384,768]{1,0:T(8,128)(2,1)S(1)}, u32[]{:S(2)}) copy-start(bf16[384,768]{1,0:T(8,128)(2,1)S(1)} %copy.174) | copy-start | bytes 1769476
  476.6 14.2 %copy-start.60 = (bf16[128,768]{1,0:T(8,128)(2,1)}, bf16[128,768]{1,0:T(8,128)(2,1)S(1)}, u32[]{:S(2)}) copy-start(bf16[128,768]{1,0:T(8,128)(2,1)S(1)} %copy.173) | copy-start | bytes 589828
  484.3 9.2 %slice-start.12 = ((s8[4718592]{0:T(1024)(128)(4,1)}), s8[4194304]{0:T(1024)(128)(4,1)S(1)}, s32[]{:S(2)}) async-start(s8[4718592]{0:T(1024)(128)(4,1)} %bitcast.645), calls=%async_computation.26 | async-start | bytes 8388608
  485.6 7.9 slice-start.2
  485.6 7.9 slice-start.10
  485.7 7.8 slice-start.3
  485.7 7.8 slice-start.11
  485.7 7.8 slice-start.13
  612.2 16.7 %copy-start.99 = (f32[768]{0:T(1024)S(1)}, f32[768]{0:T(1024)}, u32[]{:S(2)}) copy-start(f32[768]{0:T(1024)} %get-tuple-element.574) | copy-start | bytes 9220
  612.2 17.3 %copy-start.98 = (f32[768]{0:T(1024)S(1)}, f32[768]{0:T(1024)}, u32[]{:S(2)}) copy-start(f32[768]{0:T(1024)} %get-tuple-element.586) | copy-start | bytes 9220
  612.2 17.9 %copy-start.64 = (s32[384]{0:T(512)S(1)}, s32[384]{0:T(512)}, u32[]{:S(2)}) copy-start(s32[384]{0:T(512)} %copy-done.63) | copy-start | bytes 4612
  612.2 17.9 %copy-start.86 = (f32[384]{0:T(512)S(1)}, f32[384]{0:T(512)}, u32[]{:S(2)}) copy-start(f32[384]{0:T(512)} %copy-done.85) | copy-start | bytes 4612
  612.2 20.0 %copy-start.27 = (bf16[384,12,128]{0,2,1:T(8,128)(2,1)S(1)}, bf16[384,12,128]{0,2,1:T(8,128)(2,1)}, u32[]{:S(2)}) copy-start(bf16[384,12,128]{0,2,1:T(8,128)(2,1)} %copy-done.26) | copy-start | bytes 3538948
  624.6 12.0 %copy-start.13 = (f32[384,12,64]{0,2,1:T(8,128)S(1)}, f32[384,12,64]{0,2,1:T(8,128)}, u32[]{:S(2)}) copy-start(f32[384,12,64]{0,2,1:T(8,128)} %get-tuple-element.417) | copy-start | bytes 3538948
  634.7 10.1 %copy-start.103 = (f32[768]{0:T(1024)S(1)}, f32[768]{0:T(1024)}, u32[]{:S(2)}) copy-start(f32[768]{0:T(1024)} %get-tuple-element.578) | copy-start | bytes 9220
  634.7 10.7 %copy-start.102 = (f32[768]{0:T(1024)S(1)}, f32[768]{0:T(1024)}, u32[]{:S(2)}) copy-start(f32[768]{0:T(1024)} %get-tuple-element.588) | copy-start | bytes 9220
  634.7 11.3 %copy-start.101 = (f32[768]{0:T(1024)S(1)}, f32[768]{0:T(1024)}, u32[]{:S(2)}) copy-start(f32[768]{0:T(1024)} %get-tuple-element.576) | copy-start | bytes 9220
  634.7 11.9 %copy-start.100 = (f32[768]{0:T(1024)S(1)}, f32[768]{0:T(1024)}, u32[]{:S(2)}) copy-start(f32[768]{0:T(1024)} %get-tuple-element.587) | copy-start | bytes 9220
  634.7 12.4 %copy-start.48 = (bf16[384,768]{1,0:T(8,128)(2,1)S(1)}, bf16[384,768]{1,0:T(8,128)(2,1)}, u32[]{:S(2)}) copy-start(bf16[384,768]{1,0:T(8,128)(2,1)} %copy-done.47) | copy-start | bytes 1769476
  658.1 8.4 copy-start.3
  885.9 7.6 copy-start.30
  885.9 7.6 copy-start.76
  885.9 7.6 copy-start.84
  885.9 10.4 %copy-start.1 = (bf16[768,8]{0,1:T(8,128)(2,1)S(1)}, bf16[768,8]{0,1:T(8,128)(2,1)}, u32[]{:S(2)}) copy-start(bf16[768,8]{0,1:T(8,128)(2,1)} %param.26) | copy-start | bytes 36868
  (100 other events, 400.0 us)
Sparse Core Ops, SparseCore 0:
  28.9 31.2 all-gather.2
  125.7 28.5 all-gather.4
  445.9 38.3 reduce-scatter.4
  486.8 47.8 reduce-scatter.8
  537.1 47.8 reduce-scatter.10
  612.3 38.1 reduce-scatter.6

commit v2 on v1

--- a/solution.py
+++ b/solution.py
@@ -248,199 +248,431 @@
     return (inverse * inner, jnp.sum(upstream * unit_rows, axis=0), jnp.sum(upstream, axis=0))
 
 
-def as_heads(flat_rows):
-    return flat_rows.reshape(flat_rows.shape[0], HEADS, HEAD_DIM)
-
-
-def block_scores(queries, key_rows, allowed):
-    scores = jnp.einsum(
-        "qhd,khd->qhk", queries, as_heads(key_rows), preferred_element_type=jnp.float32
-    ) * HEAD_DIM ** (-0.5)
-    return jnp.where(allowed[:, None, :], scores, masked_score)
-
-
-def long_allowed(layout, first_row, row_count):
-    is_long, position = layout
-    key_place = first_row + jnp.arange(row_count, dtype=jnp.int32)
-    return is_long[:, None] & (key_place[None, :] <= position[:, None])
-
-
-def fold_block(running, queries, key_rows, value_rows, allowed):
-    running_top, running_total, weighted = running
-    scores = block_scores(queries, key_rows, allowed)
-    new_top = jnp.maximum(running_top, jnp.max(scores, axis=-1))
-    factor = jnp.exp(running_top - new_top)
-    weights = jnp.where(allowed[:, None, :], jnp.exp(scores - new_top[..., None]), 0.0)
-    running_total = running_total * factor + jnp.sum(weights, axis=-1)
-    weighted = weighted * factor[..., None] + jnp.einsum(
-        "qhk,khd->qhd",
-        weights.astype(jnp.bfloat16),
-        as_heads(value_rows),
-        preferred_element_type=jnp.float32,
-    )
-    return (new_top, running_total, weighted)
-
-
-def score_grads(queries, grad_heads, log_total, row_delta, block_keys, block_values, allowed):
-    scores = block_scores(queries, block_keys, allowed)
-    probs_block = jnp.where(allowed[:, None, :], jnp.exp(scores - log_total[..., None]), 0.0)
-    grad_probs = jnp.einsum(
-        "qhd,khd->qhk", grad_heads, as_heads(block_values), preferred_element_type=jnp.float32
-    )
-    grad_scores = (probs_block * (grad_probs - row_delta[..., None])).astype(jnp.bfloat16)
-    return (probs_block.astype(jnp.bfloat16), grad_scores)
-
-
-def attend_forward(normed_low, weight_in, layout, short_allowed):
-    model_width = normed_low.shape[1]
-    row_count = normed_low.shape[0]
-    mixed = jnp.dot(normed_low, weight_in, preferred_element_type=jnp.float32).astype(jnp.bfloat16)
-    queries = as_heads(mixed[:, :model_width])
-    key_rows = mixed[:, model_width : 2 * model_width]
-    value_rows = mixed[:, 2 * model_width :]
-    running = (
-        jnp.full((row_count, HEADS), masked_score, jnp.float32),
-        jnp.zeros((row_count, HEADS), jnp.float32),
-        jnp.zeros((row_count, HEADS, HEAD_DIM), jnp.float32),
-    )
-    running = fold_block(
-        running, queries, key_rows[LONG_DEV:], value_rows[LONG_DEV:], short_allowed
-    )
-    both = lax.all_gather(mixed[:LONG_DEV, model_width:], "dp", axis=0, tiled=True)
-    key_piece = (both[:, :model_width], both[:, model_width:])
-    running = fold_block(
-        running,
-        queries,
-        key_piece[0],
-        key_piece[1],
-        long_allowed(layout, jnp.int32(0), key_piece[0].shape[0]),
-    )
-    running_top, running_total, weighted = running
-    context = (weighted / running_total[..., None]).reshape(row_count, model_width)
-    return (mixed, context, running_top + jnp.log(running_total), key_piece)
-
-
-def attend_backward(mixed, context, log_total, gathered, grad_context, layout, short_allowed):
-    model_width = context.shape[1]
-    row_count = context.shape[0]
-    queries = as_heads(mixed[:, :model_width])
-    key_rows = mixed[:, model_width : 2 * model_width]
-    value_rows = mixed[:, 2 * model_width :]
-    grad_heads = as_heads(grad_context)
-    row_delta = jnp.sum(grad_heads.astype(jnp.float32) * as_heads(context), axis=-1)
-    head_scale = HEAD_DIM ** (-0.5)
-    short_probs, short_scores = score_grads(
-        queries,
-        grad_heads,
-        log_total,
-        row_delta,
-        key_rows[LONG_DEV:],
-        value_rows[LONG_DEV:],
-        short_allowed,
-    )
-    grad_query = (
-        jnp.einsum(
-            "qhk,khd->qhd",
-            short_scores,
-            as_heads(key_rows[LONG_DEV:]),
-            preferred_element_type=jnp.float32,
+def dot(a, b):
+    return jnp.dot(a, b, preferred_element_type=jnp.float32)
+
+
+def dot_rows(a, b):
+    return lax.dot_general(a, b, (((1,), (1,)), ((), ())), preferred_element_type=jnp.float32)
+
+
+def dot_columns(a, b):
+    return lax.dot_general(a, b, (((0,), (0,)), ((), ())), preferred_element_type=jnp.float32)
+
+
+def head_pair(rows):
+    first = lax.broadcasted_iota(jnp.int32, rows.shape, 1) < HEAD_DIM
+    zero = jnp.zeros_like(rows)
+    return jnp.concatenate([jnp.where(first, rows, zero), jnp.where(first, zero, rows)], axis=0)
+
+
+def pair_rows(both):
+    n = both.shape[1] // 2
+    return jnp.concatenate([both[:HEAD_DIM, :n], both[HEAD_DIM:, n:]], axis=0)
+
+
+def causal(keys, queries):
+    key = lax.broadcasted_iota(jnp.int32, (keys, 2 * queries), 0)
+    query = lax.broadcasted_iota(jnp.int32, (keys, 2 * queries), 1)
+    return key <= jnp.where(query >= queries, query - queries, query)
+
+
+def short_seen(doc_row, doc_col):
+    n = doc_row.shape[1]
+    same = doc_col == jnp.concatenate([doc_row, doc_row], axis=1)
+    return same & causal(n, n)
+
+
+class Links:
+    def __init__(self, n_dp):
+        self.me, self.expert = lax.axis_index("dp"), lax.axis_index("expert")
+        self.chips = n_dp // 2
+        self.chip, self.core = self.me // 2, self.me % 2
+        self.twin = self.me + 1 - 2 * self.core
+
+    def greet(self):
+        barrier = pltpu.get_barrier_semaphore()
+        pl.semaphore_signal(barrier, inc=1, device_id=(self.twin, self.expert), device_id_type=MESH)
+        for other in range(self.chips):
+
+            @pl.when(other != self.chip)
+            def _():
+                there = (2 * other + self.core, self.expert)
+                pl.semaphore_signal(barrier, inc=1, device_id=there, device_id_type=MESH)
+
+        pl.semaphore_wait(barrier, self.chips)
+
+    def copy(self, ref, send_sem, recv_sem, index):
+        return pltpu.make_async_remote_copy(
+            src_ref=ref,
+            dst_ref=ref,
+            send_sem=send_sem,
+            recv_sem=recv_sem,
+            device_id=(index, self.expert),
+            device_id_type=MESH,
         )
-        * head_scale
-    )
-    short_count = row_count - LONG_DEV
-    short_key_grad = (
-        jnp.einsum("qhk,qhd->khd", short_scores, queries, preferred_element_type=jnp.float32)
-        * head_scale
-    ).reshape(short_count, model_width)
-    short_value_grad = jnp.einsum(
-        "qhk,qhd->khd", short_probs, grad_heads, preferred_element_type=jnp.float32
-    ).reshape(short_count, model_width)
-    long_count = gathered[0].shape[0]
-
-    def visit(block_step, partial_state):
-        query_sum, key_terms, value_terms = partial_state
-        first_row = block_step * LONG_DEV
-        block_keys = lax.dynamic_slice_in_dim(gathered[0], first_row, LONG_DEV, 0)
-        block_values = lax.dynamic_slice_in_dim(gathered[1], first_row, LONG_DEV, 0)
-        probs_low, grad_scores = score_grads(
-            queries,
-            grad_heads,
-            log_total,
-            row_delta,
-            block_keys,
-            block_values,
-            long_allowed(layout, first_row, LONG_DEV),
+
+    def before(self, later, other):
+        return other > self.chip if later else other < self.chip
+
+
+class Spread:
+    def __init__(self, links, at, parts, later, far_sems, near_sems, recv_sems):
+        self.links, self.at, self.later = links, at, later
+        self.far_sems, self.near_sems, self.recv_sems = far_sems, near_sems, recv_sems
+
+    def _far(self, other, p):
+        k = self.links
+        return k.copy(self.at(k.me, p), self.far_sems.at[other, p], self.recv_sems.at[k.me, p], 2 * other + k.core)
+
+    def _near(self, block, p):
+        k = self.links
+        return k.copy(self.at(block, p), self.near_sems.at[block, p], self.recv_sems.at[block, p], k.twin)
+
+    def _twin_needs(self):
+        return self.links.core == (0 if self.later else 1)
+
+    def send(self, p):
+        k = self.links
+        for other in range(k.chips):
+
+            @pl.when(k.before(self.later, other))
+            def _():
+                self._far(other, p).start()
+
+        @pl.when(self._twin_needs())
+        def _():
+            self._near(k.me, p).start()
+
+    def sent(self, p):
+        k = self.links
+        for other in range(k.chips):
+
+            @pl.when(k.before(self.later, other))
+            def _():
+                self._far(other, p).wait_send()
+
+            @pl.when(k.before(not self.later, other))
+            def _():
+                self._near(2 * other + k.core, p).wait_send()
+
+        @pl.when(self._twin_needs())
+        def _():
+            self._near(k.me, p).wait_send()
+
+    def relay(self, p):
+        k = self.links
+        for other in range(k.chips):
+
+            @pl.when(k.before(not self.later, other))
+            def _():
+                block = 2 * other + k.core
+                copy = self._near(block, p)
+                copy.wait_recv()
+                copy.start()
+
+    def each(self, p, use):
+        k = self.links
+
+        @pl.when(k.core == (1 if self.later else 0))
+        def _():
+            self._near(k.twin, p).wait_recv()
+            use(k.twin)
+
+        for other in range(k.chips):
+
+            @pl.when(k.before(not self.later, other))
+            def _():
+                use(2 * other + k.core)
+                block = 2 * other + 1 - k.core
+                self._near(block, p).wait_recv()
+                use(block)
+
+
+def attend_kernel(
+    n_dp,
+    x_ref, gain_ref, shift_ref, w_in_ref, w_out_ref, doc_row_ref, doc_col_ref,
+    next_ref, normed_t_ref, context_ref, context_t_ref, kv_ref, q_ref, short_kv_ref, short_q_ref, lse_ref,
+    acc_ref, top_ref, total_ref,
+    kv_far, kv_near, kv_recv, q_far, q_near, q_recv,
+):
+    links = Links(n_dp)
+    me = links.me
+    pairs, long = kv_ref.shape[1], kv_ref.shape[3]
+    width = x_ref.shape[1]
+    x = x_ref[...]
+    center = x - jnp.mean(x, axis=-1, keepdims=True)
+    inverse = lax.rsqrt(jnp.mean(center * center, axis=-1, keepdims=True) + epsilon)
+    normed = (center * inverse * gain_ref[...] + shift_ref[...]).astype(jnp.bfloat16)
+
+    kv = dot(normed, w_in_ref[:, width:]).astype(jnp.bfloat16)
+    for h in range(pairs):
+        for part in range(2):
+            piece = kv[:, part * width + 128 * h : part * width + 128 * h + 128]
+            kv_ref[me, h, part] = piece[:long]
+            short_kv_ref[h, part] = piece[long:]
+    links.greet()
+    kv_spread = Spread(links, lambda b, p: kv_ref.at[b, p], pairs, True, kv_far, kv_near, kv_recv)
+    q_spread = Spread(links, lambda b, p: q_ref.at[b], 1, False, q_far, q_near, q_recv)
+    for h in range(pairs):
+        kv_spread.send(h)
+    q = (dot(normed, w_in_ref[:, :width]).astype(jnp.bfloat16) * HEAD_DIM ** (-0.5)).astype(jnp.bfloat16)
+    for h in range(pairs):
+        piece = q[:, 128 * h : 128 * h + 128]
+        q_ref[me, h] = piece[:long]
+        short_q_ref[h] = piece[long:]
+    q_spread.send(0)
+    normed_t_ref[...] = normed.T
+
+    def put_context(h, rows_t, first, count):
+        at = pl.ds(pl.multiple_of(128 * h, 128), 128)
+        context_t_ref[at, first : first + count] = rows_t.astype(jnp.bfloat16)
+        context_ref[first : first + count, at] = rows_t.T.astype(jnp.bfloat16)
+
+    def own_part(h, _):
+        seen = short_seen(doc_row_ref[...], doc_col_ref[...])
+        scores = jnp.where(seen, dot_rows(short_kv_ref[h, 0], head_pair(short_q_ref[h])), masked_score)
+        top = jnp.max(scores, axis=0, keepdims=True)
+        weights = jnp.exp(scores - top)
+        total = jnp.sum(weights, axis=0, keepdims=True)
+        rows_t = pair_rows(dot_columns(short_kv_ref[h, 1], weights.astype(jnp.bfloat16)) / total)
+        short = rows_t.shape[1]
+        put_context(h, rows_t, long, short)
+        lse = top + jnp.log(total)
+        lse_ref[h, 0:1, long:] = lse[:, :short]
+        lse_ref[h, 1:2, long:] = lse[:, short:]
+        scores = jnp.where(causal(long, long), dot_rows(kv_ref[me, h, 0], head_pair(q_ref[me, h])), masked_score)
+        top = jnp.max(scores, axis=0, keepdims=True)
+        weights = jnp.exp(scores - top)
+        top_ref[h] = top
+        total_ref[h] = jnp.sum(weights, axis=0, keepdims=True)
+        acc_ref[h] = dot_columns(kv_ref[me, h, 1], weights.astype(jnp.bfloat16))
+        return 0
+
+    lax.fori_loop(0, pairs, own_part, 0)
+
+    def other_part(h, _):
+        kv_spread.relay(h)
+        queries = head_pair(q_ref[me, h])
+
+        def use(block):
+            scores = dot_rows(kv_ref[block, h, 0], queries)
+            old = top_ref[h]
+            top = jnp.maximum(old, jnp.max(scores, axis=0, keepdims=True))
+            factor = jnp.exp(old - top)
+            weights = jnp.exp(scores - top)
+            top_ref[h] = top
+            total_ref[h] = total_ref[h] * factor + jnp.sum(weights, axis=0, keepdims=True)
+            acc_ref[h] = acc_ref[h] * factor + dot_columns(kv_ref[block, h, 1], weights.astype(jnp.bfloat16))
+
+        kv_spread.each(h, use)
+        total = total_ref[h]
+        put_context(h, pair_rows(acc_ref[h] / total), 0, long)
+        lse = top_ref[h] + jnp.log(total)
+        lse_ref[h, 0:1, :long] = lse[:, :long]
+        lse_ref[h, 1:2, :long] = lse[:, long:]
+        return 0
+
+    lax.fori_loop(0, pairs, other_part, 0)
+    next_ref[...] = x + dot(context_ref[...], w_out_ref[...])
+    q_spread.relay(0)
+    q_spread.each(0, lambda block: None)
+    q_spread.sent(0)
+    for h in range(pairs):
+        kv_spread.sent(h)
+
+
+def spread_sems(n_dp, parts):
+    return [
+        pltpu.SemaphoreType.DMA((n_dp // 2, parts)),
+        pltpu.SemaphoreType.DMA((n_dp, parts)),
+        pltpu.SemaphoreType.DMA((n_dp, parts)),
+    ]
+
+
+def attention_forward(n_dp, collective_id, stream, norm_gain, norm_shift, weight_in, weight_out, doc_row, doc_col):
+    rows, width = stream.shape
+    long, short, pairs = LONG_DEV, rows - LONG_DEV, width // 128
+    low = jnp.bfloat16
+    outs = [
+        jax.ShapeDtypeStruct((rows, width), jnp.float32),
+        jax.ShapeDtypeStruct((width, rows), low),
+        jax.ShapeDtypeStruct((rows, width), low),
+        jax.ShapeDtypeStruct((width, rows), low),
+        jax.ShapeDtypeStruct((n_dp, pairs, 2, long, 128), low),
+        jax.ShapeDtypeStruct((n_dp, pairs, long, 128), low),
+        jax.ShapeDtypeStruct((pairs, 2, short, 128), low),
+        jax.ShapeDtypeStruct((pairs, short, 128), low),
+        jax.ShapeDtypeStruct((pairs, 2, rows), jnp.float32),
+    ]
+    vmem = pl.BlockSpec(memory_space=pltpu.VMEM)
+    return pl.pallas_call(
+        functools.partial(attend_kernel, n_dp),
+        out_shape=outs,
+        in_specs=[vmem] * 7,
+        out_specs=[vmem] * len(outs),
+        scratch_shapes=[
+            pltpu.VMEM((pairs, 128, 2 * long), jnp.float32),
+            pltpu.VMEM((pairs, 1, 2 * long), jnp.float32),
+            pltpu.VMEM((pairs, 1, 2 * long), jnp.float32),
+        ]
+        + spread_sems(n_dp, pairs)
+        + spread_sems(n_dp, 1),
+        compiler_params=pltpu.CompilerParams(
+            collective_id=collective_id, has_side_effects=True, vmem_limit_bytes=48 * 1024 * 1024
+        ),
+        name="attention_forward",
+    )(stream, norm_gain, norm_shift, weight_in, weight_out, doc_row, doc_col)
+
+
+def attend_back_kernel(
+    n_dp,
+    up_ref, x_ref, gain_ref, w_in_ref, w_out_ref, doc_row_ref, doc_col_ref,
+    context_ref, kv_ref, q_ref, short_kv_ref, short_q_ref, lse_ref,
+    up_next_ref, up_low_ref, mixed_ref, sums_ref,
+    do_ref, aux_ref, short_do_ref, short_aux_ref, dq_ref, dk_ref, dv_ref,
+    do_far, do_near, do_recv, aux_far, aux_near, aux_recv,
+):
+    links = Links(n_dp)
+    me = links.me
+    pairs, long, width = kv_ref.shape[1], kv_ref.shape[3], x_ref.shape[1]
+    scale = HEAD_DIM ** (-0.5)
+    up = up_ref[...]
+    up_low = up.astype(jnp.bfloat16)
+    up_low_ref[...] = up_low
+    grad_context = dot_rows(up_low, w_out_ref[...]).astype(jnp.bfloat16)
+    lane = lax.broadcasted_iota(jnp.int32, (8, 128), 1) < HEAD_DIM
+    head = lax.broadcasted_iota(jnp.int32, (8, 128), 0)
+    picks = jnp.where(((head == 0) & lane) | ((head == 1) & ~lane), 1.0, 0.0)
+    for h in range(pairs):
+        at = slice(128 * h, 128 * h + 128)
+        piece = grad_context[:, at]
+        do_ref[me, h] = piece[:long]
+        short_do_ref[h] = piece[long:]
+        both = piece.astype(jnp.float32) * context_ref[:, at].astype(jnp.float32)
+        delta = lax.dot_general(
+            picks, both, (((1,), (1,)), ((), ())), precision=lax.Precision.HIGHEST, preferred_element_type=jnp.float32
         )
-        more_query = (
-            jnp.einsum(
-                "qhk,khd->qhd",
-                grad_scores,
-                as_heads(block_keys),
-                preferred_element_type=jnp.float32,
-            )
-            * head_scale
-        )
-        more_key = (
-            jnp.einsum("qhk,qhd->khd", grad_scores, queries, preferred_element_type=jnp.float32)
-            * head_scale
-        ).reshape(LONG_DEV, model_width)
-        more_value = jnp.einsum(
-            "qhk,qhd->khd", probs_low, grad_heads, preferred_element_type=jnp.float32
-        ).reshape(LONG_DEV, model_width)
-        return (
-            query_sum + more_query,
-            lax.dynamic_update_slice_in_dim(key_terms, more_key, first_row, 0),
-            lax.dynamic_update_slice_in_dim(value_terms, more_value, first_row, 0),
-        )
-
-    start_state = (
-        grad_query,
-        jnp.zeros((long_count, model_width), jnp.float32),
-        jnp.zeros((long_count, model_width), jnp.float32),
-    )
-    grad_query, key_terms, value_terms = lax.fori_loop(
-        0, long_count // LONG_DEV, visit, start_state
-    )
-    own = lax.psum_scatter(
-        jnp.concatenate([key_terms, value_terms], axis=1).astype(jnp.bfloat16), "dp", scatter_dimension=0, tiled=True
-    ).astype(jnp.float32)
-    own_keys, own_values = own[:, :model_width], own[:, model_width:]
-    grad_keys = jnp.concatenate([own_keys, short_key_grad], axis=0)
-    grad_values = jnp.concatenate([own_values, short_value_grad], axis=0)
-    return jnp.concatenate(
-        [grad_query.reshape(row_count, model_width), grad_keys, grad_values], axis=1
-    ).astype(jnp.bfloat16)
-
-
-def attention_forward(stream, norm_gain, norm_shift, weight_in, weight_out, layout, short_allowed):
-    normed, unit_rows, inverse = norm_forward(stream, norm_gain, norm_shift)
-    normed_low = normed.astype(jnp.bfloat16)
-    mixed, context, log_total, gathered = attend_forward(
-        normed_low, weight_in, layout, short_allowed
-    )
-    context_low = context.astype(jnp.bfloat16)
-    stream_next = stream + jnp.dot(context_low, weight_out, preferred_element_type=jnp.float32)
-    return (
-        stream_next,
-        (unit_rows, inverse, normed_low, mixed, context, context_low, log_total, gathered),
-    )
-
-
-def attention_backward(
-    upstream, kept_state, norm_gain, weight_in, weight_out, layout, short_allowed
-):
-    unit_rows, inverse, normed_low, mixed, context, context_low, log_total, gathered = kept_state
-    upstream_low = upstream.astype(jnp.bfloat16)
-    grad_context = jnp.einsum(
-        "te,de->td", upstream_low, weight_out, preferred_element_type=jnp.float32
-    ).astype(jnp.bfloat16)
-    grad_mixed = attend_backward(
-        mixed, context, log_total, gathered, grad_context, layout, short_allowed
-    )
-    grad_normed = jnp.einsum("te,de->td", grad_mixed, weight_in, preferred_element_type=jnp.float32)
-    grad_stream, grad_gain, grad_shift = norm_backward(unit_rows, inverse, norm_gain, grad_normed)
-    pairs = ((context_low, upstream_low), (normed_low, grad_mixed))
-    return (upstream + grad_stream, pairs, grad_gain, grad_shift)
+        aux_ref[me, h, 0:2] = lse_ref[h, :, :long]
+        aux_ref[me, h, 2:4] = delta[0:2, :long]
+        short_aux_ref[h, 0:2] = lse_ref[h, :, long:]
+        short_aux_ref[h, 2:4] = delta[0:2, long:]
+    links.greet()
+    do_spread = Spread(links, lambda b, p: do_ref.at[b, p], pairs, False, do_far, do_near, do_recv)
+    aux_spread = Spread(links, lambda b, p: aux_ref.at[b, p], pairs, False, aux_far, aux_near, aux_recv)
+    for h in range(pairs):
+        do_spread.send(h)
+        aux_spread.send(h)
+
+    def row_of(aux, first):
+        return jnp.concatenate([aux[first : first + 1], aux[first + 1 : first + 2]], axis=1)
+
+    def score_grads(keys, values, queries, grads, aux, seen):
+        scores = dot_rows(keys, queries)
+        probs = jnp.exp(scores - row_of(aux, 0))
+        if seen is not None:
+            probs = jnp.where(seen, probs, 0.0)
+        grad_scores = probs * (dot_rows(values, grads) - row_of(aux, 2))
+        return probs.astype(jnp.bfloat16), grad_scores.astype(jnp.bfloat16)
+
+    def put(h, third, first, value):
+        at = pl.ds(pl.multiple_of(third * width + 128 * h, 128), 128)
+        mixed_ref[first : first + value.shape[0], at] = value.astype(jnp.bfloat16)
+
+    def own_part(h, _):
+        seen = short_seen(doc_row_ref[...], doc_col_ref[...])
+        queries, grads = head_pair(short_q_ref[h]), head_pair(short_do_ref[h])
+        keys = short_kv_ref[h, 0]
+        probs, grad_scores = score_grads(keys, short_kv_ref[h, 1], queries, grads, short_aux_ref[h], seen)
+        put(h, 0, long, (pair_rows(dot_columns(keys, grad_scores)) * scale).T)
+        put(h, 1, long, dot(grad_scores, queries))
+        put(h, 2, long, dot(probs, grads))
+        queries, grads = head_pair(q_ref[me, h]), head_pair(do_ref[me, h])
+        keys = kv_ref[me, h, 0]
+        probs, grad_scores = score_grads(keys, kv_ref[me, h, 1], queries, grads, aux_ref[me, h], causal(long, long))
+        dq_ref[h] = dot_columns(keys, grad_scores)
+        dk_ref[h] = dot(grad_scores, queries)
+        dv_ref[h] = dot(probs, grads)
+        for block in range(n_dp - 1):
+
+            @pl.when(block < me)
+            def _():
+                keys = kv_ref[block, h, 0]
+                _, grad_scores = score_grads(keys, kv_ref[block, h, 1], queries, grads, aux_ref[me, h], None)
+                dq_ref[h] += dot_columns(keys, grad_scores)
+
+        put(h, 0, 0, (pair_rows(dq_ref[h]) * scale).T)
+        return 0
+
+    lax.fori_loop(0, pairs, own_part, 0)
+
+    def other_part(h, _):
+        do_spread.relay(h)
+        aux_spread.relay(h)
+        keys, values = kv_ref[me, h, 0], kv_ref[me, h, 1]
+
+        def use(block):
+            queries, grads = head_pair(q_ref[block, h]), head_pair(do_ref[block, h])
+            probs, grad_scores = score_grads(keys, values, queries, grads, aux_ref[block, h], None)
+            dk_ref[h] += dot(grad_scores, queries)
+            dv_ref[h] += dot(probs, grads)
+
+        aux_spread.each(h, lambda block: None)
+        do_spread.each(h, use)
+        put(h, 1, 0, dk_ref[h])
+        put(h, 2, 0, dv_ref[h])
+        return 0
+
+    lax.fori_loop(0, pairs, other_part, 0)
+    grad_normed = dot_rows(mixed_ref[...], w_in_ref[...])
+    x = x_ref[...]
+    center = x - jnp.mean(x, axis=-1, keepdims=True)
+    inverse = lax.rsqrt(jnp.mean(center * center, axis=-1, keepdims=True) + epsilon)
+    unit = center * inverse
+    scaled = grad_normed * gain_ref[...]
+    inner = (
+        scaled - jnp.mean(scaled, axis=-1, keepdims=True) - unit * jnp.mean(scaled * unit, axis=-1, keepdims=True)
+    )
+    up_next_ref[...] = up + inverse * inner
+    sums_ref[0:1] = jnp.sum(grad_normed * unit, axis=0, keepdims=True)
+    sums_ref[1:2] = jnp.sum(grad_normed, axis=0, keepdims=True)
+    for h in range(pairs):
+        do_spread.sent(h)
+        aux_spread.sent(h)
+
+
+def attention_backward(n_dp, collective_id, upstream, stream, norm_gain, weight_in, weight_out, doc_row, doc_col, kept):
+    rows, width = stream.shape
+    long, short, pairs = LONG_DEV, rows - LONG_DEV, width // 128
+    low = jnp.bfloat16
+    outs = [
+        jax.ShapeDtypeStruct((rows, width), jnp.float32),
+        jax.ShapeDtypeStruct((rows, width), low),
+        jax.ShapeDtypeStruct((rows, 3 * width), low),
+        jax.ShapeDtypeStruct((2, width), jnp.float32),
+    ]
+    vmem = pl.BlockSpec(memory_space=pltpu.VMEM)
+    return pl.pallas_call(
+        functools.partial(attend_back_kernel, n_dp),
+        out_shape=outs,
+        in_specs=[vmem] * 13,
+        out_specs=[vmem] * len(outs),
+        scratch_shapes=[
+            pltpu.VMEM((n_dp, pairs, long, 128), low),
+            pltpu.VMEM((n_dp, pairs, 8, long), jnp.float32),
+            pltpu.VMEM((pairs, short, 128), low),
+            pltpu.VMEM((pairs, 8, short), jnp.float32),
+            pltpu.VMEM((pairs, 128, 2 * long), jnp.float32),
+            pltpu.VMEM((pairs, long, 128), jnp.float32),
+            pltpu.VMEM((pairs, long, 128), jnp.float32),
+        ]
+        + spread_sems(n_dp, pairs)
+        + spread_sems(n_dp, pairs),
+        compiler_params=pltpu.CompilerParams(
+            collective_id=collective_id, has_side_effects=True, vmem_limit_bytes=48 * 1024 * 1024
+        ),
+        name="attention_backward",
+    )(upstream, stream, norm_gain, weight_in, weight_out, doc_row, doc_col, *kept)
 
 
 def ffn_forward(stream, norm_gain, norm_shift, weight_in, weight_out):
@@ -611,36 +843,21 @@
     expert_out,
     cotangent,
 ):
+    n_dp, n_ex = lax.axis_size("dp"), lax.axis_size("expert")
     stream_first = tokens[0].astype(jnp.float32)
     row_count = stream_first.shape[0]
-    row_index = jnp.arange(row_count, dtype=jnp.int32)
-    is_long = row_index < LONG_DEV
-    layout = (is_long, lax.axis_index("dp") * LONG_DEV + row_index)
     doc_ends = jnp.cumsum(doc_lengths[0, 0])
     short_place = jnp.arange(row_count - LONG_DEV, dtype=jnp.int32)
     short_ids = jnp.sum((short_place[:, None] >= doc_ends[None, :]).astype(jnp.int32), axis=-1)
-    row_docs = jnp.concatenate([jnp.full((LONG_DEV,), -1, jnp.int32), short_ids])
-    short_allowed = (row_docs[:, None] == short_ids[None, :]) & (
-        short_place[None, :] + LONG_DEV <= row_index[:, None]
-    )
-    stream_one, kept_one = attention_forward(
-        stream_first,
-        ln_gain[:, 0],
-        ln_bias[:, 0],
-        attn_in[:, 0],
-        attn_out[:, 0],
-        layout,
-        short_allowed,
+    doc_row, doc_col = short_ids[None, :], short_ids[:, None]
+    weights_in, weights_out = lax.optimization_barrier((attn_in.transpose(1, 0, 2), attn_out.transpose(1, 0, 2)))
+    gains, shifts = ln_gain.T, ln_bias.T
+    stream_one, *kept_one = attention_forward(
+        n_dp, 2, stream_first, gains[0:1], shifts[0:1], weights_in[0], weights_out[0], doc_row, doc_col
     )
     stream_two, kept_two = ffn_forward(stream_one, ln_gain[:, 1], ln_bias[:, 1], ffn_in, ffn_out)
-    stream_three, kept_three = attention_forward(
-        stream_two,
-        ln_gain[:, 2],
-        ln_bias[:, 2],
-        attn_in[:, 1],
-        attn_out[:, 1],
-        layout,
-        short_allowed,
+    stream_three, *kept_three = attention_forward(
+        n_dp, 3, stream_two, gains[2:3], shifts[2:3], weights_in[1], weights_out[1], doc_row, doc_col
     )
     stream_four, balance, kept_four = mixture_forward(
         stream_three, ln_gain[:, 3], ln_bias[:, 3], router, expert_in, expert_out, assign[0, :, 0]
@@ -650,22 +867,30 @@
     upstream, expert_in_grad, expert_out_grad, router_grad, gain_three, shift_three = (
         mixture_backward(upstream, kept_four, ln_gain[:, 3], router, expert_in, expert_out)
     )
-    upstream, second_pairs, gain_two, shift_two = attention_backward(
-        upstream, kept_three, ln_gain[:, 2], attn_in[:, 1], attn_out[:, 1], layout, short_allowed
+    upstream, second_low, second_mixed, second_sums = attention_backward(
+        n_dp, 4, upstream, stream_two, gains[2:3], weights_in[1], weights_out[1], doc_row, doc_col,
+        kept_three[1:2] + kept_three[3:],
     )
     upstream, dense_pairs, gain_one, shift_one = ffn_backward(upstream, kept_two, ln_gain[:, 1], ffn_in, ffn_out)
-    upstream, first_pairs, gain_zero, shift_zero = attention_backward(
-        upstream, kept_one, ln_gain[:, 0], attn_in[:, 0], attn_out[:, 0], layout, short_allowed
+    upstream, first_low, first_mixed, first_sums = attention_backward(
+        n_dp, 5, upstream, stream_first, gains[0:1], weights_in[0], weights_out[0], doc_row, doc_col,
+        kept_one[1:2] + kept_one[3:],
     )
     grad_tokens = upstream.astype(jnp.bfloat16)[None]
-    n_dp, n_ex = lax.axis_size("dp"), lax.axis_size("expert")
     model_width = tokens.shape[2]
     rows = model_width // n_dp
 
     def blocks_of(acts):
         return acts.T.reshape(n_dp, -1, rows, row_count).astype(jnp.bfloat16)
 
-    pairs = [(blocks_of(x), dy) for x, dy in second_pairs + dense_pairs + first_pairs]
+    pairs = [(blocks_of(x), dy) for x, dy in dense_pairs]
+    pairs = (
+        [(kept_three[2].reshape(n_dp, 1, rows, row_count), second_low)]
+        + [(kept_three[0].reshape(n_dp, 1, rows, row_count), second_mixed)]
+        + pairs
+        + [(kept_one[2].reshape(n_dp, 1, rows, row_count), first_low)]
+        + [(kept_one[0].reshape(n_dp, 1, rows, row_count), first_mixed)]
+    )
     chunks = reduce_grads(n_dp, n_ex, pairs, model_width).astype(jnp.float32)
 
     def wide(first, count):
@@ -684,7 +909,8 @@
     first_in = wide(at + 1, per_in)
     small = jnp.concatenate(
         [
-            jnp.stack([gain_zero, gain_one, gain_two, gain_three, shift_zero, shift_one, shift_two, shift_three], axis=0),
+            jnp.stack([first_sums[0], gain_one, second_sums[0], gain_three], axis=0),
+            jnp.stack([first_sums[1], shift_one, second_sums[1], shift_three], axis=0),
             router_grad.T,
         ],
         axis=0,

time: 916 us -> 639 us (0.70)
  matrix products: 293 us -> 118 us
  local copies, waits for them, and re-layouts: 201 us -> 70.1 us
  Pallas kernels: 144 us -> 264 us
  other arithmetic: 84.2 us -> 31.6 us
  waiting for transfers between devices: 62.2 us -> 27.2 us
    dot_general x64 -> x0, matrix products: 187 us -> none  [the longest x12 37 us: block_scores(): jnp.einsum('qhd,khd->qhk', queries, as_heads(key_rows), preferred_element...]
    pallas_call x0 -> x4, Pallas kernels: none -> 121 us  [the longest x2 66.5 us: attention_backward(): pl.pallas_call(functools.partial(attend_back_kernel, n_dp), out_shape=out...]
    slice x23 -> x4, local copies, waits for them, and re-layouts: 53 us -> 0.24 us  [the longest x6 18.3 us: attend_forward(): key_piece = (both[:, :model_width], both[:, model_width:])]
    dynamic_update_slice x24 -> x0, local copies, waits for them, and re-layouts: 47.1 us -> none  [the longest x16 31.7 us: visit(): lax.dynamic_update_slice_in_dim(value_terms, more_value, first_row, 0)]
    all_gather x2 -> x0, waiting for transfers between devices: 39 us -> none  [attend_forward(): lax.all_gather(mixed[:LONG_DEV, model_width:], 'dp', axis=0, tiled=True)]
    reduce_sum x6 -> x0, other arithmetic: 25.7 us -> none  [the longest x4 22.5 us: fold_block(): running_total = running_total * factor + jnp.sum(weights, axis=-1)]
    dynamic_slice x16 -> x0, local copies, waits for them, and re-layouts: 19.2 us -> none  [the longest x8 10.8 us: visit(): block_values = lax.dynamic_slice_in_dim(gathered[1], first_row, LONG_DEV, 0)]
    all_to_all x1, waiting for transfers between devices: 0.01 us -> 12 us  [mixture_backward(): lax.all_to_all(outgoing, 'expert', split_axis=0, concat_axis=0, tiled=True)]
  transfers between devices with their start and end apart: 10 -> 6, of which waited for: 4 -> 2; matrix products, arithmetic and copies ran while one was open for 30% -> 22% of each run, Pallas kernels for 0% -> 33%
where the time goes in v2:
time: 639 us; the launch traced here: 633 us
  Pallas kernels  264 us (41%)
  matrix products  118 us (18%)
  blocking collectives  85.7 us (13%)
  local copies, waits for them, and re-layouts  70.1 us (11%)
  other arithmetic  31.6 us (5%)
  waiting for transfers between devices  27.2 us (4%)
  starting transfers between devices  19.4 us (3%)
  between operations  17.1 us (3%)
    pallas_call x1, Pallas kernels, reduce_grads(): pl.pallas_call(functools.partial(grad_kernel, n_dp, n_ex, rows, kinds, ha...  144 us
    pallas_call x2, Pallas kernels, attention_backward(): pl.pallas_call(functools.partial(attend_back_kernel, n_dp), out_shape=out...  66.5 us
    pallas_call x2, Pallas kernels, attention_forward(): pl.pallas_call(functools.partial(attend_kernel, n_dp), out_shape=outs, in...  54.4 us
    psum x1, blocking collectives, mixture_forward(): counts = lax.psum(jnp.sum(chosen_hot, axis=0), ('dp', 'expert'))  45 us
    psum x1, blocking collectives, mixture_forward(): lax.psum(jnp.sum(gate_value[:, None] * chosen_hot, axis=0), ('dp', 'exper...  40.7 us
    unnamed x151, local copies, waits for them, and re-layouts  31.7 us
    dot_general x1, matrix products, mixture_forward(): jnp.einsum('sjcf,jfd->sjcd', active, expert_out, preferred_element_type=j...  20 us
    dot_general x1, matrix products, mixture_backward(): jnp.einsum('sjcf,sjcd->jfd', active, grouped_grad, preferred_element_type...  19.1 us
  transfers between devices with their start and end apart: 6, of which 2 were waited for; matrix products, arithmetic and copies ran while one was open for 22% of the time, Pallas kernels for 33%

profile of v2, /device:TPU:0, one launch (start us, length us, event | category | flops | bytes accessed | tf_op | source)
XLA Modules:
  0.0 633.5 jit_solution(7700088988780957217)
XLA Ops:
  8.2 4.0 copy.63
  12.6 3.4 slice_bitcast_fusion
  16.1 0.9 copy-done.46
  17.2 1.2 copy-done.7
  18.4 26.1 %attention_forward.2 = (f32[384,768]{1,0:T(8,128)S(1)}, bf16[768,384]{1,0:T(8,128)(2,1)S(1)}, bf16[384,768]{1,0:T(8,128)(2,1)S(1)}, bf16[768,384]{1,0:T(8,128)(2...) custom-call(f32[384,768]{1,0:T(8,128)S(1)} %bitcast_convert_fusion.2, ...), custom_call_target="tpu_custom_call" | custom-call | tf_op jit(solution)/shard_map/attention_forward/pallas_call | solution.py:509
  45.3 0.8 copy-done.17
  47.3 12.9 %fusion.18 = (f32[384,3072]{1,0:T(8,128)S(1)}, f32[384,3072]{1,0:T(8,128)S(1)}) fusion(bf16[768,3072]{1,0:T(8,128)(2,1)} %param.20, f32[384,768]{1,0:T(8,128)S(1)} %get-tuple-element.42, f32[768]{0:T(1024)S(1)} %get-tuple-element.115, f32[768]{0:T(1024)S(1)} %get-tuple-element.148, f32[384]{0:T(512)S(1)} %add_rsqrt_fusion.1, ...), kind=kOutput, calls=%fused_computation.32 | convolution fusion | flops 1886552064 | bytes 15344640 | tf_op jit(solution)/shard_map/dot_general | solution.py:681
  60.3 7.7 %fusion.66.x_ref = f32[384,768]{1,0:T(8,128)S(1)} fusion(f32[384,768]{1,0:T(8,128)S(1)} %get-tuple-element.42, bf16[3072,768]{1,0:T(8,128)(2,1)} %param.21, f32[384,3072]{1,0:T(8,128)S(1)} %get-tuple-element.141, f32[384,3072]{1,0:T(8,128)S(1)} %get-tuple-element.142), kind=kOutput, calls=%fused_computation.99 | convolution fusion | flops 1815773184 | bytes 16515072 | tf_op jit(solution)/shard_map/dot_general | solution.py:683
  68.1 28.3 %attention_forward.3 = (f32[384,768]{1,0:T(8,128)S(1)}, bf16[768,384]{1,0:T(8,128)(2,1)S(1)}, bf16[384,768]{1,0:T(8,128)(2,1)S(1)}, bf16[768,384]{1,0:T(8,128)(2...) custom-call(f32[384,768]{1,0:T(8,128)S(1)} %fusion.66.x_ref, ...), custom_call_target="tpu_custom_call" | custom-call | tf_op jit(solution)/shard_map/attention_forward/pallas_call | solution.py:509
  96.4 1.0 copy-done.5
  101.8 0.9 reduce-window.19
  103.3 1.5 convolution_convert_fusion.1
  104.9 2.0 reshape.224
  106.9 5.8 all-to-all-start
  113.7 1.7 convolution_convert_fusion
  115.4 2.0 reshape.229
  117.4 15.2 %all-to-all-done = bf16[8,60,768]{2,1,0:T(8,128)(2,1)} async-done(((bf16[8,60,768]{2,1,0:T(8,128)(2,1)}), bf16[8,60,768]{2,1,0:T(8,128)(2,1)}, u32[]{:S(2)}, u32[]{:S(2)}) %all-to-all-start) | async-done | bytes 737312 | tf_op jit(solution)/shard_map/all_to_all | solution.py:729
  132.6 3.5 all-to-all-start.2
  136.7 7.9 %fusion.29 = f32[8,60,3072]{2,1,0:T(8,128)} fusion(bf16[8,60,768]{2,1,0:T(8,128)(2,1)} %all-to-all-done, bf16[1,768,3072]{2,1,0:T(8,128)(2,1)} %param.23), kind=kOutput, calls=%fused_computation.47 | convolution fusion | flops 2264924160 | bytes 11354112 | tf_op jit(solution)/shard_map/sjcd,jdf->sjcf/dot_general | solution.py:732
  144.6 12.0 %all-to-all-done.2 = bf16[8,60,768]{2,1,0:T(8,128)(2,1)S(1)} async-done(((bf16[8,60,768]{2,1,0:T(8,128)(2,1)}), bf16[8,60,768]{2,1,0:T(8,128)(2,1)S(1)}, u32[]{:S(2)}, u32[]{:S(2)}) %all-to-all-start.2) | async-done | bytes 737312 | tf_op jit(solution)/shard_map/all_to_all | solution.py:782
  156.5 18.3 %fusion.6 = bf16[8,1,60,3072]{3,2,0,1:T(8,128)(2,1)S(1)} fusion(f32[8,60,3072]{2,1,0:T(8,128)} %fusion.29, bf16[8,60,768]{2,1,0:T(8,128)(2,1)S(1)} %all-to-all-done.2, bf16[1,3072,768]{2,1,0:T(8,128)(2,1)} %param.24), kind=kOutput, calls=%fused_computation.14 | convolution fusion | flops 2371092480 | bytes 14303232 | tf_op jit(solution)/shard_map/sjcd,jfd->sjcf/dot_general | solution.py:793
  174.9 1.7 copy-done.70
  176.6 5.4 fusion.49
  182.2 6.9 %fusion.58 = bf16[8,60,768]{2,1,0:T(8,128)(2,1)} fusion(bf16[1,768,3072]{2,1,0:T(8,128)(2,1)} %param.23, bf16[8,1,60,3072]{3,2,0,1:T(8,128)(2,1)} %copy-done.70), kind=kOutput, calls=%fused_computation.95 | convolution fusion | flops 2265292800 | bytes 8404992 | tf_op jit(solution)/shard_map/sjcf,jdf->sjcd/dot_general | solution.py:800
  189.0 3.6 all-to-all-start.3
  192.7 19.1 %fusion.50 = bf16[1,3072,768]{2,1,0:T(8,128)(2,1)} fusion(bf16[8,60,768]{2,1,0:T(8,128)(2,1)S(1)} %copy-done.45, f32[8,60,3072]{2,1,0:T(8,128)} %fusion.29), kind=kOutput, calls=%fused_computation.78 | convolution fusion | flops 2363129856 | bytes 11354112 | tf_op jit(solution)/shard_map/sjcf,sjcd->jfd/dot_general | solution.py:790
  211.7 20.0 %fusion.63 = bf16[8,60,768]{2,1,0:T(8,128)(2,1)} fusion(bf16[1,3072,768]{2,1,0:T(8,128)(2,1)} %param.24, f32[8,60,3072]{2,1,0:T(8,128)} %fusion.29), kind=kOutput, calls=%fused_computation.96 | convolution fusion | flops 2361139200 | bytes 11354112 | tf_op jit(solution)/shard_map/sjcf,jfd->sjcd/dot_general | solution.py:734
  231.8 5.9 all-to-all-start.1
  237.7 12.0 %fusion.21 = bf16[3072,384]{0,1:T(8,128)(2,1)} fusion(f32[384,3072]{1,0:T(8,128)} %copy-done.35), kind=kLoop, calls=%fused_computation.35 | loop fusion | flops 76677120 | bytes 7077888 | tf_op jit(solution)/shard_map/convert_element_type | solution.py:682
  249.7 45.0 %psum.21 = f32[8]{0:T(128)S(1)} all-reduce(f32[8]{0:T(128)S(1)} %convert_reduce_fusion), channel_id=1, replica_groups=mesh['dp'=4,'expert'=8] {'dp','expert'}, use_global_device_ids=true, to_apply=%region_11.12 | all-reduce | flops 8 | bytes 64 | tf_op jit(solution)/shard_map/psum | solution.py:713
  294.7 4.4 copy.53
  299.2 1.1 reshape.231
  300.3 2.1 reshape.228
  302.4 2.0 fusion.68
  305.2 0.9 multiply_reduce_fusion
  306.1 1.4 convert_add_fusion
  307.5 33.2 %attention_backward.2 = (f32[384,768]{1,0:T(8,128)S(1)}, bf16[384,768]{1,0:T(8,128)(2,1)S(1)}, bf16[384,2304]{1,0:T(8,128)(2,1)}, f32[2,768]{1,0:T(2,128)S(1)}) custom-call(f32[384,768]{1,0:T(8,128)S(1)} %get-tuple-element.129.up_ref, f32[384,768]{1,0:T(8,128)S(1)} %copy-done.6, f32[1,768]{1,0:T(1,128)S(1)} %get-tuple-element.147.gain_ref, ...), custom_call_target="tpu_custom_call" | custom-call | tf_op jit(solution)/shard_map/attention_backward/pallas_call | solution.py:655
  340.8 7.0 %add_convert_fusion.refs_9_ = bf16[384,3072]{1,0:T(8,128)(2,1)S(1)} fusion(f32[384,3072]{1,0:T(8,128)} %copy-done.38, f32[384,3072]{1,0:T(8,128)S(1)} %bitcast.286, bf16[384,768]{1,0:T(8,128)(2,1)S(1)} %convert_element_type.119.refs_8_, bf16[3072,768]{1,0:T(8,128)(2,1)} %param.21), kind=kOutput, calls=%fused_computation.61 | convolution fusion | flops 1828454400 | bytes 17104896 | tf_op jit(solution)/shard_map/td,fd->tf/dot_general | solution.py:690
  347.9 5.2 fusion.104
  353.3 1.3 multiply_reduce_fusion.1
  355.2 33.2 %attention_backward.3 = (f32[384,768]{1,0:T(8,128)S(1)}, bf16[384,768]{1,0:T(8,128)(2,1)S(1)}, bf16[384,2304]{1,0:T(8,128)(2,1)}, f32[2,768]{1,0:T(2,128)S(1)}) custom-call(f32[384,768]{1,0:T(8,128)S(1)} %multiply_add_fusion.up_ref, f32[384,768]{1,0:T(8,128)S(1)} %copy-done.9, f32[1,768]{1,0:T(1,128)S(1)} %copy-done.32, ...), custom_call_target="tpu_custom_call" | custom-call | tf_op jit(solution)/shard_map/attention_backward/pallas_call | solution.py:655
  389.7 40.7 %all-reduce = (f32[8]{0:T(128)S(1)}, f32[16,768]{1,0:T(8,128)S(1)}) all-reduce(f32[8]{0:T(128)S(1)} %get-tuple-element.117, f32[16,768]{1,0:T(8,128)S(1)} %concatenate.3), channel_id=1, replica_groups=mesh['dp'=4,'expert'=8] {'dp','expert'}, use_global_device_ids=true, to_apply=%region_13.14 | all-reduce | flops 12296 | bytes 98368 | tf_op jit(solution)/shard_map/psum | solution.py:714
  430.4 1.4 copy.54
  431.7 1.1 copy-done.12
  432.8 1.1 copy-done.14
  433.9 1.1 copy-done.16
  434.9 1.1 copy-done.22
  436.0 1.1 copy-done.24
  437.1 143.6 %dense_grads.1 = bf16[16,192,768]{2,1,0:T(8,128)(2,1)} custom-call(bf16[4,1,192,384]{3,2,1,0:T(8,128)(2,1)S(1)} %bitcast.278, bf16[4,1,192,384]{3,2,1,0:T(8,128)(2,1)S(1)} %bitcast.277, bf16[4,4,192,384]{3,2,1,0:T(8,128)(2,1)} %bitcast.287, bf16[4,1,192,384]{3,2,1,0:T(8,128)(2,1)S(1)} %bitcast.274, bf16[4,1,192,384]{3,2,1,0:T(8,128)(2,1)S(1)} %bitcast.276, ...), custom_call_target="tpu_custom_call" | custom-call | tf_op jit(solution)/shard_map/dense_grads/pallas_call | solution.py:211
  580.7 3.5 convert_element_type.123
  584.4 1.8 slice.128
  586.4 2.6 copy.59
  589.2 1.4 slice_bitcast_fusion.4
  590.6 2.6 copy.55
  593.2 4.2 stack_reshape.6
  597.4 4.1 copy.56
  601.5 4.3 stack_reshape.7
  605.8 2.2 pad_maximum_fusion
  608.1 4.5 copy.58
  612.6 1.8 slice_bitcast_fusion.2
  614.4 1.7 copy.60
  618.6 0.9 convert_bitcast_fusion
  619.5 2.9 convert_element_type.126
  622.4 2.8 convert_element_type.129
  (195 shorter events, 15.3 us)
Async XLA Ops:
  7.2 105.6 %copy-start = (bf16[768,8]{0,1:T(8,128)(2,1)S(1)}, bf16[768,8]{0,1:T(8,128)(2,1)}, u32[]{:S(2)}) copy-start(bf16[768,8]{0,1:T(8,128)(2,1)} %param.22) | copy-start | bytes 36868
  8.2 4.0 copy-start.43
  16.0 1.2 copy-start.67
  16.0 1.2 copy-start.68
  17.0 1.4 copy-start.7
  17.0 51.0 %copy-start.10 = (bf16[768,768]{1,0:T(8,128)(2,1)}, bf16[768,768]{1,0:T(8,128)(2,1)S(1)}, u32[]{:S(2)}) copy-start(bf16[768,768]{1,0:T(8,128)(2,1)S(1)} %get-tuple-element.126.w_out_ref) | copy-start | bytes 3538948
  17.1 27.4 %copy-start.8 = (f32[384,768]{1,0:T(8,128)}, f32[384,768]{1,0:T(8,128)S(1)}, u32[]{:S(2)}) copy-start(f32[384,768]{1,0:T(8,128)S(1)} %bitcast_convert_fusion.2.x_ref) | copy-start | bytes 3538948
  17.2 43.1 %copy-start.51 = (f32[768]{0:T(1024)}, f32[768]{0:T(1024)S(1)}, u32[]{:S(2)}) copy-start(f32[768]{0:T(1024)S(1)} %get-tuple-element.148) | copy-start | bytes 9220
  17.2 43.1 %copy-start.65 = (f32[768]{0:T(1024)}, f32[768]{0:T(1024)S(1)}, u32[]{:S(2)}) copy-start(f32[768]{0:T(1024)S(1)} %get-tuple-element.115) | copy-start | bytes 9220
  17.2 85.9 %copy-start.47 = (f32[768]{0:T(1024)}, f32[768]{0:T(1024)S(1)}, u32[]{:S(2)}) copy-start(f32[768]{0:T(1024)S(1)} %get-tuple-element.149) | copy-start | bytes 9220
  17.2 27.3 %copy-start.31 = (f32[1,768]{1,0:T(1,128)}, f32[1,768]{1,0:T(1,128)S(1)}, u32[]{:S(2)}) copy-start(f32[1,768]{1,0:T(1,128)S(1)} %get-tuple-element.146.gain_ref) | copy-start | bytes 9220
  46.9 13.4 %copy-start.1 = (f32[384,768]{1,0:T(8,128)}, f32[384,768]{1,0:T(8,128)S(1)}, u32[]{:S(2)}) copy-start(f32[384,768]{1,0:T(8,128)S(1)} %get-tuple-element.42) | copy-start | bytes 3538948
  47.0 13.2 %copy-start.55 = (f32[384]{0:T(512)}, f32[384]{0:T(512)S(1)}, u32[]{:S(2)}) copy-start(f32[384]{0:T(512)S(1)} %broadcast_multiply_fusion.5) | copy-start | bytes 4612
  47.3 13.0 %copy-start.63 = (f32[384]{0:T(512)}, f32[384]{0:T(512)S(1)}, u32[]{:S(2)}) copy-start(f32[384]{0:T(512)S(1)} %add_rsqrt_fusion.1) | copy-start | bytes 4612
  60.3 7.8 %copy-start.35 = (f32[384,3072]{1,0:T(8,128)}, f32[384,3072]{1,0:T(8,128)S(1)}, u32[]{:S(2)}) copy-start(f32[384,3072]{1,0:T(8,128)S(1)} %get-tuple-element.142) | copy-start | bytes 14155780
  60.3 7.8 %copy-start.38 = (f32[384,3072]{1,0:T(8,128)}, f32[384,3072]{1,0:T(8,128)S(1)}, u32[]{:S(2)}) copy-start(f32[384,3072]{1,0:T(8,128)S(1)} %get-tuple-element.141) | copy-start | bytes 14155780
  68.1 33.7 %copy-start.69 = (s32[1,384,1]{1,2,0:T(1,128)S(1)}, s32[1,384,1]{1,2,0:T(1,128)}, u32[]{:S(2)}) copy-start(s32[1,384,1]{1,2,0:T(1,128)} %param.15) | copy-start | bytes 4612
  101.3 14.0 %copy-start.3 = (f32[384,768]{1,0:T(8,128)}, f32[384,768]{1,0:T(8,128)S(1)}, u32[]{:S(2)}) copy-start(f32[384,768]{1,0:T(8,128)S(1)} %get-tuple-element.43) | copy-start | bytes 3538948
  101.3 12.3 %copy-start.41 = (bf16[1,384,768]{2,1,0:T(8,128)(2,1)S(1)}, bf16[1,384,768]{2,1,0:T(8,128)(2,1)}, u32[]{:S(2)}) copy-start(bf16[1,384,768]{2,1,0:T(8,128)(2,1)} %param.25) | copy-start | bytes 1769476
  101.5 13.9 %copy-start.49 = (f32[384]{0:T(512)}, f32[384]{0:T(512)S(1)}, u32[]{:S(2)}) copy-start(f32[384]{0:T(512)S(1)} %broadcast_multiply_fusion.4) | copy-start | bytes 4612
  101.8 15.6 %copy-start.53 = (f32[384]{0:T(512)}, f32[384]{0:T(512)S(1)}, u32[]{:S(2)}) copy-start(f32[384]{0:T(512)S(1)} %add_rsqrt_fusion) | copy-start | bytes 4612
  103.1 14.3 %copy-start.57 = (s32[384]{0:T(512)}, s32[384]{0:T(512)S(1)}, u32[]{:S(2)}) copy-start(s32[384]{0:T(512)S(1)} %add_select_fusion) | copy-start | bytes 4612
  103.3 29.3 %copy-start.36 = (bf16[384,768]{1,0:T(8,128)(2,1)}, bf16[384,768]{1,0:T(8,128)(2,1)S(1)}, u32[]{:S(2)}) copy-start(bf16[384,768]{1,0:T(8,128)(2,1)S(1)} %add_convert_fusion.2) | copy-start | bytes 1769476
  106.9 25.7 %all-to-all-start = ((bf16[8,60,768]{2,1,0:T(8,128)(2,1)}), bf16[8,60,768]{2,1,0:T(8,128)(2,1)}, u32[]{:S(2)}, u32[]{:S(2)}) async-start(bf16[8,60,768]{2,1,0:T(8,128)(2,1)} %reshape.224), calls=%async_computation | async-start | bytes 1572864 | tf_op jit(solution)/shard_map/all_to_all | solution.py:729
  113.7 30.9 %copy-start.59 = (f32[384]{0:T(512)}, f32[384]{0:T(512)S(1)}, u32[]{:S(2)}) copy-start(f32[384]{0:T(512)S(1)} %add_divide_fusion) | copy-start | bytes 4612
  132.6 23.9 %all-to-all-start.2 = ((bf16[8,60,768]{2,1,0:T(8,128)(2,1)}), bf16[8,60,768]{2,1,0:T(8,128)(2,1)S(1)}, u32[]{:S(2)}, u32[]{:S(2)}) async-start(bf16[8,60,768]{2,1,0:T(8,128)(2,1)} %reshape.229), calls=%async_computation.2 | async-start | bytes 1572864 | tf_op jit(solution)/shard_map/all_to_all | solution.py:782
  136.2 483.3 %reduce-scatter.3.cloned.1.call-start = ((), (), s32[]{:S(2)}) async-start(), calls=%async_computation.6 | async-start | bytes 5898240 | tf_op jit(solution)/shard_map/reduce_scatter | solution.py:930
  156.5 18.4 %copy-start.44 = (bf16[8,60,768]{2,1,0:T(8,128)(2,1)}, bf16[8,60,768]{2,1,0:T(8,128)(2,1)S(1)}, u32[]{:S(2)}) copy-start(bf16[8,60,768]{2,1,0:T(8,128)(2,1)S(1)} %all-to-all-done.2) | copy-start | bytes 2211844
  174.9 1.7 copy-start.70
  182.2 10.5 %copy-start.45 = (bf16[8,60,768]{2,1,0:T(8,128)(2,1)S(1)}, bf16[8,60,768]{2,1,0:T(8,128)(2,1)}, u32[]{:S(2)}) copy-start(bf16[8,60,768]{2,1,0:T(8,128)(2,1)} %copy-done.44) | copy-start | bytes 2211844
  189.0 42.7 %all-to-all-start.3 = ((bf16[8,60,768]{2,1,0:T(8,128)(2,1)}), bf16[8,60,768]{2,1,0:T(8,128)(2,1)S(1)}, u32[]{:S(2)}, u32[]{:S(2)}) async-start(bf16[8,60,768]{2,1,0:T(8,128)(2,1)} %fusion.58), calls=%async_computation.3 | async-start | bytes 1572864 | tf_op jit(solution)/shard_map/all_to_all | solution.py:803
  192.6 429.8 %reduce-scatter.5.cloned.1.call-start = ((), (), s32[]{:S(2)}) async-start(), calls=%async_computation.7 | async-start | bytes 5898240 | tf_op jit(solution)/shard_map/reduce_scatter | solution.py:933
  231.8 68.5 %all-to-all-start.1 = ((bf16[8,60,768]{2,1,0:T(8,128)(2,1)}), bf16[8,60,768]{2,1,0:T(8,128)(2,1)}, u32[]{:S(2)}, u32[]{:S(2)}) async-start(bf16[8,60,768]{2,1,0:T(8,128)(2,1)} %fusion.63), calls=%async_computation.1 | async-start | bytes 1572864 | tf_op jit(solution)/shard_map/all_to_all | solution.py:737
  237.7 61.4 %copy-start.60 = (f32[384]{0:T(512)S(1)}, f32[384]{0:T(512)}, u32[]{:S(2)}) copy-start(f32[384]{0:T(512)} %copy-done.59) | copy-start | bytes 4612
  249.7 52.7 %copy-start.58 = (s32[384]{0:T(512)S(1)}, s32[384]{0:T(512)}, u32[]{:S(2)}) copy-start(s32[384]{0:T(512)} %copy-done.57) | copy-start | bytes 4612
  294.7 9.7 %copy-start.62 = (f32[384]{0:T(512)S(1)}, f32[384]{0:T(512)}, u32[]{:S(2)}) copy-start(f32[384]{0:T(512)} %copy-done.61) | copy-start | bytes 4612
  294.7 10.4 %copy-start.4 = (f32[384,768]{1,0:T(8,128)S(1)}, f32[384,768]{1,0:T(8,128)}, u32[]{:S(2)}) copy-start(f32[384,768]{1,0:T(8,128)} %copy-done.3) | copy-start | bytes 3538948
  294.7 10.4 %copy-start.48 = (f32[768]{0:T(1024)S(1)}, f32[768]{0:T(1024)}, u32[]{:S(2)}) copy-start(f32[768]{0:T(1024)} %copy-done.47) | copy-start | bytes 9220
  294.7 10.4 %copy-start.50 = (f32[384]{0:T(512)S(1)}, f32[384]{0:T(512)}, u32[]{:S(2)}) copy-start(f32[384]{0:T(512)} %copy-done.49) | copy-start | bytes 4612
  294.7 10.4 %copy-start.54 = (f32[384]{0:T(512)S(1)}, f32[384]{0:T(512)}, u32[]{:S(2)}) copy-start(f32[384]{0:T(512)} %copy-done.53) | copy-start | bytes 4612
  300.3 4.8 copy-start.39
  302.4 3.7 copy-start.42
  305.1 2.4 copy-start.6
  305.1 2.4 copy-start.20
  305.1 2.3 copy-start.26
  305.2 2.3 copy-start.30
  306.1 34.7 %slice-start = ((s8[4718592]{0:T(1024)(128)(4,1)}), s8[4194304]{0:T(1024)(128)(4,1)S(1)}, s32[]{:S(2)}) async-start(s8[4718592]{0:T(1024)(128)(4,1)} %bitcast.285), calls=%async_computation.8 | async-start | bytes 8388608
  307.5 33.3 %slice-start.1 = ((s8[4718592]{0:T(1024)(128)(4,1)}), s8[524288]{0:T(1024)(128)(4,1)S(1)}, s32[]{:S(2)}) async-start(s8[4718592]{0:T(1024)(128)(4,1)} %bitcast.285), calls=%async_computation.9 | async-start | bytes 1048576
  340.7 7.1 %copy-start.21 = (bf16[384,768]{1,0:T(8,128)(2,1)}, bf16[384,768]{1,0:T(8,128)(2,1)S(1)}, u32[]{:S(2)}) copy-start(bf16[384,768]{1,0:T(8,128)(2,1)S(1)} %get-tuple-element.64.refs_6_) | copy-start | bytes 1769476
  347.9 5.3 copy-start.40
  347.9 5.3 copy-start.2
  347.9 5.3 copy-start.52
  347.9 5.3 copy-start.56
  347.9 5.3 copy-start.64
  347.9 5.3 copy-start.66
  353.3 1.9 copy-start.9
  353.3 1.9 copy-start.18
  353.3 1.9 copy-start.28
  353.3 1.9 copy-start.32
  355.2 34.1 %copy-start.37 = (bf16[384,768]{1,0:T(8,128)(2,1)S(1)}, bf16[384,768]{1,0:T(8,128)(2,1)}, u32[]{:S(2)}) copy-start(bf16[384,768]{1,0:T(8,128)(2,1)} %copy-done.36) | copy-start | bytes 1769476
  431.7 1.1 copy-start.12
  434.9 1.1 copy-start.22
  580.7 3.8 copy-start.33
  584.4 4.7 copy-start.34
  (15 other events, 12.9 us)
Sparse Core Ops, SparseCore 0:
  182.2 51.1 reduce-scatter.2
  236.0 49.6 reduce-scatter.4

commit v3 on v2

--- a/solution.py
+++ b/solution.py
@@ -50,14 +50,16 @@
 
 def grad_kernel(n_dp, n_ex, rows, kinds, halvings, firsts, chunks, fin_slots, *refs):
     count, groups = len(kinds), len(firsts)
-    x_refs, dy_refs, out_ref = refs[:groups], refs[groups : 2 * groups], refs[2 * groups]
-    it = iter(refs[2 * groups + 1 :])
+    x_refs, dy_refs = refs[:groups], refs[groups : 2 * groups]
+    small_ref, out_ref, small_out_ref = refs[2 * groups : 2 * groups + 3]
+    it = iter(refs[2 * groups + 3 :])
     send_bufs = [next(it) if k[0] != "back" else None for k in kinds]
     recv_bufs = [next(it) if k[0] != "back" else None for k in kinds]
     keep_bufs = [next(it) if k[0] != "back" else None for k in kinds]
     fin = next(it)
     send_sems = [next(it) for _ in kinds]
     recv_sems = [next(it) for _ in kinds]
+    small_send, small_recv, small_send_sem, small_recv_sem = it
     t = pl.program_id(0)
     d, e = lax.axis_index("dp"), lax.axis_index("expert")
     dp_levels, ex_levels = n_dp.bit_length() - 1, n_ex.bit_length() - 1
@@ -139,6 +141,33 @@
         elif kind == "both":
             keep_bufs[s][slot] = value.astype(jnp.bfloat16).astype(jnp.float32)
 
+    levels = [("dp", b) for b in range(dp_levels)] + [("ex", b) for b in range(ex_levels)]
+
+    def small_copy(i):
+        return pltpu.make_async_remote_copy(
+            src_ref=small_send.at[i],
+            dst_ref=small_recv.at[i],
+            send_sem=small_send_sem.at[i],
+            recv_sem=small_recv_sem.at[i],
+            device_id=peer(*levels[i]),
+            device_id_type=MESH,
+        )
+
+    for i in range(len(levels) + 1):
+
+        @pl.when(t == i)
+        def _(i=i):
+            if i == 0:
+                value = small_ref[...]
+            else:
+                small_copy(i - 1).wait()
+                value = small_send[i - 1] + small_recv[i - 1]
+            if i < len(levels):
+                small_send[i] = value
+                small_copy(i).start()
+            else:
+                small_out_ref[...] = value
+
     ends = list(firsts[1:]) + [chunks]
     for s in reversed(range(count + 1)):
         c = t - s
@@ -173,7 +202,7 @@
                     out_ref[...] = values[0].astype(jnp.bfloat16)
 
 
-def reduce_grads(n_dp, n_ex, pairs, width):
+def reduce_grads(n_dp, n_ex, pairs, small, width):
     _, _, rows, tokens = pairs[0][0].shape
     sizes = [x.shape[1] * (dy.shape[1] // width) for x, dy in pairs]
     firsts = [sum(sizes[:i]) for i in range(len(sizes))]
@@ -193,6 +222,9 @@
     scratch += [pltpu.VMEM((2,) + s, jnp.float32) for s in shapes]
     scratch += [pltpu.VMEM((fin_slots, rows, width), jnp.bfloat16)]
     scratch += [pltpu.SemaphoreType.DMA((2,)) for _ in kinds] * 2
+    hops = (n_dp * n_ex).bit_length() - 1
+    scratch += [pltpu.VMEM((hops,) + small.shape, jnp.float32)] * 2
+    scratch += [pltpu.SemaphoreType.DMA((hops,))] * 2
     in_specs = []
     for (x, dy), first, size in zip(pairs, firsts, sizes):
         many = x.shape[1] > 1
@@ -211,41 +243,61 @@
     return pl.pallas_call(
         functools.partial(grad_kernel, n_dp, n_ex, rows, kinds, halvings, firsts, chunks, fin_slots),
         grid=(chunks + count,),
-        out_shape=jax.ShapeDtypeStruct((chunks, rows, width), jnp.bfloat16),
-        in_specs=in_specs,
-        out_specs=pl.BlockSpec((None, rows, width), lambda t: (jnp.maximum(t - count, 0), 0, 0)),
+        out_shape=[
+            jax.ShapeDtypeStruct((chunks, rows, width), jnp.bfloat16),
+            jax.ShapeDtypeStruct(small.shape, jnp.float32),
+        ],
+        in_specs=in_specs + [pl.BlockSpec(small.shape, lambda t: (0, 0))],
+        out_specs=[
+            pl.BlockSpec((None, rows, width), lambda t: (jnp.maximum(t - count, 0), 0, 0)),
+            pl.BlockSpec(small.shape, lambda t: (0, 0)),
+        ],
         scratch_shapes=scratch,
         compiler_params=pltpu.CompilerParams(
             collective_id=1, has_side_effects=True, vmem_limit_bytes=48 * 1024 * 1024
         ),
         name="dense_grads",
-    )(*[x for x, _ in pairs], *[dy for _, dy in pairs])
-
-
-def exact_gelu(values):
-    return jax.nn.gelu(values, approximate=False)
-
-
-def gelu_backward(hidden, upstream):
-    _, pullback = jax.vjp(exact_gelu, hidden)
-    return pullback(upstream)[0]
-
-
-def norm_forward(stream, norm_gain, norm_shift):
-    center = stream - jnp.mean(stream, axis=-1, keepdims=True)
-    inverse = lax.rsqrt(jnp.mean(center * center, axis=-1, keepdims=True) + epsilon)
-    unit_rows = center * inverse
-    return (unit_rows * norm_gain + norm_shift, unit_rows, inverse)
-
-
-def norm_backward(unit_rows, inverse, norm_gain, upstream):
-    scaled = upstream * norm_gain
-    inner = (
-        scaled
-        - jnp.mean(scaled, axis=-1, keepdims=True)
-        - unit_rows * jnp.mean(scaled * unit_rows, axis=-1, keepdims=True)
-    )
-    return (inverse * inner, jnp.sum(upstream * unit_rows, axis=0), jnp.sum(upstream, axis=0))
+    )(*[x for x, _ in pairs], *[dy for _, dy in pairs], small)
+
+
+def unpack_kernel(per_in, per_ffn, chunk_ref, in_ref, out_ref, ffn_in_ref, ffn_out_ref):
+    width = chunk_ref.shape[2]
+    at = 0
+    for layer in (1, 0):
+        out_ref[:, layer, :] = chunk_ref[at].astype(jnp.float32)
+        for j in range(per_in):
+            in_ref[:, layer, width * j : width * j + width] = chunk_ref[at + 1 + j].astype(jnp.float32)
+        at += 1 + per_in
+        if layer:
+            for j in range(per_ffn):
+                ffn_out_ref[j] = chunk_ref[at + j].astype(jnp.float32)
+                ffn_in_ref[:, width * j : width * j + width] = chunk_ref[at + per_ffn + j].astype(jnp.float32)
+            at += 2 * per_ffn
+
+
+def unpack(chunks, per_in, per_ffn):
+    count, rows, width = chunks.shape
+    step = 48 if rows % 48 == 0 else rows
+    wide = jnp.float32
+    return pl.pallas_call(
+        functools.partial(unpack_kernel, per_in, per_ffn),
+        grid=(rows // step,),
+        out_shape=[
+            jax.ShapeDtypeStruct((rows, 2, per_in * width), wide),
+            jax.ShapeDtypeStruct((rows, 2, width), wide),
+            jax.ShapeDtypeStruct((rows, per_ffn * width), wide),
+            jax.ShapeDtypeStruct((per_ffn, rows, width), wide),
+        ],
+        in_specs=[pl.BlockSpec((count, step, width), lambda i: (0, i, 0))],
+        out_specs=[
+            pl.BlockSpec((step, 2, per_in * width), lambda i: (i, 0, 0)),
+            pl.BlockSpec((step, 2, width), lambda i: (i, 0, 0)),
+            pl.BlockSpec((step, per_ffn * width), lambda i: (i, 0)),
+            pl.BlockSpec((per_ffn, step, width), lambda i: (0, i, 0)),
+        ],
+        compiler_params=pltpu.CompilerParams(vmem_limit_bytes=40 * 1024 * 1024),
+        name="unpack",
+    )(chunks)
 
 
 def dot(a, b):
@@ -258,6 +310,392 @@
 
 def dot_columns(a, b):
     return lax.dot_general(a, b, (((0,), (0,)), ((), ())), preferred_element_type=jnp.float32)
+
+
+def gelu_parts(hidden):
+    lower = 0.5 + 0.5 * lax.erf(hidden * 0.7071067811865476)
+    slope = lower + hidden * jnp.exp(-0.5 * hidden * hidden) * 0.3989422804014327
+    return hidden * lower, slope
+
+
+def norm_parts(x):
+    center = x - jnp.mean(x, axis=-1, keepdims=True)
+    inverse = lax.rsqrt(jnp.mean(center * center, axis=-1, keepdims=True) + epsilon)
+    return center * inverse, inverse
+
+
+def norm_back(unit, inverse, gain, upstream):
+    scaled = upstream * gain
+    return inverse * (
+        scaled - jnp.mean(scaled, axis=-1, keepdims=True) - unit * jnp.mean(scaled * unit, axis=-1, keepdims=True)
+    )
+
+
+def ffn_kernel(x_ref, gain_ref, shift_ref, w_in_ref, w_out_ref, next_ref, normed_t_ref, active_t_ref, slope_ref, normed_ref):
+    @pl.when(pl.program_id(0) == 0)
+    def _():
+        x = x_ref[...]
+        unit, _ = norm_parts(x)
+        normed = (unit * gain_ref[...] + shift_ref[...]).astype(jnp.bfloat16)
+        normed_ref[...] = normed
+        normed_t_ref[...] = normed.T
+        next_ref[...] = x
+
+    active, slope = gelu_parts(dot(normed_ref[...], w_in_ref[...]))
+    active = active.astype(jnp.bfloat16)
+    slope_ref[...] = slope.astype(jnp.bfloat16)
+    active_t_ref[...] = active.T
+    next_ref[...] += dot(active, w_out_ref[...])
+
+
+def ffn_forward(stream, norm_gain, norm_shift, weight_in, weight_out):
+    rows, width = stream.shape
+    hidden = weight_in.shape[1]
+    low = jnp.bfloat16
+    return pl.pallas_call(
+        ffn_kernel,
+        grid=(hidden // width,),
+        out_shape=[
+            jax.ShapeDtypeStruct((rows, width), jnp.float32),
+            jax.ShapeDtypeStruct((width, rows), low),
+            jax.ShapeDtypeStruct((hidden, rows), low),
+            jax.ShapeDtypeStruct((rows, hidden), low),
+        ],
+        in_specs=[
+            pl.BlockSpec((rows, width), lambda i: (0, 0)),
+            pl.BlockSpec((1, width), lambda i: (0, 0)),
+            pl.BlockSpec((1, width), lambda i: (0, 0)),
+            pl.BlockSpec((width, width), lambda i: (0, i)),
+            pl.BlockSpec((width, width), lambda i: (i, 0)),
+        ],
+        out_specs=[
+            pl.BlockSpec((rows, width), lambda i: (0, 0)),
+            pl.BlockSpec((width, rows), lambda i: (0, 0)),
+            pl.BlockSpec((width, rows), lambda i: (i, 0)),
+            pl.BlockSpec((rows, width), lambda i: (0, i)),
+        ],
+        scratch_shapes=[pltpu.VMEM((rows, width), low)],
+        compiler_params=pltpu.CompilerParams(vmem_limit_bytes=48 * 1024 * 1024),
+        name="ffn_forward",
+    )(stream, norm_gain, norm_shift, weight_in, weight_out)
+
+
+def ffn_back_kernel(steps, up_ref, x_ref, gain_ref, w_in_ref, w_out_ref, slope_ref, next_ref, low_ref, hidden_ref, sums_ref, acc_ref):
+    i = pl.program_id(0)
+
+    @pl.when(i == 0)
+    def _():
+        low_ref[...] = up_ref[...].astype(jnp.bfloat16)
+        acc_ref[...] = jnp.zeros_like(acc_ref)
+
+    grad = (dot_rows(low_ref[...], w_out_ref[...]) * slope_ref[...].astype(jnp.float32)).astype(jnp.bfloat16)
+    hidden_ref[...] = grad
+    acc_ref[...] += dot_rows(grad, w_in_ref[...])
+
+    @pl.when(i == steps - 1)
+    def _():
+        unit, inverse = norm_parts(x_ref[...])
+        grad_normed = acc_ref[...]
+        next_ref[...] = up_ref[...] + norm_back(unit, inverse, gain_ref[...], grad_normed)
+        sums_ref[0:1] = jnp.sum(grad_normed * unit, axis=0, keepdims=True)
+        sums_ref[1:2] = jnp.sum(grad_normed, axis=0, keepdims=True)
+
+
+def ffn_backward(upstream, stream, norm_gain, weight_in, weight_out, slope):
+    rows, width = stream.shape
+    hidden = weight_in.shape[1]
+    low = jnp.bfloat16
+    whole = pl.BlockSpec((rows, width), lambda i: (0, 0))
+    return pl.pallas_call(
+        functools.partial(ffn_back_kernel, hidden // width),
+        grid=(hidden // width,),
+        out_shape=[
+            jax.ShapeDtypeStruct((rows, width), jnp.float32),
+            jax.ShapeDtypeStruct((rows, width), low),
+            jax.ShapeDtypeStruct((rows, hidden), low),
+            jax.ShapeDtypeStruct((2, width), jnp.float32),
+        ],
+        in_specs=[
+            whole,
+            whole,
+            pl.BlockSpec((1, width), lambda i: (0, 0)),
+            pl.BlockSpec((width, width), lambda i: (0, i)),
+            pl.BlockSpec((width, width), lambda i: (i, 0)),
+            pl.BlockSpec((rows, width), lambda i: (0, i)),
+        ],
+        out_specs=[
+            whole,
+            whole,
+            pl.BlockSpec((rows, width), lambda i: (0, i)),
+            pl.BlockSpec((2, width), lambda i: (0, 0)),
+        ],
+        scratch_shapes=[pltpu.VMEM((rows, width), jnp.float32)],
+        compiler_params=pltpu.CompilerParams(vmem_limit_bytes=48 * 1024 * 1024),
+        name="ffn_backward",
+    )(upstream, stream, norm_gain, weight_in, weight_out, slope)
+
+
+def capacity_of(rows, experts):
+    capacity = (5 * rows + 4 * experts - 1) // (4 * experts)
+    return capacity, -(-capacity // 16) * 16
+
+
+def chosen_rows(assign, experts):
+    expert = lax.broadcasted_iota(jnp.int32, (experts, assign.shape[1]), 0)
+    return jnp.where(assign == expert, 1.0, 0.0)
+
+
+def dispatch_of(assign, experts):
+    tokens = assign.shape[1]
+    capacity, padded = capacity_of(tokens, experts)
+    hot = chosen_rows(assign, experts)
+    earlier = lax.broadcasted_iota(jnp.int32, (tokens, tokens), 0) < lax.broadcasted_iota(jnp.int32, (tokens, tokens), 1)
+    before = dot(hot.astype(jnp.bfloat16), jnp.where(earlier, 1.0, 0.0).astype(jnp.bfloat16))
+    place = jnp.sum(hot * before, axis=0, keepdims=True)
+    slot = jnp.where(place < capacity, assign.astype(jnp.float32) * padded + place, -1.0)
+    number = lax.broadcasted_iota(jnp.int32, (experts * padded, tokens), 0).astype(jnp.float32)
+    return jnp.where(number == slot, 1.0, 0.0).astype(jnp.bfloat16)
+
+
+class Across:
+    def __init__(self, experts, out, into, send_sems, recv_sems):
+        self.experts, self.out, self.into = experts, out, into
+        self.send_sems, self.recv_sems = send_sems, recv_sems
+        self.dp, self.me = lax.axis_index("dp"), lax.axis_index("expert")
+
+    def copy(self, slab, place, to):
+        return pltpu.make_async_remote_copy(
+            src_ref=self.out.at[slab],
+            dst_ref=self.into.at[place],
+            send_sem=self.send_sems.at[slab],
+            recv_sem=self.recv_sems.at[place],
+            device_id=(self.dp, to),
+            device_id_type=MESH,
+        )
+
+    def start(self, j):
+        self.copy(j, self.me, j).start()
+
+    def wait_from(self, j):
+        self.copy(j, j, j).wait_recv()
+
+    def wait_to(self, j):
+        self.copy(j, self.me, j).wait_send()
+
+    def others(self, use):
+        def body(k, _):
+            use(lax.rem(self.me + k, self.experts))
+            return 0
+
+        lax.fori_loop(1, self.experts, body, 0)
+
+    def start_all(self):
+        self.others(self.start)
+
+    def wait_all(self):
+        def both(j):
+            self.wait_from(j)
+            self.wait_to(j)
+
+        self.others(both)
+
+
+def greet(targets):
+    barrier = pltpu.get_barrier_semaphore()
+    for device in targets:
+        pl.semaphore_signal(barrier, inc=1, device_id=device, device_id_type=MESH)
+    pl.semaphore_wait(barrier, len(targets))
+
+
+def across_peers(experts):
+    d, e = lax.axis_index("dp"), lax.axis_index("expert")
+    return [(d, lax.rem(e + k, experts)) for k in range(1, experts)]
+
+
+def mixture_kernel(
+    n_dp, n_ex,
+    x_ref, gain_ref, shift_ref, router_ref, assign_ref, cot_ref, far_cot_ref, w_in_ref, w_out_ref,
+    up_ref, sums_ref, router_grad_ref, rows_ref, back_ref, active_ref, hidden_ref, result_ref, gate_ref, stats_ref,
+    send_ref, grad_ref, home_ref, dgate_ref, home_dgate_ref, stat_send, stat_recv, dispatch_ref, result_acc, grad_acc,
+    x_send_sem, x_recv_sem, grad_send_sem, grad_recv_sem, dgate_send_sem, dgate_recv_sem, stat_send_sem, stat_recv_sem,
+):
+    d, e = lax.axis_index("dp"), lax.axis_index("expert")
+    dp_levels, ex_levels = n_dp.bit_length() - 1, n_ex.bit_length() - 1
+    tokens, width = x_ref.shape
+    padded = send_ref.shape[1]
+    group = min(4, n_ex)
+    groups = n_ex // group
+    exact = dict(precision=lax.Precision.HIGHEST, preferred_element_type=jnp.float32)
+    hops = [(flip(d, b), e) for b in range(dp_levels)] + [(d, flip(e, b)) for b in range(ex_levels)]
+    greet([(flip(d, b), e) for b in range(dp_levels)] + across_peers(n_ex))
+
+    unit, inverse = norm_parts(x_ref[...])
+    routed = (unit * gain_ref[...] + shift_ref[...]).astype(jnp.bfloat16)
+    assign = assign_ref[...]
+    dispatch = dispatch_of(assign, n_ex)
+    dispatch_ref[...] = dispatch
+    send_ref[...] = dot(dispatch, routed).astype(jnp.bfloat16).reshape(send_ref.shape)
+    x_across = Across(n_ex, send_ref, rows_ref, x_send_sem, x_recv_sem)
+    x_across.start_all()
+    rows_ref[e] = send_ref[e]
+    hot = chosen_rows(assign, n_ex)
+    gate = jax.nn.sigmoid(jnp.sum(hot * dot_rows(router_ref[...], routed), axis=0, keepdims=True))
+    gate_ref[...] = gate
+
+    def stat_copy(i):
+        return pltpu.make_async_remote_copy(
+            src_ref=stat_send.at[i],
+            dst_ref=stat_recv.at[i],
+            send_sem=stat_send_sem.at[i],
+            recv_sem=stat_recv_sem.at[i],
+            device_id=hops[i],
+            device_id_type=MESH,
+        )
+
+    lane = lax.broadcasted_iota(jnp.int32, stats_ref.shape, 1)
+    stat_send[0] = jnp.where(
+        lane == 0, jnp.sum(hot, axis=1, keepdims=True), jnp.sum(hot * gate, axis=1, keepdims=True)
+    )
+    stat_copy(0).start()
+
+    def stat_step(i):
+        stat_copy(i).wait()
+        value = stat_send[i] + stat_recv[i]
+        if i + 1 < len(hops):
+            stat_send[i + 1] = value
+            stat_copy(i + 1).start()
+        else:
+            stats_ref[...] = value
+
+    grad_across = Across(n_ex, grad_ref, home_ref, grad_send_sem, grad_recv_sem)
+    dgate_across = Across(n_ex, dgate_ref, home_dgate_ref, dgate_send_sem, dgate_recv_sem)
+    step = 768 if w_in_ref.shape[1] % 768 == 0 else w_in_ref.shape[1]
+    done = 0
+    for k in range(groups):
+        first = lax.rem(e // group + k, groups) * group
+        for m in range(group):
+
+            @pl.when(first + m != e)
+            def _(m=m):
+                x_across.wait_from(first + m)
+
+        at = pl.ds(first, group)
+        rows = rows_ref[at].reshape(group * padded, width)
+        cot = far_cot_ref[at].reshape(group * padded, width).astype(jnp.float32)
+        logits = dot_rows(rows, router_ref[...])
+        own = lax.broadcasted_iota(jnp.int32, logits.shape, 1) == e
+        slot_gate = jax.nn.sigmoid(jnp.sum(jnp.where(own, logits, 0.0), axis=1, keepdims=True))
+        back = (slot_gate * cot).astype(jnp.bfloat16)
+        back_ref[at] = back.reshape(group, padded, width)
+        result_acc[...] = jnp.zeros_like(result_acc)
+        grad_acc[...] = jnp.zeros_like(grad_acc)
+        span = pl.ds(pl.multiple_of(first * padded, group * padded), group * padded)
+
+        def block(i, _):
+            cols = pl.ds(pl.multiple_of(i * step, step), step)
+            active, slope = gelu_parts(dot(rows, w_in_ref[:, cols]))
+            active = active.astype(jnp.bfloat16)
+            hidden = (slope * dot_rows(back, w_out_ref[cols, :])).astype(jnp.bfloat16)
+            active_ref[span, cols] = active
+            hidden_ref[span, cols] = hidden
+            result_acc[...] += dot(active, w_out_ref[cols, :])
+            grad_acc[...] += dot_rows(hidden, w_in_ref[:, cols])
+            return 0
+
+        lax.fori_loop(0, w_in_ref.shape[1] // step, block, 0)
+        grad_ref[at] = grad_acc[...].astype(jnp.bfloat16).reshape(group, padded, width)
+        result = result_acc[...].astype(jnp.bfloat16)
+        result_ref[at] = result.reshape(group, padded, width)
+        dgate = lax.dot_general(
+            jnp.ones((8, width), jnp.float32), cot * result.astype(jnp.float32), (((1,), (1,)), ((), ())), **exact
+        )
+        for m in range(group):
+            dgate_ref[first + m, :, :padded] = dgate[:, m * padded : (m + 1) * padded]
+
+            @pl.when(first + m != e)
+            def _(m=m):
+                grad_across.start(first + m)
+                dgate_across.start(first + m)
+
+            @pl.when(first + m == e)
+            def _():
+                home_ref[e] = grad_ref[e]
+                home_dgate_ref[e] = dgate_ref[e]
+
+        if done < len(hops):
+            stat_step(done)
+            done += 1
+
+    for i in range(done, len(hops)):
+        stat_step(i)
+    x_across.others(x_across.wait_to)
+    dgate_across.wait_all()
+    dgate = jnp.zeros((8, tokens), jnp.float32)
+    for j in range(n_ex):
+        part = dispatch_ref[j * padded : (j + 1) * padded].astype(jnp.float32)
+        dgate = dgate + jnp.dot(home_dgate_ref[j, :, :padded], part, **exact)
+    everyone = tokens * n_dp * n_ex
+    share = jnp.sum(jnp.where(lane == 0, stats_ref[...], 0.0), axis=1, keepdims=True) / everyone
+    weight = balance_weight * n_ex * (share - 1.0 / n_ex) / everyone
+    grad_gate = dgate[0:1] + jnp.sum(hot * weight, axis=0, keepdims=True)
+    grad_logits = hot * (grad_gate * gate * (1.0 - gate))
+    router_grad_ref[...] = jnp.dot(grad_logits, routed.astype(jnp.float32), **exact)
+    grad_normed = lax.dot_general(
+        grad_logits, router_ref[...].astype(jnp.float32), (((0,), (0,)), ((), ())), **exact
+    )
+    grad_across.wait_all()
+    grad_normed = grad_normed + dot_columns(dispatch_ref[...], home_ref[...].reshape(n_ex * padded, width))
+    up_ref[...] = cot_ref[...].astype(jnp.float32) + norm_back(unit, inverse, gain_ref[...], grad_normed)
+    sums_ref[0:1] = jnp.sum(grad_normed * unit, axis=0, keepdims=True)
+    sums_ref[1:2] = jnp.sum(grad_normed, axis=0, keepdims=True)
+
+
+def mixture(n_dp, n_ex, collective_id, stream, norm_gain, norm_shift, router_t, assign, cot, far_cot, weight_in, weight_out):
+    tokens, width = stream.shape
+    hidden = weight_in.shape[1]
+    _, padded = capacity_of(tokens, n_ex)
+    slots = n_ex * padded
+    group = min(4, n_ex) * padded
+    low, wide = jnp.bfloat16, jnp.float32
+    slab = (n_ex, padded, width)
+    hops = (n_dp * n_ex).bit_length() - 1
+    outs = [
+        jax.ShapeDtypeStruct((tokens, width), wide),
+        jax.ShapeDtypeStruct((2, width), wide),
+        jax.ShapeDtypeStruct((n_ex, width), wide),
+        jax.ShapeDtypeStruct(slab, low),
+        jax.ShapeDtypeStruct(slab, low),
+        jax.ShapeDtypeStruct((slots, hidden), low),
+        jax.ShapeDtypeStruct((slots, hidden), low),
+        jax.ShapeDtypeStruct(slab, low),
+        jax.ShapeDtypeStruct((1, tokens), wide),
+        jax.ShapeDtypeStruct((n_ex, 128), wide),
+    ]
+    vmem = pl.BlockSpec(memory_space=pltpu.VMEM)
+    return pl.pallas_call(
+        functools.partial(mixture_kernel, n_dp, n_ex),
+        out_shape=outs,
+        in_specs=[vmem] * 9,
+        out_specs=[vmem] * len(outs),
+        scratch_shapes=[
+            pltpu.VMEM(slab, low),
+            pltpu.VMEM(slab, low),
+            pltpu.VMEM(slab, low),
+            pltpu.VMEM((n_ex, 8, 128), wide),
+            pltpu.VMEM((n_ex, 8, 128), wide),
+            pltpu.VMEM((hops, n_ex, 128), wide),
+            pltpu.VMEM((hops, n_ex, 128), wide),
+            pltpu.VMEM((slots, tokens), low),
+            pltpu.VMEM((group, width), wide),
+            pltpu.VMEM((group, width), wide),
+        ]
+        + [pltpu.SemaphoreType.DMA((n_ex,)) for _ in range(6)]
+        + [pltpu.SemaphoreType.DMA((hops,)) for _ in range(2)],
+        compiler_params=pltpu.CompilerParams(
+            collective_id=collective_id, has_side_effects=True, vmem_limit_bytes=56 * 1024 * 1024
+        ),
+        name="mixture",
+    )(stream, norm_gain, norm_shift, router_t, assign, cot, far_cot, weight_in, weight_out)
 
 
 def head_pair(rows):
@@ -290,17 +728,9 @@
         self.chip, self.core = self.me // 2, self.me % 2
         self.twin = self.me + 1 - 2 * self.core
 
-    def greet(self):
-        barrier = pltpu.get_barrier_semaphore()
-        pl.semaphore_signal(barrier, inc=1, device_id=(self.twin, self.expert), device_id_type=MESH)
-        for other in range(self.chips):
-
-            @pl.when(other != self.chip)
-            def _():
-                there = (2 * other + self.core, self.expert)
-                pl.semaphore_signal(barrier, inc=1, device_id=there, device_id_type=MESH)
-
-        pl.semaphore_wait(barrier, self.chips)
+    def peers(self):
+        ring = [lax.rem(self.chip + k, self.chips) for k in range(1, self.chips)]
+        return [(self.twin, self.expert)] + [(2 * other + self.core, self.expert) for other in ring]
 
     def copy(self, ref, send_sem, recv_sem, index):
         return pltpu.make_async_remote_copy(
@@ -390,12 +820,17 @@
 
 
 def attend_kernel(
-    n_dp,
-    x_ref, gain_ref, shift_ref, w_in_ref, w_out_ref, doc_row_ref, doc_col_ref,
-    next_ref, normed_t_ref, context_ref, context_t_ref, kv_ref, q_ref, short_kv_ref, short_q_ref, lse_ref,
-    acc_ref, top_ref, total_ref,
-    kv_far, kv_near, kv_recv, q_far, q_near, q_recv,
+    n_dp, n_ex, inputs, *refs
 ):
+    (x_ref, gain_ref, shift_ref, w_in_ref, w_out_ref, doc_row_ref, doc_col_ref), rest = refs[:7], refs[7:]
+    if inputs > 7:
+        (assign_ref, cot_ref), rest = rest[:2], rest[2:]
+    (
+        next_ref, normed_t_ref, context_ref, context_t_ref, kv_ref, q_ref, short_kv_ref, short_q_ref, lse_ref,
+    ), rest = rest[:9], rest[9:]
+    if inputs > 7:
+        (far_cot_ref,), rest = rest[:1], rest[1:]
+    (acc_ref, top_ref, total_ref, kv_far, kv_near, kv_recv, q_far, q_near, q_recv), rest = rest[:9], rest[9:]
     links = Links(n_dp)
     me = links.me
     pairs, long = kv_ref.shape[1], kv_ref.shape[3]
@@ -411,7 +846,7 @@
             piece = kv[:, part * width + 128 * h : part * width + 128 * h + 128]
             kv_ref[me, h, part] = piece[:long]
             short_kv_ref[h, part] = piece[long:]
-    links.greet()
+    greet(links.peers() + (across_peers(n_ex) if inputs > 7 else []))
     kv_spread = Spread(links, lambda b, p: kv_ref.at[b, p], pairs, True, kv_far, kv_near, kv_recv)
     q_spread = Spread(links, lambda b, p: q_ref.at[b], 1, False, q_far, q_near, q_recv)
     for h in range(pairs):
@@ -422,6 +857,14 @@
         q_ref[me, h] = piece[:long]
         short_q_ref[h] = piece[long:]
     q_spread.send(0)
+    if inputs > 7:
+        cot_send_ref, cot_send_sem, cot_recv_sem = rest
+        cot_send_ref[...] = dot(dispatch_of(assign_ref[...], n_ex), cot_ref[...]).astype(jnp.bfloat16).reshape(
+            cot_send_ref.shape
+        )
+        cot_across = Across(n_ex, cot_send_ref, far_cot_ref, cot_send_sem, cot_recv_sem)
+        cot_across.start_all()
+        far_cot_ref[links.expert] = cot_send_ref[links.expert]
     normed_t_ref[...] = normed.T
 
     def put_context(h, rows_t, first, count):
@@ -480,6 +923,8 @@
     q_spread.sent(0)
     for h in range(pairs):
         kv_spread.sent(h)
+    if inputs > 7:
+        cot_across.wait_all()
 
 
 def spread_sems(n_dp, parts):
@@ -490,7 +935,9 @@
     ]
 
 
-def attention_forward(n_dp, collective_id, stream, norm_gain, norm_shift, weight_in, weight_out, doc_row, doc_col):
+def attention_forward(
+    n_dp, n_ex, collective_id, stream, norm_gain, norm_shift, weight_in, weight_out, doc_row, doc_col, routing=()
+):
     rows, width = stream.shape
     long, short, pairs = LONG_DEV, rows - LONG_DEV, width // 128
     low = jnp.bfloat16
@@ -505,34 +952,41 @@
         jax.ShapeDtypeStruct((pairs, short, 128), low),
         jax.ShapeDtypeStruct((pairs, 2, rows), jnp.float32),
     ]
+    scratch = [
+        pltpu.VMEM((pairs, 128, 2 * long), jnp.float32),
+        pltpu.VMEM((pairs, 1, 2 * long), jnp.float32),
+        pltpu.VMEM((pairs, 1, 2 * long), jnp.float32),
+    ]
+    scratch += spread_sems(n_dp, pairs) + spread_sems(n_dp, 1)
+    if routing:
+        slab = (n_ex, capacity_of(rows, n_ex)[1], width)
+        outs += [jax.ShapeDtypeStruct(slab, low)]
+        scratch += [pltpu.VMEM(slab, low)] + [pltpu.SemaphoreType.DMA((n_ex,))] * 2
+    inputs = (stream, norm_gain, norm_shift, weight_in, weight_out, doc_row, doc_col) + tuple(routing)
     vmem = pl.BlockSpec(memory_space=pltpu.VMEM)
     return pl.pallas_call(
-        functools.partial(attend_kernel, n_dp),
+        functools.partial(attend_kernel, n_dp, n_ex, len(inputs)),
         out_shape=outs,
-        in_specs=[vmem] * 7,
+        in_specs=[vmem] * len(inputs),
         out_specs=[vmem] * len(outs),
-        scratch_shapes=[
-            pltpu.VMEM((pairs, 128, 2 * long), jnp.float32),
-            pltpu.VMEM((pairs, 1, 2 * long), jnp.float32),
-            pltpu.VMEM((pairs, 1, 2 * long), jnp.float32),
-        ]
-        + spread_sems(n_dp, pairs)
-        + spread_sems(n_dp, 1),
+        scratch_shapes=scratch,
         compiler_params=pltpu.CompilerParams(
             collective_id=collective_id, has_side_effects=True, vmem_limit_bytes=48 * 1024 * 1024
         ),
         name="attention_forward",
-    )(stream, norm_gain, norm_shift, weight_in, weight_out, doc_row, doc_col)
-
-
-def attend_back_kernel(
-    n_dp,
-    up_ref, x_ref, gain_ref, w_in_ref, w_out_ref, doc_row_ref, doc_col_ref,
-    context_ref, kv_ref, q_ref, short_kv_ref, short_q_ref, lse_ref,
-    up_next_ref, up_low_ref, mixed_ref, sums_ref,
-    do_ref, aux_ref, short_do_ref, short_aux_ref, dq_ref, dk_ref, dv_ref,
-    do_far, do_near, do_recv, aux_far, aux_near, aux_recv,
-):
+    )(*inputs)
+
+
+def attend_back_kernel(n_dp, n_ex, inputs, *refs):
+    (up_ref, x_ref, gain_ref, w_in_ref, w_out_ref, doc_row_ref, doc_col_ref), rest = refs[:7], refs[7:]
+    (context_ref, kv_ref, q_ref, short_kv_ref, short_q_ref, lse_ref), rest = rest[:6], rest[6:]
+    if inputs > 13:
+        (assign_ref, gate_ref, stream_ref, result_ref), rest = rest[:4], rest[4:]
+    (up_next_ref, up_low_ref, mixed_ref, sums_ref), rest = rest[:4], rest[4:]
+    if inputs > 13:
+        (output_ref,), rest = rest[:1], rest[1:]
+    (do_ref, aux_ref, short_do_ref, short_aux_ref, dq_ref, dk_ref, dv_ref), rest = rest[:7], rest[7:]
+    (do_far, do_near, do_recv, aux_far, aux_near, aux_recv), rest = rest[:6], rest[6:]
     links = Links(n_dp)
     me = links.me
     pairs, long, width = kv_ref.shape[1], kv_ref.shape[3], x_ref.shape[1]
@@ -557,12 +1011,17 @@
         aux_ref[me, h, 2:4] = delta[0:2, :long]
         short_aux_ref[h, 0:2] = lse_ref[h, :, long:]
         short_aux_ref[h, 2:4] = delta[0:2, long:]
-    links.greet()
+    greet(links.peers() + (across_peers(n_ex) if inputs > 13 else []))
     do_spread = Spread(links, lambda b, p: do_ref.at[b, p], pairs, False, do_far, do_near, do_recv)
     aux_spread = Spread(links, lambda b, p: aux_ref.at[b, p], pairs, False, aux_far, aux_near, aux_recv)
     for h in range(pairs):
         do_spread.send(h)
         aux_spread.send(h)
+    if inputs > 13:
+        home_ref, result_send_sem, result_recv_sem = rest
+        result_across = Across(n_ex, result_ref, home_ref, result_send_sem, result_recv_sem)
+        result_across.start_all()
+        home_ref[links.expert] = result_ref[links.expert]
 
     def row_of(aux, first):
         return jnp.concatenate([aux[first : first + 1], aux[first + 1 : first + 2]], axis=1)
@@ -639,9 +1098,17 @@
     for h in range(pairs):
         do_spread.sent(h)
         aux_spread.sent(h)
-
-
-def attention_backward(n_dp, collective_id, upstream, stream, norm_gain, weight_in, weight_out, doc_row, doc_col, kept):
+    if inputs > 13:
+        result_across.wait_all()
+        dispatch = dispatch_of(assign_ref[...], n_ex)
+        result = dot_columns(dispatch, home_ref[...].reshape(dispatch.shape[0], width))
+        gate = jnp.broadcast_to(gate_ref[...], (128, gate_ref.shape[1])).T[:, 0:1]
+        output_ref[...] = (stream_ref[...] + gate * result).astype(jnp.bfloat16)
+
+
+def attention_backward(
+    n_dp, n_ex, collective_id, upstream, stream, norm_gain, weight_in, weight_out, doc_row, doc_col, kept, routing=()
+):
     rows, width = stream.shape
     long, short, pairs = LONG_DEV, rows - LONG_DEV, width // 128
     low = jnp.bfloat16
@@ -651,181 +1118,32 @@
         jax.ShapeDtypeStruct((rows, 3 * width), low),
         jax.ShapeDtypeStruct((2, width), jnp.float32),
     ]
+    scratch = [
+        pltpu.VMEM((n_dp, pairs, long, 128), low),
+        pltpu.VMEM((n_dp, pairs, 8, long), jnp.float32),
+        pltpu.VMEM((pairs, short, 128), low),
+        pltpu.VMEM((pairs, 8, short), jnp.float32),
+        pltpu.VMEM((pairs, 128, 2 * long), jnp.float32),
+        pltpu.VMEM((pairs, long, 128), jnp.float32),
+        pltpu.VMEM((pairs, long, 128), jnp.float32),
+    ]
+    scratch += spread_sems(n_dp, pairs) + spread_sems(n_dp, pairs)
+    if routing:
+        outs += [jax.ShapeDtypeStruct((rows, width), low)]
+        scratch += [pltpu.VMEM(routing[3].shape, low)] + [pltpu.SemaphoreType.DMA((n_ex,))] * 2
+    inputs = (upstream, stream, norm_gain, weight_in, weight_out, doc_row, doc_col) + tuple(kept) + tuple(routing)
     vmem = pl.BlockSpec(memory_space=pltpu.VMEM)
     return pl.pallas_call(
-        functools.partial(attend_back_kernel, n_dp),
+        functools.partial(attend_back_kernel, n_dp, n_ex, len(inputs)),
         out_shape=outs,
-        in_specs=[vmem] * 13,
+        in_specs=[vmem] * len(inputs),
         out_specs=[vmem] * len(outs),
-        scratch_shapes=[
-            pltpu.VMEM((n_dp, pairs, long, 128), low),
-            pltpu.VMEM((n_dp, pairs, 8, long), jnp.float32),
-            pltpu.VMEM((pairs, short, 128), low),
-            pltpu.VMEM((pairs, 8, short), jnp.float32),
-            pltpu.VMEM((pairs, 128, 2 * long), jnp.float32),
-            pltpu.VMEM((pairs, long, 128), jnp.float32),
-            pltpu.VMEM((pairs, long, 128), jnp.float32),
-        ]
-        + spread_sems(n_dp, pairs)
-        + spread_sems(n_dp, pairs),
+        scratch_shapes=scratch,
         compiler_params=pltpu.CompilerParams(
-            collective_id=collective_id, has_side_effects=True, vmem_limit_bytes=48 * 1024 * 1024
+            collective_id=collective_id, has_side_effects=True, vmem_limit_bytes=56 * 1024 * 1024
         ),
         name="attention_backward",
-    )(upstream, stream, norm_gain, weight_in, weight_out, doc_row, doc_col, *kept)
-
-
-def ffn_forward(stream, norm_gain, norm_shift, weight_in, weight_out):
-    normed, unit_rows, inverse = norm_forward(stream, norm_gain, norm_shift)
-    normed_low = normed.astype(jnp.bfloat16)
-    hidden = jnp.dot(normed_low, weight_in, preferred_element_type=jnp.float32)
-    active = exact_gelu(hidden).astype(jnp.bfloat16)
-    stream_next = stream + jnp.dot(active, weight_out, preferred_element_type=jnp.float32)
-    return (stream_next, (unit_rows, inverse, normed_low, hidden, active))
-
-
-def ffn_backward(upstream, kept_state, norm_gain, weight_in, weight_out):
-    unit_rows, inverse, normed_low, hidden, active = kept_state
-    upstream_low = upstream.astype(jnp.bfloat16)
-    grad_active = jnp.einsum(
-        "td,fd->tf", upstream_low, weight_out, preferred_element_type=jnp.float32
-    )
-    grad_hidden = gelu_backward(hidden, grad_active).astype(jnp.bfloat16)
-    grad_normed = jnp.einsum(
-        "tf,df->td", grad_hidden, weight_in, preferred_element_type=jnp.float32
-    )
-    grad_stream, grad_gain, grad_shift = norm_backward(unit_rows, inverse, norm_gain, grad_normed)
-    pairs = ((active, upstream_low), (normed_low, grad_hidden))
-    return (upstream + grad_stream, pairs, grad_gain, grad_shift)
-
-
-def mixture_forward(stream, norm_gain, norm_shift, router, expert_in, expert_out, assign_ids):
-    normed, unit_rows, inverse = norm_forward(stream, norm_gain, norm_shift)
-    normed_low = normed.astype(jnp.bfloat16)
-    model_width = stream.shape[1]
-    row_count = stream.shape[0]
-    experts_all = router.shape[1]
-    capacity = (5 * row_count + 4 * experts_all - 1) // (4 * experts_all)
-    logits = jnp.dot(normed_low, router, preferred_element_type=jnp.float32)
-    expert_numbers = jnp.arange(experts_all, dtype=jnp.int32)
-    chosen_hot = (assign_ids[:, None] == expert_numbers[None, :]).astype(jnp.float32)
-    gate_value = jax.nn.sigmoid(jnp.sum(logits * chosen_hot, axis=-1))
-    counts = lax.psum(jnp.sum(chosen_hot, axis=0), ("dp", "expert"))
-    gate_sums = lax.psum(jnp.sum(gate_value[:, None] * chosen_hot, axis=0), ("dp", "expert"))
-    tokens_all = row_count * lax.axis_size("dp") * lax.axis_size("expert")
-    token_share = counts / tokens_all
-    balance = experts_all * jnp.sum((token_share - 1.0 / experts_all) * (gate_sums / tokens_all))
-    hot_count = (assign_ids[:, None] == expert_numbers[None, :]).astype(jnp.int32)
-    before = jnp.cumsum(hot_count, axis=0) - hot_count
-    slot_place = jnp.sum(before * hot_count, axis=-1)
-    slot_index = jnp.where(slot_place < capacity, assign_ids * capacity + slot_place, -1)
-    dispatch = (
-        slot_index[:, None] == jnp.arange(experts_all * capacity, dtype=jnp.int32)[None, :]
-    ).astype(jnp.bfloat16)
-    outgoing = jnp.einsum(
-        "tc,td->cd", dispatch, normed_low, preferred_element_type=jnp.float32
-    ).astype(jnp.bfloat16)
-    outgoing = outgoing.reshape(experts_all, capacity, model_width)
-    incoming = lax.all_to_all(outgoing, "expert", split_axis=0, concat_axis=0, tiled=True)
-    slot_count = incoming.shape[1]
-    grouped = incoming.reshape(-1, expert_in.shape[0], slot_count, model_width)
-    hidden = jnp.einsum("sjcd,jdf->sjcf", grouped, expert_in, preferred_element_type=jnp.float32)
-    active = exact_gelu(hidden).astype(jnp.bfloat16)
-    result = jnp.einsum(
-        "sjcf,jfd->sjcd", active, expert_out, preferred_element_type=jnp.float32
-    ).astype(jnp.bfloat16)
-    homeward = lax.all_to_all(
-        result.reshape(incoming.shape), "expert", split_axis=0, concat_axis=0, tiled=True
-    )
-    gathered = jnp.dot(
-        dispatch,
-        homeward.reshape(experts_all * capacity, model_width),
-        preferred_element_type=jnp.float32,
-    )
-    stream_next = stream + gate_value[:, None] * gathered
-    kept_state = (
-        unit_rows,
-        inverse,
-        normed_low,
-        gate_value,
-        token_share,
-        tokens_all,
-        chosen_hot,
-        dispatch,
-        gathered,
-        incoming,
-    )
-    return (stream_next, balance, kept_state)
-
-
-def mixture_backward(upstream, kept_state, norm_gain, router, expert_in, expert_out):
-    (
-        unit_rows,
-        inverse,
-        normed_low,
-        gate_value,
-        token_share,
-        tokens_all,
-        chosen_hot,
-        dispatch,
-        gathered,
-        arrived,
-    ) = kept_state
-    model_width = upstream.shape[1]
-    experts_all = router.shape[1]
-    grad_gate = jnp.sum(upstream * gathered, axis=-1)
-    grad_return = (gate_value[:, None] * upstream).astype(jnp.bfloat16)
-    outgoing = jnp.einsum(
-        "tc,td->cd", dispatch, grad_return, preferred_element_type=jnp.float32
-    ).astype(jnp.bfloat16)
-    outgoing = outgoing.reshape(experts_all, -1, model_width)
-    incoming = lax.all_to_all(outgoing, "expert", split_axis=0, concat_axis=0, tiled=True)
-    slot_count = incoming.shape[1]
-    grouped_grad = incoming.reshape(-1, expert_in.shape[0], slot_count, model_width)
-    grouped_rows = arrived.reshape(-1, expert_in.shape[0], slot_count, model_width)
-    hidden = jnp.einsum(
-        "sjcd,jdf->sjcf", grouped_rows, expert_in, preferred_element_type=jnp.float32
-    )
-    active = exact_gelu(hidden).astype(jnp.bfloat16)
-    grad_out_weight = jnp.einsum(
-        "sjcf,sjcd->jfd", active, grouped_grad, preferred_element_type=jnp.float32
-    )
-    grad_active = jnp.einsum(
-        "sjcd,jfd->sjcf", grouped_grad, expert_out, preferred_element_type=jnp.float32
-    )
-    grad_hidden = gelu_backward(hidden, grad_active).astype(jnp.bfloat16)
-    grad_in_weight = jnp.einsum(
-        "sjcd,sjcf->jdf", grouped_rows, grad_hidden, preferred_element_type=jnp.float32
-    )
-    grad_rows = jnp.einsum(
-        "sjcf,jdf->sjcd", grad_hidden, expert_in, preferred_element_type=jnp.float32
-    ).astype(jnp.bfloat16)
-    homeward = lax.all_to_all(
-        grad_rows.reshape(incoming.shape), "expert", split_axis=0, concat_axis=0, tiled=True
-    )
-    grad_normed = jnp.dot(
-        dispatch, homeward.reshape(-1, model_width), preferred_element_type=jnp.float32
-    )
-    share_weight = balance_weight * experts_all * (token_share - 1.0 / experts_all) / tokens_all
-    grad_gate = grad_gate + jnp.sum(chosen_hot * share_weight[None, :], axis=-1)
-    grad_chosen = grad_gate * gate_value * (1.0 - gate_value)
-    grad_logits = grad_chosen[:, None] * chosen_hot
-    router_float = router.astype(jnp.float32)
-    grad_router = jnp.einsum(
-        "td,te->de", normed_low.astype(jnp.float32), grad_logits, precision=lax.Precision.HIGHEST
-    )
-    grad_normed = grad_normed + jnp.einsum(
-        "te,de->td", grad_logits, router_float, precision=lax.Precision.HIGHEST
-    )
-    grad_stream, grad_gain, grad_shift = norm_backward(unit_rows, inverse, norm_gain, grad_normed)
-    return (
-        upstream + grad_stream,
-        grad_in_weight,
-        grad_out_weight,
-        grad_router,
-        grad_gain,
-        grad_shift,
-    )
+    )(*inputs)
 
 
 def shards(
@@ -852,76 +1170,75 @@
     doc_row, doc_col = short_ids[None, :], short_ids[:, None]
     weights_in, weights_out = lax.optimization_barrier((attn_in.transpose(1, 0, 2), attn_out.transpose(1, 0, 2)))
     gains, shifts = ln_gain.T, ln_bias.T
+    assign_row = assign[0].T
     stream_one, *kept_one = attention_forward(
-        n_dp, 2, stream_first, gains[0:1], shifts[0:1], weights_in[0], weights_out[0], doc_row, doc_col
-    )
-    stream_two, kept_two = ffn_forward(stream_one, ln_gain[:, 1], ln_bias[:, 1], ffn_in, ffn_out)
-    stream_three, *kept_three = attention_forward(
-        n_dp, 3, stream_two, gains[2:3], shifts[2:3], weights_in[1], weights_out[1], doc_row, doc_col
-    )
-    stream_four, balance, kept_four = mixture_forward(
-        stream_three, ln_gain[:, 3], ln_bias[:, 3], router, expert_in, expert_out, assign[0, :, 0]
-    )
-    output = stream_four.astype(jnp.bfloat16)[None]
-    upstream = cotangent[0].astype(jnp.float32)
-    upstream, expert_in_grad, expert_out_grad, router_grad, gain_three, shift_three = (
-        mixture_backward(upstream, kept_four, ln_gain[:, 3], router, expert_in, expert_out)
-    )
-    upstream, second_low, second_mixed, second_sums = attention_backward(
-        n_dp, 4, upstream, stream_two, gains[2:3], weights_in[1], weights_out[1], doc_row, doc_col,
-        kept_three[1:2] + kept_three[3:],
-    )
-    upstream, dense_pairs, gain_one, shift_one = ffn_backward(upstream, kept_two, ln_gain[:, 1], ffn_in, ffn_out)
+        n_dp, n_ex, 2, stream_first, gains[0:1], shifts[0:1], weights_in[0], weights_out[0], doc_row, doc_col
+    )
+    stream_two, dense_normed_t, active_t, slope = ffn_forward(stream_one, gains[1:2], shifts[1:2], ffn_in, ffn_out)
+    stream_three, *kept_three, far_cot = attention_forward(
+        n_dp, n_ex, 3, stream_two, gains[2:3], shifts[2:3], weights_in[1], weights_out[1], doc_row, doc_col,
+        (assign_row, cotangent[0]),
+    )
+    (
+        upstream, fourth_sums, router_grad, expert_rows, expert_back, expert_active, expert_hidden, result, gate, stats
+    ) = mixture(
+        n_dp, n_ex, 6, stream_three, gains[3:4], shifts[3:4], router.T, assign_row, cotangent[0], far_cot,
+        expert_in[0], expert_out[0],
+    )
+    everyone = row_count * n_dp * n_ex
+    balance = n_ex * jnp.sum((stats[:, 0] / everyone - 1.0 / n_ex) * (stats[:, 1] / everyone))
+    expert_slots = expert_active.shape[0]
+    expert_in_grad = jnp.einsum(
+        "sd,sf->df", expert_rows.reshape(expert_slots, -1), expert_hidden, preferred_element_type=jnp.float32
+    )[None]
+    expert_out_grad = jnp.einsum(
+        "sf,sd->fd", expert_active, expert_back.reshape(expert_slots, -1), preferred_element_type=jnp.float32
+    )[None]
+    upstream, second_low, second_mixed, second_sums, output = attention_backward(
+        n_dp, n_ex, 4, upstream, stream_two, gains[2:3], weights_in[1], weights_out[1], doc_row, doc_col,
+        kept_three[1:2] + kept_three[3:], (assign_row, gate, stream_three, result),
+    )
+    output = output[None]
+    upstream, dense_low, dense_hidden, dense_sums = ffn_backward(
+        upstream, stream_one, gains[1:2], ffn_in, ffn_out, slope
+    )
     upstream, first_low, first_mixed, first_sums = attention_backward(
-        n_dp, 5, upstream, stream_first, gains[0:1], weights_in[0], weights_out[0], doc_row, doc_col,
+        n_dp, n_ex, 5, upstream, stream_first, gains[0:1], weights_in[0], weights_out[0], doc_row, doc_col,
         kept_one[1:2] + kept_one[3:],
     )
     grad_tokens = upstream.astype(jnp.bfloat16)[None]
     model_width = tokens.shape[2]
     rows = model_width // n_dp
 
-    def blocks_of(acts):
-        return acts.T.reshape(n_dp, -1, rows, row_count).astype(jnp.bfloat16)
-
-    pairs = [(blocks_of(x), dy) for x, dy in dense_pairs]
-    pairs = (
-        [(kept_three[2].reshape(n_dp, 1, rows, row_count), second_low)]
-        + [(kept_three[0].reshape(n_dp, 1, rows, row_count), second_mixed)]
-        + pairs
-        + [(kept_one[2].reshape(n_dp, 1, rows, row_count), first_low)]
-        + [(kept_one[0].reshape(n_dp, 1, rows, row_count), first_mixed)]
-    )
-    chunks = reduce_grads(n_dp, n_ex, pairs, model_width).astype(jnp.float32)
-
-    def wide(first, count):
-        return chunks[first : first + count].transpose(1, 0, 2).reshape(rows, count * model_width)
-
-    per_in = attn_in.shape[2] // model_width
-    per_ffn = ffn_in.shape[1] // model_width
-    at = 0
-    second_out = chunks[0]
-    second_in = wide(1, per_in)
-    at = 1 + per_in
-    ffn_out_sum = chunks[at : at + per_ffn].reshape(per_ffn * rows, model_width)
-    ffn_in_sum = wide(at + per_ffn, per_ffn)
-    at = at + 2 * per_ffn
-    first_out = chunks[at]
-    first_in = wide(at + 1, per_in)
+    def blocks_of(rows_t):
+        return rows_t.reshape(n_dp, -1, rows, row_count)
+
+    pairs = [
+        (blocks_of(kept_three[2]), second_low),
+        (blocks_of(kept_three[0]), second_mixed),
+        (blocks_of(active_t), dense_low),
+        (blocks_of(dense_normed_t), dense_hidden),
+        (blocks_of(kept_one[2]), first_low),
+        (blocks_of(kept_one[0]), first_mixed),
+    ]
     small = jnp.concatenate(
         [
-            jnp.stack([first_sums[0], gain_one, second_sums[0], gain_three], axis=0),
-            jnp.stack([first_sums[1], shift_one, second_sums[1], shift_three], axis=0),
-            router_grad.T,
+            first_sums[0:1], dense_sums[0:1], second_sums[0:1], fourth_sums[0:1],
+            first_sums[1:2], dense_sums[1:2], second_sums[1:2], fourth_sums[1:2],
+            router_grad,
         ],
         axis=0,
     )
-    small = lax.psum(small, ("dp", "expert"))
+    chunks, small = reduce_grads(n_dp, n_ex, pairs, small, model_width)
+    attn_in_sum, attn_out_sum, ffn_in_sum, ffn_out_sum = unpack(
+        chunks, attn_in.shape[2] // model_width, ffn_in.shape[1] // model_width
+    )
     small = lax.dynamic_slice_in_dim(small, lax.axis_index("dp") * rows, rows, 1).T
     summed = [
-        jnp.stack([first_in, second_in], axis=1),
-        jnp.stack([first_out, second_out], axis=1),
+        attn_in_sum,
+        attn_out_sum,
         ffn_in_sum,
-        ffn_out_sum,
+        ffn_out_sum.reshape(-1, model_width),
         small[:, 8:],
         small[:, :4],
         small[:, 4:8],

time: 639 us -> 443 us (0.69)
  matrix products: 118 us -> 13.7 us
  Pallas kernels: 264 us -> 362 us
  blocking collectives: 85.7 us -> 0 us
  local copies, waits for them, and re-layouts: 70.1 us -> 37.3 us
  waiting for transfers between devices: 27.2 us -> 0.04 us
  other arithmetic: 31.6 us -> 9.44 us
  starting transfers between devices: 19.4 us -> 0.08 us
    dot_general x17 -> x2, matrix products: 118 us -> 13.7 us  [the longest x1 6.96 us: shards(): jnp.einsum('sd,sf->df', expert_rows.reshape(expert_slots, -1), expert_hid...]
    pallas_call x4 -> x8, Pallas kernels: 121 us -> 220 us  [the longest x2 78.1 us: attention_backward(): pl.pallas_call(functools.partial(attend_back_kernel, n_dp, n_ex, len(inpu...]
    psum x2 -> x0, blocking collectives: 85.7 us -> none  [the longest x1 45 us: mixture_forward(): counts = lax.psum(jnp.sum(chosen_hot, axis=0), ('dp', 'expert'))]
    all_to_all x4 -> x0, waiting for transfers between devices: 27.2 us -> none  [the longest x1 15.2 us: mixture_forward(): lax.all_to_all(outgoing, 'expert', split_axis=0, concat_axis=0, tiled=True)]
    all_to_all x4 -> x0, starting transfers between devices: 18.9 us -> none  [the longest x1 5.93 us: mixture_forward(): lax.all_to_all(result.reshape(incoming.shape), 'expert', split_axis=0, co...]
    convert_element_type x5 -> x0, other arithmetic: 15.8 us -> none  [the longest x1 12 us: ffn_forward(): active = exact_gelu(hidden).astype(jnp.bfloat16)]
    transpose x4 -> x0, local copies, waits for them, and re-layouts: 9.52 us -> none  [the longest x3 8.15 us: wide(): chunks[first:first + count].transpose(1, 0, 2)]
    reshape x5 -> x0, local copies, waits for them, and re-layouts: 8.89 us -> none  [the longest x1 2.1 us: mixture_forward(): homeward.reshape(experts_all * capacity, model_width)]
  transfers between devices with their start and end apart: 6 -> 2, of which waited for: 2 -> 0; matrix products, arithmetic and copies ran while one was open for 22% -> 4% of each run, Pallas kernels for 33% -> 53%
where the time goes in v3:
time: 443 us; the launch traced here: 438 us
  Pallas kernels  362 us (82%)
  local copies, waits for them, and re-layouts  37.3 us (8%)
  between operations  16.4 us (4%)
  matrix products  13.7 us (3%)
  other arithmetic  9.44 us (2%)
    pallas_call x1, Pallas kernels, reduce_grads(): pl.pallas_call(functools.partial(grad_kernel, n_dp, n_ex, rows, kinds, ha...  142 us
    pallas_call x2, Pallas kernels, attention_backward(): pl.pallas_call(functools.partial(attend_back_kernel, n_dp, n_ex, len(inpu...  78.1 us
    pallas_call x1, Pallas kernels, mixture(): pl.pallas_call(functools.partial(mixture_kernel, n_dp, n_ex), out_shape=o...  63.6 us
    pallas_call x2, Pallas kernels, attention_forward(): pl.pallas_call(functools.partial(attend_kernel, n_dp, n_ex, len(inputs)),...  55.3 us
    unnamed x91, local copies, waits for them, and re-layouts  25.3 us
    pallas_call x1, Pallas kernels, ffn_backward(): pl.pallas_call(functools.partial(ffn_back_kernel, hidden // width), grid=...  9.59 us
    pallas_call x1, Pallas kernels, ffn_forward(): pl.pallas_call(ffn_kernel, grid=(hidden // width,), out_shape=[jax.ShapeD...  9.36 us
  transfers between devices with their start and end apart: 2, of which 0 were waited for; matrix products, arithmetic and copies ran while one was open for 4% of the time, Pallas kernels for 53%

profile of v3, /device:TPU:0, one launch (start us, length us, event | category | flops | bytes accessed | tf_op | source)
XLA Modules:
  0.0 438.5 jit_solution(1754258901214063017)
XLA Ops:
  7.2 0.0 reduce-scatter.3.cloned.1.call-start
  7.2 0.8 reduce-window.8
  8.1 0.1 convert_reduce_fusion
  8.1 0.7 copy.33.refs_6_
  8.9 1.1 bitcast_convert_fusion.refs_0_.refs_1_
  10.0 2.4 copy.40
  12.4 3.9 copy.39
  16.3 3.5 slice_bitcast_fusion
  19.8 1.2 slice_bitcast_fusion.2
  21.0 0.0 copy-done.39
  21.0 0.7 fusion.3
  21.7 0.0 copy-done.7
  21.7 26.0 %attention_forward.2 = (f32[384,768]{1,0:T(8,128)S(1)}, bf16[768,384]{1,0:T(8,128)(2,1)S(1)}, bf16[384,768]{1,0:T(8,128)(2,1)S(1)}, bf16[768,384]{1,0:T(8,128)(2...) custom-call(f32[384,768]{1,0:T(8,128)S(1)} %bitcast_convert_fusion.r, ...), custom_call_target="tpu_custom_call" | custom-call | tf_op jit(solution)/shard_map/attention_forward/pallas_call | solution.py:967
  47.8 0.8 copy-done.13
  48.6 0.0 copy-start.6
  48.6 0.0 copy-start.34
  48.6 9.4 %ffn_forward.1 = (f32[384,768]{1,0:T(8,128)S(1)}, bf16[768,384]{1,0:T(8,128)(2,1)S(1)}, bf16[3072,384]{1,0:T(8,128)(2,1)S(1)}, bf16[384,3072]{1,0:T(8,128)(2,1)}) custom-call(f32[384,768]{1,0:T(8,128)S(1)} %get-tuple-element.68.x_ref, f32[1,768]{1,0:T(1,128)S(1)} %get-tuple-element.143.gain_ref, f32[1,768]{1,0:T(1,128)S(1)} %get-tuple-element.128.shift_ref, ...), custom_call_target="tpu_custom_call" | custom-call | tf_op jit(solution)/shard_map/ffn_forward/pallas_call | solution.py:355
  58.0 0.0 copy-done.29
  58.0 0.0 copy-done.33
  58.0 0.0 copy-start.5
  58.0 1.4 copy-done.5
  59.5 29.3 %attention_forward.3 = (f32[384,768]{1,0:T(8,128)S(1)}, bf16[768,384]{1,0:T(8,128)(2,1)S(1)}, bf16[384,768]{1,0:T(8,128)(2,1)S(1)}, bf16[768,384]{1,0:T(8,128)(2...) custom-call(f32[384,768]{1,0:T(8,128)S(1)} %get-tuple-element.69.ref, ...), custom_call_target="tpu_custom_call" | custom-call | tf_op jit(solution)/shard_map/attention_forward/pallas_call | solution.py:967
  88.7 0.0 copy-start.3
  88.8 1.0 copy-done.3
  89.8 0.9 copy-done.10
  90.7 0.8 copy-done.15
  91.5 0.8 copy-done.17
  92.3 0.8 copy-done.21
  93.1 0.8 copy-done.26
  93.9 0.7 copy-done.27
  94.6 0.6 copy-done.32
  95.2 63.6 %mixture.1 = (f32[384,768]{1,0:T(8,128)}, f32[2,768]{1,0:T(2,128)}, f32[8,768]{1,0:T(8,128)}, bf16[8,64,768]{2,1,0:T(8,128)(2,1)}, bf16[8,64,768]{2,1,0:T(8,128)...) custom-call(f32[384,768]{1,0:T(8,128)} %copy-done.3, ...), custom_call_target="tpu_custom_call" | custom-call | tf_op jit(solution)/shard_map/mixture/pallas_call | solution.py:675
  158.8 7.0 %fusion = bf16[1,768,3072]{2,1,0:T(8,128)(2,1)} fusion(bf16[512,768]{1,0:T(8,128)(2,1)} %bitcast.76, bf16[512,3072]{1,0:T(8,128)(2,1)} %get-tuple-element.117), kind=kOutput, calls=%fused_computation.3 | convolution fusion | flops 2418278400 | bytes 8650752 | tf_op jit(solution)/shard_map/sd,sf->df/dot_general | solution.py:1191
  165.8 0.0 reduce-scatter.3.cloned.1.call-update
  165.8 0.0 reduce-scatter.5.cloned.1.call-start
  165.9 1.1 copy-done.43
  166.9 6.7 %fusion.1 = bf16[1,3072,768]{2,1,0:T(8,128)(2,1)} fusion(bf16[512,3072]{1,0:T(8,128)(2,1)} %get-tuple-element.118, bf16[512,768]{1,0:T(8,128)(2,1)S(1)} %bitcast.75), kind=kOutput, calls=%fused_computation.4 | convolution fusion | flops 2418278400 | bytes 8650752 | tf_op jit(solution)/shard_map/sf,sd->fd/dot_general | solution.py:1194
  173.7 0.0 reduce-scatter.5.cloned.1.call-update
  173.7 41.6 %attention_backward.2 = (f32[384,768]{1,0:T(8,128)}, bf16[384,768]{1,0:T(8,128)(2,1)}, bf16[384,2304]{1,0:T(8,128)(2,1)}, f32[2,768]{1,0:T(2,128)}, bf16[384,768]{1,0:T(8,128)(2,1)}) custom-call(f32[384,768]{1,0:T(8,128)} %get-tuple-element.72.refs_0_, f32[384,768]{1,0:T(8,128)} %copy-done.2, f32[1,768]{1,0:T(1,128)} %copy-done.31, ...), custom_call_target="tpu_custom_call" | custom-call | tf_op jit(solution)/shard_map/attention_backward/pallas_call | solution.py:1136
  215.3 0.0 copy-start.9
  215.3 1.3 copy-done.9
  216.6 9.6 %ffn_backward.1 = (f32[384,768]{1,0:T(8,128)S(1)}, bf16[384,768]{1,0:T(8,128)(2,1)S(1)}, bf16[384,3072]{1,0:T(8,128)(2,1)}, f32[2,768]{1,0:T(2,128)S(1)}) custom-call(f32[384,768]{1,0:T(8,128)S(1)} %copy-done.9, f32[384,768]{1,0:T(8,128)S(1)} %get-tuple-element.68.x_ref, f32[1,768]{1,0:T(1,128)S(1)} %get-tuple-element.143.gain_ref, ...), custom_call_target="tpu_custom_call" | custom-call | tf_op jit(solution)/shard_map/ffn_backward/pallas_call | solution.py:409
  226.2 1.0 copy-done.8
  227.2 0.8 copy-done.22
  228.1 36.5 %attention_backward.3 = (f32[384,768]{1,0:T(8,128)}, bf16[384,768]{1,0:T(8,128)(2,1)}, bf16[384,2304]{1,0:T(8,128)(2,1)}, f32[2,768]{1,0:T(2,128)}) custom-call(f32[384,768]{1,0:T(8,128)} %copy-done.8, f32[384,768]{1,0:T(8,128)} %copy-done, f32[1,768]{1,0:T(1,128)} %copy-done.30, bf16[768,2304]{1,0:T(8,128)(2,1)} %get-tuple-element.121.refs_3_, ...), custom_call_target="tpu_custom_call" | custom-call | tf_op jit(solution)/shard_map/attention_backward/pallas_call | solution.py:1136
  264.6 0.0 copy-done.41
  264.6 1.4 fusion.8
  265.9 0.6 fusion.7
  266.5 2.7 concatenate.3.refs_12_
  269.3 0.0 copy-start.23
  269.3 1.1 copy-done.23
  270.4 1.1 copy-done.24
  271.4 0.8 copy-done.28
  272.2 141.6 %dense_grads.1 = (bf16[16,192,768]{2,1,0:T(8,128)(2,1)}, f32[16,768]{1,0:T(8,128)S(1)}) custom-call(bf16[4,1,192,384]{3,2,1,0:T(8,128)(2,1)S(1)} %bitcast.57, bf16[4,1,192,384]{3,2,1,0:T(8,128)(2,1)S(1)} %bitcast.56, bf16[4,4,192,384]{3,2,1,0:T(8,128)(2,1)} %bitcast.50, bf16[4,1,192,384]{3,2,1,0:T(8,128)(2,1)S(1)} %bitcast.55, ...), custom_call_target="tpu_custom_call" | custom-call | tf_op jit(solution)/shard_map/dense_grads/pallas_call | solution.py:243
  413.9 0.1 dynamic-slice_bitcast_fusion
  413.9 0.6 slice.117
  414.5 2.3 copy-done.4
  416.9 3.9 unpack.1
  420.8 0.7 multiply_reduce_fusion
  422.1 0.6 fusion.2
  422.7 0.9 convert_bitcast_fusion
  423.6 2.9 convert_element_type.35
  426.6 2.9 convert_element_type.38
  429.5 0.8 copy.42
  (63 shorter events, 0.1 us)
Async XLA Ops:
  7.2 416.4 %reduce-scatter.3.cloned.1.call-start = ((), (), s32[]{:S(2)}) async-start(), calls=%async_computation.2 | async-start | bytes 5898240 | tf_op jit(solution)/shard_map/reduce_scatter | solution.py:1247
  8.1 51.3 %copy-start.35 = (s32[128]{0:T(128)}, s32[128]{0:T(128)S(1)}, u32[]{:S(2)}) copy-start(s32[128]{0:T(128)S(1)} %convert_reduce_fusion) | copy-start | bytes 1540
  10.0 11.7 %copy-start = (f32[384,768]{1,0:T(8,128)}, f32[384,768]{1,0:T(8,128)S(1)}, u32[]{:S(2)}) copy-start(f32[384,768]{1,0:T(8,128)S(1)} %bitcast_convert_fusion.refs_0_.refs_1_) | copy-start | bytes 3538948
  19.8 1.2 copy-start.39
  19.8 1.2 copy-start.40
  19.8 1.9 copy-start.7
  21.0 26.7 %copy-start.1 = (bf16[768,768]{1,0:T(8,128)(2,1)}, bf16[768,768]{1,0:T(8,128)(2,1)S(1)}, u32[]{:S(2)}) copy-start(bf16[768,768]{1,0:T(8,128)(2,1)S(1)} %get-tuple-element.123.refs_4_) | copy-start | bytes 3538948
  21.7 26.1 %copy-start.30 = (f32[1,768]{1,0:T(1,128)}, f32[1,768]{1,0:T(1,128)S(1)}, u32[]{:S(2)}) copy-start(f32[1,768]{1,0:T(1,128)S(1)} %get-tuple-element.142.refs_1_.refs_2_) | copy-start | bytes 9220
  21.7 37.8 %copy-start.31 = (f32[1,768]{1,0:T(1,128)}, f32[1,768]{1,0:T(1,128)S(1)}, u32[]{:S(2)}) copy-start(f32[1,768]{1,0:T(1,128)S(1)} %get-tuple-element.144.refs_1_.refs_2_) | copy-start | bytes 9220
  47.8 0.8 copy-start.13
  48.6 9.4 %copy-start.11 = (bf16[768,384]{1,0:T(8,128)(2,1)}, bf16[768,384]{1,0:T(8,128)(2,1)S(1)}, u32[]{:S(2)}) copy-start(bf16[768,384]{1,0:T(8,128)(2,1)S(1)} %get-tuple-element.98) | copy-start | bytes 1769476
  48.6 9.4 %copy-start.19 = (bf16[384,768]{1,0:T(8,128)(2,1)}, bf16[384,768]{1,0:T(8,128)(2,1)S(1)}, u32[]{:S(2)}) copy-start(bf16[384,768]{1,0:T(8,128)(2,1)S(1)} %get-tuple-element.86.refs_7_) | copy-start | bytes 1769476
  48.6 9.4 %copy-start.25 = (bf16[6,2,128,128]{3,2,1,0:T(8,128)(2,1)}, bf16[6,2,128,128]{3,2,1,0:T(8,128)(2,1)S(1)}, u32[]{:S(2)}) copy-start(bf16[6,2,128,128]{3,2,1,0:T(8,128)(2,1)S(1)} %get-tuple-element.89.refs_10_) | copy-start | bytes 1179652
  48.6 9.4 %copy-start.29 = (bf16[6,128,128]{2,1,0:T(8,128)(2,1)}, bf16[6,128,128]{2,1,0:T(8,128)(2,1)S(1)}, u32[]{:S(2)}) copy-start(bf16[6,128,128]{2,1,0:T(8,128)(2,1)S(1)} %get-tuple-element.90.refs_11_) | copy-start | bytes 589828
  48.6 9.4 %copy-start.33 = (f32[6,2,384]{2,1,0:T(2,128)}, f32[6,2,384]{2,1,0:T(2,128)S(1)}, u32[]{:S(2)}) copy-start(f32[6,2,384]{2,1,0:T(2,128)S(1)} %get-tuple-element.91.refs_12_) | copy-start | bytes 55300
  48.6 10.8 %copy-start.6 = (bf16[1,384,768]{2,1,0:T(8,128)(2,1)S(1)}, bf16[1,384,768]{2,1,0:T(8,128)(2,1)}, u32[]{:S(2)}) copy-start(bf16[1,384,768]{2,1,0:T(8,128)(2,1)} %param.25) | copy-start | bytes 1769476
  48.6 10.8 %copy-start.34 = (s32[1,384,1]{1,2,0:T(1,128)S(1)}, s32[1,384,1]{1,2,0:T(1,128)}, u32[]{:S(2)}) copy-start(s32[1,384,1]{1,2,0:T(1,128)} %param.15) | copy-start | bytes 4612
  58.0 1.4 copy-start.5
  59.4 29.3 %copy-start.2 = (f32[384,768]{1,0:T(8,128)}, f32[384,768]{1,0:T(8,128)S(1)}, u32[]{:S(2)}) copy-start(f32[384,768]{1,0:T(8,128)S(1)} %get-tuple-element.69.refs_0_.refs_1_) | copy-start | bytes 3538948
  88.7 1.0 copy-start.3
  89.8 0.9 copy-start.10
  90.7 0.8 copy-start.15
  91.5 0.8 copy-start.17
  92.3 0.8 copy-start.21
  93.1 0.8 copy-start.26
  93.9 0.7 copy-start.27
  94.6 0.6 copy-start.32
  165.8 1.1 copy-start.43
  165.8 260.7 %reduce-scatter.5.cloned.1.call-start = ((), (), s32[]{:S(2)}) async-start(), calls=%async_computation.3 | async-start | bytes 5898240 | tf_op jit(solution)/shard_map/reduce_scatter | solution.py:1250
  215.3 1.3 copy-start.9
  226.2 1.0 copy-start.8
  227.2 0.8 copy-start.22
  228.0 36.5 %copy-start.42 = (f32[2,768]{1,0:T(2,128)S(1)}, f32[2,768]{1,0:T(2,128)}, u32[]{:S(2)}) copy-start(f32[2,768]{1,0:T(2,128)} %get-tuple-element.107) | copy-start | bytes 18436
  228.0 36.5 %copy-start.41 = (f32[2,768]{1,0:T(2,128)S(1)}, f32[2,768]{1,0:T(2,128)}, u32[]{:S(2)}) copy-start(f32[2,768]{1,0:T(2,128)} %get-tuple-element.108) | copy-start | bytes 18436
  228.0 41.2 %copy-start.12 = (bf16[768,384]{1,0:T(8,128)(2,1)S(1)}, bf16[768,384]{1,0:T(8,128)(2,1)}, u32[]{:S(2)}) copy-start(bf16[768,384]{1,0:T(8,128)(2,1)} %copy-done.11) | copy-start | bytes 1769476
  228.0 41.2 %copy-start.14 = (bf16[768,384]{1,0:T(8,128)(2,1)S(1)}, bf16[768,384]{1,0:T(8,128)(2,1)}, u32[]{:S(2)}) copy-start(bf16[768,384]{1,0:T(8,128)(2,1)} %copy-done.13) | copy-start | bytes 1769476
  228.0 41.2 %copy-start.16 = (bf16[768,384]{1,0:T(8,128)(2,1)S(1)}, bf16[768,384]{1,0:T(8,128)(2,1)}, u32[]{:S(2)}) copy-start(bf16[768,384]{1,0:T(8,128)(2,1)} %copy-done.15) | copy-start | bytes 1769476
  228.0 41.2 %copy-start.18 = (bf16[768,384]{1,0:T(8,128)(2,1)S(1)}, bf16[768,384]{1,0:T(8,128)(2,1)}, u32[]{:S(2)}) copy-start(bf16[768,384]{1,0:T(8,128)(2,1)} %copy-done.17) | copy-start | bytes 1769476
  228.0 41.2 %copy-start.20 = (bf16[384,768]{1,0:T(8,128)(2,1)S(1)}, bf16[384,768]{1,0:T(8,128)(2,1)}, u32[]{:S(2)}) copy-start(bf16[384,768]{1,0:T(8,128)(2,1)} %get-tuple-element.99.refs_6_) | copy-start | bytes 1769476
  269.3 1.1 copy-start.23
  270.3 1.1 copy-start.24
  271.4 0.8 copy-start.28
  414.5 2.3 copy-start.4
  416.9 3.9 copy-start.38
  416.9 5.9 %copy-start.36 = (f32[384,768]{1,0:T(8,128)S(1)}, f32[384,768]{1,0:T(8,128)}, u32[]{:S(2)}) copy-start(f32[384,768]{1,0:T(8,128)} %get-tuple-element.92) | copy-start | bytes 3538948
  426.6 2.9 copy-start.37
Sparse Core Ops, SparseCore 0:
  165.9 57.4 reduce-scatter.2
  226.2 49.3 reduce-scatter.4

commit v4 on v3

--- a/solution.py
+++ b/solution.py
@@ -34,233 +34,10 @@
     return total
 
 
-def reduce_plan(n_dp, n_ex, rows):
-    dp_levels = n_dp.bit_length() - 1
-    ex_levels = n_ex.bit_length() - 1
-    halvings, piece = 0, rows
-    while halvings < ex_levels and piece % 32 == 0:
-        piece //= 2
-        halvings += 1
-    kinds = [("dp", b) for b in range(dp_levels)]
-    kinds += [("half", b) for b in range(halvings)]
-    kinds += [("both", b) for b in range(halvings, ex_levels)]
-    kinds += [("back", b) for b in reversed(range(halvings))]
-    return kinds, halvings, piece
-
-
-def grad_kernel(n_dp, n_ex, rows, kinds, halvings, firsts, chunks, fin_slots, *refs):
-    count, groups = len(kinds), len(firsts)
-    x_refs, dy_refs = refs[:groups], refs[groups : 2 * groups]
-    small_ref, out_ref, small_out_ref = refs[2 * groups : 2 * groups + 3]
-    it = iter(refs[2 * groups + 3 :])
-    send_bufs = [next(it) if k[0] != "back" else None for k in kinds]
-    recv_bufs = [next(it) if k[0] != "back" else None for k in kinds]
-    keep_bufs = [next(it) if k[0] != "back" else None for k in kinds]
-    fin = next(it)
-    send_sems = [next(it) for _ in kinds]
-    recv_sems = [next(it) for _ in kinds]
-    small_send, small_recv, small_send_sem, small_recv_sem = it
-    t = pl.program_id(0)
-    d, e = lax.axis_index("dp"), lax.axis_index("expert")
-    dp_levels, ex_levels = n_dp.bit_length() - 1, n_ex.bit_length() - 1
-
-    def peer(kind, level):
-        return (flip(d, level), e) if kind == "dp" else (d, flip(e, level))
-
-    @pl.when(t == 0)
-    def _():
-        barrier = pltpu.get_barrier_semaphore()
-        for level in range(dp_levels):
-            pl.semaphore_signal(barrier, inc=1, device_id=peer("dp", level), device_id_type=MESH)
-        for level in range(ex_levels):
-            pl.semaphore_signal(barrier, inc=1, device_id=peer("ex", level), device_id_type=MESH)
-        pl.semaphore_wait(barrier, dp_levels + ex_levels)
-
-    def kept_rows(depth):
-        start = 0
-        for b in range(depth):
-            start = start + bit_of(e, b) * (rows >> (b + 1))
-        return start
-
-    def copy_of(s, c):
-        kind, level = kinds[s]
-        slot = lax.rem(c, 2)
-        if kind == "back":
-            span = rows >> (level + 1)
-            at = pl.ds(pl.multiple_of(kept_rows(level + 1), span), span)
-            src = fin.at[lax.rem(c, fin_slots), at]
-            dst = src
-        else:
-            src, dst = send_bufs[s].at[slot], recv_bufs[s].at[slot]
-        return pltpu.make_async_remote_copy(
-            src_ref=src,
-            dst_ref=dst,
-            send_sem=send_sems[s].at[slot],
-            recv_sem=recv_sems[s].at[slot],
-            device_id=peer(kind, level),
-            device_id_type=MESH,
-        )
-
-    def arrive(s, c):
-        kind, level = kinds[s]
-        copy_of(s, c).wait()
-        slot = lax.rem(c, 2)
-        if kind == "back":
-            return None
-        if kind == "dp":
-            n = recv_bufs[s].shape[1]
-            return [keep_bufs[s][slot, i] + recv_bufs[s][slot, i].astype(jnp.float32) for i in range(n)]
-        return [keep_bufs[s][slot] + recv_bufs[s][slot].astype(jnp.float32)]
-
-    def leave(s, c, values):
-        kind, level = kinds[s]
-        slot = lax.rem(c, 2)
-        if kind == "dp":
-            for i in range(len(values) // 2):
-                send_bufs[s][slot, i] = values[2 * i + 1].astype(jnp.bfloat16)
-        elif kind == "half":
-            (value,) = values
-            half = value.shape[0] // 2
-            own = bit_of(e, level)
-            top, low = value[:half], value[half:]
-            send_bufs[s][slot] = jnp.where(own == 0, low, top).astype(jnp.bfloat16)
-        elif kind == "both":
-            (value,) = values
-            send_bufs[s][slot] = value.astype(jnp.bfloat16)
-        elif values is not None:
-            (value,) = values
-            span = value.shape[0]
-            at = pl.ds(pl.multiple_of(kept_rows(halvings), span), span)
-            fin[lax.rem(c, fin_slots), at] = value.astype(jnp.bfloat16)
-        copy_of(s, c).start()
-        if kind == "dp":
-            for i in range(len(values) // 2):
-                keep_bufs[s][slot, i] = values[2 * i]
-        elif kind == "half":
-            keep_bufs[s][slot] = jnp.where(own == 0, top, low)
-        elif kind == "both":
-            keep_bufs[s][slot] = value.astype(jnp.bfloat16).astype(jnp.float32)
-
-    levels = [("dp", b) for b in range(dp_levels)] + [("ex", b) for b in range(ex_levels)]
-
-    def small_copy(i):
-        return pltpu.make_async_remote_copy(
-            src_ref=small_send.at[i],
-            dst_ref=small_recv.at[i],
-            send_sem=small_send_sem.at[i],
-            recv_sem=small_recv_sem.at[i],
-            device_id=peer(*levels[i]),
-            device_id_type=MESH,
-        )
-
-    for i in range(len(levels) + 1):
-
-        @pl.when(t == i)
-        def _(i=i):
-            if i == 0:
-                value = small_ref[...]
-            else:
-                small_copy(i - 1).wait()
-                value = small_send[i - 1] + small_recv[i - 1]
-            if i < len(levels):
-                small_send[i] = value
-                small_copy(i).start()
-            else:
-                small_out_ref[...] = value
-
-    ends = list(firsts[1:]) + [chunks]
-    for s in reversed(range(count + 1)):
-        c = t - s
-        if s == 0:
-            for g in range(groups):
-
-                @pl.when((c >= firsts[g]) & (c < ends[g]))
-                def _(g=g):
-                    dy = dy_refs[g][...]
-                    slot = lax.rem(c, 2)
-
-                    def piece(mask):
-                        q = partner_index(d, mask, dp_levels)
-                        return jnp.dot(x_refs[g][q], dy, preferred_element_type=jnp.float32)
-
-                    for i in range(n_dp // 2):
-                        send_bufs[0][slot, i] = piece(2 * i + 1).astype(jnp.bfloat16)
-                    copy_of(0, c).start()
-                    for i in range(n_dp // 2):
-                        keep_bufs[0][slot, i] = piece(2 * i)
-
-        else:
-
-            @pl.when((c >= 0) & (c < chunks))
-            def _(s=s, c=c):
-                values = arrive(s - 1, c)
-                if s < count:
-                    leave(s, c, values)
-                elif kinds[s - 1][0] == "back":
-                    out_ref[...] = fin[lax.rem(c, fin_slots)]
-                else:
-                    out_ref[...] = values[0].astype(jnp.bfloat16)
-
-
-def reduce_grads(n_dp, n_ex, pairs, small, width):
-    _, _, rows, tokens = pairs[0][0].shape
-    sizes = [x.shape[1] * (dy.shape[1] // width) for x, dy in pairs]
-    firsts = [sum(sizes[:i]) for i in range(len(sizes))]
-    chunks = sum(sizes)
-    kinds, halvings, piece = reduce_plan(n_dp, n_ex, rows)
-    count = len(kinds)
-    fin_slots = max(1, halvings + 1)
-    shapes = []
-    for kind, level in kinds:
-        if kind == "dp":
-            shapes.append((n_dp >> (level + 1), rows, width))
-        elif kind == "half":
-            shapes.append((rows >> (level + 1), width))
-        elif kind == "both":
-            shapes.append((piece, width))
-    scratch = [pltpu.VMEM((2,) + s, jnp.bfloat16) for s in shapes] * 2
-    scratch += [pltpu.VMEM((2,) + s, jnp.float32) for s in shapes]
-    scratch += [pltpu.VMEM((fin_slots, rows, width), jnp.bfloat16)]
-    scratch += [pltpu.SemaphoreType.DMA((2,)) for _ in kinds] * 2
-    hops = (n_dp * n_ex).bit_length() - 1
-    scratch += [pltpu.VMEM((hops,) + small.shape, jnp.float32)] * 2
-    scratch += [pltpu.SemaphoreType.DMA((hops,))] * 2
-    in_specs = []
-    for (x, dy), first, size in zip(pairs, firsts, sizes):
-        many = x.shape[1] > 1
-
-        def x_place(t, first=first, size=size, many=many):
-            return (0, jnp.clip(t - first, 0, size - 1) if many else 0, 0, 0)
-
-        in_specs.append(pl.BlockSpec((n_dp, None, rows, tokens), x_place))
-    for (x, dy), first, size in zip(pairs, firsts, sizes):
-        many = dy.shape[1] > width
-
-        def dy_place(t, first=first, size=size, many=many):
-            return (0, jnp.clip(t - first, 0, size - 1) if many else 0)
-
-        in_specs.append(pl.BlockSpec((tokens, width), dy_place))
-    return pl.pallas_call(
-        functools.partial(grad_kernel, n_dp, n_ex, rows, kinds, halvings, firsts, chunks, fin_slots),
-        grid=(chunks + count,),
-        out_shape=[
-            jax.ShapeDtypeStruct((chunks, rows, width), jnp.bfloat16),
-            jax.ShapeDtypeStruct(small.shape, jnp.float32),
-        ],
-        in_specs=in_specs + [pl.BlockSpec(small.shape, lambda t: (0, 0))],
-        out_specs=[
-            pl.BlockSpec((None, rows, width), lambda t: (jnp.maximum(t - count, 0), 0, 0)),
-            pl.BlockSpec(small.shape, lambda t: (0, 0)),
-        ],
-        scratch_shapes=scratch,
-        compiler_params=pltpu.CompilerParams(
-            collective_id=1, has_side_effects=True, vmem_limit_bytes=48 * 1024 * 1024
-        ),
-        name="dense_grads",
-    )(*[x for x, _ in pairs], *[dy for _, dy in pairs], small)
-
-
-def unpack_kernel(per_in, per_ffn, chunk_ref, in_ref, out_ref, ffn_in_ref, ffn_out_ref):
+def unpack_kernel(
+    per_in, per_ffn, chunk_ref, expert_ref, in_ref, out_ref, ffn_in_ref, ffn_out_ref, expert_in_ref, expert_out_ref
+):
+    per_expert = expert_ref.shape[0] // 2
     width = chunk_ref.shape[2]
     at = 0
     for layer in (1, 0):
@@ -273,10 +50,14 @@
                 ffn_out_ref[j] = chunk_ref[at + j].astype(jnp.float32)
                 ffn_in_ref[:, width * j : width * j + width] = chunk_ref[at + per_ffn + j].astype(jnp.float32)
             at += 2 * per_ffn
-
-
-def unpack(chunks, per_in, per_ffn):
+    for j in range(per_expert):
+        expert_in_ref[:, width * j : width * j + width] = expert_ref[j].astype(jnp.float32)
+        expert_out_ref[j] = expert_ref[per_expert + j].astype(jnp.float32)
+
+
+def unpack(chunks, expert_chunks, per_in, per_ffn):
     count, rows, width = chunks.shape
+    experts = expert_chunks.shape[0]
     step = 48 if rows % 48 == 0 else rows
     wide = jnp.float32
     return pl.pallas_call(
@@ -287,17 +68,24 @@
             jax.ShapeDtypeStruct((rows, 2, width), wide),
             jax.ShapeDtypeStruct((rows, per_ffn * width), wide),
             jax.ShapeDtypeStruct((per_ffn, rows, width), wide),
+            jax.ShapeDtypeStruct((rows, experts // 2 * width), wide),
+            jax.ShapeDtypeStruct((experts // 2, rows, width), wide),
         ],
-        in_specs=[pl.BlockSpec((count, step, width), lambda i: (0, i, 0))],
+        in_specs=[
+            pl.BlockSpec((count, step, width), lambda i: (0, i, 0)),
+            pl.BlockSpec((experts, step, width), lambda i: (0, i, 0)),
+        ],
         out_specs=[
             pl.BlockSpec((step, 2, per_in * width), lambda i: (i, 0, 0)),
             pl.BlockSpec((step, 2, width), lambda i: (i, 0, 0)),
             pl.BlockSpec((step, per_ffn * width), lambda i: (i, 0)),
             pl.BlockSpec((per_ffn, step, width), lambda i: (0, i, 0)),
+            pl.BlockSpec((step, experts // 2 * width), lambda i: (i, 0)),
+            pl.BlockSpec((experts // 2, step, width), lambda i: (0, i, 0)),
         ],
         compiler_params=pltpu.CompilerParams(vmem_limit_bytes=40 * 1024 * 1024),
         name="unpack",
-    )(chunks)
+    )(chunks, expert_chunks)
 
 
 def dot(a, b):
@@ -380,61 +168,6 @@
     )(stream, norm_gain, norm_shift, weight_in, weight_out)
 
 
-def ffn_back_kernel(steps, up_ref, x_ref, gain_ref, w_in_ref, w_out_ref, slope_ref, next_ref, low_ref, hidden_ref, sums_ref, acc_ref):
-    i = pl.program_id(0)
-
-    @pl.when(i == 0)
-    def _():
-        low_ref[...] = up_ref[...].astype(jnp.bfloat16)
-        acc_ref[...] = jnp.zeros_like(acc_ref)
-
-    grad = (dot_rows(low_ref[...], w_out_ref[...]) * slope_ref[...].astype(jnp.float32)).astype(jnp.bfloat16)
-    hidden_ref[...] = grad
-    acc_ref[...] += dot_rows(grad, w_in_ref[...])
-
-    @pl.when(i == steps - 1)
-    def _():
-        unit, inverse = norm_parts(x_ref[...])
-        grad_normed = acc_ref[...]
-        next_ref[...] = up_ref[...] + norm_back(unit, inverse, gain_ref[...], grad_normed)
-        sums_ref[0:1] = jnp.sum(grad_normed * unit, axis=0, keepdims=True)
-        sums_ref[1:2] = jnp.sum(grad_normed, axis=0, keepdims=True)
-
-
-def ffn_backward(upstream, stream, norm_gain, weight_in, weight_out, slope):
-    rows, width = stream.shape
-    hidden = weight_in.shape[1]
-    low = jnp.bfloat16
-    whole = pl.BlockSpec((rows, width), lambda i: (0, 0))
-    return pl.pallas_call(
-        functools.partial(ffn_back_kernel, hidden // width),
-        grid=(hidden // width,),
-        out_shape=[
-            jax.ShapeDtypeStruct((rows, width), jnp.float32),
-            jax.ShapeDtypeStruct((rows, width), low),
-            jax.ShapeDtypeStruct((rows, hidden), low),
-            jax.ShapeDtypeStruct((2, width), jnp.float32),
-        ],
-        in_specs=[
-            whole,
-            whole,
-            pl.BlockSpec((1, width), lambda i: (0, 0)),
-            pl.BlockSpec((width, width), lambda i: (0, i)),
-            pl.BlockSpec((width, width), lambda i: (i, 0)),
-            pl.BlockSpec((rows, width), lambda i: (0, i)),
-        ],
-        out_specs=[
-            whole,
-            whole,
-            pl.BlockSpec((rows, width), lambda i: (0, i)),
-            pl.BlockSpec((2, width), lambda i: (0, 0)),
-        ],
-        scratch_shapes=[pltpu.VMEM((rows, width), jnp.float32)],
-        compiler_params=pltpu.CompilerParams(vmem_limit_bytes=48 * 1024 * 1024),
-        name="ffn_backward",
-    )(upstream, stream, norm_gain, weight_in, weight_out, slope)
-
-
 def capacity_of(rows, experts):
     capacity = (5 * rows + 4 * experts - 1) // (4 * experts)
     return capacity, -(-capacity // 16) * 16
@@ -515,15 +248,15 @@
 def mixture_kernel(
     n_dp, n_ex,
     x_ref, gain_ref, shift_ref, router_ref, assign_ref, cot_ref, far_cot_ref, w_in_ref, w_out_ref,
-    up_ref, sums_ref, router_grad_ref, rows_ref, back_ref, active_ref, hidden_ref, result_ref, gate_ref, stats_ref,
-    send_ref, grad_ref, home_ref, dgate_ref, home_dgate_ref, stat_send, stat_recv, dispatch_ref, result_acc, grad_acc,
+    up_ref, sums_ref, router_grad_ref, rows_t_ref, back_ref, active_t_ref, hidden_ref, result_ref, gate_ref, stats_ref,
+    rows_ref, send_ref, grad_ref, home_ref, dgate_ref, home_dgate_ref, stat_send, stat_recv, dispatch_ref, result_acc, grad_acc,
     x_send_sem, x_recv_sem, grad_send_sem, grad_recv_sem, dgate_send_sem, dgate_recv_sem, stat_send_sem, stat_recv_sem,
 ):
     d, e = lax.axis_index("dp"), lax.axis_index("expert")
     dp_levels, ex_levels = n_dp.bit_length() - 1, n_ex.bit_length() - 1
     tokens, width = x_ref.shape
     padded = send_ref.shape[1]
-    group = min(4, n_ex)
+    group = min(max(4, 128 // padded), n_ex)
     groups = n_ex // group
     exact = dict(precision=lax.Precision.HIGHEST, preferred_element_type=jnp.float32)
     hops = [(flip(d, b), e) for b in range(dp_levels)] + [(d, flip(e, b)) for b in range(ex_levels)]
@@ -587,16 +320,17 @@
         slot_gate = jax.nn.sigmoid(jnp.sum(jnp.where(own, logits, 0.0), axis=1, keepdims=True))
         back = (slot_gate * cot).astype(jnp.bfloat16)
         back_ref[at] = back.reshape(group, padded, width)
+        span = pl.ds(pl.multiple_of(first * padded, group * padded), group * padded)
+        rows_t_ref[:, span] = rows.T
         result_acc[...] = jnp.zeros_like(result_acc)
         grad_acc[...] = jnp.zeros_like(grad_acc)
-        span = pl.ds(pl.multiple_of(first * padded, group * padded), group * padded)
 
         def block(i, _):
             cols = pl.ds(pl.multiple_of(i * step, step), step)
             active, slope = gelu_parts(dot(rows, w_in_ref[:, cols]))
             active = active.astype(jnp.bfloat16)
             hidden = (slope * dot_rows(back, w_out_ref[cols, :])).astype(jnp.bfloat16)
-            active_ref[span, cols] = active
+            active_t_ref[cols, span] = active.T
             hidden_ref[span, cols] = hidden
             result_acc[...] += dot(active, w_out_ref[cols, :])
             grad_acc[...] += dot_rows(hidden, w_in_ref[:, cols])
@@ -655,7 +389,7 @@
     hidden = weight_in.shape[1]
     _, padded = capacity_of(tokens, n_ex)
     slots = n_ex * padded
-    group = min(4, n_ex) * padded
+    group = min(max(4, 128 // padded), n_ex) * padded
     low, wide = jnp.bfloat16, jnp.float32
     slab = (n_ex, padded, width)
     hops = (n_dp * n_ex).bit_length() - 1
@@ -663,9 +397,9 @@
         jax.ShapeDtypeStruct((tokens, width), wide),
         jax.ShapeDtypeStruct((2, width), wide),
         jax.ShapeDtypeStruct((n_ex, width), wide),
+        jax.ShapeDtypeStruct((width, slots), low),
         jax.ShapeDtypeStruct(slab, low),
-        jax.ShapeDtypeStruct(slab, low),
-        jax.ShapeDtypeStruct((slots, hidden), low),
+        jax.ShapeDtypeStruct((hidden, slots), low),
         jax.ShapeDtypeStruct((slots, hidden), low),
         jax.ShapeDtypeStruct(slab, low),
         jax.ShapeDtypeStruct((1, tokens), wide),
@@ -678,6 +412,7 @@
         in_specs=[vmem] * 9,
         out_specs=[vmem] * len(outs),
         scratch_shapes=[
+            pltpu.VMEM(slab, low),
             pltpu.VMEM(slab, low),
             pltpu.VMEM(slab, low),
             pltpu.VMEM(slab, low),
@@ -977,51 +712,29 @@
     )(*inputs)
 
 
-def attend_back_kernel(n_dp, n_ex, inputs, *refs):
-    (up_ref, x_ref, gain_ref, w_in_ref, w_out_ref, doc_row_ref, doc_col_ref), rest = refs[:7], refs[7:]
-    (context_ref, kv_ref, q_ref, short_kv_ref, short_q_ref, lse_ref), rest = rest[:6], rest[6:]
-    if inputs > 13:
-        (assign_ref, gate_ref, stream_ref, result_ref), rest = rest[:4], rest[4:]
-    (up_next_ref, up_low_ref, mixed_ref, sums_ref), rest = rest[:4], rest[4:]
-    if inputs > 13:
-        (output_ref,), rest = rest[:1], rest[1:]
-    (do_ref, aux_ref, short_do_ref, short_aux_ref, dq_ref, dk_ref, dv_ref), rest = rest[:7], rest[7:]
-    (do_far, do_near, do_recv, aux_far, aux_near, aux_recv), rest = rest[:6], rest[6:]
-    links = Links(n_dp)
-    me = links.me
-    pairs, long, width = kv_ref.shape[1], kv_ref.shape[3], x_ref.shape[1]
-    scale = HEAD_DIM ** (-0.5)
-    up = up_ref[...]
-    up_low = up.astype(jnp.bfloat16)
-    up_low_ref[...] = up_low
-    grad_context = dot_rows(up_low, w_out_ref[...]).astype(jnp.bfloat16)
+def share_context(context, lse, grad_context, do_ref, aux_ref, short_do_ref, short_aux_ref, me, long):
     lane = lax.broadcasted_iota(jnp.int32, (8, 128), 1) < HEAD_DIM
     head = lax.broadcasted_iota(jnp.int32, (8, 128), 0)
     picks = jnp.where(((head == 0) & lane) | ((head == 1) & ~lane), 1.0, 0.0)
-    for h in range(pairs):
+    for h in range(do_ref.shape[1]):
         at = slice(128 * h, 128 * h + 128)
         piece = grad_context[:, at]
         do_ref[me, h] = piece[:long]
         short_do_ref[h] = piece[long:]
-        both = piece.astype(jnp.float32) * context_ref[:, at].astype(jnp.float32)
+        both = piece.astype(jnp.float32) * context[:, at].astype(jnp.float32)
         delta = lax.dot_general(
             picks, both, (((1,), (1,)), ((), ())), precision=lax.Precision.HIGHEST, preferred_element_type=jnp.float32
         )
-        aux_ref[me, h, 0:2] = lse_ref[h, :, :long]
+        aux_ref[me, h, 0:2] = lse[h, :, :long]
         aux_ref[me, h, 2:4] = delta[0:2, :long]
-        short_aux_ref[h, 0:2] = lse_ref[h, :, long:]
+        short_aux_ref[h, 0:2] = lse[h, :, long:]
         short_aux_ref[h, 2:4] = delta[0:2, long:]
-    greet(links.peers() + (across_peers(n_ex) if inputs > 13 else []))
-    do_spread = Spread(links, lambda b, p: do_ref.at[b, p], pairs, False, do_far, do_near, do_recv)
-    aux_spread = Spread(links, lambda b, p: aux_ref.at[b, p], pairs, False, aux_far, aux_near, aux_recv)
-    for h in range(pairs):
-        do_spread.send(h)
-        aux_spread.send(h)
-    if inputs > 13:
-        home_ref, result_send_sem, result_recv_sem = rest
-        result_across = Across(n_ex, result_ref, home_ref, result_send_sem, result_recv_sem)
-        result_across.start_all()
-        home_ref[links.expert] = result_ref[links.expert]
+
+
+def attend_back_pair(n_dp, me, width, r, do_spread, aux_spread, h):
+    scale = HEAD_DIM ** (-0.5)
+    mixed_ref = r["mixed"]
+    long = r["kv"].shape[3]
 
     def row_of(aux, first):
         return jnp.concatenate([aux[first : first + 1], aux[first + 1 : first + 2]], axis=1)
@@ -1034,80 +747,346 @@
         grad_scores = probs * (dot_rows(values, grads) - row_of(aux, 2))
         return probs.astype(jnp.bfloat16), grad_scores.astype(jnp.bfloat16)
 
-    def put(h, third, first, value):
+    def put(third, first, value):
         at = pl.ds(pl.multiple_of(third * width + 128 * h, 128), 128)
         mixed_ref[first : first + value.shape[0], at] = value.astype(jnp.bfloat16)
 
-    def own_part(h, _):
-        seen = short_seen(doc_row_ref[...], doc_col_ref[...])
-        queries, grads = head_pair(short_q_ref[h]), head_pair(short_do_ref[h])
-        keys = short_kv_ref[h, 0]
-        probs, grad_scores = score_grads(keys, short_kv_ref[h, 1], queries, grads, short_aux_ref[h], seen)
-        put(h, 0, long, (pair_rows(dot_columns(keys, grad_scores)) * scale).T)
-        put(h, 1, long, dot(grad_scores, queries))
-        put(h, 2, long, dot(probs, grads))
-        queries, grads = head_pair(q_ref[me, h]), head_pair(do_ref[me, h])
-        keys = kv_ref[me, h, 0]
-        probs, grad_scores = score_grads(keys, kv_ref[me, h, 1], queries, grads, aux_ref[me, h], causal(long, long))
-        dq_ref[h] = dot_columns(keys, grad_scores)
-        dk_ref[h] = dot(grad_scores, queries)
-        dv_ref[h] = dot(probs, grads)
-        for block in range(n_dp - 1):
-
-            @pl.when(block < me)
-            def _():
-                keys = kv_ref[block, h, 0]
-                _, grad_scores = score_grads(keys, kv_ref[block, h, 1], queries, grads, aux_ref[me, h], None)
-                dq_ref[h] += dot_columns(keys, grad_scores)
-
-        put(h, 0, 0, (pair_rows(dq_ref[h]) * scale).T)
+    seen = short_seen(r["doc_row"][...], r["doc_col"][...])
+    queries, grads = head_pair(r["short_q"][h]), head_pair(r["short_do"][h])
+    keys = r["short_kv"][h, 0]
+    probs, grad_scores = score_grads(keys, r["short_kv"][h, 1], queries, grads, r["short_aux"][h], seen)
+    put(0, long, (pair_rows(dot_columns(keys, grad_scores)) * scale).T)
+    put(1, long, dot(grad_scores, queries))
+    put(2, long, dot(probs, grads))
+    queries, grads = head_pair(r["q"][me, h]), head_pair(r["do"][me, h])
+    own_keys, own_values = r["kv"][me, h, 0], r["kv"][me, h, 1]
+    probs, grad_scores = score_grads(own_keys, own_values, queries, grads, r["aux"][me, h], causal(long, long))
+    r["dq"][...] = dot_columns(own_keys, grad_scores)
+    r["dk"][...] = dot(grad_scores, queries)
+    r["dv"][...] = dot(probs, grads)
+    for block in range(n_dp - 1):
+
+        @pl.when(block < me)
+        def _():
+            keys = r["kv"][block, h, 0]
+            _, grad_scores = score_grads(keys, r["kv"][block, h, 1], queries, grads, r["aux"][me, h], None)
+            r["dq"][...] += dot_columns(keys, grad_scores)
+
+    put(0, 0, (pair_rows(r["dq"][...]) * scale).T)
+    do_spread.relay(h)
+    aux_spread.relay(h)
+
+    def use(block):
+        queries, grads = head_pair(r["q"][block, h]), head_pair(r["do"][block, h])
+        probs, grad_scores = score_grads(own_keys, own_values, queries, grads, r["aux"][block, h], None)
+        r["dk"][...] += dot(grad_scores, queries)
+        r["dv"][...] += dot(probs, grads)
+
+    aux_spread.each(h, lambda block: None)
+    do_spread.each(h, use)
+    put(1, 0, r["dk"][...])
+    put(2, 0, r["dv"][...])
+
+
+def back_scratch(n_dp, pairs, long, short):
+    return (
+        [
+            pltpu.VMEM((n_dp, pairs, long, 128), jnp.bfloat16),
+            pltpu.VMEM((n_dp, pairs, 8, long), jnp.float32),
+            pltpu.VMEM((pairs, short, 128), jnp.bfloat16),
+            pltpu.VMEM((pairs, 8, short), jnp.float32),
+            pltpu.VMEM((128, 2 * long), jnp.float32),
+            pltpu.VMEM((long, 128), jnp.float32),
+            pltpu.VMEM((long, 128), jnp.float32),
+        ]
+        + spread_sems(n_dp, pairs)
+        + spread_sems(n_dp, pairs)
+    )
+
+
+def lane_plan(n_dp, n_ex, rows, order):
+    dp_levels = [("dp", b) for b in range(n_dp.bit_length() - 1)]
+    ex_levels = n_ex.bit_length() - 1
+    halved, piece = [], rows
+    for level in ((0, 1), (1, 0))[order]:
+        if level < ex_levels and piece % 32 == 0:
+            halved.append(level)
+            piece //= 2
+    halves = [("half", b) for b in halved]
+    if order:
+        kinds = dp_levels[:1] + halves[:1] + dp_levels[1:] + halves[1:]
+    else:
+        kinds = dp_levels + halves
+    kinds += [("both", b) for b in range(ex_levels) if b not in halved]
+    kinds += [("back", b) for b in reversed(halved)]
+    return kinds, halved
+
+
+class Lane:
+    def __init__(self, n_dp, n_ex, rows, columns, order, refs):
+        self.rows, self.columns = rows, columns
+        self.kinds, self.halved = lane_plan(n_dp, n_ex, rows, order)
+        self.count = len(self.kinds)
+        moving = [k[0] != "back" for k in self.kinds]
+        self.send = [next(refs) if m else None for m in moving]
+        self.recv = [next(refs) if m else None for m in moving]
+        self.keep = [next(refs) if m else None for m in moving]
+        self.fin = next(refs)
+        self.send_sems = [next(refs) for _ in moving]
+        self.recv_sems = [next(refs) for _ in moving]
+        self.d, self.e = lax.axis_index("dp"), lax.axis_index("expert")
+
+    @staticmethod
+    def scratch(n_dp, n_ex, rows, columns, order):
+        kinds, halved = lane_plan(n_dp, n_ex, rows, order)
+        width, pieces, height, shapes = columns[1] - columns[0], n_dp, rows, []
+        for kind, _ in kinds:
+            if kind == "dp":
+                pieces //= 2
+            elif kind == "half":
+                height //= 2
+            if kind != "back":
+                shapes.append((pieces, height, width))
+        scratch = [pltpu.VMEM((2,) + s, jnp.bfloat16) for s in shapes]
+        scratch += [pltpu.VMEM((4,) + s, jnp.bfloat16) for s in shapes]
+        scratch += [pltpu.VMEM((2,) + s, jnp.float32) for s in shapes]
+        scratch += [pltpu.VMEM((len(halved) + 3, rows, width), jnp.bfloat16)]
+        return scratch + [pltpu.SemaphoreType.DMA((4,)) for _ in kinds] * 2
+
+    def peer(self, kind, level):
+        return (flip(self.d, level), self.e) if kind == "dp" else (self.d, flip(self.e, level))
+
+    def kept_rows(self, depth):
+        start = 0
+        for i, level in enumerate(self.halved[:depth]):
+            start = start + bit_of(self.e, level) * (self.rows >> (i + 1))
+        return start
+
+    def copy_of(self, s, c):
+        kind, level = self.kinds[s]
+        slot, place = lax.rem(c, 2), lax.rem(c, 4)
+        if kind == "back":
+            depth = self.halved.index(level) + 1
+            span = self.rows >> depth
+            at = pl.ds(pl.multiple_of(self.kept_rows(depth), span), span)
+            src = self.fin.at[lax.rem(c, len(self.halved) + 3), at]
+            dst = src
+        else:
+            src, dst = self.send[s].at[slot], self.recv[s].at[place]
+        return pltpu.make_async_remote_copy(
+            src_ref=src,
+            dst_ref=dst,
+            send_sem=self.send_sems[s].at[place],
+            recv_sem=self.recv_sems[s].at[place],
+            device_id=self.peer(kind, level),
+            device_id_type=MESH,
+        )
+
+    def arrive(self, s, c):
+        self.copy_of(s, c).wait()
+        slot, place = lax.rem(c, 2), lax.rem(c, 4)
+        if self.kinds[s][0] == "back":
+            return None
+        return [
+            self.keep[s][slot, i] + self.recv[s][place, i].astype(jnp.float32) for i in range(self.keep[s].shape[1])
+        ]
+
+    def leave(self, s, c, values):
+        kind, level = self.kinds[s]
+        slot = lax.rem(c, 2)
+        kept = None
+        if kind == "dp":
+            sent, kept = values[1::2], values[0::2]
+        elif kind == "half":
+            half = values[0].shape[0] // 2
+            own = bit_of(self.e, level)
+            sent = [jnp.where(own == 0, v[half:], v[:half]) for v in values]
+            kept = [jnp.where(own == 0, v[:half], v[half:]) for v in values]
+        elif kind == "both":
+            sent = values
+            kept = [v.astype(jnp.bfloat16).astype(jnp.float32) for v in values]
+        elif values is not None:
+            span = values[0].shape[0]
+            at = pl.ds(pl.multiple_of(self.kept_rows(len(self.halved)), span), span)
+            self.fin[lax.rem(c, len(self.halved) + 3), at] = values[0].astype(jnp.bfloat16)
+        if kept is not None:
+            for i, v in enumerate(sent):
+                self.send[s][slot, i] = v.astype(jnp.bfloat16)
+        self.copy_of(s, c).start()
+        if kept is not None:
+            for i, v in enumerate(kept):
+                self.keep[s][slot, i] = v
+
+    def final(self, c):
+        values = self.arrive(self.count - 1, c)
+        if values is None:
+            return self.fin[lax.rem(c, len(self.halved) + 3)]
+        return values[0].astype(jnp.bfloat16)
+
+
+class Reduction:
+    def __init__(self, n_dp, n_ex, rows, groups, lanes, refs):
+        self.n_dp, self.rows, self.groups = n_dp, rows, groups
+        refs = iter(refs)
+        self.lanes = [Lane(n_dp, n_ex, rows, columns, order, refs) for columns, order in lanes]
+        self.stage_ref, self.stage_sem, self.out = next(refs), next(refs), next(refs)
+        self.count = self.lanes[0].count
+        self.chunks = sum(g[0] for g in groups)
+        self.firsts = [sum(g[0] for g in groups[:i]) for i in range(len(groups))]
+        self.ticks = self.chunks + self.count
+        self.d = lax.axis_index("dp")
+        self.peer = self.lanes[0].peer
+
+    @staticmethod
+    def scratch(n_dp, n_ex, rows, width, lanes):
+        scratch = []
+        for columns, order in lanes:
+            scratch += Lane.scratch(n_dp, n_ex, rows, columns, order)
+        return scratch + [pltpu.VMEM((2, rows, width), jnp.bfloat16), pltpu.SemaphoreType.DMA((2,))]
+
+    def out_copy(self, c):
+        slot = lax.rem(c, 2)
+        return pltpu.make_async_copy(self.stage_ref.at[slot], self.out.at[c], self.stage_sem.at[slot])
+
+    def first(self, g, c):
+        _, piece, factor = self.groups[g]
+        j = c - self.firsts[g]
+        dy = factor(j)
+        slot = lax.rem(c, 2)
+        levels = self.n_dp.bit_length() - 1
+        half = self.n_dp // 2
+
+        def products(odd):
+            parts = [piece(j, partner_index(self.d, 2 * i + odd, levels)) for i in range(half)]
+            return dot(jnp.concatenate(parts, axis=0), dy)
+
+        value = products(1)
+        for lane in self.lanes:
+            for i in range(half):
+                part = value[i * self.rows : (i + 1) * self.rows, slice(*lane.columns)]
+                lane.send[0][slot, i] = part.astype(jnp.bfloat16)
+            lane.copy_of(0, c).start()
+        value = products(0)
+        for lane in self.lanes:
+            for i in range(half):
+                lane.keep[0][slot, i] = value[i * self.rows : (i + 1) * self.rows, slice(*lane.columns)]
+
+    def last(self, c):
+        slot = lax.rem(c, 2)
+
+        @pl.when(c >= 2)
+        def _():
+            self.out_copy(c - 2).wait()
+
+        for lane in self.lanes:
+            self.stage_ref[slot, :, slice(*lane.columns)] = lane.final(c)
+        self.out_copy(c).start()
+
+    def tick(self, t, low, high):
+        for s in range(self.count + 1):
+            if high - s <= 0 or low - s >= self.chunks:
+                continue
+            c = t - s
+            if s > 0:
+
+                @pl.when((c >= 0) & (c < self.chunks))
+                def _(s=s, c=c):
+                    if s < self.count:
+                        for lane in self.lanes:
+                            lane.leave(s, c, lane.arrive(s - 1, c))
+                    else:
+                        self.last(c)
+
+                continue
+            for g, (size, _, _) in enumerate(self.groups):
+                begin, end = self.firsts[g], self.firsts[g] + size
+                if high <= begin or low >= end:
+                    continue
+
+                @pl.when((c >= begin) & (c < end))
+                def _(g=g):
+                    self.first(g, c)
+
+    def finish(self):
+        for c in range(max(0, self.chunks - 2), self.chunks):
+            self.out_copy(c).wait()
+
+
+def dense_lanes(width):
+    cut = width // 768 * 640
+    return [((0, cut), 0), ((cut, width), 1)]
+
+
+def attend_back_kernel(n_dp, n_ex, *refs):
+    (up_ref, x_ref, gain_ref, w_in_ref, w_out_ref, doc_row_ref, doc_col_ref), rest = refs[:7], refs[7:]
+    (context_ref, kv_ref, q_ref, short_kv_ref, short_q_ref, lse_ref), rest = rest[:6], rest[6:]
+    (assign_ref, gate_ref, stream_ref, result_ref), rest = rest[:4], rest[4:]
+    (rows_t_ref, hidden_ref, active_t_ref, back_ref), rest = rest[:4], rest[4:]
+    (up_next_ref, up_low_ref, mixed_ref, sums_ref, output_ref, chunks_ref), rest = rest[:6], rest[6:]
+    (do_ref, aux_ref, short_do_ref, short_aux_ref, dq_ref, dk_ref, dv_ref), rest = rest[:7], rest[7:]
+    (do_far, do_near, do_recv, aux_far, aux_near, aux_recv), rest = rest[:6], rest[6:]
+    (home_ref, result_send_sem, result_recv_sem), rest = rest[:3], rest[3:]
+    links = Links(n_dp)
+    me = links.me
+    pairs, long, width = kv_ref.shape[1], kv_ref.shape[3], x_ref.shape[1]
+    up = up_ref[...]
+    up_low = up.astype(jnp.bfloat16)
+    up_low_ref[...] = up_low
+    grad_context = dot_rows(up_low, w_out_ref[...]).astype(jnp.bfloat16)
+    share_context(context_ref, lse_ref, grad_context, do_ref, aux_ref, short_do_ref, short_aux_ref, me, long)
+    blocks = hidden_ref.shape[1] // width
+    groups = [
+        (blocks, lambda j, q: rows_t_ref[q, 0], lambda j: hidden_ref[:, pl.ds(pl.multiple_of(j * width, width), width)]),
+        (blocks, lambda j, q: active_t_ref[q, j], lambda j: back_ref[...]),
+    ]
+    red = Reduction(n_dp, 1, width // n_dp, groups, [((0, width), 0)], list(rest) + [chunks_ref])
+    greet(links.peers() + across_peers(n_ex))
+    do_spread = Spread(links, lambda b, p: do_ref.at[b, p], pairs, False, do_far, do_near, do_recv)
+    aux_spread = Spread(links, lambda b, p: aux_ref.at[b, p], pairs, False, aux_far, aux_near, aux_recv)
+    for h in range(pairs):
+        do_spread.send(h)
+        aux_spread.send(h)
+    result_across = Across(n_ex, result_ref, home_ref, result_send_sem, result_recv_sem)
+    result_across.start_all()
+    home_ref[links.expert] = result_ref[links.expert]
+    red.tick(0, 0, 1)
+    sequence = dict(
+        doc_row=doc_row_ref, doc_col=doc_col_ref, kv=kv_ref, q=q_ref, short_kv=short_kv_ref, short_q=short_q_ref,
+        do=do_ref, aux=aux_ref, short_do=short_do_ref, short_aux=short_aux_ref, dq=dq_ref, dk=dk_ref, dv=dv_ref,
+        mixed=mixed_ref,
+    )
+
+    def pair(h, _):
+        attend_back_pair(n_dp, me, width, sequence, do_spread, aux_spread, h)
+        red.tick(1 + h, 1, 1 + pairs)
         return 0
 
-    lax.fori_loop(0, pairs, own_part, 0)
-
-    def other_part(h, _):
-        do_spread.relay(h)
-        aux_spread.relay(h)
-        keys, values = kv_ref[me, h, 0], kv_ref[me, h, 1]
-
-        def use(block):
-            queries, grads = head_pair(q_ref[block, h]), head_pair(do_ref[block, h])
-            probs, grad_scores = score_grads(keys, values, queries, grads, aux_ref[block, h], None)
-            dk_ref[h] += dot(grad_scores, queries)
-            dv_ref[h] += dot(probs, grads)
-
-        aux_spread.each(h, lambda block: None)
-        do_spread.each(h, use)
-        put(h, 1, 0, dk_ref[h])
-        put(h, 2, 0, dv_ref[h])
-        return 0
-
-    lax.fori_loop(0, pairs, other_part, 0)
+    lax.fori_loop(0, pairs, pair, 0)
     grad_normed = dot_rows(mixed_ref[...], w_in_ref[...])
-    x = x_ref[...]
-    center = x - jnp.mean(x, axis=-1, keepdims=True)
-    inverse = lax.rsqrt(jnp.mean(center * center, axis=-1, keepdims=True) + epsilon)
-    unit = center * inverse
-    scaled = grad_normed * gain_ref[...]
-    inner = (
-        scaled - jnp.mean(scaled, axis=-1, keepdims=True) - unit * jnp.mean(scaled * unit, axis=-1, keepdims=True)
-    )
-    up_next_ref[...] = up + inverse * inner
+    unit, inverse = norm_parts(x_ref[...])
+    up_next_ref[...] = up + norm_back(unit, inverse, gain_ref[...], grad_normed)
     sums_ref[0:1] = jnp.sum(grad_normed * unit, axis=0, keepdims=True)
     sums_ref[1:2] = jnp.sum(grad_normed, axis=0, keepdims=True)
+    red.tick(1 + pairs, 1 + pairs, 2 + pairs)
+    result_across.wait_all()
+    dispatch = dispatch_of(assign_ref[...], n_ex)
+    result = dot_columns(dispatch, home_ref[...].reshape(dispatch.shape[0], width))
+    gate = jnp.broadcast_to(gate_ref[...], (128, gate_ref.shape[1])).T[:, 0:1]
+    output_ref[...] = (stream_ref[...] + gate * result).astype(jnp.bfloat16)
+
+    def rest_tick(t, _):
+        red.tick(t, 2 + pairs, red.ticks)
+        return 0
+
+    lax.fori_loop(2 + pairs, red.ticks, rest_tick, 0)
+    red.finish()
     for h in range(pairs):
         do_spread.sent(h)
         aux_spread.sent(h)
-    if inputs > 13:
-        result_across.wait_all()
-        dispatch = dispatch_of(assign_ref[...], n_ex)
-        result = dot_columns(dispatch, home_ref[...].reshape(dispatch.shape[0], width))
-        gate = jnp.broadcast_to(gate_ref[...], (128, gate_ref.shape[1])).T[:, 0:1]
-        output_ref[...] = (stream_ref[...] + gate * result).astype(jnp.bfloat16)
 
 
 def attention_backward(
-    n_dp, n_ex, collective_id, upstream, stream, norm_gain, weight_in, weight_out, doc_row, doc_col, kept, routing=()
+    n_dp, n_ex, collective_id, upstream, stream, norm_gain, weight_in, weight_out, doc_row, doc_col, kept, routing
 ):
     rows, width = stream.shape
     long, short, pairs = LONG_DEV, rows - LONG_DEV, width // 128
@@ -1117,33 +1096,252 @@
         jax.ShapeDtypeStruct((rows, width), low),
         jax.ShapeDtypeStruct((rows, 3 * width), low),
         jax.ShapeDtypeStruct((2, width), jnp.float32),
+        jax.ShapeDtypeStruct((rows, width), low),
+        jax.ShapeDtypeStruct((2 * (routing[5].shape[1] // width), width // n_dp, width), low),
     ]
-    scratch = [
-        pltpu.VMEM((n_dp, pairs, long, 128), low),
-        pltpu.VMEM((n_dp, pairs, 8, long), jnp.float32),
-        pltpu.VMEM((pairs, short, 128), low),
-        pltpu.VMEM((pairs, 8, short), jnp.float32),
-        pltpu.VMEM((pairs, 128, 2 * long), jnp.float32),
-        pltpu.VMEM((pairs, long, 128), jnp.float32),
-        pltpu.VMEM((pairs, long, 128), jnp.float32),
-    ]
-    scratch += spread_sems(n_dp, pairs) + spread_sems(n_dp, pairs)
-    if routing:
-        outs += [jax.ShapeDtypeStruct((rows, width), low)]
-        scratch += [pltpu.VMEM(routing[3].shape, low)] + [pltpu.SemaphoreType.DMA((n_ex,))] * 2
+    scratch = back_scratch(n_dp, pairs, long, short)
+    scratch += [pltpu.VMEM(routing[3].shape, low)] + [pltpu.SemaphoreType.DMA((n_ex,))] * 2
+    scratch += Reduction.scratch(n_dp, 1, width // n_dp, width, [((0, width), 0)])
     inputs = (upstream, stream, norm_gain, weight_in, weight_out, doc_row, doc_col) + tuple(kept) + tuple(routing)
     vmem = pl.BlockSpec(memory_space=pltpu.VMEM)
     return pl.pallas_call(
-        functools.partial(attend_back_kernel, n_dp, n_ex, len(inputs)),
+        functools.partial(attend_back_kernel, n_dp, n_ex),
         out_shape=outs,
         in_specs=[vmem] * len(inputs),
-        out_specs=[vmem] * len(outs),
+        out_specs=[vmem] * (len(outs) - 1) + [pl.BlockSpec(memory_space=pl.ANY)],
         scratch_shapes=scratch,
         compiler_params=pltpu.CompilerParams(
             collective_id=collective_id, has_side_effects=True, vmem_limit_bytes=56 * 1024 * 1024
         ),
         name="attention_backward",
     )(*inputs)
+
+
+def tail_kernel(n_dp, n_ex, names, staged, *refs):
+    r = dict(zip(names, refs))
+    extra = iter(refs[len(names) :])
+    loads = {}
+    for name in staged:
+        buffer, sem = next(extra), next(extra)
+        loads[name] = pltpu.make_async_copy(r[name], buffer, sem)
+        r[name] = buffer
+    weights_in, weights_out, slopes, weight_sem = (next(extra) for _ in range(4))
+    first_sem = next(extra)
+    up_ref, acc_ref, dense_low_ref, dense_hidden_ref, first_low_ref, mixed_ref = (next(extra) for _ in range(6))
+    do_ref, aux_ref, short_do_ref, short_aux_ref, dq_ref, dk_ref, dv_ref = (next(extra) for _ in range(7))
+    do_far, do_near, do_recv, aux_far, aux_near, aux_recv = (next(extra) for _ in range(6))
+    small_send, small_recv, small_send_sem, small_recv_sem = (next(extra) for _ in range(4))
+    links = Links(n_dp)
+    me = links.me
+    width = up_ref.shape[1]
+    rows = width // n_dp
+    pairs, long = r["kv"].shape[1], r["kv"].shape[3]
+    blocks = r["dense_in"].shape[1] // width
+    per_in = mixed_ref.shape[1] // width
+
+    def block_loads(i):
+        slot = lax.rem(i, 2)
+        at = pl.ds(pl.multiple_of(i * width, width), width)
+        return [
+            pltpu.make_async_copy(r["dense_out"].at[at, :], weights_out.at[slot], weight_sem.at[slot, 0]),
+            pltpu.make_async_copy(r["dense_in"].at[:, at], weights_in.at[slot], weight_sem.at[slot, 1]),
+            pltpu.make_async_copy(r["slope"].at[:, at], slopes.at[slot], weight_sem.at[slot, 2]),
+        ]
+
+    for i in range(min(2, blocks)):
+        for load in block_loads(i):
+            load.start()
+    for name in staged:
+        loads[name].start()
+    free, busy = blocks % 2, (blocks - 1) % 2
+    out_load = pltpu.make_async_copy(r["attn_out"].at[0], weights_out.at[free], first_sem.at[0])
+    thirds = [weights_in.at[free], weights_in.at[busy], weights_out.at[busy]]
+    in_loads = [
+        pltpu.make_async_copy(r["attn_in"].at[0, :, pl.ds(i * width, width)], third, first_sem.at[1 + i])
+        for i, third in enumerate(thirds)
+    ]
+
+    def columns(ref):
+        return lambda j: ref[:, pl.ds(pl.multiple_of(j * width, width), width)]
+
+    def one(ref):
+        return lambda j, q: ref[q, 0]
+
+    groups = [
+        (1, one(r["second_context_t"]), columns(r["second_low"])),
+        (per_in, one(r["second_normed_t"]), columns(r["second_mixed"])),
+        (blocks, lambda j, q: r["active_t"][q, j], lambda j: dense_low_ref[...]),
+        (blocks, one(r["dense_normed_t"]), columns(dense_hidden_ref)),
+        (1, one(r["first_context_t"]), columns(first_low_ref)),
+        (per_in, one(r["first_normed_t"]), columns(mixed_ref)),
+    ]
+    red_refs = list(extra) + [r["chunks"]]
+    red = Reduction(n_dp, n_ex, rows, groups, dense_lanes(width), red_refs)
+    levels = [("dp", b) for b in range(n_dp.bit_length() - 1)] + [("ex", b) for b in range(n_ex.bit_length() - 1)]
+    greet([red.peer(*level) for level in levels] + (links.peers()[1:] if links.chips > 2 else []))
+
+    up = r["up"][...]
+    dense_low_ref[...] = up.astype(jnp.bfloat16)
+    acc_ref[...] = jnp.zeros_like(acc_ref)
+    for name in ("second_context_t", "second_low", "second_normed_t", "second_mixed"):
+        loads[name].wait()
+
+    def dense(i, _):
+        slot = lax.rem(i, 2)
+        for load in block_loads(i):
+            load.wait()
+        grad = dot_rows(dense_low_ref[...], weights_out[slot]) * slopes[slot].astype(jnp.float32)
+        grad = grad.astype(jnp.bfloat16)
+        dense_hidden_ref[:, pl.ds(pl.multiple_of(i * width, width), width)] = grad
+        acc_ref[...] += dot_rows(grad, weights_in[slot])
+
+        @pl.when(i + 2 < blocks)
+        def _():
+            for load in block_loads(i + 2):
+                load.start()
+
+        @pl.when(i == blocks - 2)
+        def _():
+            out_load.start()
+            in_loads[0].start()
+
+        @pl.when(lax.rem(i, 2) == 1)
+        def _():
+            red.tick(i // 2, 0, 2)
+
+        return 0
+
+    lax.fori_loop(0, blocks, dense, 0)
+    for load in in_loads[1:]:
+        load.start()
+    for name in staged:
+        if not name.startswith("second"):
+            loads[name].wait()
+    unit, inverse = norm_parts(r["dense_x"][...])
+    grad_normed = acc_ref[...]
+    up = up + norm_back(unit, inverse, r["dense_gain"][...], grad_normed)
+    up_ref[...] = up
+    small_send[0] = r["small"][...]
+    small_send[0, 1:2] = jnp.sum(grad_normed * unit, axis=0, keepdims=True)
+    small_send[0, 5:6] = jnp.sum(grad_normed, axis=0, keepdims=True)
+    at_tick = blocks // 2
+
+    scale = HEAD_DIM ** (-0.5)
+    up_low = up.astype(jnp.bfloat16)
+    first_low_ref[...] = up_low
+    out_load.wait()
+    grad_context = dot_rows(up_low, weights_out[free]).astype(jnp.bfloat16)
+    share_context(r["context"], r["lse"], grad_context, do_ref, aux_ref, short_do_ref, short_aux_ref, me, long)
+    do_spread = Spread(links, lambda b, p: do_ref.at[b, p], pairs, False, do_far, do_near, do_recv)
+    aux_spread = Spread(links, lambda b, p: aux_ref.at[b, p], pairs, False, aux_far, aux_near, aux_recv)
+    for h in range(pairs):
+        do_spread.send(h)
+        aux_spread.send(h)
+    red.tick(at_tick, at_tick, at_tick + 1)
+    at_tick += 1
+    sequence = dict(
+        doc_row=r["doc_row"], doc_col=r["doc_col"], kv=r["kv"], q=r["q"], short_kv=r["short_kv"], short_q=r["short_q"],
+        do=do_ref, aux=aux_ref, short_do=short_do_ref, short_aux=short_aux_ref, dq=dq_ref, dk=dk_ref, dv=dv_ref,
+        mixed=mixed_ref,
+    )
+
+    def pair(h, _):
+        attend_back_pair(n_dp, me, width, sequence, do_spread, aux_spread, h)
+        red.tick(at_tick + h, at_tick, at_tick + pairs)
+        return 0
+
+    lax.fori_loop(0, pairs, pair, 0)
+    at_tick += pairs
+    grad_normed = jnp.zeros((up_ref.shape[0], width), jnp.float32)
+    for i, third in enumerate(thirds):
+        in_loads[i].wait()
+        grad_normed = grad_normed + dot_rows(mixed_ref[:, i * width : (i + 1) * width], third[...])
+    unit, inverse = norm_parts(r["first_x"][...].astype(jnp.float32))
+    r["grad_tokens"][...] = (
+        up_ref[...] + norm_back(unit, inverse, r["first_gain"][...], grad_normed)
+    ).astype(jnp.bfloat16)
+    small_send[0, 0:1] = jnp.sum(grad_normed * unit, axis=0, keepdims=True)
+    small_send[0, 4:5] = jnp.sum(grad_normed, axis=0, keepdims=True)
+
+    def small_copy(i):
+        return pltpu.make_async_remote_copy(
+            src_ref=small_send.at[i],
+            dst_ref=small_recv.at[i],
+            send_sem=small_send_sem.at[i],
+            recv_sem=small_recv_sem.at[i],
+            device_id=red.peer(*levels[i]),
+            device_id_type=MESH,
+        )
+
+    small_copy(0).start()
+
+    def rest(t, _):
+        red.tick(t, at_tick, red.ticks)
+        for i in range(1, len(levels) + 1):
+
+            @pl.when(t == at_tick + i)
+            def _(i=i):
+                small_copy(i - 1).wait()
+                value = small_send[i - 1] + small_recv[i - 1]
+                if i < len(levels):
+                    small_send[i] = value
+                    small_copy(i).start()
+                else:
+                    r["small_sum"][...] = value
+
+        return 0
+
+    lax.fori_loop(at_tick, red.ticks, rest, 0)
+    red.finish()
+    for h in range(pairs):
+        do_spread.sent(h)
+        aux_spread.sent(h)
+
+
+def tail(n_dp, n_ex, collective_id, arrays):
+    staged = (
+        "second_context_t", "second_low", "second_normed_t", "second_mixed", "active_t", "dense_normed_t", "dense_x",
+        "kv", "q", "short_kv", "short_q", "context", "first_x", "first_context_t", "first_normed_t",
+    )
+    far = staged + ("dense_in", "dense_out", "slope", "attn_in", "attn_out")
+    low, wide = jnp.bfloat16, jnp.float32
+    tokens, width = arrays["up"].shape
+    hidden = arrays["dense_in"].shape[1]
+    mixed = arrays["attn_in"].shape[2]
+    rows = width // n_dp
+    long, short, pairs = LONG_DEV, tokens - LONG_DEV, width // 128
+    chunks = 2 * (hidden // width) + 2 * (1 + mixed // width)
+    small = arrays["small"].shape
+    outs = dict(
+        chunks=jax.ShapeDtypeStruct((chunks, rows, width), low),
+        grad_tokens=jax.ShapeDtypeStruct((tokens, width), low),
+        small_sum=jax.ShapeDtypeStruct(small, wide),
+    )
+    scratch = []
+    for name in staged:
+        scratch += [pltpu.VMEM(arrays[name].shape, arrays[name].dtype), pltpu.SemaphoreType.DMA]
+    scratch += [pltpu.VMEM((2, width, width), low)] * 2
+    scratch += [pltpu.VMEM((2, tokens, width), low), pltpu.SemaphoreType.DMA((2, 3))]
+    scratch += [pltpu.SemaphoreType.DMA((4,))]
+    scratch += [pltpu.VMEM((tokens, width), wide)] * 2
+    scratch += [pltpu.VMEM((tokens, n), low) for n in (width, hidden, width, mixed)]
+    scratch += back_scratch(n_dp, pairs, long, short)
+    hops = (n_dp * n_ex).bit_length() - 1
+    scratch += [pltpu.VMEM((hops,) + small, wide)] * 2 + [pltpu.SemaphoreType.DMA((hops,))] * 2
+    scratch += Reduction.scratch(n_dp, n_ex, rows, width, dense_lanes(width))
+    vmem, anywhere = pl.BlockSpec(memory_space=pltpu.VMEM), pl.BlockSpec(memory_space=pl.ANY)
+    names = tuple(arrays) + tuple(outs)
+    return pl.pallas_call(
+        functools.partial(tail_kernel, n_dp, n_ex, names, staged),
+        out_shape=list(outs.values()),
+        in_specs=[anywhere if name in far else vmem for name in arrays],
+        out_specs=[anywhere if name == "chunks" else vmem for name in outs],
+        scratch_shapes=scratch,
+        compiler_params=pltpu.CompilerParams(
+            collective_id=collective_id, has_side_effects=True, vmem_limit_bytes=61 * 1024 * 1024
+        ),
+        name="tail",
+    )(*arrays.values())
 
 
 def shards(
@@ -1180,58 +1378,71 @@
         (assign_row, cotangent[0]),
     )
     (
-        upstream, fourth_sums, router_grad, expert_rows, expert_back, expert_active, expert_hidden, result, gate, stats
+        upstream, fourth_sums, router_grad, rows_t, expert_back, expert_active_t, expert_hidden, result, gate, stats
     ) = mixture(
         n_dp, n_ex, 6, stream_three, gains[3:4], shifts[3:4], router.T, assign_row, cotangent[0], far_cot,
         expert_in[0], expert_out[0],
     )
     everyone = row_count * n_dp * n_ex
     balance = n_ex * jnp.sum((stats[:, 0] / everyone - 1.0 / n_ex) * (stats[:, 1] / everyone))
-    expert_slots = expert_active.shape[0]
-    expert_in_grad = jnp.einsum(
-        "sd,sf->df", expert_rows.reshape(expert_slots, -1), expert_hidden, preferred_element_type=jnp.float32
-    )[None]
-    expert_out_grad = jnp.einsum(
-        "sf,sd->fd", expert_active, expert_back.reshape(expert_slots, -1), preferred_element_type=jnp.float32
-    )[None]
-    upstream, second_low, second_mixed, second_sums, output = attention_backward(
-        n_dp, n_ex, 4, upstream, stream_two, gains[2:3], weights_in[1], weights_out[1], doc_row, doc_col,
-        kept_three[1:2] + kept_three[3:], (assign_row, gate, stream_three, result),
-    )
-    output = output[None]
-    upstream, dense_low, dense_hidden, dense_sums = ffn_backward(
-        upstream, stream_one, gains[1:2], ffn_in, ffn_out, slope
-    )
-    upstream, first_low, first_mixed, first_sums = attention_backward(
-        n_dp, n_ex, 5, upstream, stream_first, gains[0:1], weights_in[0], weights_out[0], doc_row, doc_col,
-        kept_one[1:2] + kept_one[3:],
-    )
-    grad_tokens = upstream.astype(jnp.bfloat16)[None]
     model_width = tokens.shape[2]
     rows = model_width // n_dp
+    expert_factors = (
+        rows_t.reshape(n_dp, 1, rows, -1),
+        expert_hidden,
+        expert_active_t.reshape(n_dp, -1, rows, expert_hidden.shape[0]),
+        expert_back.reshape(-1, model_width),
+    )
+    upstream, second_low, second_mixed, second_sums, output, expert_chunks = attention_backward(
+        n_dp, n_ex, 4, upstream, stream_two, gains[2:3], weights_in[1], weights_out[1], doc_row, doc_col,
+        kept_three[1:2] + kept_three[3:], (assign_row, gate, stream_three, result) + expert_factors,
+    )
+    output = output[None]
 
     def blocks_of(rows_t):
         return rows_t.reshape(n_dp, -1, rows, row_count)
 
-    pairs = [
-        (blocks_of(kept_three[2]), second_low),
-        (blocks_of(kept_three[0]), second_mixed),
-        (blocks_of(active_t), dense_low),
-        (blocks_of(dense_normed_t), dense_hidden),
-        (blocks_of(kept_one[2]), first_low),
-        (blocks_of(kept_one[0]), first_mixed),
-    ]
+    none = jnp.zeros((2, model_width), jnp.float32)
     small = jnp.concatenate(
-        [
-            first_sums[0:1], dense_sums[0:1], second_sums[0:1], fourth_sums[0:1],
-            first_sums[1:2], dense_sums[1:2], second_sums[1:2], fourth_sums[1:2],
-            router_grad,
-        ],
-        axis=0,
-    )
-    chunks, small = reduce_grads(n_dp, n_ex, pairs, small, model_width)
-    attn_in_sum, attn_out_sum, ffn_in_sum, ffn_out_sum = unpack(
-        chunks, attn_in.shape[2] // model_width, ffn_in.shape[1] // model_width
+        [none, second_sums[0:1], fourth_sums[0:1], none, second_sums[1:2], fourth_sums[1:2], router_grad], axis=0
+    )
+    chunks, grad_tokens, small = tail(
+        n_dp,
+        n_ex,
+        5,
+        dict(
+            up=upstream,
+            dense_x=stream_one,
+            dense_gain=gains[1:2],
+            first_gain=gains[0:1],
+            dense_in=ffn_in,
+            dense_out=ffn_out,
+            slope=slope,
+            first_x=tokens[0],
+            attn_in=weights_in,
+            attn_out=weights_out,
+            doc_row=doc_row,
+            doc_col=doc_col,
+            context=kept_one[1],
+            kv=kept_one[3],
+            q=kept_one[4],
+            short_kv=kept_one[5],
+            short_q=kept_one[6],
+            lse=kept_one[7],
+            second_context_t=blocks_of(kept_three[2]),
+            second_normed_t=blocks_of(kept_three[0]),
+            active_t=blocks_of(active_t),
+            dense_normed_t=blocks_of(dense_normed_t),
+            first_context_t=blocks_of(kept_one[2]),
+            first_normed_t=blocks_of(kept_one[0]),
+            second_low=second_low,
+            second_mixed=second_mixed,
+            small=small,
+        ),
+    )
+    grad_tokens = grad_tokens[None]
+    attn_in_sum, attn_out_sum, ffn_in_sum, ffn_out_sum, expert_in_sum, expert_out_sum = unpack(
+        chunks, expert_chunks, attn_in.shape[2] // model_width, ffn_in.shape[1] // model_width
     )
     small = lax.dynamic_slice_in_dim(small, lax.axis_index("dp") * rows, rows, 1).T
     summed = [
@@ -1243,14 +1454,6 @@
         small[:, :4],
         small[:, 4:8],
     ]
-    expert_in_sum, expert_out_sum = (
-        lax.psum_scatter(
-            expert_in_grad.astype(jnp.bfloat16), "dp", scatter_dimension=1, tiled=True
-        ).astype(jnp.float32),
-        lax.psum_scatter(
-            expert_out_grad.astype(jnp.bfloat16), "dp", scatter_dimension=1, tiled=True
-        ).astype(jnp.float32),
-    )
     return (
         output,
         balance,
@@ -1262,8 +1465,8 @@
         summed[2],
         summed[3],
         summed[4],
-        expert_in_sum,
-        expert_out_sum,
+        expert_in_sum[None],
+        expert_out_sum.reshape(1, -1, model_width),
     )
 
 

time: 443 us -> 398 us (0.90)
  matrix products: 13.7 us -> 0 us
  between operations: 16.4 us -> 3.03 us
  local copies, waits for them, and re-layouts: 37.3 us -> 27.3 us
  other arithmetic: 9.44 us -> 1.66 us
    dot_general x2 -> x0, matrix products: 13.7 us -> none  [the longest x1 6.96 us: shards(): jnp.einsum('sd,sf->df', expert_rows.reshape(expert_slots, -1), expert_hid...]
    unnamed x91 -> x76, local copies, waits for them, and re-layouts: 25.3 us -> 16.8 us
    convert_element_type x2 -> x0, other arithmetic: 5.84 us -> none  [shards(): expert_in_sum, expert_out_sum = (lax.psum_scatter(expert_in_grad.astype(j...]
    pallas_call x4 -> x2, Pallas kernels: 229 us -> 227 us  [the longest x1 146 us: tail(): pl.pallas_call(functools.partial(tail_kernel, n_dp, n_ex, names, staged),...]
  transfers between devices with their start and end apart: 2 -> 0, of which waited for: 0 -> 0; matrix products, arithmetic and copies ran while one was open for 4% -> 0% of each run, Pallas kernels for 53% -> 0%
where the time goes in v4:
time: 398 us; the launch traced here: 394 us
  Pallas kernels  362 us (91%)
  local copies, waits for them, and re-layouts  27.3 us (7%)
    pallas_call x1, Pallas kernels, tail(): pl.pallas_call(functools.partial(tail_kernel, n_dp, n_ex, names, staged),...  146 us
    pallas_call x1, Pallas kernels, attention_backward(): pl.pallas_call(functools.partial(attend_back_kernel, n_dp, n_ex), out_sha...  80.3 us
    pallas_call x1, Pallas kernels, mixture(): pl.pallas_call(functools.partial(mixture_kernel, n_dp, n_ex), out_shape=o...  63.7 us
    pallas_call x2, Pallas kernels, attention_forward(): pl.pallas_call(functools.partial(attend_kernel, n_dp, n_ex, len(inputs)),...  56.3 us
    unnamed x76, local copies, waits for them, and re-layouts  16.8 us
    pallas_call x1, Pallas kernels, ffn_forward(): pl.pallas_call(ffn_kernel, grid=(hidden // width,), out_shape=[jax.ShapeD...  9.74 us

profile of v4, /device:TPU:0, one launch (start us, length us, event | category | flops | bytes accessed | tf_op | source)
XLA Modules:
  0.0 393.9 jit_solution(10768072636508003640)
XLA Ops:
  0.6 1.5 fusion.1
  2.1 0.0 copy-start.22
  2.1 0.8 reduce-window.8
  3.0 0.1 convert_reduce_fusion
  3.0 0.1 copy.33.refs_6_.refs_11_
  3.2 0.0 copy-start.29
  3.2 4.0 %copy.39 = bf16[768,2,2304]{2,0,1:T(8,128)(2,1)S(1)} copy(bf16[768,2,2304]{2,1,0:T(2,128)(2,1)} %param.18) | data formatting | bytes 14155776 | tf_op args[5]
  7.2 0.0 copy-start.27
  7.2 0.0 copy-done.29
  7.2 0.3 copy.40
  7.5 0.0 copy-start.28
  7.5 3.8 slice_bitcast_fusion
  11.3 1.0 copy-done.27
  12.3 0.7 copy-done.28
  13.1 1.2 slice_bitcast_fusion.2
  14.2 0.0 copy-done.30
  14.2 0.1 bitcast_convert_fusion.refs_0_
  14.3 0.0 copy-done.20
  14.3 26.1 %attention_forward.2 = (f32[384,768]{1,0:T(8,128)S(1)}, bf16[768,384]{1,0:T(8,128)(2,1)S(1)}, bf16[384,768]{1,0:T(8,128)(2,1)S(1)}, bf16[768,384]{1,0:T(8,128)(2...) custom-call(f32[384,768]{1,0:T(8,128)S(1)} %bitcast_convert_fusion.r, ...), custom_call_target="tpu_custom_call" | custom-call | tf_op jit(solution)/shard_map/attention_forward/pallas_call | solution.py:702
  40.4 0.0 copy-start.11
  40.4 0.8 copy-done.11
  41.2 0.0 copy-start.18
  41.2 0.0 copy-start.23
  41.3 0.0 copy-done.21
  41.3 0.0 copy-start.6
  41.3 0.0 copy-start.25
  41.3 9.7 %ffn_forward.1 = (f32[384,768]{1,0:T(8,128)S(1)}, bf16[768,384]{1,0:T(8,128)(2,1)S(1)}, bf16[3072,384]{1,0:T(8,128)(2,1)S(1)}, bf16[384,3072]{1,0:T(8,128)(2,1)}) custom-call(f32[384,768]{1,0:T(8,128)S(1)} %get-tuple-element.64.x_ref.refs_1_, f32[1,768]{1,0:T(1,128)S(1)} %get-tuple-element.131.gain_ref.refs_2_, f32[1,768]{1,0:T(1,128)S(1)} %get-tuple-element.120.shift_ref, ...), custom_call_target="tpu_custom_call" | custom-call | tf_op jit(solution)/shard_map/ffn_forward/pallas_call | solution.py:143
  51.0 0.0 copy-done
  51.0 0.0 copy-done.9
  51.0 0.0 copy-done.10
  51.0 0.0 copy-done.16
  51.1 0.0 copy-done.18
  51.1 0.0 copy-done.23
  51.1 0.0 copy-start.2
  51.1 0.0 copy-start.4
  51.1 0.0 copy-start.12
  51.1 0.0 copy-done.22
  51.1 0.0 copy-done.26
  51.1 0.0 copy-done.7
  51.1 0.0 copy-done.6
  51.1 0.0 copy-done.25
  51.2 30.2 %attention_forward.3 = (f32[384,768]{1,0:T(8,128)S(1)}, bf16[768,384]{1,0:T(8,128)(2,1)S(1)}, bf16[384,768]{1,0:T(8,128)(2,1)S(1)}, bf16[768,384]{1,0:T(8,128)(2...) custom-call(f32[384,768]{1,0:T(8,128)S(1)} %get-tuple-element.65.ref, ...), custom_call_target="tpu_custom_call" | custom-call | tf_op jit(solution)/shard_map/attention_forward/pallas_call | solution.py:702
  81.4 0.0 copy-start.3
  81.4 1.0 copy-done.3
  82.4 0.9 copy-done.8
  83.3 0.8 copy-done.13
  84.1 0.8 copy-done.14
  85.0 0.8 copy-done.15
  85.8 0.8 copy-done.17
  86.5 0.7 copy-done.19
  87.2 63.7 %mixture.1 = (f32[384,768]{1,0:T(8,128)}, f32[2,768]{1,0:T(2,128)}, f32[8,768]{1,0:T(8,128)}, bf16[768,512]{1,0:T(8,128)(2,1)}, bf16[8,64,768]{2,1,0:T(8,128)(2,...) custom-call(f32[384,768]{1,0:T(8,128)} %copy-done.3, ...), custom_call_target="tpu_custom_call" | custom-call | tf_op jit(solution)/shard_map/mixture/pallas_call | solution.py:409
  150.9 80.3 %attention_backward.1 = (f32[384,768]{1,0:T(8,128)}, bf16[384,768]{1,0:T(8,128)(2,1)}, bf16[384,2304]{1,0:T(8,128)(2,1)}, f32[2,768]{1,0:T(2,128)}, bf16[384,768...) custom-call(f32[384,768]{1,0:T(8,128)} %get-tuple-element.68.refs_0_, f32[384,768]{1,0:T(8,128)} %copy-done.2, ...), custom_call_target="tpu_custom_call" | custom-call | tf_op jit(solution)/shard_map/attention_backward/pallas_call | solution.py:1107
  231.3 0.8 fusion.4
  232.1 1.3 concatenate.3.refs_26_
  233.3 146.4 %tail.1 = (bf16[16,192,768]{2,1,0:T(8,128)(2,1)}, bf16[384,768]{1,0:T(8,128)(2,1)}, f32[16,768]{1,0:T(8,128)}) custom-call(f32[384,768]{1,0:T(8,128)} %get-tuple-element.83.refs_0_, f32[384,768]{1,0:T(8,128)} %copy-done, f32[1,768]{1,0:T(1,128)} %copy-done.21, f32[1,768]{1,0:T(1,128)} %copy-done.20, bf16[768,3072]{1,0:T(8,128)(2,1)} %refs_4_.1, ...), custom_call_target="tpu_custom_call" | custom-call | tf_op jit(solution)/shard_map/tail/pallas_call | solution.py:1334
  379.8 2.3 copy-done.1
  382.1 5.4 %unpack.1 = (f32[192,2,2304]{2,1,0:T(2,128)}, f32[192,2,768]{2,1,0:T(2,128)}, f32[192,3072]{1,0:T(8,128)}, f32[4,192,768]{2,1,0:T(8,128)}, f32[192,3072]{1,0:T(8,128)}, /*index=5*/f32[4,192,768]{2,1,0:T(8,128)}) custom-call(bf16[16,192,768]{2,1,0:T(8,128)(2,1)S(1)} %copy-done.1, bf16[8,192,768]{2,1,0:T(8,128)(2,1)S(1)} %copy-done.5), custom_call_target="tpu_custom_call" | custom-call | tf_op jit(solution)/shard_map/unpack/pallas_call | solution.py:63
  387.5 0.8 dynamic-slice_bitcast_fusion
  388.3 0.6 fusion
  388.9 0.6 slice.99
  389.5 0.7 multiply_reduce_fusion
  390.9 0.8 copy.43
  391.7 0.0 copy-done.32
  391.7 0.8 copy.44
  (34 shorter events, 0.1 us)
Async XLA Ops:
  2.1 12.2 %copy-start.20 = (f32[1,768]{1,0:T(1,128)}, f32[1,768]{1,0:T(1,128)S(1)}, u32[]{:S(2)}) copy-start(f32[1,768]{1,0:T(1,128)S(1)} %get-tuple-element.130.refs_1_.refs_3_) | copy-start | bytes 9220
  2.1 39.1 %copy-start.21 = (f32[1,768]{1,0:T(1,128)}, f32[1,768]{1,0:T(1,128)S(1)}, u32[]{:S(2)}) copy-start(f32[1,768]{1,0:T(1,128)S(1)} %get-tuple-element.131.gain_ref.refs_2_) | copy-start | bytes 9220
  2.1 49.0 %copy-start.22 = (f32[1,768]{1,0:T(1,128)}, f32[1,768]{1,0:T(1,128)S(1)}, u32[]{:S(2)}) copy-start(f32[1,768]{1,0:T(1,128)S(1)} %get-tuple-element.132.refs_1_.refs_2_) | copy-start | bytes 9220
  3.0 48.1 %copy-start.26 = (s32[128]{0:T(128)}, s32[128]{0:T(128)S(1)}, u32[]{:S(2)}) copy-start(s32[128]{0:T(128)S(1)} %convert_reduce_fusion) | copy-start | bytes 1540
  3.2 48.0 %copy-start.7 = (s32[128,1]{1,0:T(8,128)}, s32[128,1]{1,0:T(8,128)S(1)}, u32[]{:S(2)}) copy-start(s32[128,1]{1,0:T(8,128)S(1)} %copy.33.refs_6_.refs_11_) | copy-start | bytes 1540
  3.2 4.1 %copy-start.29 = (bf16[768,2,768]{2,1,0:T(2,128)(2,1)S(1)}, bf16[768,2,768]{2,1,0:T(2,128)(2,1)}, u32[]{:S(2)}) copy-start(bf16[768,2,768]{2,1,0:T(2,128)(2,1)} %param.19) | copy-start | bytes 7077892
  7.2 5.1 %copy-start.27 = (bf16[768,2,2304]{2,0,1:T(8,128)(2,1)}, bf16[768,2,2304]{2,0,1:T(8,128)(2,1)S(1)}, u32[]{:S(2)}) copy-start(bf16[768,2,2304]{2,0,1:T(8,128)(2,1)S(1)} %copy.39) | copy-start | bytes 21233668
  7.5 5.5 %copy-start.28 = (bf16[768,2,768]{2,0,1:T(8,128)(2,1)}, bf16[768,2,768]{2,0,1:T(8,128)(2,1)S(1)}, u32[]{:S(2)}) copy-start(bf16[768,2,768]{2,0,1:T(8,128)(2,1)S(1)} %copy.40) | copy-start | bytes 7077892
  13.1 1.2 copy-start.30
  40.4 0.8 copy-start.11
  41.2 9.8 %copy-start = (f32[384,768]{1,0:T(8,128)}, f32[384,768]{1,0:T(8,128)S(1)}, u32[]{:S(2)}) copy-start(f32[384,768]{1,0:T(8,128)S(1)} %get-tuple-element.64.x_ref.refs_1_) | copy-start | bytes 3538948
  41.2 9.8 %copy-start.9 = (bf16[768,384]{1,0:T(8,128)(2,1)}, bf16[768,384]{1,0:T(8,128)(2,1)S(1)}, u32[]{:S(2)}) copy-start(bf16[768,384]{1,0:T(8,128)(2,1)S(1)} %get-tuple-element.96) | copy-start | bytes 1769476
  41.2 9.8 %copy-start.10 = (bf16[384,768]{1,0:T(8,128)(2,1)}, bf16[384,768]{1,0:T(8,128)(2,1)S(1)}, u32[]{:S(2)}) copy-start(bf16[384,768]{1,0:T(8,128)(2,1)S(1)} %get-tuple-element.85.refs_12_) | copy-start | bytes 1769476
  41.2 9.8 %copy-start.16 = (bf16[6,2,128,128]{3,2,1,0:T(8,128)(2,1)}, bf16[6,2,128,128]{3,2,1,0:T(8,128)(2,1)S(1)}, u32[]{:S(2)}) copy-start(bf16[6,2,128,128]{3,2,1,0:T(8,128)(2,1)S(1)} %get-tuple-element.88.refs_15_) | copy-start | bytes 1179652
  41.2 9.8 %copy-start.18 = (bf16[6,128,128]{2,1,0:T(8,128)(2,1)}, bf16[6,128,128]{2,1,0:T(8,128)(2,1)S(1)}, u32[]{:S(2)}) copy-start(bf16[6,128,128]{2,1,0:T(8,128)(2,1)S(1)} %get-tuple-element.89.refs_16_) | copy-start | bytes 589828
  41.2 9.8 %copy-start.23 = (f32[6,2,384]{2,1,0:T(2,128)}, f32[6,2,384]{2,1,0:T(2,128)S(1)}, u32[]{:S(2)}) copy-start(f32[6,2,384]{2,1,0:T(2,128)S(1)} %get-tuple-element.90.refs_17_) | copy-start | bytes 55300
  41.3 9.9 %copy-start.6 = (bf16[1,384,768]{2,1,0:T(8,128)(2,1)S(1)}, bf16[1,384,768]{2,1,0:T(8,128)(2,1)}, u32[]{:S(2)}) copy-start(bf16[1,384,768]{2,1,0:T(8,128)(2,1)} %param.25) | copy-start | bytes 1769476
  41.3 9.9 %copy-start.25 = (s32[1,384,1]{1,2,0:T(1,128)S(1)}, s32[1,384,1]{1,2,0:T(1,128)}, u32[]{:S(2)}) copy-start(s32[1,384,1]{1,2,0:T(1,128)} %param.15) | copy-start | bytes 4612
  51.1 30.3 %copy-start.2 = (f32[384,768]{1,0:T(8,128)}, f32[384,768]{1,0:T(8,128)S(1)}, u32[]{:S(2)}) copy-start(f32[384,768]{1,0:T(8,128)S(1)} %get-tuple-element.65.refs_0_.refs_1_) | copy-start | bytes 3538948
  51.1 30.3 %copy-start.4 = (bf16[3072,384]{1,0:T(8,128)(2,1)}, bf16[3072,384]{1,0:T(8,128)(2,1)S(1)}, u32[]{:S(2)}) copy-start(bf16[3072,384]{1,0:T(8,128)(2,1)S(1)} %get-tuple-element.93) | copy-start | bytes 7077892
  51.1 30.3 %copy-start.12 = (bf16[768,384]{1,0:T(8,128)(2,1)}, bf16[768,384]{1,0:T(8,128)(2,1)S(1)}, u32[]{:S(2)}) copy-start(bf16[768,384]{1,0:T(8,128)(2,1)S(1)} %get-tuple-element.94) | copy-start | bytes 1769476
  81.4 1.0 copy-start.3
  82.4 0.9 copy-start.8
  83.3 0.8 copy-start.13
  84.1 0.8 copy-start.14
  85.0 0.8 copy-start.15
  85.8 0.8 copy-start.17
  86.5 0.7 copy-start.19
  87.2 63.7 %copy-start.24 = (f32[6,2,384]{2,1,0:T(2,128)}, f32[6,2,384]{2,1,0:T(2,128)S(1)}, u32[]{:S(2)}) copy-start(f32[6,2,384]{2,1,0:T(2,128)S(1)} %get-tuple-element.74.refs_12_) | copy-start | bytes 55300
  150.9 81.1 %copy-start.35 = (f32[2,768]{1,0:T(2,128)S(1)}, f32[2,768]{1,0:T(2,128)}, u32[]{:S(2)}) copy-start(f32[2,768]{1,0:T(2,128)} %get-tuple-element.100) | copy-start | bytes 18436
  150.9 81.1 %copy-start.33 = (f32[8,768]{1,0:T(8,128)S(1)}, f32[8,768]{1,0:T(8,128)}, u32[]{:S(2)}) copy-start(f32[8,768]{1,0:T(8,128)} %get-tuple-element.101) | copy-start | bytes 73732
  233.3 146.4 %copy-start.5 = (bf16[8,192,768]{2,1,0:T(8,128)(2,1)S(1)}, bf16[8,192,768]{2,1,0:T(8,128)(2,1)}, u32[]{:S(2)}) copy-start(bf16[8,192,768]{2,1,0:T(8,128)(2,1)} %get-tuple-element.105.expert_ref) | copy-start | bytes 7077892
  379.8 2.3 copy-start.1
  382.1 7.4 %copy-start.34 = (f32[8,128]{1,0:T(8,128)S(1)}, f32[8,128]{1,0:T(8,128)}, u32[]{:S(2)}) copy-start(f32[8,128]{1,0:T(8,128)} %get-tuple-element.82) | copy-start | bytes 12292
  382.1 8.7 %copy-start.31 = (bf16[384,768]{1,0:T(8,128)(2,1)S(1)}, bf16[384,768]{1,0:T(8,128)(2,1)}, u32[]{:S(2)}) copy-start(bf16[384,768]{1,0:T(8,128)(2,1)} %get-tuple-element.81) | copy-start | bytes 1769476
  382.1 9.6 %copy-start.32 = (bf16[384,768]{1,0:T(8,128)(2,1)S(1)}, bf16[384,768]{1,0:T(8,128)(2,1)}, u32[]{:S(2)}) copy-start(bf16[384,768]{1,0:T(8,128)(2,1)} %get-tuple-element.102) | copy-start | bytes 1769476

commit v5 on v4

--- a/solution.py
+++ b/solution.py
@@ -1,4 +1,5 @@
 import functools
+import types
 
 import jax
 import jax.numpy as jnp
@@ -243,194 +244,6 @@
 def across_peers(experts):
     d, e = lax.axis_index("dp"), lax.axis_index("expert")
     return [(d, lax.rem(e + k, experts)) for k in range(1, experts)]
-
-
-def mixture_kernel(
-    n_dp, n_ex,
-    x_ref, gain_ref, shift_ref, router_ref, assign_ref, cot_ref, far_cot_ref, w_in_ref, w_out_ref,
-    up_ref, sums_ref, router_grad_ref, rows_t_ref, back_ref, active_t_ref, hidden_ref, result_ref, gate_ref, stats_ref,
-    rows_ref, send_ref, grad_ref, home_ref, dgate_ref, home_dgate_ref, stat_send, stat_recv, dispatch_ref, result_acc, grad_acc,
-    x_send_sem, x_recv_sem, grad_send_sem, grad_recv_sem, dgate_send_sem, dgate_recv_sem, stat_send_sem, stat_recv_sem,
-):
-    d, e = lax.axis_index("dp"), lax.axis_index("expert")
-    dp_levels, ex_levels = n_dp.bit_length() - 1, n_ex.bit_length() - 1
-    tokens, width = x_ref.shape
-    padded = send_ref.shape[1]
-    group = min(max(4, 128 // padded), n_ex)
-    groups = n_ex // group
-    exact = dict(precision=lax.Precision.HIGHEST, preferred_element_type=jnp.float32)
-    hops = [(flip(d, b), e) for b in range(dp_levels)] + [(d, flip(e, b)) for b in range(ex_levels)]
-    greet([(flip(d, b), e) for b in range(dp_levels)] + across_peers(n_ex))
-
-    unit, inverse = norm_parts(x_ref[...])
-    routed = (unit * gain_ref[...] + shift_ref[...]).astype(jnp.bfloat16)
-    assign = assign_ref[...]
-    dispatch = dispatch_of(assign, n_ex)
-    dispatch_ref[...] = dispatch
-    send_ref[...] = dot(dispatch, routed).astype(jnp.bfloat16).reshape(send_ref.shape)
-    x_across = Across(n_ex, send_ref, rows_ref, x_send_sem, x_recv_sem)
-    x_across.start_all()
-    rows_ref[e] = send_ref[e]
-    hot = chosen_rows(assign, n_ex)
-    gate = jax.nn.sigmoid(jnp.sum(hot * dot_rows(router_ref[...], routed), axis=0, keepdims=True))
-    gate_ref[...] = gate
-
-    def stat_copy(i):
-        return pltpu.make_async_remote_copy(
-            src_ref=stat_send.at[i],
-            dst_ref=stat_recv.at[i],
-            send_sem=stat_send_sem.at[i],
-            recv_sem=stat_recv_sem.at[i],
-            device_id=hops[i],
-            device_id_type=MESH,
-        )
-
-    lane = lax.broadcasted_iota(jnp.int32, stats_ref.shape, 1)
-    stat_send[0] = jnp.where(
-        lane == 0, jnp.sum(hot, axis=1, keepdims=True), jnp.sum(hot * gate, axis=1, keepdims=True)
-    )
-    stat_copy(0).start()
-
-    def stat_step(i):
-        stat_copy(i).wait()
-        value = stat_send[i] + stat_recv[i]
-        if i + 1 < len(hops):
-            stat_send[i + 1] = value
-            stat_copy(i + 1).start()
-        else:
-            stats_ref[...] = value
-
-    grad_across = Across(n_ex, grad_ref, home_ref, grad_send_sem, grad_recv_sem)
-    dgate_across = Across(n_ex, dgate_ref, home_dgate_ref, dgate_send_sem, dgate_recv_sem)
-    step = 768 if w_in_ref.shape[1] % 768 == 0 else w_in_ref.shape[1]
-    done = 0
-    for k in range(groups):
-        first = lax.rem(e // group + k, groups) * group
-        for m in range(group):
-
-            @pl.when(first + m != e)
-            def _(m=m):
-                x_across.wait_from(first + m)
-
-        at = pl.ds(first, group)
-        rows = rows_ref[at].reshape(group * padded, width)
-        cot = far_cot_ref[at].reshape(group * padded, width).astype(jnp.float32)
-        logits = dot_rows(rows, router_ref[...])
-        own = lax.broadcasted_iota(jnp.int32, logits.shape, 1) == e
-        slot_gate = jax.nn.sigmoid(jnp.sum(jnp.where(own, logits, 0.0), axis=1, keepdims=True))
-        back = (slot_gate * cot).astype(jnp.bfloat16)
-        back_ref[at] = back.reshape(group, padded, width)
-        span = pl.ds(pl.multiple_of(first * padded, group * padded), group * padded)
-        rows_t_ref[:, span] = rows.T
-        result_acc[...] = jnp.zeros_like(result_acc)
-        grad_acc[...] = jnp.zeros_like(grad_acc)
-
-        def block(i, _):
-            cols = pl.ds(pl.multiple_of(i * step, step), step)
-            active, slope = gelu_parts(dot(rows, w_in_ref[:, cols]))
-            active = active.astype(jnp.bfloat16)
-            hidden = (slope * dot_rows(back, w_out_ref[cols, :])).astype(jnp.bfloat16)
-            active_t_ref[cols, span] = active.T
-            hidden_ref[span, cols] = hidden
-            result_acc[...] += dot(active, w_out_ref[cols, :])
-            grad_acc[...] += dot_rows(hidden, w_in_ref[:, cols])
-            return 0
-
-        lax.fori_loop(0, w_in_ref.shape[1] // step, block, 0)
-        grad_ref[at] = grad_acc[...].astype(jnp.bfloat16).reshape(group, padded, width)
-        result = result_acc[...].astype(jnp.bfloat16)
-        result_ref[at] = result.reshape(group, padded, width)
-        dgate = lax.dot_general(
-            jnp.ones((8, width), jnp.float32), cot * result.astype(jnp.float32), (((1,), (1,)), ((), ())), **exact
-        )
-        for m in range(group):
-            dgate_ref[first + m, :, :padded] = dgate[:, m * padded : (m + 1) * padded]
-
-            @pl.when(first + m != e)
-            def _(m=m):
-                grad_across.start(first + m)
-                dgate_across.start(first + m)
-
-            @pl.when(first + m == e)
-            def _():
-                home_ref[e] = grad_ref[e]
-                home_dgate_ref[e] = dgate_ref[e]
-
-        if done < len(hops):
-            stat_step(done)
-            done += 1
-
-    for i in range(done, len(hops)):
-        stat_step(i)
-    x_across.others(x_across.wait_to)
-    dgate_across.wait_all()
-    dgate = jnp.zeros((8, tokens), jnp.float32)
-    for j in range(n_ex):
-        part = dispatch_ref[j * padded : (j + 1) * padded].astype(jnp.float32)
-        dgate = dgate + jnp.dot(home_dgate_ref[j, :, :padded], part, **exact)
-    everyone = tokens * n_dp * n_ex
-    share = jnp.sum(jnp.where(lane == 0, stats_ref[...], 0.0), axis=1, keepdims=True) / everyone
-    weight = balance_weight * n_ex * (share - 1.0 / n_ex) / everyone
-    grad_gate = dgate[0:1] + jnp.sum(hot * weight, axis=0, keepdims=True)
-    grad_logits = hot * (grad_gate * gate * (1.0 - gate))
-    router_grad_ref[...] = jnp.dot(grad_logits, routed.astype(jnp.float32), **exact)
-    grad_normed = lax.dot_general(
-        grad_logits, router_ref[...].astype(jnp.float32), (((0,), (0,)), ((), ())), **exact
-    )
-    grad_across.wait_all()
-    grad_normed = grad_normed + dot_columns(dispatch_ref[...], home_ref[...].reshape(n_ex * padded, width))
-    up_ref[...] = cot_ref[...].astype(jnp.float32) + norm_back(unit, inverse, gain_ref[...], grad_normed)
-    sums_ref[0:1] = jnp.sum(grad_normed * unit, axis=0, keepdims=True)
-    sums_ref[1:2] = jnp.sum(grad_normed, axis=0, keepdims=True)
-
-
-def mixture(n_dp, n_ex, collective_id, stream, norm_gain, norm_shift, router_t, assign, cot, far_cot, weight_in, weight_out):
-    tokens, width = stream.shape
-    hidden = weight_in.shape[1]
-    _, padded = capacity_of(tokens, n_ex)
-    slots = n_ex * padded
-    group = min(max(4, 128 // padded), n_ex) * padded
-    low, wide = jnp.bfloat16, jnp.float32
-    slab = (n_ex, padded, width)
-    hops = (n_dp * n_ex).bit_length() - 1
-    outs = [
-        jax.ShapeDtypeStruct((tokens, width), wide),
-        jax.ShapeDtypeStruct((2, width), wide),
-        jax.ShapeDtypeStruct((n_ex, width), wide),
-        jax.ShapeDtypeStruct((width, slots), low),
-        jax.ShapeDtypeStruct(slab, low),
-        jax.ShapeDtypeStruct((hidden, slots), low),
-        jax.ShapeDtypeStruct((slots, hidden), low),
-        jax.ShapeDtypeStruct(slab, low),
-        jax.ShapeDtypeStruct((1, tokens), wide),
-        jax.ShapeDtypeStruct((n_ex, 128), wide),
-    ]
-    vmem = pl.BlockSpec(memory_space=pltpu.VMEM)
-    return pl.pallas_call(
-        functools.partial(mixture_kernel, n_dp, n_ex),
-        out_shape=outs,
-        in_specs=[vmem] * 9,
-        out_specs=[vmem] * len(outs),
-        scratch_shapes=[
-            pltpu.VMEM(slab, low),
-            pltpu.VMEM(slab, low),
-            pltpu.VMEM(slab, low),
-            pltpu.VMEM(slab, low),
-            pltpu.VMEM((n_ex, 8, 128), wide),
-            pltpu.VMEM((n_ex, 8, 128), wide),
-            pltpu.VMEM((hops, n_ex, 128), wide),
-            pltpu.VMEM((hops, n_ex, 128), wide),
-            pltpu.VMEM((slots, tokens), low),
-            pltpu.VMEM((group, width), wide),
-            pltpu.VMEM((group, width), wide),
-        ]
-        + [pltpu.SemaphoreType.DMA((n_ex,)) for _ in range(6)]
-        + [pltpu.SemaphoreType.DMA((hops,)) for _ in range(2)],
-        compiler_params=pltpu.CompilerParams(
-            collective_id=collective_id, has_side_effects=True, vmem_limit_bytes=56 * 1024 * 1024
-        ),
-        name="mixture",
-    )(stream, norm_gain, norm_shift, router_t, assign, cot, far_cot, weight_in, weight_out)
 
 
 def head_pair(rows):
@@ -733,8 +546,8 @@
 
 def attend_back_pair(n_dp, me, width, r, do_spread, aux_spread, h):
     scale = HEAD_DIM ** (-0.5)
-    mixed_ref = r["mixed"]
-    long = r["kv"].shape[3]
+    mixed_ref = r.mixed
+    long = r.kv.shape[3]
 
     def row_of(aux, first):
         return jnp.concatenate([aux[first : first + 1], aux[first + 1 : first + 2]], axis=1)
@@ -751,41 +564,41 @@
         at = pl.ds(pl.multiple_of(third * width + 128 * h, 128), 128)
         mixed_ref[first : first + value.shape[0], at] = value.astype(jnp.bfloat16)
 
-    seen = short_seen(r["doc_row"][...], r["doc_col"][...])
-    queries, grads = head_pair(r["short_q"][h]), head_pair(r["short_do"][h])
-    keys = r["short_kv"][h, 0]
-    probs, grad_scores = score_grads(keys, r["short_kv"][h, 1], queries, grads, r["short_aux"][h], seen)
+    seen = short_seen(r.doc_row[...], r.doc_col[...])
+    queries, grads = head_pair(r.short_q[h]), head_pair(r.short_do[h])
+    keys = r.short_kv[h, 0]
+    probs, grad_scores = score_grads(keys, r.short_kv[h, 1], queries, grads, r.short_aux[h], seen)
     put(0, long, (pair_rows(dot_columns(keys, grad_scores)) * scale).T)
     put(1, long, dot(grad_scores, queries))
     put(2, long, dot(probs, grads))
-    queries, grads = head_pair(r["q"][me, h]), head_pair(r["do"][me, h])
-    own_keys, own_values = r["kv"][me, h, 0], r["kv"][me, h, 1]
-    probs, grad_scores = score_grads(own_keys, own_values, queries, grads, r["aux"][me, h], causal(long, long))
-    r["dq"][...] = dot_columns(own_keys, grad_scores)
-    r["dk"][...] = dot(grad_scores, queries)
-    r["dv"][...] = dot(probs, grads)
+    queries, grads = head_pair(r.q[me, h]), head_pair(r.do[me, h])
+    own_keys, own_values = r.kv[me, h, 0], r.kv[me, h, 1]
+    probs, grad_scores = score_grads(own_keys, own_values, queries, grads, r.aux[me, h], causal(long, long))
+    r.dq[...] = dot_columns(own_keys, grad_scores)
+    r.dk[...] = dot(grad_scores, queries)
+    r.dv[...] = dot(probs, grads)
     for block in range(n_dp - 1):
 
         @pl.when(block < me)
         def _():
-            keys = r["kv"][block, h, 0]
-            _, grad_scores = score_grads(keys, r["kv"][block, h, 1], queries, grads, r["aux"][me, h], None)
-            r["dq"][...] += dot_columns(keys, grad_scores)
-
-    put(0, 0, (pair_rows(r["dq"][...]) * scale).T)
+            keys = r.kv[block, h, 0]
+            _, grad_scores = score_grads(keys, r.kv[block, h, 1], queries, grads, r.aux[me, h], None)
+            r.dq[...] += dot_columns(keys, grad_scores)
+
+    put(0, 0, (pair_rows(r.dq[...]) * scale).T)
     do_spread.relay(h)
     aux_spread.relay(h)
 
     def use(block):
-        queries, grads = head_pair(r["q"][block, h]), head_pair(r["do"][block, h])
-        probs, grad_scores = score_grads(own_keys, own_values, queries, grads, r["aux"][block, h], None)
-        r["dk"][...] += dot(grad_scores, queries)
-        r["dv"][...] += dot(probs, grads)
+        queries, grads = head_pair(r.q[block, h]), head_pair(r.do[block, h])
+        probs, grad_scores = score_grads(own_keys, own_values, queries, grads, r.aux[block, h], None)
+        r.dk[...] += dot(grad_scores, queries)
+        r.dv[...] += dot(probs, grads)
 
     aux_spread.each(h, lambda block: None)
     do_spread.each(h, use)
-    put(1, 0, r["dk"][...])
-    put(2, 0, r["dv"][...])
+    put(1, 0, r.dk[...])
+    put(2, 0, r.dv[...])
 
 
 def back_scratch(n_dp, pairs, long, short):
@@ -1017,114 +830,336 @@
     return [((0, cut), 0), ((cut, width), 1)]
 
 
-def attend_back_kernel(n_dp, n_ex, *refs):
-    (up_ref, x_ref, gain_ref, w_in_ref, w_out_ref, doc_row_ref, doc_col_ref), rest = refs[:7], refs[7:]
-    (context_ref, kv_ref, q_ref, short_kv_ref, short_q_ref, lse_ref), rest = rest[:6], rest[6:]
-    (assign_ref, gate_ref, stream_ref, result_ref), rest = rest[:4], rest[4:]
-    (rows_t_ref, hidden_ref, active_t_ref, back_ref), rest = rest[:4], rest[4:]
-    (up_next_ref, up_low_ref, mixed_ref, sums_ref, output_ref, chunks_ref), rest = rest[:6], rest[6:]
-    (do_ref, aux_ref, short_do_ref, short_aux_ref, dq_ref, dk_ref, dv_ref), rest = rest[:7], rest[7:]
-    (do_far, do_near, do_recv, aux_far, aux_near, aux_recv), rest = rest[:6], rest[6:]
-    (home_ref, result_send_sem, result_recv_sem), rest = rest[:3], rest[3:]
+def middle_kernel(n_dp, n_ex, names, staged, *refs):
+    r = types.SimpleNamespace(**dict(zip(names, refs)))
+    extra = iter(refs[len(names) :])
+    loads = types.SimpleNamespace()
+    for name in staged:
+        buffer, sem = next(extra), next(extra)
+        setattr(loads, name, pltpu.make_async_copy(getattr(r, name), buffer, sem))
+        setattr(r, name, buffer)
+    w_in_ref, w_out_ref, weight_sem = (next(extra) for _ in range(3))
+    rows_ref, send_ref, grad_ref, home_ref, result_ref, result_home_ref = (next(extra) for _ in range(6))
+    rows_t_ref, back_ref, active_t_ref, hidden_ref, dispatch_ref, gate_ref = (next(extra) for _ in range(6))
+    dgate_ref, home_dgate_ref, stat_send, stat_recv, result_acc, grad_acc = (next(extra) for _ in range(6))
+    (
+        x_send_sem, x_recv_sem, grad_send_sem, grad_recv_sem, dgate_send_sem, dgate_recv_sem,
+        result_send_sem, result_recv_sem, stat_send_sem, stat_recv_sem,
+    ) = (next(extra) for _ in range(10))
+    do_ref, aux_ref, short_do_ref, short_aux_ref, dq_ref, dk_ref, dv_ref = (next(extra) for _ in range(7))
+    do_far, do_near, do_recv, aux_far, aux_near, aux_recv = (next(extra) for _ in range(6))
     links = Links(n_dp)
-    me = links.me
-    pairs, long, width = kv_ref.shape[1], kv_ref.shape[3], x_ref.shape[1]
-    up = up_ref[...]
+    d, e, me = links.me, links.expert, links.me
+    dp_levels, ex_levels = n_dp.bit_length() - 1, n_ex.bit_length() - 1
+    tokens, width = r.stream.shape
+    padded = send_ref.shape[1]
+    blocks = r.expert_in.shape[1] // width
+    pairs, long = r.kv.shape[1], r.kv.shape[3]
+    group = min(max(4, 128 // padded), n_ex)
+    groups = n_ex // group
+    exact = dict(precision=lax.Precision.HIGHEST, preferred_element_type=jnp.float32)
+    hops = [(flip(d, b), e) for b in range(dp_levels)] + [(d, flip(e, b)) for b in range(ex_levels)]
+
+    def column(i):
+        return pl.ds(i * width, width)
+
+    expert_loads = [
+        (
+            pltpu.make_async_copy(r.expert_in.at[:, column(i)], w_in_ref.at[i], weight_sem.at[0, i]),
+            pltpu.make_async_copy(r.expert_out.at[column(i), :], w_out_ref.at[i], weight_sem.at[1, i]),
+        )
+        for i in range(blocks)
+    ]
+    for both in expert_loads:
+        for load in both:
+            load.start()
+    for name in staged:
+        getattr(loads, name).start()
+    greet(links.peers() + across_peers(n_ex))
+
+    unit, inverse = norm_parts(r.stream[...])
+    routed = (unit * r.gain[...] + r.shift[...]).astype(jnp.bfloat16)
+    assign = r.assign[...]
+    dispatch = dispatch_of(assign, n_ex)
+    dispatch_ref[...] = dispatch
+    send_ref[...] = dot(dispatch, routed).astype(jnp.bfloat16).reshape(send_ref.shape)
+    x_across = Across(n_ex, send_ref, rows_ref, x_send_sem, x_recv_sem)
+
+    def place(k, i):
+        return lax.rem(e // group + k, groups) * group + lax.rem(e + i, group)
+
+    def source(k, i):
+        return lax.rem(e // group + k, groups) * group + lax.rem(e + group - i, group)
+
+    for i in range(group):
+        if i:
+            x_across.start(place(0, i))
+        for k in range(1, groups):
+            x_across.start(place(k, i))
+    rows_ref[e] = send_ref[e]
+    router = r.router[...]
+    hot = chosen_rows(assign, n_ex)
+    gate = jax.nn.sigmoid(jnp.sum(hot * dot_rows(router, routed), axis=0, keepdims=True))
+    gate_ref[...] = gate
+
+    def stat_copy(i):
+        return pltpu.make_async_remote_copy(
+            src_ref=stat_send.at[i],
+            dst_ref=stat_recv.at[i],
+            send_sem=stat_send_sem.at[i],
+            recv_sem=stat_recv_sem.at[i],
+            device_id=hops[i],
+            device_id_type=MESH,
+        )
+
+    lane = lax.broadcasted_iota(jnp.int32, r.stats.shape, 1)
+    stat_send[0] = jnp.where(
+        lane == 0, jnp.sum(hot, axis=1, keepdims=True), jnp.sum(hot * gate, axis=1, keepdims=True)
+    )
+    stat_copy(0).start()
+
+    def stat_step(i):
+        stat_copy(i).wait()
+        value = stat_send[i] + stat_recv[i]
+        if i + 1 < len(hops):
+            stat_send[i + 1] = value
+            stat_copy(i + 1).start()
+        else:
+            r.stats[...] = value
+
+    grad_across = Across(n_ex, grad_ref, home_ref, grad_send_sem, grad_recv_sem)
+    dgate_across = Across(n_ex, dgate_ref, home_dgate_ref, dgate_send_sem, dgate_recv_sem)
+    steps = [[(0, i) for i in range(group)]]
+    cut = group // 2 if (group // 2) * padded % 128 == 0 else group
+    for k in range(1, groups):
+        steps += [[(k, i) for i in range(first, first + cut)] for first in range(0, group, cut)]
+    done, at = 0, 0
+    for number, members in enumerate(steps):
+        count = len(members) * padded
+        sources = [source(k, i) for k, i in members]
+        for (k, i), j in zip(members, sources):
+            if (k, i) != (0, 0):
+                x_across.wait_from(j)
+        rows = jnp.concatenate([rows_ref[j] for j in sources], axis=0)
+        cot = jnp.concatenate([r.far_cot[j] for j in sources], axis=0).astype(jnp.float32)
+        logits = dot_rows(rows, router)
+        own = lax.broadcasted_iota(jnp.int32, logits.shape, 1) == e
+        slot_gate = jax.nn.sigmoid(jnp.sum(jnp.where(own, logits, 0.0), axis=1, keepdims=True))
+        back = (slot_gate * cot).astype(jnp.bfloat16)
+        span = slice(at, at + count)
+        back_ref[span] = back
+        rows_t_ref[:, span] = rows.T
+        result_acc[:count] = jnp.zeros((count, width), jnp.float32)
+        grad_acc[:count] = jnp.zeros((count, width), jnp.float32)
+
+        def block(i, _, rows=rows, back=back, span=span, count=count):
+            cols = pl.ds(pl.multiple_of(i * width, width), width)
+            active, slope = gelu_parts(dot(rows, w_in_ref[i]))
+            active = active.astype(jnp.bfloat16)
+            hidden = (slope * dot_rows(back, w_out_ref[i])).astype(jnp.bfloat16)
+            active_t_ref[cols, span] = active.T
+            hidden_ref[span, cols] = hidden
+            result_acc[:count] += dot(active, w_out_ref[i])
+            grad_acc[:count] += dot_rows(hidden, w_in_ref[i])
+            return 0
+
+        if number == 0:
+            for both in expert_loads:
+                for load in both:
+                    load.wait()
+        lax.fori_loop(0, blocks, block, 0)
+        grad = grad_acc[:count].astype(jnp.bfloat16)
+        result = result_acc[:count].astype(jnp.bfloat16)
+        dgate = lax.dot_general(
+            jnp.ones((8, width), jnp.float32), cot * result.astype(jnp.float32), (((1,), (1,)), ((), ())), **exact
+        )
+        for m, (k, i) in enumerate(members):
+            j, part = sources[m], slice(m * padded, (m + 1) * padded)
+            grad_ref[j] = grad[part]
+            result_ref[j] = result[part]
+            dgate_ref[j, :, :padded] = dgate[:, part]
+            if (k, i) == (0, 0):
+                home_ref[e] = grad_ref[e]
+                home_dgate_ref[e] = dgate_ref[e]
+            else:
+                grad_across.start(j)
+                dgate_across.start(j)
+        at += count
+        if done < len(hops):
+            stat_step(done)
+            done += 1
+
+    thirds = [w_in_ref.at[i] for i in range(3)]
+    in_loads = [
+        pltpu.make_async_copy(r.attn_in.at[1, :, column(i)], third, weight_sem.at[0, i])
+        for i, third in enumerate(thirds)
+    ]
+    out_load = pltpu.make_async_copy(r.attn_out.at[1], w_out_ref.at[0], weight_sem.at[1, 0])
+    for load in in_loads + [out_load]:
+        load.start()
+    rows = width // n_dp
+
+    def rows_of(ref, j, q):
+        return ref[pl.ds(pl.multiple_of((q * (ref.shape[0] // width) + j) * rows, rows), rows), :]
+
+    factors = [
+        (blocks, lambda j, q: rows_of(rows_t_ref, 0, q), lambda j: hidden_ref[:, pl.ds(pl.multiple_of(j * width, width), width)]),
+        (blocks, lambda j, q: rows_of(active_t_ref, j, q), lambda j: back_ref[...]),
+    ]
+    red = Reduction(n_dp, 1, rows, factors, [((0, width), 0)], list(extra) + [r.chunks])
+    red.tick(0, 0, 1)
+    early = 1
+    while done < len(hops):
+        stat_step(done)
+        done += 1
+    x_across.others(x_across.wait_to)
+    red.tick(1, 1, 2)
+    early += 1
+    dgate_across.wait_all()
+    dgate = jnp.zeros((8, tokens), jnp.float32)
+    for j in range(n_ex):
+        part = dispatch_ref[j * padded : (j + 1) * padded].astype(jnp.float32)
+        dgate = dgate + jnp.dot(home_dgate_ref[j, :, :padded], part, **exact)
+    everyone = tokens * n_dp * n_ex
+    share = jnp.sum(jnp.where(lane == 0, r.stats[...], 0.0), axis=1, keepdims=True) / everyone
+    weight = balance_weight * n_ex * (share - 1.0 / n_ex) / everyone
+    gate = gate_ref[...]
+    grad_gate = dgate[0:1] + jnp.sum(hot * weight, axis=0, keepdims=True)
+    grad_logits = hot * (grad_gate * gate * (1.0 - gate))
+    r.router_grad[...] = jnp.dot(grad_logits, routed.astype(jnp.float32), **exact)
+    grad_normed = lax.dot_general(grad_logits, router.astype(jnp.float32), (((0,), (0,)), ((), ())), **exact)
+    red.tick(2, 2, 3)
+    early += 1
+    grad_across.wait_all()
+    grad_normed = grad_normed + dot_columns(dispatch_ref[...], home_ref[...].reshape(n_ex * padded, width))
+    unit, inverse = norm_parts(r.stream[...])
+    up = r.cot[...].astype(jnp.float32) + norm_back(unit, inverse, r.gain[...], grad_normed)
+    r.sums[0:1] = jnp.sum(grad_normed * unit, axis=0, keepdims=True)
+    r.sums[1:2] = jnp.sum(grad_normed, axis=0, keepdims=True)
+
+    r.up_next[...] = up
     up_low = up.astype(jnp.bfloat16)
-    up_low_ref[...] = up_low
-    grad_context = dot_rows(up_low, w_out_ref[...]).astype(jnp.bfloat16)
-    share_context(context_ref, lse_ref, grad_context, do_ref, aux_ref, short_do_ref, short_aux_ref, me, long)
-    blocks = hidden_ref.shape[1] // width
-    groups = [
-        (blocks, lambda j, q: rows_t_ref[q, 0], lambda j: hidden_ref[:, pl.ds(pl.multiple_of(j * width, width), width)]),
-        (blocks, lambda j, q: active_t_ref[q, j], lambda j: back_ref[...]),
-    ]
-    red = Reduction(n_dp, 1, width // n_dp, groups, [((0, width), 0)], list(rest) + [chunks_ref])
-    greet(links.peers() + across_peers(n_ex))
+    r.up_low[...] = up_low
+    out_load.wait()
+    for name in staged:
+        getattr(loads, name).wait()
+    grad_context = dot_rows(up_low, w_out_ref[0]).astype(jnp.bfloat16)
+    share_context(r.context, r.lse, grad_context, do_ref, aux_ref, short_do_ref, short_aux_ref, me, long)
     do_spread = Spread(links, lambda b, p: do_ref.at[b, p], pairs, False, do_far, do_near, do_recv)
     aux_spread = Spread(links, lambda b, p: aux_ref.at[b, p], pairs, False, aux_far, aux_near, aux_recv)
     for h in range(pairs):
         do_spread.send(h)
         aux_spread.send(h)
-    result_across = Across(n_ex, result_ref, home_ref, result_send_sem, result_recv_sem)
+    result_across = Across(n_ex, result_ref, result_home_ref, result_send_sem, result_recv_sem)
     result_across.start_all()
-    home_ref[links.expert] = result_ref[links.expert]
-    red.tick(0, 0, 1)
-    sequence = dict(
-        doc_row=doc_row_ref, doc_col=doc_col_ref, kv=kv_ref, q=q_ref, short_kv=short_kv_ref, short_q=short_q_ref,
+    result_home_ref[e] = result_ref[e]
+    sequence = types.SimpleNamespace(
+        doc_row=r.doc_row, doc_col=r.doc_col, kv=r.kv, q=r.q, short_kv=r.short_kv, short_q=r.short_q,
         do=do_ref, aux=aux_ref, short_do=short_do_ref, short_aux=short_aux_ref, dq=dq_ref, dk=dk_ref, dv=dv_ref,
-        mixed=mixed_ref,
+        mixed=r.mixed,
     )
 
     def pair(h, _):
         attend_back_pair(n_dp, me, width, sequence, do_spread, aux_spread, h)
-        red.tick(1 + h, 1, 1 + pairs)
+        red.tick(early + h, early, early + pairs)
         return 0
 
     lax.fori_loop(0, pairs, pair, 0)
-    grad_normed = dot_rows(mixed_ref[...], w_in_ref[...])
-    unit, inverse = norm_parts(x_ref[...])
-    up_next_ref[...] = up + norm_back(unit, inverse, gain_ref[...], grad_normed)
-    sums_ref[0:1] = jnp.sum(grad_normed * unit, axis=0, keepdims=True)
-    sums_ref[1:2] = jnp.sum(grad_normed, axis=0, keepdims=True)
-    red.tick(1 + pairs, 1 + pairs, 2 + pairs)
+    grad_normed = jnp.zeros((tokens, width), jnp.float32)
+    for i, third in enumerate(thirds):
+        in_loads[i].wait()
+        grad_normed = grad_normed + dot_rows(r.mixed[:, i * width : (i + 1) * width], third[...])
+    unit, inverse = norm_parts(r.attn_x[...])
+    r.up_next[...] += norm_back(unit, inverse, r.attn_gain[...], grad_normed)
+    r.attn_sums[0:1] = jnp.sum(grad_normed * unit, axis=0, keepdims=True)
+    r.attn_sums[1:2] = jnp.sum(grad_normed, axis=0, keepdims=True)
+
+    def rest(t, _):
+        red.tick(t, early + pairs, red.ticks)
+        return 0
+
+    lax.fori_loop(early + pairs, red.ticks, rest, 0)
     result_across.wait_all()
-    dispatch = dispatch_of(assign_ref[...], n_ex)
-    result = dot_columns(dispatch, home_ref[...].reshape(dispatch.shape[0], width))
-    gate = jnp.broadcast_to(gate_ref[...], (128, gate_ref.shape[1])).T[:, 0:1]
-    output_ref[...] = (stream_ref[...] + gate * result).astype(jnp.bfloat16)
-
-    def rest_tick(t, _):
-        red.tick(t, 2 + pairs, red.ticks)
-        return 0
-
-    lax.fori_loop(2 + pairs, red.ticks, rest_tick, 0)
+    result = dot_columns(dispatch_ref[...], result_home_ref[...].reshape(n_ex * padded, width))
+    gate = jnp.broadcast_to(gate_ref[...], (128, tokens)).T[:, 0:1]
+    r.output[...] = (r.stream[...] + gate * result).astype(jnp.bfloat16)
     red.finish()
     for h in range(pairs):
         do_spread.sent(h)
         aux_spread.sent(h)
 
 
-def attention_backward(
-    n_dp, n_ex, collective_id, upstream, stream, norm_gain, weight_in, weight_out, doc_row, doc_col, kept, routing
-):
-    rows, width = stream.shape
-    long, short, pairs = LONG_DEV, rows - LONG_DEV, width // 128
-    low = jnp.bfloat16
-    outs = [
-        jax.ShapeDtypeStruct((rows, width), jnp.float32),
-        jax.ShapeDtypeStruct((rows, width), low),
-        jax.ShapeDtypeStruct((rows, 3 * width), low),
-        jax.ShapeDtypeStruct((2, width), jnp.float32),
-        jax.ShapeDtypeStruct((rows, width), low),
-        jax.ShapeDtypeStruct((2 * (routing[5].shape[1] // width), width // n_dp, width), low),
+def middle(n_dp, n_ex, collective_id, near, staged, far):
+    arrays = {**near, **staged, **far}
+    a = types.SimpleNamespace(**arrays)
+    low, wide = jnp.bfloat16, jnp.float32
+    tokens, width = a.stream.shape
+    hidden = a.expert_in.shape[1]
+    mixed = a.attn_in.shape[2]
+    blocks, rows = hidden // width, width // n_dp
+    long, short, pairs = LONG_DEV, tokens - LONG_DEV, width // 128
+    _, padded = capacity_of(tokens, n_ex)
+    slots = n_ex * padded
+    group = min(max(4, 128 // padded), n_ex) * padded
+    slab = (n_ex, padded, width)
+    hops = (n_dp * n_ex).bit_length() - 1
+    outs = dict(
+        up_next=jax.ShapeDtypeStruct((tokens, width), wide),
+        up_low=jax.ShapeDtypeStruct((tokens, width), low),
+        mixed=jax.ShapeDtypeStruct((tokens, mixed), low),
+        sums=jax.ShapeDtypeStruct((2, width), wide),
+        attn_sums=jax.ShapeDtypeStruct((2, width), wide),
+        router_grad=jax.ShapeDtypeStruct((n_ex, width), wide),
+        stats=jax.ShapeDtypeStruct((n_ex, 128), wide),
+        output=jax.ShapeDtypeStruct((tokens, width), low),
+        chunks=jax.ShapeDtypeStruct((2 * blocks, rows, width), low),
+    )
+    scratch = []
+    for name in staged:
+        scratch += [pltpu.VMEM(arrays[name].shape, arrays[name].dtype), pltpu.SemaphoreType.DMA]
+    scratch += [pltpu.VMEM((blocks, width, width), low)] * 2 + [pltpu.SemaphoreType.DMA((2, blocks))]
+    scratch += [pltpu.VMEM(slab, low)] * 6
+    scratch += [
+        pltpu.VMEM((width, slots), low),
+        pltpu.VMEM((slots, width), low),
+        pltpu.VMEM((hidden, slots), low),
+        pltpu.VMEM((slots, hidden), low),
+        pltpu.VMEM((slots, tokens), low),
+        pltpu.VMEM((1, tokens), wide),
+        pltpu.VMEM((n_ex, 8, 128), wide),
+        pltpu.VMEM((n_ex, 8, 128), wide),
+        pltpu.VMEM((hops, n_ex, 128), wide),
+        pltpu.VMEM((hops, n_ex, 128), wide),
+        pltpu.VMEM((group, width), wide),
+        pltpu.VMEM((group, width), wide),
     ]
-    scratch = back_scratch(n_dp, pairs, long, short)
-    scratch += [pltpu.VMEM(routing[3].shape, low)] + [pltpu.SemaphoreType.DMA((n_ex,))] * 2
-    scratch += Reduction.scratch(n_dp, 1, width // n_dp, width, [((0, width), 0)])
-    inputs = (upstream, stream, norm_gain, weight_in, weight_out, doc_row, doc_col) + tuple(kept) + tuple(routing)
-    vmem = pl.BlockSpec(memory_space=pltpu.VMEM)
-    return pl.pallas_call(
-        functools.partial(attend_back_kernel, n_dp, n_ex),
-        out_shape=outs,
-        in_specs=[vmem] * len(inputs),
-        out_specs=[vmem] * (len(outs) - 1) + [pl.BlockSpec(memory_space=pl.ANY)],
+    scratch += [pltpu.SemaphoreType.DMA((n_ex,))] * 8 + [pltpu.SemaphoreType.DMA((hops,))] * 2
+    scratch += back_scratch(n_dp, pairs, long, short)
+    scratch += Reduction.scratch(n_dp, 1, rows, width, [((0, width), 0)])
+    vmem, anywhere = pl.BlockSpec(memory_space=pltpu.VMEM), pl.BlockSpec(memory_space=pl.ANY)
+    names = tuple(arrays) + tuple(outs)
+    values = pl.pallas_call(
+        functools.partial(middle_kernel, n_dp, n_ex, names, tuple(staged)),
+        out_shape=list(outs.values()),
+        in_specs=[vmem] * len(near) + [anywhere] * (len(staged) + len(far)),
+        out_specs=[vmem] * (len(outs) - 1) + [anywhere],
         scratch_shapes=scratch,
         compiler_params=pltpu.CompilerParams(
-            collective_id=collective_id, has_side_effects=True, vmem_limit_bytes=56 * 1024 * 1024
+            collective_id=collective_id, has_side_effects=True, vmem_limit_bytes=61 * 1024 * 1024
         ),
-        name="attention_backward",
-    )(*inputs)
+        name="middle",
+    )(*arrays.values())
+    return types.SimpleNamespace(**dict(zip(outs, values)))
 
 
 def tail_kernel(n_dp, n_ex, names, staged, *refs):
-    r = dict(zip(names, refs))
+    r = types.SimpleNamespace(**dict(zip(names, refs)))
     extra = iter(refs[len(names) :])
-    loads = {}
+    loads = types.SimpleNamespace()
     for name in staged:
         buffer, sem = next(extra), next(extra)
-        loads[name] = pltpu.make_async_copy(r[name], buffer, sem)
-        r[name] = buffer
+        setattr(loads, name, pltpu.make_async_copy(getattr(r, name), buffer, sem))
+        setattr(r, name, buffer)
     weights_in, weights_out, slopes, weight_sem = (next(extra) for _ in range(4))
     first_sem = next(extra)
     up_ref, acc_ref, dense_low_ref, dense_hidden_ref, first_low_ref, mixed_ref = (next(extra) for _ in range(6))
@@ -1135,29 +1170,29 @@
     me = links.me
     width = up_ref.shape[1]
     rows = width // n_dp
-    pairs, long = r["kv"].shape[1], r["kv"].shape[3]
-    blocks = r["dense_in"].shape[1] // width
+    pairs, long = r.kv.shape[1], r.kv.shape[3]
+    blocks = r.dense_in.shape[1] // width
     per_in = mixed_ref.shape[1] // width
 
     def block_loads(i):
         slot = lax.rem(i, 2)
         at = pl.ds(pl.multiple_of(i * width, width), width)
         return [
-            pltpu.make_async_copy(r["dense_out"].at[at, :], weights_out.at[slot], weight_sem.at[slot, 0]),
-            pltpu.make_async_copy(r["dense_in"].at[:, at], weights_in.at[slot], weight_sem.at[slot, 1]),
-            pltpu.make_async_copy(r["slope"].at[:, at], slopes.at[slot], weight_sem.at[slot, 2]),
+            pltpu.make_async_copy(r.dense_out.at[at, :], weights_out.at[slot], weight_sem.at[slot, 0]),
+            pltpu.make_async_copy(r.dense_in.at[:, at], weights_in.at[slot], weight_sem.at[slot, 1]),
+            pltpu.make_async_copy(r.slope.at[:, at], slopes.at[slot], weight_sem.at[slot, 2]),
         ]
 
     for i in range(min(2, blocks)):
         for load in block_loads(i):
             load.start()
     for name in staged:
-        loads[name].start()
+        getattr(loads, name).start()
     free, busy = blocks % 2, (blocks - 1) % 2
-    out_load = pltpu.make_async_copy(r["attn_out"].at[0], weights_out.at[free], first_sem.at[0])
+    out_load = pltpu.make_async_copy(r.attn_out.at[0], weights_out.at[free], first_sem.at[0])
     thirds = [weights_in.at[free], weights_in.at[busy], weights_out.at[busy]]
     in_loads = [
-        pltpu.make_async_copy(r["attn_in"].at[0, :, pl.ds(i * width, width)], third, first_sem.at[1 + i])
+        pltpu.make_async_copy(r.attn_in.at[0, :, pl.ds(i * width, width)], third, first_sem.at[1 + i])
         for i, third in enumerate(thirds)
     ]
 
@@ -1168,23 +1203,24 @@
         return lambda j, q: ref[q, 0]
 
     groups = [
-        (1, one(r["second_context_t"]), columns(r["second_low"])),
-        (per_in, one(r["second_normed_t"]), columns(r["second_mixed"])),
-        (blocks, lambda j, q: r["active_t"][q, j], lambda j: dense_low_ref[...]),
-        (blocks, one(r["dense_normed_t"]), columns(dense_hidden_ref)),
-        (1, one(r["first_context_t"]), columns(first_low_ref)),
-        (per_in, one(r["first_normed_t"]), columns(mixed_ref)),
+        (1, one(r.second_context_t), columns(r.second_low)),
+        (per_in, one(r.second_normed_t), columns(r.second_mixed)),
+        (blocks, lambda j, q: r.active_t[q, j], lambda j: dense_low_ref[...]),
+        (blocks, one(r.dense_normed_t), columns(dense_hidden_ref)),
+        (1, one(r.first_context_t), columns(first_low_ref)),
+        (per_in, one(r.first_normed_t), columns(mixed_ref)),
     ]
-    red_refs = list(extra) + [r["chunks"]]
+    red_refs = list(extra) + [r.chunks]
     red = Reduction(n_dp, n_ex, rows, groups, dense_lanes(width), red_refs)
     levels = [("dp", b) for b in range(n_dp.bit_length() - 1)] + [("ex", b) for b in range(n_ex.bit_length() - 1)]
     greet([red.peer(*level) for level in levels] + (links.peers()[1:] if links.chips > 2 else []))
 
-    up = r["up"][...]
+    up = r.up[...]
     dense_low_ref[...] = up.astype(jnp.bfloat16)
     acc_ref[...] = jnp.zeros_like(acc_ref)
-    for name in ("second_context_t", "second_low", "second_normed_t", "second_mixed"):
-        loads[name].wait()
+    ready = (loads.second_context_t, loads.second_low, loads.second_normed_t, loads.second_mixed)
+    for load in ready:
+        load.wait()
 
     def dense(i, _):
         slot = lax.rem(i, 2)
@@ -1215,13 +1251,13 @@
     for load in in_loads[1:]:
         load.start()
     for name in staged:
-        if not name.startswith("second"):
-            loads[name].wait()
-    unit, inverse = norm_parts(r["dense_x"][...])
+        if all(getattr(loads, name) is not load for load in ready):
+            getattr(loads, name).wait()
+    unit, inverse = norm_parts(r.dense_x[...])
     grad_normed = acc_ref[...]
-    up = up + norm_back(unit, inverse, r["dense_gain"][...], grad_normed)
+    up = up + norm_back(unit, inverse, r.dense_gain[...], grad_normed)
     up_ref[...] = up
-    small_send[0] = r["small"][...]
+    small_send[0] = r.small[...]
     small_send[0, 1:2] = jnp.sum(grad_normed * unit, axis=0, keepdims=True)
     small_send[0, 5:6] = jnp.sum(grad_normed, axis=0, keepdims=True)
     at_tick = blocks // 2
@@ -1231,7 +1267,7 @@
     first_low_ref[...] = up_low
     out_load.wait()
     grad_context = dot_rows(up_low, weights_out[free]).astype(jnp.bfloat16)
-    share_context(r["context"], r["lse"], grad_context, do_ref, aux_ref, short_do_ref, short_aux_ref, me, long)
+    share_context(r.context, r.lse, grad_context, do_ref, aux_ref, short_do_ref, short_aux_ref, me, long)
     do_spread = Spread(links, lambda b, p: do_ref.at[b, p], pairs, False, do_far, do_near, do_recv)
     aux_spread = Spread(links, lambda b, p: aux_ref.at[b, p], pairs, False, aux_far, aux_near, aux_recv)
     for h in range(pairs):
@@ -1239,8 +1275,8 @@
         aux_spread.send(h)
     red.tick(at_tick, at_tick, at_tick + 1)
     at_tick += 1
-    sequence = dict(
-        doc_row=r["doc_row"], doc_col=r["doc_col"], kv=r["kv"], q=r["q"], short_kv=r["short_kv"], short_q=r["short_q"],
+    sequence = types.SimpleNamespace(
+        doc_row=r.doc_row, doc_col=r.doc_col, kv=r.kv, q=r.q, short_kv=r.short_kv, short_q=r.short_q,
         do=do_ref, aux=aux_ref, short_do=short_do_ref, short_aux=short_aux_ref, dq=dq_ref, dk=dk_ref, dv=dv_ref,
         mixed=mixed_ref,
     )
@@ -1256,9 +1292,9 @@
     for i, third in enumerate(thirds):
         in_loads[i].wait()
         grad_normed = grad_normed + dot_rows(mixed_ref[:, i * width : (i + 1) * width], third[...])
-    unit, inverse = norm_parts(r["first_x"][...].astype(jnp.float32))
-    r["grad_tokens"][...] = (
-        up_ref[...] + norm_back(unit, inverse, r["first_gain"][...], grad_normed)
+    unit, inverse = norm_parts(r.first_x[...].astype(jnp.float32))
+    r.grad_tokens[...] = (
+        up_ref[...] + norm_back(unit, inverse, r.first_gain[...], grad_normed)
     ).astype(jnp.bfloat16)
     small_send[0, 0:1] = jnp.sum(grad_normed * unit, axis=0, keepdims=True)
     small_send[0, 4:5] = jnp.sum(grad_normed, axis=0, keepdims=True)
@@ -1287,7 +1323,7 @@
                     small_send[i] = value
                     small_copy(i).start()
                 else:
-                    r["small_sum"][...] = value
+                    r.small_sum[...] = value
 
         return 0
 
@@ -1298,24 +1334,21 @@
         aux_spread.sent(h)
 
 
-def tail(n_dp, n_ex, collective_id, arrays):
-    staged = (
-        "second_context_t", "second_low", "second_normed_t", "second_mixed", "active_t", "dense_normed_t", "dense_x",
-        "kv", "q", "short_kv", "short_q", "context", "first_x", "first_context_t", "first_normed_t",
-    )
-    far = staged + ("dense_in", "dense_out", "slope", "attn_in", "attn_out")
+def tail(n_dp, n_ex, collective_id, near, staged, far):
+    arrays = {**near, **staged, **far}
+    a = types.SimpleNamespace(**arrays)
     low, wide = jnp.bfloat16, jnp.float32
-    tokens, width = arrays["up"].shape
-    hidden = arrays["dense_in"].shape[1]
-    mixed = arrays["attn_in"].shape[2]
+    tokens, width = a.up.shape
+    hidden = a.dense_in.shape[1]
+    mixed = a.attn_in.shape[2]
     rows = width // n_dp
     long, short, pairs = LONG_DEV, tokens - LONG_DEV, width // 128
     chunks = 2 * (hidden // width) + 2 * (1 + mixed // width)
-    small = arrays["small"].shape
+    small = a.small.shape
     outs = dict(
-        chunks=jax.ShapeDtypeStruct((chunks, rows, width), low),
         grad_tokens=jax.ShapeDtypeStruct((tokens, width), low),
         small_sum=jax.ShapeDtypeStruct(small, wide),
+        chunks=jax.ShapeDtypeStruct((chunks, rows, width), low),
     )
     scratch = []
     for name in staged:
@@ -1332,10 +1365,10 @@
     vmem, anywhere = pl.BlockSpec(memory_space=pltpu.VMEM), pl.BlockSpec(memory_space=pl.ANY)
     names = tuple(arrays) + tuple(outs)
     return pl.pallas_call(
-        functools.partial(tail_kernel, n_dp, n_ex, names, staged),
+        functools.partial(tail_kernel, n_dp, n_ex, names, tuple(staged)),
         out_shape=list(outs.values()),
-        in_specs=[anywhere if name in far else vmem for name in arrays],
-        out_specs=[anywhere if name == "chunks" else vmem for name in outs],
+        in_specs=[vmem] * len(near) + [anywhere] * (len(staged) + len(far)),
+        out_specs=[vmem] * (len(outs) - 1) + [anywhere],
         scratch_shapes=scratch,
         compiler_params=pltpu.CompilerParams(
             collective_id=collective_id, has_side_effects=True, vmem_limit_bytes=61 * 1024 * 1024
@@ -1377,72 +1410,94 @@
         n_dp, n_ex, 3, stream_two, gains[2:3], shifts[2:3], weights_in[1], weights_out[1], doc_row, doc_col,
         (assign_row, cotangent[0]),
     )
-    (
-        upstream, fourth_sums, router_grad, rows_t, expert_back, expert_active_t, expert_hidden, result, gate, stats
-    ) = mixture(
-        n_dp, n_ex, 6, stream_three, gains[3:4], shifts[3:4], router.T, assign_row, cotangent[0], far_cot,
-        expert_in[0], expert_out[0],
+    model_width = tokens.shape[2]
+    rows = model_width // n_dp
+    mid = middle(
+        n_dp,
+        n_ex,
+        4,
+        dict(
+            stream=stream_three,
+            gain=gains[3:4],
+            shift=shifts[3:4],
+            router=router.T,
+            assign=assign_row,
+            cot=cotangent[0],
+            far_cot=far_cot,
+            attn_gain=gains[2:3],
+            doc_row=doc_row,
+            doc_col=doc_col,
+            lse=kept_three[7],
+        ),
+        dict(
+            attn_x=stream_two,
+            context=kept_three[1],
+            kv=kept_three[3],
+            q=kept_three[4],
+            short_kv=kept_three[5],
+            short_q=kept_three[6],
+        ),
+        dict(
+            expert_in=expert_in[0],
+            expert_out=expert_out[0],
+            attn_in=weights_in,
+            attn_out=weights_out,
+        ),
     )
     everyone = row_count * n_dp * n_ex
+    stats = mid.stats
     balance = n_ex * jnp.sum((stats[:, 0] / everyone - 1.0 / n_ex) * (stats[:, 1] / everyone))
-    model_width = tokens.shape[2]
-    rows = model_width // n_dp
-    expert_factors = (
-        rows_t.reshape(n_dp, 1, rows, -1),
-        expert_hidden,
-        expert_active_t.reshape(n_dp, -1, rows, expert_hidden.shape[0]),
-        expert_back.reshape(-1, model_width),
-    )
-    upstream, second_low, second_mixed, second_sums, output, expert_chunks = attention_backward(
-        n_dp, n_ex, 4, upstream, stream_two, gains[2:3], weights_in[1], weights_out[1], doc_row, doc_col,
-        kept_three[1:2] + kept_three[3:], (assign_row, gate, stream_three, result) + expert_factors,
-    )
-    output = output[None]
+    output = mid.output[None]
+    second_sums, fourth_sums = mid.attn_sums, mid.sums
 
     def blocks_of(rows_t):
         return rows_t.reshape(n_dp, -1, rows, row_count)
 
     none = jnp.zeros((2, model_width), jnp.float32)
     small = jnp.concatenate(
-        [none, second_sums[0:1], fourth_sums[0:1], none, second_sums[1:2], fourth_sums[1:2], router_grad], axis=0
+        [none, second_sums[0:1], fourth_sums[0:1], none, second_sums[1:2], fourth_sums[1:2], mid.router_grad], axis=0
     )
-    chunks, grad_tokens, small = tail(
+    grad_tokens, small, chunks = tail(
         n_dp,
         n_ex,
         5,
         dict(
-            up=upstream,
-            dense_x=stream_one,
+            up=mid.up_next,
             dense_gain=gains[1:2],
             first_gain=gains[0:1],
-            dense_in=ffn_in,
-            dense_out=ffn_out,
-            slope=slope,
-            first_x=tokens[0],
-            attn_in=weights_in,
-            attn_out=weights_out,
             doc_row=doc_row,
             doc_col=doc_col,
+            lse=kept_one[7],
+            small=small,
+        ),
+        dict(
+            dense_x=stream_one,
+            first_x=tokens[0],
             context=kept_one[1],
             kv=kept_one[3],
             q=kept_one[4],
             short_kv=kept_one[5],
             short_q=kept_one[6],
-            lse=kept_one[7],
             second_context_t=blocks_of(kept_three[2]),
             second_normed_t=blocks_of(kept_three[0]),
             active_t=blocks_of(active_t),
             dense_normed_t=blocks_of(dense_normed_t),
             first_context_t=blocks_of(kept_one[2]),
             first_normed_t=blocks_of(kept_one[0]),
-            second_low=second_low,
-            second_mixed=second_mixed,
-            small=small,
+            second_low=mid.up_low,
+            second_mixed=mid.mixed,
+        ),
+        dict(
+            dense_in=ffn_in,
+            dense_out=ffn_out,
+            slope=slope,
+            attn_in=weights_in,
+            attn_out=weights_out,
         ),
     )
     grad_tokens = grad_tokens[None]
     attn_in_sum, attn_out_sum, ffn_in_sum, ffn_out_sum, expert_in_sum, expert_out_sum = unpack(
-        chunks, expert_chunks, attn_in.shape[2] // model_width, ffn_in.shape[1] // model_width
+        chunks, mid.chunks, attn_in.shape[2] // model_width, ffn_in.shape[1] // model_width
     )
     small = lax.dynamic_slice_in_dim(small, lax.axis_index("dp") * rows, rows, 1).T
     summed = [

time: 398 us -> 382 us (0.960)
  Pallas kernels: 362 us -> 341 us
  local copies, waits for them, and re-layouts: 27.3 us -> 32.9 us
    pallas_call x3 -> x2, Pallas kernels: 290 us -> 271 us  [the longest x1 153 us: tail(): pl.pallas_call(functools.partial(tail_kernel, n_dp, n_ex, names, tuple(st...]
    unnamed x76 -> x74, local copies, waits for them, and re-layouts: 16.8 us -> 20.8 us
where the time goes in v5:
time: 382 us; the launch traced here: 378 us
  Pallas kernels  341 us (89%)
  local copies, waits for them, and re-layouts  32.9 us (9%)
    pallas_call x1, Pallas kernels, tail(): pl.pallas_call(functools.partial(tail_kernel, n_dp, n_ex, names, tuple(st...  153 us
    pallas_call x1, Pallas kernels, middle(): pl.pallas_call(functools.partial(middle_kernel, n_dp, n_ex, names, tuple(...  118 us
    pallas_call x2, Pallas kernels, attention_forward(): pl.pallas_call(functools.partial(attend_kernel, n_dp, n_ex, len(inputs)),...  55.4 us
    unnamed x74, local copies, waits for them, and re-layouts  20.8 us
    pallas_call x1, Pallas kernels, ffn_forward(): pl.pallas_call(ffn_kernel, grid=(hidden // width,), out_shape=[jax.ShapeD...  9.55 us

profile of v5, /device:TPU:0, one launch (start us, length us, event | category | flops | bytes accessed | tf_op | source)
XLA Modules:
  0.0 378.0 jit_solution(12060441660591970520)
XLA Ops:
  0.6 1.5 fusion.1
  2.1 0.0 copy-start.22
  2.1 0.0 copy-start.29
  2.1 4.0 %copy.39 = bf16[768,2,2304]{2,0,1:T(8,128)(2,1)S(1)} copy(bf16[768,2,2304]{2,1,0:T(2,128)(2,1)} %param.18) | data formatting | bytes 14155776 | tf_op args[5]
  6.2 0.0 copy-start.27
  6.2 0.0 copy-done.29
  6.2 0.3 copy.40
  6.5 0.0 copy-start.28
  6.5 3.8 slice_bitcast_fusion
  10.3 1.0 copy-done.27
  11.3 0.8 copy-done.28
  12.0 1.2 slice_bitcast_fusion.2
  13.2 0.0 copy-done.34
  13.2 0.2 reduce-window.8
  13.4 0.1 convert_reduce_fusion
  13.5 0.1 copy.33.refs_6_.refs_9_.refs_4_
  13.6 0.0 copy-done.30
  13.6 0.1 bitcast_convert_fusion.refs_0_
  13.7 0.0 copy-done.20
  13.7 26.0 %attention_forward.2 = (f32[384,768]{1,0:T(8,128)S(1)}, bf16[768,384]{1,0:T(8,128)(2,1)S(1)}, bf16[384,768]{1,0:T(8,128)(2,1)S(1)}, bf16[768,384]{1,0:T(8,128)(2...) custom-call(f32[384,768]{1,0:T(8,128)S(1)} %bitcast_convert_fusion.r, ...), custom_call_target="tpu_custom_call" | custom-call | tf_op jit(solution)/shard_map/attention_forward/pallas_call | solution.py:515
  39.7 0.0 copy-start.9
  39.7 0.9 copy-done.9
  40.6 0.8 copy-done.16
  41.3 0.7 copy-done.18
  42.0 0.6 copy-done.23
  42.6 0.0 copy-done.21
  42.6 0.0 copy-start.5
  42.6 0.0 copy-start.26
  42.6 9.5 %ffn_forward.1 = (f32[384,768]{1,0:T(8,128)S(1)}, bf16[768,384]{1,0:T(8,128)(2,1)S(1)}, bf16[3072,384]{1,0:T(8,128)(2,1)S(1)}, bf16[384,3072]{1,0:T(8,128)(2,1)}) custom-call(f32[384,768]{1,0:T(8,128)S(1)} %get-tuple-element.57.x_ref.refs_7_, f32[1,768]{1,0:T(1,128)S(1)} %get-tuple-element.117.gain_ref.refs_1_, f32[1,768]{1,0:T(1,128)S(1)} %get-tuple-element.106.shift_ref, ...), custom_call_target="tpu_custom_call" | custom-call | tf_op jit(solution)/shard_map/ffn_forward/pallas_call | solution.py:144
  52.2 0.0 copy-done
  52.2 0.0 copy-done.10
  52.2 0.0 copy-done.11
  52.2 0.0 copy-start.3
  52.2 1.4 copy-done.3
  53.6 0.0 copy-done.22
  53.6 0.0 copy-done.25
  53.6 0.0 copy-done.6
  53.6 0.0 copy-done.5
  53.6 0.0 copy-done.26
  53.6 29.4 %attention_forward.3 = (f32[384,768]{1,0:T(8,128)S(1)}, bf16[768,384]{1,0:T(8,128)(2,1)S(1)}, bf16[384,768]{1,0:T(8,128)(2,1)S(1)}, bf16[768,384]{1,0:T(8,128)(2...) custom-call(f32[384,768]{1,0:T(8,128)S(1)} %get-tuple-element.58.ref, ...), custom_call_target="tpu_custom_call" | custom-call | tf_op jit(solution)/shard_map/attention_forward/pallas_call | solution.py:515
  83.0 0.0 copy-done.2
  83.1 0.0 copy-start.7
  83.1 1.0 copy-done.7
  84.1 0.9 copy-done.8
  85.0 0.8 copy-done.13
  85.8 0.9 copy-done.14
  86.7 0.8 copy-done.15
  87.5 0.8 copy-done.17
  88.2 0.7 copy-done.19
  88.9 0.6 copy-done.24
  89.5 117.7 %middle.1 = (f32[384,768]{1,0:T(8,128)}, bf16[384,768]{1,0:T(8,128)(2,1)}, bf16[384,2304]{1,0:T(8,128)(2,1)}, f32[2,768]{1,0:T(2,128)}, f32[2,768]{1,0:T(2,128)}...) custom-call(f32[384,768]{1,0:T(8,128)} %copy-done.7, ...), custom_call_target="tpu_custom_call" | custom-call | tf_op jit(solution)/shard_map/middle/pallas_call | solution.py:1141
  207.2 0.8 fusion.3
  208.0 0.8 fusion.4
  208.8 2.0 concatenate.3.refs_6_
  210.8 153.2 %tail.1 = (bf16[384,768]{1,0:T(8,128)(2,1)}, f32[16,768]{1,0:T(8,128)}, bf16[16,192,768]{2,1,0:T(8,128)(2,1)}) custom-call(f32[384,768]{1,0:T(8,128)} %get-tuple-element.69.refs_0_, f32[1,768]{1,0:T(1,128)} %copy-done.21, f32[1,768]{1,0:T(1,128)} %copy-done.20, s32[1,128]{1,0:T(1,128)} %bitcast.52, s32[128,1]{1,0:T(8,128)} %copy-done.6, ...), custom_call_target="tpu_custom_call" | custom-call | tf_op jit(solution)/shard_map/tail/pallas_call | solution.py:1367
  364.0 2.3 copy-done.1
  366.3 5.4 %unpack.1 = (f32[192,2,2304]{2,1,0:T(2,128)}, f32[192,2,768]{2,1,0:T(2,128)}, f32[192,3072]{1,0:T(8,128)}, f32[4,192,768]{2,1,0:T(8,128)}, f32[192,3072]{1,0:T(8,128)}, /*index=5*/f32[4,192,768]{2,1,0:T(8,128)}) custom-call(bf16[16,192,768]{2,1,0:T(8,128)(2,1)S(1)} %copy-done.1, bf16[8,192,768]{2,1,0:T(8,128)(2,1)S(1)} %copy-done.4), custom_call_target="tpu_custom_call" | custom-call | tf_op jit(solution)/shard_map/unpack/pallas_call | solution.py:64
  371.7 0.8 dynamic-slice_bitcast_fusion
  372.5 0.6 fusion
  373.1 0.6 slice.97
  373.7 0.0 copy-done.33
  373.7 0.7 multiply_reduce_fusion
  375.1 0.8 copy.43
  375.9 0.8 copy.44
  (31 shorter events, 0.1 us)
Async XLA Ops:
  2.1 11.6 %copy-start.20 = (f32[1,768]{1,0:T(1,128)}, f32[1,768]{1,0:T(1,128)S(1)}, u32[]{:S(2)}) copy-start(f32[1,768]{1,0:T(1,128)S(1)} %get-tuple-element.116.refs_1_.refs_2_) | copy-start | bytes 9220
  2.1 40.5 %copy-start.21 = (f32[1,768]{1,0:T(1,128)}, f32[1,768]{1,0:T(1,128)S(1)}, u32[]{:S(2)}) copy-start(f32[1,768]{1,0:T(1,128)S(1)} %get-tuple-element.117.gain_ref.refs_1_) | copy-start | bytes 9220
  2.1 51.5 %copy-start.22 = (f32[1,768]{1,0:T(1,128)}, f32[1,768]{1,0:T(1,128)S(1)}, u32[]{:S(2)}) copy-start(f32[1,768]{1,0:T(1,128)S(1)} %get-tuple-element.118.refs_1_.refs_7_) | copy-start | bytes 9220
  2.1 4.1 %copy-start.29 = (bf16[768,2,768]{2,1,0:T(2,128)(2,1)S(1)}, bf16[768,2,768]{2,1,0:T(2,128)(2,1)}, u32[]{:S(2)}) copy-start(bf16[768,2,768]{2,1,0:T(2,128)(2,1)} %param.19) | copy-start | bytes 7077892
  6.2 5.1 %copy-start.27 = (bf16[768,2,2304]{2,0,1:T(8,128)(2,1)}, bf16[768,2,2304]{2,0,1:T(8,128)(2,1)S(1)}, u32[]{:S(2)}) copy-start(bf16[768,2,2304]{2,0,1:T(8,128)(2,1)S(1)} %copy.39) | copy-start | bytes 21233668
  6.5 5.5 %copy-start.28 = (bf16[768,2,768]{2,0,1:T(8,128)(2,1)}, bf16[768,2,768]{2,0,1:T(8,128)(2,1)S(1)}, u32[]{:S(2)}) copy-start(bf16[768,2,768]{2,0,1:T(8,128)(2,1)S(1)} %copy.40) | copy-start | bytes 7077892
  12.0 1.2 copy-start.34
  12.0 1.6 copy-start.30
  13.5 40.1 %copy-start.25 = (s32[128]{0:T(128)}, s32[128]{0:T(128)S(1)}, u32[]{:S(2)}) copy-start(s32[128]{0:T(128)S(1)} %convert_reduce_fusion) | copy-start | bytes 1540
  13.6 40.0 %copy-start.6 = (s32[128,1]{1,0:T(8,128)}, s32[128,1]{1,0:T(8,128)S(1)}, u32[]{:S(2)}) copy-start(s32[128,1]{1,0:T(8,128)S(1)} %copy.33.refs_6_.refs_9_.refs_4_) | copy-start | bytes 1540
  39.7 0.9 copy-start.9
  40.6 0.8 copy-start.16
  41.3 0.7 copy-start.18
  42.0 0.6 copy-start.23
  42.6 9.6 %copy-start = (f32[384,768]{1,0:T(8,128)}, f32[384,768]{1,0:T(8,128)S(1)}, u32[]{:S(2)}) copy-start(f32[384,768]{1,0:T(8,128)S(1)} %get-tuple-element.57.x_ref.refs_7_) | copy-start | bytes 3538948
  42.6 9.6 %copy-start.10 = (bf16[384,768]{1,0:T(8,128)(2,1)}, bf16[384,768]{1,0:T(8,128)(2,1)S(1)}, u32[]{:S(2)}) copy-start(bf16[384,768]{1,0:T(8,128)(2,1)S(1)} %get-tuple-element.74.refs_9_) | copy-start | bytes 1769476
  42.6 9.6 %copy-start.11 = (bf16[768,384]{1,0:T(8,128)(2,1)}, bf16[768,384]{1,0:T(8,128)(2,1)S(1)}, u32[]{:S(2)}) copy-start(bf16[768,384]{1,0:T(8,128)(2,1)S(1)} %get-tuple-element.83) | copy-start | bytes 1769476
  42.6 11.0 %copy-start.5 = (bf16[1,384,768]{2,1,0:T(8,128)(2,1)S(1)}, bf16[1,384,768]{2,1,0:T(8,128)(2,1)}, u32[]{:S(2)}) copy-start(bf16[1,384,768]{2,1,0:T(8,128)(2,1)} %param.25) | copy-start | bytes 1769476
  42.6 11.0 %copy-start.26 = (s32[1,384,1]{1,2,0:T(1,128)S(1)}, s32[1,384,1]{1,2,0:T(1,128)}, u32[]{:S(2)}) copy-start(s32[1,384,1]{1,2,0:T(1,128)} %param.15) | copy-start | bytes 4612
  52.2 1.4 copy-start.3
  53.6 29.4 %copy-start.2 = (f32[384,768]{1,0:T(8,128)}, f32[384,768]{1,0:T(8,128)S(1)}, u32[]{:S(2)}) copy-start(f32[384,768]{1,0:T(8,128)S(1)} %get-tuple-element.58.refs_0_.refs_11_) | copy-start | bytes 3538948
  53.6 29.4 %copy-start.12 = (bf16[768,384]{1,0:T(8,128)(2,1)}, bf16[768,384]{1,0:T(8,128)(2,1)S(1)}, u32[]{:S(2)}) copy-start(bf16[768,384]{1,0:T(8,128)(2,1)S(1)} %get-tuple-element.82) | copy-start | bytes 1769476
  83.1 1.0 copy-start.7
  84.1 0.9 copy-start.8
  85.0 0.8 copy-start.13
  85.8 0.9 copy-start.14
  86.7 0.8 copy-start.15
  87.5 0.8 copy-start.17
  88.2 0.7 copy-start.19
  88.9 0.6 copy-start.24
  210.8 153.2 %copy-start.4 = (bf16[8,192,768]{2,1,0:T(8,128)(2,1)S(1)}, bf16[8,192,768]{2,1,0:T(8,128)(2,1)}, u32[]{:S(2)}) copy-start(bf16[8,192,768]{2,1,0:T(8,128)(2,1)} %get-tuple-element.91.expert_ref) | copy-start | bytes 7077892
  364.0 2.3 copy-start.1
  366.3 7.4 %copy-start.33 = (f32[8,128]{1,0:T(8,128)S(1)}, f32[8,128]{1,0:T(8,128)}, u32[]{:S(2)}) copy-start(f32[8,128]{1,0:T(8,128)} %get-tuple-element.68) | copy-start | bytes 12292
  366.3 8.7 %copy-start.31 = (bf16[384,768]{1,0:T(8,128)(2,1)S(1)}, bf16[384,768]{1,0:T(8,128)(2,1)}, u32[]{:S(2)}) copy-start(bf16[384,768]{1,0:T(8,128)(2,1)} %get-tuple-element.67) | copy-start | bytes 1769476
  366.3 9.6 %copy-start.32 = (bf16[384,768]{1,0:T(8,128)(2,1)S(1)}, bf16[384,768]{1,0:T(8,128)(2,1)}, u32[]{:S(2)}) copy-start(bf16[384,768]{1,0:T(8,128)(2,1)} %get-tuple-element.88) | copy-start | bytes 1769476

commit v6 on v5

--- a/solution.py
+++ b/solution.py
@@ -120,55 +120,6 @@
     )
 
 
-def ffn_kernel(x_ref, gain_ref, shift_ref, w_in_ref, w_out_ref, next_ref, normed_t_ref, active_t_ref, slope_ref, normed_ref):
-    @pl.when(pl.program_id(0) == 0)
-    def _():
-        x = x_ref[...]
-        unit, _ = norm_parts(x)
-        normed = (unit * gain_ref[...] + shift_ref[...]).astype(jnp.bfloat16)
-        normed_ref[...] = normed
-        normed_t_ref[...] = normed.T
-        next_ref[...] = x
-
-    active, slope = gelu_parts(dot(normed_ref[...], w_in_ref[...]))
-    active = active.astype(jnp.bfloat16)
-    slope_ref[...] = slope.astype(jnp.bfloat16)
-    active_t_ref[...] = active.T
-    next_ref[...] += dot(active, w_out_ref[...])
-
-
-def ffn_forward(stream, norm_gain, norm_shift, weight_in, weight_out):
-    rows, width = stream.shape
-    hidden = weight_in.shape[1]
-    low = jnp.bfloat16
-    return pl.pallas_call(
-        ffn_kernel,
-        grid=(hidden // width,),
-        out_shape=[
-            jax.ShapeDtypeStruct((rows, width), jnp.float32),
-            jax.ShapeDtypeStruct((width, rows), low),
-            jax.ShapeDtypeStruct((hidden, rows), low),
-            jax.ShapeDtypeStruct((rows, hidden), low),
-        ],
-        in_specs=[
-            pl.BlockSpec((rows, width), lambda i: (0, 0)),
-            pl.BlockSpec((1, width), lambda i: (0, 0)),
-            pl.BlockSpec((1, width), lambda i: (0, 0)),
-            pl.BlockSpec((width, width), lambda i: (0, i)),
-            pl.BlockSpec((width, width), lambda i: (i, 0)),
-        ],
-        out_specs=[
-            pl.BlockSpec((rows, width), lambda i: (0, 0)),
-            pl.BlockSpec((width, rows), lambda i: (0, 0)),
-            pl.BlockSpec((width, rows), lambda i: (i, 0)),
-            pl.BlockSpec((rows, width), lambda i: (0, i)),
-        ],
-        scratch_shapes=[pltpu.VMEM((rows, width), low)],
-        compiler_params=pltpu.CompilerParams(vmem_limit_bytes=48 * 1024 * 1024),
-        name="ffn_forward",
-    )(stream, norm_gain, norm_shift, weight_in, weight_out)
-
-
 def capacity_of(rows, experts):
     capacity = (5 * rows + 4 * experts - 1) // (4 * experts)
     return capacity, -(-capacity // 16) * 16
@@ -367,114 +318,6 @@
                 use(block)
 
 
-def attend_kernel(
-    n_dp, n_ex, inputs, *refs
-):
-    (x_ref, gain_ref, shift_ref, w_in_ref, w_out_ref, doc_row_ref, doc_col_ref), rest = refs[:7], refs[7:]
-    if inputs > 7:
-        (assign_ref, cot_ref), rest = rest[:2], rest[2:]
-    (
-        next_ref, normed_t_ref, context_ref, context_t_ref, kv_ref, q_ref, short_kv_ref, short_q_ref, lse_ref,
-    ), rest = rest[:9], rest[9:]
-    if inputs > 7:
-        (far_cot_ref,), rest = rest[:1], rest[1:]
-    (acc_ref, top_ref, total_ref, kv_far, kv_near, kv_recv, q_far, q_near, q_recv), rest = rest[:9], rest[9:]
-    links = Links(n_dp)
-    me = links.me
-    pairs, long = kv_ref.shape[1], kv_ref.shape[3]
-    width = x_ref.shape[1]
-    x = x_ref[...]
-    center = x - jnp.mean(x, axis=-1, keepdims=True)
-    inverse = lax.rsqrt(jnp.mean(center * center, axis=-1, keepdims=True) + epsilon)
-    normed = (center * inverse * gain_ref[...] + shift_ref[...]).astype(jnp.bfloat16)
-
-    kv = dot(normed, w_in_ref[:, width:]).astype(jnp.bfloat16)
-    for h in range(pairs):
-        for part in range(2):
-            piece = kv[:, part * width + 128 * h : part * width + 128 * h + 128]
-            kv_ref[me, h, part] = piece[:long]
-            short_kv_ref[h, part] = piece[long:]
-    greet(links.peers() + (across_peers(n_ex) if inputs > 7 else []))
-    kv_spread = Spread(links, lambda b, p: kv_ref.at[b, p], pairs, True, kv_far, kv_near, kv_recv)
-    q_spread = Spread(links, lambda b, p: q_ref.at[b], 1, False, q_far, q_near, q_recv)
-    for h in range(pairs):
-        kv_spread.send(h)
-    q = (dot(normed, w_in_ref[:, :width]).astype(jnp.bfloat16) * HEAD_DIM ** (-0.5)).astype(jnp.bfloat16)
-    for h in range(pairs):
-        piece = q[:, 128 * h : 128 * h + 128]
-        q_ref[me, h] = piece[:long]
-        short_q_ref[h] = piece[long:]
-    q_spread.send(0)
-    if inputs > 7:
-        cot_send_ref, cot_send_sem, cot_recv_sem = rest
-        cot_send_ref[...] = dot(dispatch_of(assign_ref[...], n_ex), cot_ref[...]).astype(jnp.bfloat16).reshape(
-            cot_send_ref.shape
-        )
-        cot_across = Across(n_ex, cot_send_ref, far_cot_ref, cot_send_sem, cot_recv_sem)
-        cot_across.start_all()
-        far_cot_ref[links.expert] = cot_send_ref[links.expert]
-    normed_t_ref[...] = normed.T
-
-    def put_context(h, rows_t, first, count):
-        at = pl.ds(pl.multiple_of(128 * h, 128), 128)
-        context_t_ref[at, first : first + count] = rows_t.astype(jnp.bfloat16)
-        context_ref[first : first + count, at] = rows_t.T.astype(jnp.bfloat16)
-
-    def own_part(h, _):
-        seen = short_seen(doc_row_ref[...], doc_col_ref[...])
-        scores = jnp.where(seen, dot_rows(short_kv_ref[h, 0], head_pair(short_q_ref[h])), masked_score)
-        top = jnp.max(scores, axis=0, keepdims=True)
-        weights = jnp.exp(scores - top)
-        total = jnp.sum(weights, axis=0, keepdims=True)
-        rows_t = pair_rows(dot_columns(short_kv_ref[h, 1], weights.astype(jnp.bfloat16)) / total)
-        short = rows_t.shape[1]
-        put_context(h, rows_t, long, short)
-        lse = top + jnp.log(total)
-        lse_ref[h, 0:1, long:] = lse[:, :short]
-        lse_ref[h, 1:2, long:] = lse[:, short:]
-        scores = jnp.where(causal(long, long), dot_rows(kv_ref[me, h, 0], head_pair(q_ref[me, h])), masked_score)
-        top = jnp.max(scores, axis=0, keepdims=True)
-        weights = jnp.exp(scores - top)
-        top_ref[h] = top
-        total_ref[h] = jnp.sum(weights, axis=0, keepdims=True)
-        acc_ref[h] = dot_columns(kv_ref[me, h, 1], weights.astype(jnp.bfloat16))
-        return 0
-
-    lax.fori_loop(0, pairs, own_part, 0)
-
-    def other_part(h, _):
-        kv_spread.relay(h)
-        queries = head_pair(q_ref[me, h])
-
-        def use(block):
-            scores = dot_rows(kv_ref[block, h, 0], queries)
-            old = top_ref[h]
-            top = jnp.maximum(old, jnp.max(scores, axis=0, keepdims=True))
-            factor = jnp.exp(old - top)
-            weights = jnp.exp(scores - top)
-            top_ref[h] = top
-            total_ref[h] = total_ref[h] * factor + jnp.sum(weights, axis=0, keepdims=True)
-            acc_ref[h] = acc_ref[h] * factor + dot_columns(kv_ref[block, h, 1], weights.astype(jnp.bfloat16))
-
-        kv_spread.each(h, use)
-        total = total_ref[h]
-        put_context(h, pair_rows(acc_ref[h] / total), 0, long)
-        lse = top_ref[h] + jnp.log(total)
-        lse_ref[h, 0:1, :long] = lse[:, :long]
-        lse_ref[h, 1:2, :long] = lse[:, long:]
-        return 0
-
-    lax.fori_loop(0, pairs, other_part, 0)
-    next_ref[...] = x + dot(context_ref[...], w_out_ref[...])
-    q_spread.relay(0)
-    q_spread.each(0, lambda block: None)
-    q_spread.sent(0)
-    for h in range(pairs):
-        kv_spread.sent(h)
-    if inputs > 7:
-        cot_across.wait_all()
-
-
 def spread_sems(n_dp, parts):
     return [
         pltpu.SemaphoreType.DMA((n_dp // 2, parts)),
@@ -483,46 +326,284 @@
     ]
 
 
-def attention_forward(
-    n_dp, n_ex, collective_id, stream, norm_gain, norm_shift, weight_in, weight_out, doc_row, doc_col, routing=()
-):
-    rows, width = stream.shape
-    long, short, pairs = LONG_DEV, rows - LONG_DEV, width // 128
+def attend(n_dp, links, s, x, gain, shift, w_in, w_out, doc_row, doc_col, ready, between):
+    me = links.me
+    pairs, long, width = s.kv.shape[1], s.kv.shape[3], x.shape[1]
+    unit, _ = norm_parts(x)
+    normed = (unit * gain + shift).astype(jnp.bfloat16)
+    ready(0)
+    kv = dot(normed, w_in[:, width:]).astype(jnp.bfloat16)
+    for h in range(pairs):
+        for part in range(2):
+            piece = kv[:, part * width + 128 * h : part * width + 128 * h + 128]
+            s.kv[me, h, part] = piece[:long]
+            s.short_kv[h, part] = piece[long:]
+    kv_spread = Spread(links, lambda b, p: s.kv.at[b, p], pairs, True, *s.kv_sems)
+    q_spread = Spread(links, lambda b, p: s.q.at[b], 1, False, *s.q_sems)
+    for h in range(pairs):
+        kv_spread.send(h)
+    ready(1)
+    q = (dot(normed, w_in[:, :width]).astype(jnp.bfloat16) * HEAD_DIM ** (-0.5)).astype(jnp.bfloat16)
+    for h in range(pairs):
+        piece = q[:, 128 * h : 128 * h + 128]
+        s.q[me, h] = piece[:long]
+        s.short_q[h] = piece[long:]
+    q_spread.send(0)
+    between()
+    s.normed_t[...] = normed.T
+
+    def put_context(h, rows_t, first, count):
+        at = pl.ds(pl.multiple_of(128 * h, 128), 128)
+        s.context_t[at, first : first + count] = rows_t.astype(jnp.bfloat16)
+        s.context[first : first + count, at] = rows_t.T.astype(jnp.bfloat16)
+
+    def own_part(h, _):
+        seen = short_seen(doc_row, doc_col)
+        scores = jnp.where(seen, dot_rows(s.short_kv[h, 0], head_pair(s.short_q[h])), masked_score)
+        top = jnp.max(scores, axis=0, keepdims=True)
+        weights = jnp.exp(scores - top)
+        total = jnp.sum(weights, axis=0, keepdims=True)
+        rows_t = pair_rows(dot_columns(s.short_kv[h, 1], weights.astype(jnp.bfloat16)) / total)
+        short = rows_t.shape[1]
+        put_context(h, rows_t, long, short)
+        lse = top + jnp.log(total)
+        s.lse[h, 0:1, long:] = lse[:, :short]
+        s.lse[h, 1:2, long:] = lse[:, short:]
+        scores = jnp.where(causal(long, long), dot_rows(s.kv[me, h, 0], head_pair(s.q[me, h])), masked_score)
+        top = jnp.max(scores, axis=0, keepdims=True)
+        weights = jnp.exp(scores - top)
+        s.top[h] = top
+        s.total[h] = jnp.sum(weights, axis=0, keepdims=True)
+        s.acc[h] = dot_columns(s.kv[me, h, 1], weights.astype(jnp.bfloat16))
+        return 0
+
+    lax.fori_loop(0, pairs, own_part, 0)
+
+    def other_part(h, _):
+        kv_spread.relay(h)
+        queries = head_pair(s.q[me, h])
+
+        def use(block):
+            scores = dot_rows(s.kv[block, h, 0], queries)
+            old = s.top[h]
+            top = jnp.maximum(old, jnp.max(scores, axis=0, keepdims=True))
+            factor = jnp.exp(old - top)
+            weights = jnp.exp(scores - top)
+            s.top[h] = top
+            s.total[h] = s.total[h] * factor + jnp.sum(weights, axis=0, keepdims=True)
+            s.acc[h] = s.acc[h] * factor + dot_columns(s.kv[block, h, 1], weights.astype(jnp.bfloat16))
+
+        kv_spread.each(h, use)
+        total = s.total[h]
+        put_context(h, pair_rows(s.acc[h] / total), 0, long)
+        lse = s.top[h] + jnp.log(total)
+        s.lse[h, 0:1, :long] = lse[:, :long]
+        s.lse[h, 1:2, :long] = lse[:, long:]
+        return 0
+
+    lax.fori_loop(0, pairs, other_part, 0)
+    ready(2)
+    following = x + dot(s.context[...], w_out[...])
+
+    def settle():
+        q_spread.relay(0)
+        q_spread.each(0, lambda block: None)
+        q_spread.sent(0)
+        for h in range(pairs):
+            kv_spread.sent(h)
+
+    return following, settle
+
+
+def front_kernel(n_dp, n_ex, names, saved, *refs):
+    r = types.SimpleNamespace(**dict(zip(names, refs)))
+    extra = iter(refs[len(names) :])
+    buffers = []
+    for layer in range(2):
+        s = types.SimpleNamespace()
+        for name in saved:
+            setattr(s, name, next(extra))
+        s.acc, s.top, s.total = next(extra), next(extra), next(extra)
+        s.kv_sems = [next(extra) for _ in range(3)]
+        s.q_sems = [next(extra) for _ in range(3)]
+        s.stored = next(extra)
+        buffers.append(s)
+    w_in, w_out, w_sem, dense_in, dense_out, dense_sem = (next(extra) for _ in range(6))
+    stream_ref, dense_normed, active_ref, slope_ref, dense_normed_t, far_cot = (next(extra) for _ in range(6))
+    stored, cot_send, cot_send_sem, cot_recv_sem = (next(extra) for _ in range(4))
+    links = Links(n_dp)
+    tokens, width = r.tokens.shape
+    blocks = r.dense_in.shape[1] // width
     low = jnp.bfloat16
-    outs = [
-        jax.ShapeDtypeStruct((rows, width), jnp.float32),
-        jax.ShapeDtypeStruct((width, rows), low),
-        jax.ShapeDtypeStruct((rows, width), low),
-        jax.ShapeDtypeStruct((width, rows), low),
-        jax.ShapeDtypeStruct((n_dp, pairs, 2, long, 128), low),
-        jax.ShapeDtypeStruct((n_dp, pairs, long, 128), low),
-        jax.ShapeDtypeStruct((pairs, 2, short, 128), low),
-        jax.ShapeDtypeStruct((pairs, short, 128), low),
-        jax.ShapeDtypeStruct((pairs, 2, rows), jnp.float32),
+
+    def block_loads(i):
+        slot = lax.rem(i, 2)
+        at = pl.ds(pl.multiple_of(i * width, width), width)
+        return [
+            pltpu.make_async_copy(r.dense_in.at[:, at], dense_in.at[slot], dense_sem.at[slot, 0]),
+            pltpu.make_async_copy(r.dense_out.at[at, :], dense_out.at[slot], dense_sem.at[slot, 1]),
+        ]
+
+    def weight_loads(layer):
+        return [
+            pltpu.make_async_copy(
+                r.attn_in.at[layer, :, pl.ds(width, 2 * width)], w_in.at[layer, :, pl.ds(width, 2 * width)], w_sem.at[layer, 0]
+            ),
+            pltpu.make_async_copy(
+                r.attn_in.at[layer, :, pl.ds(0, width)], w_in.at[layer, :, pl.ds(0, width)], w_sem.at[layer, 1]
+            ),
+            pltpu.make_async_copy(r.attn_out.at[layer], w_out.at[layer], w_sem.at[layer, 2]),
+        ]
+
+    loads = [weight_loads(0), weight_loads(1)]
+    for load in loads[0]:
+        load.start()
+    for i in range(min(2, blocks)):
+        for load in block_loads(i):
+            load.start()
+    for load in loads[1]:
+        load.start()
+    greet(links.peers() + across_peers(n_ex))
+    writes = []
+
+    def write(source, target, sem):
+        copy = pltpu.make_async_copy(source, target, sem)
+        copy.start()
+        writes.append(copy)
+
+    def layer(number, x, between):
+        s = buffers[number]
+        column = 2 * number
+        following, settle = attend(
+            n_dp, links, s, x, r.gains[column : column + 1], r.shifts[column : column + 1], w_in.at[number], w_out.at[number],
+            r.doc_row[...], r.doc_col[...], lambda i: loads[number][i].wait(), between,
+        )
+        return following, settle
+
+    def save(number, settle):
+        s = buffers[number]
+        settle()
+        for i, name in enumerate(saved):
+            write(getattr(s, name), getattr(r, name + str(number)), s.stored.at[i])
+
+    x, settle = layer(0, r.tokens[...].astype(jnp.float32), lambda: None)
+    r.stream0[...] = x
+    stream_ref[...] = x
+    unit, _ = norm_parts(x)
+    normed = (unit * r.gains[1:2] + r.shifts[1:2]).astype(low)
+    dense_normed[...] = normed
+    save(0, settle)
+    dense_normed_t[...] = normed.T
+
+    def dense(i, _):
+        slot = lax.rem(i, 2)
+        for load in block_loads(i):
+            load.wait()
+        active, slope = gelu_parts(dot(dense_normed[...], dense_in[slot]))
+        active = active.astype(low)
+        at = pl.ds(pl.multiple_of(i * width, width), width)
+        slope_ref[:, at] = slope.astype(low)
+        active_ref[at, :] = active.T
+        stream_ref[...] += dot(active, dense_out[slot])
+
+        @pl.when(i + 2 < blocks)
+        def _():
+            for load in block_loads(i + 2):
+                load.start()
+
+        return 0
+
+    lax.fori_loop(0, blocks, dense, 0)
+    write(dense_normed_t, r.dense_normed_t, stored.at[0])
+    write(active_ref, r.active_t, stored.at[1])
+    write(slope_ref, r.slope, stored.at[2])
+    x = stream_ref[...]
+    r.stream1[...] = x
+
+    cot_across = Across(n_ex, cot_send, far_cot, cot_send_sem, cot_recv_sem)
+
+    def send_cotangent():
+        cot_send[...] = dot(dispatch_of(r.assign[...], n_ex), r.cot[...]).astype(low).reshape(cot_send.shape)
+        cot_across.start_all()
+        far_cot[links.expert] = cot_send[links.expert]
+
+    x, settle = layer(1, x, send_cotangent)
+    r.stream2[...] = x
+    save(1, settle)
+    cot_across.wait_all()
+    write(far_cot, r.far_cot, stored.at[3])
+    for copy in writes:
+        copy.wait()
+
+
+def front(n_dp, n_ex, collective_id, near, far):
+    arrays = {**near, **far}
+    a = types.SimpleNamespace(**arrays)
+    low, wide = jnp.bfloat16, jnp.float32
+    tokens, width = a.tokens.shape
+    hidden, mixed = a.dense_in.shape[1], a.attn_in.shape[2]
+    long, short, pairs = LONG_DEV, tokens - LONG_DEV, width // 128
+    slab = (n_ex, capacity_of(tokens, n_ex)[1], width)
+    saved = dict(
+        normed_t=jax.ShapeDtypeStruct((width, tokens), low),
+        context=jax.ShapeDtypeStruct((tokens, width), low),
+        context_t=jax.ShapeDtypeStruct((width, tokens), low),
+        kv=jax.ShapeDtypeStruct((n_dp, pairs, 2, long, 128), low),
+        q=jax.ShapeDtypeStruct((n_dp, pairs, long, 128), low),
+        short_kv=jax.ShapeDtypeStruct((pairs, 2, short, 128), low),
+        short_q=jax.ShapeDtypeStruct((pairs, short, 128), low),
+        lse=jax.ShapeDtypeStruct((pairs, 2, tokens), wide),
+    )
+    stream = jax.ShapeDtypeStruct((tokens, width), wide)
+    outs = dict(stream0=stream, stream1=stream, stream2=stream)
+    direct = len(outs)
+    for layer in range(2):
+        for name, shape in saved.items():
+            outs[name + str(layer)] = shape
+    outs.update(
+        dense_normed_t=jax.ShapeDtypeStruct((width, tokens), low),
+        active_t=jax.ShapeDtypeStruct((hidden, tokens), low),
+        slope=jax.ShapeDtypeStruct((tokens, hidden), low),
+        far_cot=jax.ShapeDtypeStruct(slab, low),
+    )
+    scratch = []
+    for layer in range(2):
+        scratch += [pltpu.VMEM(shape.shape, shape.dtype) for shape in saved.values()]
+        scratch += [
+            pltpu.VMEM((pairs, 128, 2 * long), wide),
+            pltpu.VMEM((pairs, 1, 2 * long), wide),
+            pltpu.VMEM((pairs, 1, 2 * long), wide),
+        ]
+        scratch += spread_sems(n_dp, pairs) + spread_sems(n_dp, 1)
+        scratch += [pltpu.SemaphoreType.DMA((len(saved),))]
+    scratch += [pltpu.VMEM((2, width, mixed), low), pltpu.VMEM((2, width, width), low), pltpu.SemaphoreType.DMA((2, 3))]
+    scratch += [pltpu.VMEM((2, width, width), low)] * 2 + [pltpu.SemaphoreType.DMA((2, 2))]
+    scratch += [
+        pltpu.VMEM((tokens, width), wide),
+        pltpu.VMEM((tokens, width), low),
+        pltpu.VMEM((hidden, tokens), low),
+        pltpu.VMEM((tokens, hidden), low),
+        pltpu.VMEM((width, tokens), low),
+        pltpu.VMEM(slab, low),
+        pltpu.SemaphoreType.DMA((4,)),
+        pltpu.VMEM(slab, low),
+        pltpu.SemaphoreType.DMA((n_ex,)),
+        pltpu.SemaphoreType.DMA((n_ex,)),
     ]
-    scratch = [
-        pltpu.VMEM((pairs, 128, 2 * long), jnp.float32),
-        pltpu.VMEM((pairs, 1, 2 * long), jnp.float32),
-        pltpu.VMEM((pairs, 1, 2 * long), jnp.float32),
-    ]
-    scratch += spread_sems(n_dp, pairs) + spread_sems(n_dp, 1)
-    if routing:
-        slab = (n_ex, capacity_of(rows, n_ex)[1], width)
-        outs += [jax.ShapeDtypeStruct(slab, low)]
-        scratch += [pltpu.VMEM(slab, low)] + [pltpu.SemaphoreType.DMA((n_ex,))] * 2
-    inputs = (stream, norm_gain, norm_shift, weight_in, weight_out, doc_row, doc_col) + tuple(routing)
-    vmem = pl.BlockSpec(memory_space=pltpu.VMEM)
-    return pl.pallas_call(
-        functools.partial(attend_kernel, n_dp, n_ex, len(inputs)),
-        out_shape=outs,
-        in_specs=[vmem] * len(inputs),
-        out_specs=[vmem] * len(outs),
+    vmem, anywhere = pl.BlockSpec(memory_space=pltpu.VMEM), pl.BlockSpec(memory_space=pl.ANY)
+    names = tuple(arrays) + tuple(outs)
+    values = pl.pallas_call(
+        functools.partial(front_kernel, n_dp, n_ex, names, tuple(saved)),
+        out_shape=list(outs.values()),
+        in_specs=[vmem] * len(near) + [anywhere] * len(far),
+        out_specs=[vmem] * direct + [anywhere] * (len(outs) - direct),
         scratch_shapes=scratch,
         compiler_params=pltpu.CompilerParams(
-            collective_id=collective_id, has_side_effects=True, vmem_limit_bytes=48 * 1024 * 1024
+            collective_id=collective_id, has_side_effects=True, vmem_limit_bytes=61 * 1024 * 1024
         ),
-        name="attention_forward",
-    )(*inputs)
+        name="front",
+    )(*arrays.values())
+    return types.SimpleNamespace(**dict(zip(outs, values)))
 
 
 def share_context(context, lse, grad_context, do_ref, aux_ref, short_do_ref, short_aux_ref, me, long):
@@ -850,6 +931,9 @@
     do_far, do_near, do_recv, aux_far, aux_near, aux_recv = (next(extra) for _ in range(6))
     links = Links(n_dp)
     d, e, me = links.me, links.expert, links.me
+    shared = links.chips == 2
+    if shared:
+        peer_rows_ref, peer_cot_ref, peer_row_sems, peer_cot_sems = (next(extra) for _ in range(4))
     dp_levels, ex_levels = n_dp.bit_length() - 1, n_ex.bit_length() - 1
     tokens, width = r.stream.shape
     padded = send_ref.shape[1]
@@ -877,6 +961,23 @@
         getattr(loads, name).start()
     greet(links.peers() + across_peers(n_ex))
 
+    def peer_copy(source, target, sems):
+        return pltpu.make_async_remote_copy(
+            src_ref=source,
+            dst_ref=target,
+            send_sem=sems.at[0],
+            recv_sem=sems.at[1],
+            device_id=(flip(d, 1), e),
+            device_id_type=MESH,
+        )
+
+    def row_copy(j):
+        return peer_copy(rows_ref.at[j], peer_rows_ref.at[j], peer_row_sems.at[j])
+
+    if shared:
+        cot_copy = peer_copy(r.far_cot, peer_cot_ref, peer_cot_sems)
+        cot_copy.start()
+
     unit, inverse = norm_parts(r.stream[...])
     routed = (unit * r.gain[...] + r.shift[...]).astype(jnp.bfloat16)
     assign = r.assign[...]
@@ -933,6 +1034,33 @@
     cut = group // 2 if (group // 2) * padded % 128 == 0 else group
     for k in range(1, groups):
         steps += [[(k, i) for i in range(first, first + cut)] for first in range(0, group, cut)]
+    def expert_rows(rows, cot, at, whole):
+        count = rows.shape[0]
+        logits = dot_rows(rows, router)
+        own = lax.broadcasted_iota(jnp.int32, logits.shape, 1) == e
+        slot_gate = jax.nn.sigmoid(jnp.sum(jnp.where(own, logits, 0.0), axis=1, keepdims=True))
+        back = (slot_gate * cot).astype(jnp.bfloat16)
+        span = slice(at, at + count)
+        back_ref[span] = back
+        rows_t_ref[:, span] = rows.T
+        if whole:
+            result_acc[:count] = jnp.zeros((count, width), jnp.float32)
+            grad_acc[:count] = jnp.zeros((count, width), jnp.float32)
+
+        def block(i, _):
+            cols = pl.ds(pl.multiple_of(i * width, width), width)
+            active, slope = gelu_parts(dot(rows, w_in_ref[i]))
+            active = active.astype(jnp.bfloat16)
+            hidden = (slope * dot_rows(back, w_out_ref[i])).astype(jnp.bfloat16)
+            active_t_ref[cols, span] = active.T
+            hidden_ref[span, cols] = hidden
+            if whole:
+                result_acc[:count] += dot(active, w_out_ref[i])
+                grad_acc[:count] += dot_rows(hidden, w_in_ref[i])
+            return 0
+
+        lax.fori_loop(0, blocks, block, 0)
+
     done, at = 0, 0
     for number, members in enumerate(steps):
         count = len(members) * padded
@@ -940,34 +1068,15 @@
         for (k, i), j in zip(members, sources):
             if (k, i) != (0, 0):
                 x_across.wait_from(j)
+            if shared:
+                row_copy(j).start()
         rows = jnp.concatenate([rows_ref[j] for j in sources], axis=0)
         cot = jnp.concatenate([r.far_cot[j] for j in sources], axis=0).astype(jnp.float32)
-        logits = dot_rows(rows, router)
-        own = lax.broadcasted_iota(jnp.int32, logits.shape, 1) == e
-        slot_gate = jax.nn.sigmoid(jnp.sum(jnp.where(own, logits, 0.0), axis=1, keepdims=True))
-        back = (slot_gate * cot).astype(jnp.bfloat16)
-        span = slice(at, at + count)
-        back_ref[span] = back
-        rows_t_ref[:, span] = rows.T
-        result_acc[:count] = jnp.zeros((count, width), jnp.float32)
-        grad_acc[:count] = jnp.zeros((count, width), jnp.float32)
-
-        def block(i, _, rows=rows, back=back, span=span, count=count):
-            cols = pl.ds(pl.multiple_of(i * width, width), width)
-            active, slope = gelu_parts(dot(rows, w_in_ref[i]))
-            active = active.astype(jnp.bfloat16)
-            hidden = (slope * dot_rows(back, w_out_ref[i])).astype(jnp.bfloat16)
-            active_t_ref[cols, span] = active.T
-            hidden_ref[span, cols] = hidden
-            result_acc[:count] += dot(active, w_out_ref[i])
-            grad_acc[:count] += dot_rows(hidden, w_in_ref[i])
-            return 0
-
         if number == 0:
             for both in expert_loads:
                 for load in both:
                     load.wait()
-        lax.fori_loop(0, blocks, block, 0)
+        expert_rows(rows, cot, at, True)
         grad = grad_acc[:count].astype(jnp.bfloat16)
         result = result_acc[:count].astype(jnp.bfloat16)
         dgate = lax.dot_general(
@@ -989,6 +1098,20 @@
             stat_step(done)
             done += 1
 
+    if shared:
+        cot_copy.wait()
+        for k in range(groups):
+            sources = [source(k, i) for i in range(group)]
+            for j in sources:
+                row_copy(j).wait()
+            rows = jnp.concatenate([peer_rows_ref[j] for j in sources], axis=0)
+            cot = jnp.concatenate([peer_cot_ref[j] for j in sources], axis=0).astype(jnp.float32)
+            expert_rows(rows, cot, at, False)
+            at += group * padded
+            if done < len(hops):
+                stat_step(done)
+                done += 1
+
     thirds = [w_in_ref.at[i] for i in range(3)]
     in_loads = [
         pltpu.make_async_copy(r.attn_in.at[1, :, column(i)], third, weight_sem.at[0, i])
@@ -1002,11 +1125,12 @@
     def rows_of(ref, j, q):
         return ref[pl.ds(pl.multiple_of((q * (ref.shape[0] // width) + j) * rows, rows), rows), :]
 
+    base = 2 * links.chip if shared else 0
     factors = [
-        (blocks, lambda j, q: rows_of(rows_t_ref, 0, q), lambda j: hidden_ref[:, pl.ds(pl.multiple_of(j * width, width), width)]),
-        (blocks, lambda j, q: rows_of(active_t_ref, j, q), lambda j: back_ref[...]),
+        (blocks, lambda j, q: rows_of(rows_t_ref, 0, base + q), lambda j: hidden_ref[:, pl.ds(pl.multiple_of(j * width, width), width)]),
+        (blocks, lambda j, q: rows_of(active_t_ref, j, base + q), lambda j: back_ref[...]),
     ]
-    red = Reduction(n_dp, 1, rows, factors, [((0, width), 0)], list(extra) + [r.chunks])
+    red = Reduction(2 if shared else n_dp, 1, rows, factors, [((0, width), 0)], list(extra) + [r.chunks])
     red.tick(0, 0, 1)
     early = 1
     while done < len(hops):
@@ -1119,11 +1243,13 @@
         scratch += [pltpu.VMEM(arrays[name].shape, arrays[name].dtype), pltpu.SemaphoreType.DMA]
     scratch += [pltpu.VMEM((blocks, width, width), low)] * 2 + [pltpu.SemaphoreType.DMA((2, blocks))]
     scratch += [pltpu.VMEM(slab, low)] * 6
+    shared = n_dp == 4
+    known = 2 * slots if shared else slots
     scratch += [
-        pltpu.VMEM((width, slots), low),
-        pltpu.VMEM((slots, width), low),
-        pltpu.VMEM((hidden, slots), low),
-        pltpu.VMEM((slots, hidden), low),
+        pltpu.VMEM((width, known), low),
+        pltpu.VMEM((known, width), low),
+        pltpu.VMEM((hidden, known), low),
+        pltpu.VMEM((known, hidden), low),
         pltpu.VMEM((slots, tokens), low),
         pltpu.VMEM((1, tokens), wide),
         pltpu.VMEM((n_ex, 8, 128), wide),
@@ -1135,7 +1261,9 @@
     ]
     scratch += [pltpu.SemaphoreType.DMA((n_ex,))] * 8 + [pltpu.SemaphoreType.DMA((hops,))] * 2
     scratch += back_scratch(n_dp, pairs, long, short)
-    scratch += Reduction.scratch(n_dp, 1, rows, width, [((0, width), 0)])
+    if shared:
+        scratch += [pltpu.VMEM(slab, low)] * 2 + [pltpu.SemaphoreType.DMA((n_ex, 2)), pltpu.SemaphoreType.DMA((2,))]
+    scratch += Reduction.scratch(2 if shared else n_dp, 1, rows, width, [((0, width), 0)])
     vmem, anywhere = pl.BlockSpec(memory_space=pltpu.VMEM), pl.BlockSpec(memory_space=pl.ANY)
     names = tuple(arrays) + tuple(outs)
     values = pl.pallas_call(
@@ -1183,11 +1311,16 @@
             pltpu.make_async_copy(r.slope.at[:, at], slopes.at[slot], weight_sem.at[slot, 2]),
         ]
 
+    ready = (loads.second_context_t, loads.second_low, loads.second_normed_t, loads.second_mixed)
+    for load in ready:
+        load.start()
     for i in range(min(2, blocks)):
         for load in block_loads(i):
             load.start()
+    loads.active_t.start()
     for name in staged:
-        getattr(loads, name).start()
+        if all(getattr(loads, name) is not load for load in ready + (loads.active_t,)):
+            getattr(loads, name).start()
     free, busy = blocks % 2, (blocks - 1) % 2
     out_load = pltpu.make_async_copy(r.attn_out.at[0], weights_out.at[free], first_sem.at[0])
     thirds = [weights_in.at[free], weights_in.at[busy], weights_out.at[busy]]
@@ -1218,9 +1351,10 @@
     up = r.up[...]
     dense_low_ref[...] = up.astype(jnp.bfloat16)
     acc_ref[...] = jnp.zeros_like(acc_ref)
-    ready = (loads.second_context_t, loads.second_low, loads.second_normed_t, loads.second_mixed)
     for load in ready:
         load.wait()
+    red.tick(0, 0, 1)
+    loads.active_t.wait()
 
     def dense(i, _):
         slot = lax.rem(i, 2)
@@ -1241,17 +1375,14 @@
             out_load.start()
             in_loads[0].start()
 
-        @pl.when(lax.rem(i, 2) == 1)
-        def _():
-            red.tick(i // 2, 0, 2)
-
+        red.tick(1 + i, 1, 1 + blocks)
         return 0
 
     lax.fori_loop(0, blocks, dense, 0)
     for load in in_loads[1:]:
         load.start()
     for name in staged:
-        if all(getattr(loads, name) is not load for load in ready):
+        if all(getattr(loads, name) is not load for load in ready + (loads.active_t,)):
             getattr(loads, name).wait()
     unit, inverse = norm_parts(r.dense_x[...])
     grad_normed = acc_ref[...]
@@ -1260,7 +1391,7 @@
     small_send[0] = r.small[...]
     small_send[0, 1:2] = jnp.sum(grad_normed * unit, axis=0, keepdims=True)
     small_send[0, 5:6] = jnp.sum(grad_normed, axis=0, keepdims=True)
-    at_tick = blocks // 2
+    at_tick = 1 + blocks
 
     scale = HEAD_DIM ** (-0.5)
     up_low = up.astype(jnp.bfloat16)
@@ -1393,8 +1524,7 @@
     cotangent,
 ):
     n_dp, n_ex = lax.axis_size("dp"), lax.axis_size("expert")
-    stream_first = tokens[0].astype(jnp.float32)
-    row_count = stream_first.shape[0]
+    row_count = tokens.shape[1]
     doc_ends = jnp.cumsum(doc_lengths[0, 0])
     short_place = jnp.arange(row_count - LONG_DEV, dtype=jnp.int32)
     short_ids = jnp.sum((short_place[:, None] >= doc_ends[None, :]).astype(jnp.int32), axis=-1)
@@ -1402,13 +1532,20 @@
     weights_in, weights_out = lax.optimization_barrier((attn_in.transpose(1, 0, 2), attn_out.transpose(1, 0, 2)))
     gains, shifts = ln_gain.T, ln_bias.T
     assign_row = assign[0].T
-    stream_one, *kept_one = attention_forward(
-        n_dp, n_ex, 2, stream_first, gains[0:1], shifts[0:1], weights_in[0], weights_out[0], doc_row, doc_col
-    )
-    stream_two, dense_normed_t, active_t, slope = ffn_forward(stream_one, gains[1:2], shifts[1:2], ffn_in, ffn_out)
-    stream_three, *kept_three, far_cot = attention_forward(
-        n_dp, n_ex, 3, stream_two, gains[2:3], shifts[2:3], weights_in[1], weights_out[1], doc_row, doc_col,
-        (assign_row, cotangent[0]),
+    fore = front(
+        n_dp,
+        n_ex,
+        2,
+        dict(
+            tokens=tokens[0],
+            gains=gains,
+            shifts=shifts,
+            doc_row=doc_row,
+            doc_col=doc_col,
+            assign=assign_row,
+            cot=cotangent[0],
+        ),
+        dict(attn_in=weights_in, attn_out=weights_out, dense_in=ffn_in, dense_out=ffn_out),
     )
     model_width = tokens.shape[2]
     rows = model_width // n_dp
@@ -1417,25 +1554,25 @@
         n_ex,
         4,
         dict(
-            stream=stream_three,
+            stream=fore.stream2,
             gain=gains[3:4],
             shift=shifts[3:4],
             router=router.T,
             assign=assign_row,
             cot=cotangent[0],
-            far_cot=far_cot,
+            far_cot=fore.far_cot,
             attn_gain=gains[2:3],
             doc_row=doc_row,
             doc_col=doc_col,
-            lse=kept_three[7],
+            lse=fore.lse1,
         ),
         dict(
-            attn_x=stream_two,
-            context=kept_three[1],
-            kv=kept_three[3],
-            q=kept_three[4],
-            short_kv=kept_three[5],
-            short_q=kept_three[6],
+            attn_x=fore.stream1,
+            context=fore.context1,
+            kv=fore.kv1,
+            q=fore.q1,
+            short_kv=fore.short_kv1,
+            short_q=fore.short_q1,
         ),
         dict(
             expert_in=expert_in[0],
@@ -1467,30 +1604,30 @@
             first_gain=gains[0:1],
             doc_row=doc_row,
             doc_col=doc_col,
-            lse=kept_one[7],
+            lse=fore.lse0,
             small=small,
         ),
         dict(
-            dense_x=stream_one,
+            dense_x=fore.stream0,
             first_x=tokens[0],
-            context=kept_one[1],
-            kv=kept_one[3],
-            q=kept_one[4],
-            short_kv=kept_one[5],
-            short_q=kept_one[6],
-            second_context_t=blocks_of(kept_three[2]),
-            second_normed_t=blocks_of(kept_three[0]),
-            active_t=blocks_of(active_t),
-            dense_normed_t=blocks_of(dense_normed_t),
-            first_context_t=blocks_of(kept_one[2]),
-            first_normed_t=blocks_of(kept_one[0]),
+            context=fore.context0,
+            kv=fore.kv0,
+            q=fore.q0,
+            short_kv=fore.short_kv0,
+            short_q=fore.short_q0,
+            second_context_t=blocks_of(fore.context_t1),
+            second_normed_t=blocks_of(fore.normed_t1),
+            active_t=blocks_of(fore.active_t),
+            dense_normed_t=blocks_of(fore.dense_normed_t),
+            first_context_t=blocks_of(fore.context_t0),
+            first_normed_t=blocks_of(fore.normed_t0),
             second_low=mid.up_low,
             second_mixed=mid.mixed,
         ),
         dict(
             dense_in=ffn_in,
             dense_out=ffn_out,
-            slope=slope,
+            slope=fore.slope,
             attn_in=weights_in,
             attn_out=weights_out,
         ),

time: 382 us -> 332 us (0.87)
  Pallas kernels: 341 us -> 304 us
  local copies, waits for them, and re-layouts: 32.9 us -> 20.1 us
    pallas_call x1, Pallas kernels: 118 us -> 97.4 us  [middle(): pl.pallas_call(functools.partial(middle_kernel, n_dp, n_ex, names, tuple(...]
    pallas_call x1, Pallas kernels: 153 us -> 144 us  [tail(): pl.pallas_call(functools.partial(tail_kernel, n_dp, n_ex, names, tuple(st...]
    unnamed x74 -> x22, local copies, waits for them, and re-layouts: 20.8 us -> 12.6 us
    pallas_call x3 -> x1, Pallas kernels: 64.9 us -> 57.7 us  [front(): pl.pallas_call(functools.partial(front_kernel, n_dp, n_ex, names, tuple(s...]
    squeeze x2 -> x0, local copies, waits for them, and re-layouts: 4.93 us -> none  [the longest x1 3.77 us: shards(): weights_in[1]]
where the time goes in v6:
time: 332 us; the launch traced here: 328 us
  Pallas kernels  304 us (92%)
  local copies, waits for them, and re-layouts  20.1 us (6%)
    pallas_call x1, Pallas kernels, tail(): pl.pallas_call(functools.partial(tail_kernel, n_dp, n_ex, names, tuple(st...  144 us
    pallas_call x1, Pallas kernels, middle(): pl.pallas_call(functools.partial(middle_kernel, n_dp, n_ex, names, tuple(...  97.4 us
    pallas_call x1, Pallas kernels, front(): pl.pallas_call(functools.partial(front_kernel, n_dp, n_ex, names, tuple(s...  57.7 us
    unnamed x22, local copies, waits for them, and re-layouts  12.6 us

profile of v6, /device:TPU:0, one launch (start us, length us, event | category | flops | bytes accessed | tf_op | source)
XLA Modules:
  0.0 328.0 jit_solution(402129091578908095)
XLA Ops:
  0.6 0.0 copy-start.2
  0.7 6.9 %copy.37 = bf16[768,2,2304]{2,0,1:T(8,128)(2,1)} copy(bf16[768,2,2304]{2,1,0:T(2,128)(2,1)} %param.18) | data formatting | bytes 14155776 | tf_op args[5]
  7.6 0.0 copy-done.2
  7.6 0.0 copy-start.8
  7.6 1.7 copy.38
  9.3 0.0 copy-done.8
  9.3 0.2 reduce-window.8
  9.5 0.1 convert_reduce_fusion
  9.6 0.0 copy-start.7
  9.6 0.7 copy.32.refs_4_.refs_9_
  10.3 0.0 copy-done.7
  10.3 0.0 copy-start.5
  10.3 57.7 %front.1 = (f32[384,768]{1,0:T(8,128)}, f32[384,768]{1,0:T(8,128)}, f32[384,768]{1,0:T(8,128)}, bf16[768,384]{1,0:T(8,128)(2,1)}, bf16[384,768]{1,0:T(8,128)(2,1...) custom-call(bf16[384,768]{1,0:T(8,128)(2,1)} %bitcast.42, ...), custom_call_target="tpu_custom_call" | custom-call | tf_op jit(solution)/shard_map/front/pallas_call | solution.py:595
  68.0 0.0 copy-done.5
  68.0 0.6 fusion.1
  68.6 1.3 slice.57.refs_2_
  69.9 97.4 %middle.1 = (f32[384,768]{1,0:T(8,128)}, bf16[384,768]{1,0:T(8,128)(2,1)}, bf16[384,2304]{1,0:T(8,128)(2,1)}, f32[2,768]{1,0:T(2,128)}, f32[2,768]{1,0:T(2,128)}...) custom-call(f32[384,768]{1,0:T(8,128)} %get-tuple-element.57.refs_0_, ...), custom_call_target="tpu_custom_call" | custom-call | tf_op jit(solution)/shard_map/middle/pallas_call | solution.py:1269
  167.3 0.8 fusion.2
  168.1 2.0 concatenate.3.refs_6_
  170.1 0.0 copy-start.1
  170.1 143.8 %tail.1 = (bf16[384,768]{1,0:T(8,128)(2,1)}, f32[16,768]{1,0:T(8,128)}, bf16[16,192,768]{2,1,0:T(8,128)(2,1)}) custom-call(f32[384,768]{1,0:T(8,128)} %get-tuple-element.68.refs_0_, f32[1,768]{1,0:T(1,128)} %get-tuple-element.101.refs_1_, f32[1,768]{1,0:T(1,128)} %get-tuple-element.100.refs_2_, s32[1,128]{1,0:T(1,128)} %bitcast.59, ...), custom_call_target="tpu_custom_call" | custom-call | tf_op jit(solution)/shard_map/tail/pallas_call | solution.py:1498
  313.9 0.0 copy-done.1
  313.9 0.0 copy-start
  313.9 2.3 copy-done
  316.2 0.0 copy-start.6
  316.2 0.0 copy-start.3
  316.2 0.0 copy-start.4
  316.3 5.4 %unpack.1 = (f32[192,2,2304]{2,1,0:T(2,128)}, f32[192,2,768]{2,1,0:T(2,128)}, f32[192,3072]{1,0:T(8,128)}, f32[4,192,768]{2,1,0:T(8,128)}, f32[192,3072]{1,0:T(8,128)}, /*index=5*/f32[4,192,768]{2,1,0:T(8,128)}) custom-call(bf16[16,192,768]{2,1,0:T(8,128)(2,1)S(1)} %copy-done, bf16[8,192,768]{2,1,0:T(8,128)(2,1)S(1)} %copy-done.1), custom_call_target="tpu_custom_call" | custom-call | tf_op jit(solution)/shard_map/unpack/pallas_call | solution.py:64
  321.7 0.8 dynamic-slice_bitcast_fusion
  322.5 0.6 fusion
  323.1 0.6 slice.63
  323.7 0.0 copy-done.6
  323.7 0.7 multiply_reduce_fusion
  325.0 0.0 copy-done.3
  325.0 0.8 copy.41
  325.8 0.0 copy-done.4
  325.8 0.8 copy.42
  (1 shorter events, 0.0 us)
Async XLA Ops:
  0.6 7.0 %copy-start.2 = (bf16[768,2,768]{2,1,0:T(2,128)(2,1)S(1)}, bf16[768,2,768]{2,1,0:T(2,128)(2,1)}, u32[]{:S(2)}) copy-start(bf16[768,2,768]{2,1,0:T(2,128)(2,1)} %param.19) | copy-start | bytes 7077892
  7.6 1.7 copy-start.8
  9.6 0.7 copy-start.7
  10.3 57.7 %copy-start.5 = (f32[768,4]{0,1:T(4,128)S(1)}, f32[768,4]{0,1:T(4,128)}, u32[]{:S(2)}) copy-start(f32[768,4]{0,1:T(4,128)} %param.16) | copy-start | bytes 36868
  170.1 143.8 %copy-start.1 = (bf16[8,192,768]{2,1,0:T(8,128)(2,1)S(1)}, bf16[8,192,768]{2,1,0:T(8,128)(2,1)}, u32[]{:S(2)}) copy-start(bf16[8,192,768]{2,1,0:T(8,128)(2,1)} %get-tuple-element.91.expert_ref) | copy-start | bytes 7077892
  313.9 2.3 copy-start
  316.2 7.4 %copy-start.6 = (f32[8,128]{1,0:T(8,128)S(1)}, f32[8,128]{1,0:T(8,128)}, u32[]{:S(2)}) copy-start(f32[8,128]{1,0:T(8,128)} %get-tuple-element.67) | copy-start | bytes 12292
  316.2 8.7 %copy-start.3 = (bf16[384,768]{1,0:T(8,128)(2,1)S(1)}, bf16[384,768]{1,0:T(8,128)(2,1)}, u32[]{:S(2)}) copy-start(bf16[384,768]{1,0:T(8,128)(2,1)} %get-tuple-element.66) | copy-start | bytes 1769476
  316.2 9.6 %copy-start.4 = (bf16[384,768]{1,0:T(8,128)(2,1)S(1)}, bf16[384,768]{1,0:T(8,128)(2,1)}, u32[]{:S(2)}) copy-start(bf16[384,768]{1,0:T(8,128)(2,1)} %get-tuple-element.88) | copy-start | bytes 1769476

commit v7 on v6

--- a/solution.py
+++ b/solution.py
@@ -36,7 +36,10 @@
 
 
 def unpack_kernel(
-    per_in, per_ffn, chunk_ref, expert_ref, in_ref, out_ref, ffn_in_ref, ffn_out_ref, expert_in_ref, expert_out_ref
+    per_in, per_ffn,
+    chunk_ref, expert_ref, small_ref, tokens_ref, output_ref,
+    in_ref, out_ref, ffn_in_ref, ffn_out_ref, expert_in_ref, expert_out_ref,
+    gain_ref, shift_ref, router_ref, tokens_out_ref, output_out_ref,
 ):
     per_expert = expert_ref.shape[0] // 2
     width = chunk_ref.shape[2]
@@ -54,13 +57,24 @@
     for j in range(per_expert):
         expert_in_ref[:, width * j : width * j + width] = expert_ref[j].astype(jnp.float32)
         expert_out_ref[j] = expert_ref[per_expert + j].astype(jnp.float32)
-
-
-def unpack(chunks, expert_chunks, per_in, per_ffn):
+    gain_ref[...] = small_ref[0:4]
+    shift_ref[...] = small_ref[4:8]
+    router_ref[...] = small_ref[8:]
+    tokens_out_ref[...] = tokens_ref[...]
+    output_out_ref[...] = output_ref[...]
+
+
+def unpack(chunks, expert_chunks, small, grad_tokens, output, per_in, per_ffn):
     count, rows, width = chunks.shape
     experts = expert_chunks.shape[0]
+    tokens = output.shape[0]
     step = 48 if rows % 48 == 0 else rows
-    wide = jnp.float32
+    wide, low = jnp.float32, jnp.bfloat16
+    token_spec = pl.BlockSpec((tokens // (rows // step), width), lambda i: (i, 0))
+
+    def fixed(shape):
+        return pl.BlockSpec(shape, lambda i: (0, 0))
+
     return pl.pallas_call(
         functools.partial(unpack_kernel, per_in, per_ffn),
         grid=(rows // step,),
@@ -71,10 +85,18 @@
             jax.ShapeDtypeStruct((per_ffn, rows, width), wide),
             jax.ShapeDtypeStruct((rows, experts // 2 * width), wide),
             jax.ShapeDtypeStruct((experts // 2, rows, width), wide),
+            jax.ShapeDtypeStruct((4, rows), wide),
+            jax.ShapeDtypeStruct((4, rows), wide),
+            jax.ShapeDtypeStruct((small.shape[0] - 8, rows), wide),
+            jax.ShapeDtypeStruct((tokens, width), low),
+            jax.ShapeDtypeStruct((tokens, width), low),
         ],
         in_specs=[
             pl.BlockSpec((count, step, width), lambda i: (0, i, 0)),
             pl.BlockSpec((experts, step, width), lambda i: (0, i, 0)),
+            fixed(small.shape),
+            token_spec,
+            token_spec,
         ],
         out_specs=[
             pl.BlockSpec((step, 2, per_in * width), lambda i: (i, 0, 0)),
@@ -83,10 +105,15 @@
             pl.BlockSpec((per_ffn, step, width), lambda i: (0, i, 0)),
             pl.BlockSpec((step, experts // 2 * width), lambda i: (i, 0)),
             pl.BlockSpec((experts // 2, step, width), lambda i: (0, i, 0)),
+            fixed((4, rows)),
+            fixed((4, rows)),
+            fixed((small.shape[0] - 8, rows)),
+            token_spec,
+            token_spec,
         ],
-        compiler_params=pltpu.CompilerParams(vmem_limit_bytes=40 * 1024 * 1024),
+        compiler_params=pltpu.CompilerParams(vmem_limit_bytes=62 * 1024 * 1024),
         name="unpack",
-    )(chunks, expert_chunks)
+    )(chunks, expert_chunks, small, grad_tokens, output)
 
 
 def dot(a, b):
@@ -105,6 +132,14 @@
     lower = 0.5 + 0.5 * lax.erf(hidden * 0.7071067811865476)
     slope = lower + hidden * jnp.exp(-0.5 * hidden * hidden) * 0.3989422804014327
     return hidden * lower, slope
+
+
+def split(value):
+    high = value.astype(jnp.bfloat16)
+    rest = value - high.astype(jnp.float32)
+    middle_part = rest.astype(jnp.bfloat16)
+    low = (rest - middle_part.astype(jnp.float32)).astype(jnp.bfloat16)
+    return jnp.concatenate([high, middle_part, low], axis=0)
 
 
 def norm_parts(x):
@@ -214,9 +249,10 @@
     return key <= jnp.where(query >= queries, query - queries, query)
 
 
-def short_seen(doc_row, doc_col):
+def short_seen(doc_row):
     n = doc_row.shape[1]
-    same = doc_col == jnp.concatenate([doc_row, doc_row], axis=1)
+    doc_col = jnp.broadcast_to(doc_row, (n, n)).T
+    same = jnp.concatenate([doc_col, doc_col], axis=1) == jnp.concatenate([doc_row, doc_row], axis=1)
     return same & causal(n, n)
 
 
@@ -326,7 +362,7 @@
     ]
 
 
-def attend(n_dp, links, s, x, gain, shift, w_in, w_out, doc_row, doc_col, ready, between):
+def attend(n_dp, links, s, x, gain, shift, w_in, w_out, doc_row, ready, between):
     me = links.me
     pairs, long, width = s.kv.shape[1], s.kv.shape[3], x.shape[1]
     unit, _ = norm_parts(x)
@@ -358,7 +394,7 @@
         s.context[first : first + count, at] = rows_t.T.astype(jnp.bfloat16)
 
     def own_part(h, _):
-        seen = short_seen(doc_row, doc_col)
+        seen = short_seen(doc_row)
         scores = jnp.where(seen, dot_rows(s.short_kv[h, 0], head_pair(s.short_q[h])), masked_score)
         top = jnp.max(scores, axis=0, keepdims=True)
         weights = jnp.exp(scores - top)
@@ -476,7 +512,7 @@
         column = 2 * number
         following, settle = attend(
             n_dp, links, s, x, r.gains[column : column + 1], r.shifts[column : column + 1], w_in.at[number], w_out.at[number],
-            r.doc_row[...], r.doc_col[...], lambda i: loads[number][i].wait(), between,
+            r.doc_row[...], lambda i: loads[number][i].wait(), between,
         )
         return following, settle
 
@@ -599,30 +635,44 @@
         out_specs=[vmem] * direct + [anywhere] * (len(outs) - direct),
         scratch_shapes=scratch,
         compiler_params=pltpu.CompilerParams(
-            collective_id=collective_id, has_side_effects=True, vmem_limit_bytes=61 * 1024 * 1024
+            collective_id=collective_id, has_side_effects=True, vmem_limit_bytes=62 * 1024 * 1024
         ),
         name="front",
     )(*arrays.values())
     return types.SimpleNamespace(**dict(zip(outs, values)))
 
 
-def share_context(context, lse, grad_context, do_ref, aux_ref, short_do_ref, short_aux_ref, me, long):
-    lane = lax.broadcasted_iota(jnp.int32, (8, 128), 1) < HEAD_DIM
-    head = lax.broadcasted_iota(jnp.int32, (8, 128), 0)
-    picks = jnp.where(((head == 0) & lane) | ((head == 1) & ~lane), 1.0, 0.0)
+def runs(most, count, use):
+    for first in range(0, most, 3):
+        for size in range(1, min(3, most - first) + 1):
+            exactly = count - first == size if size < 3 else count - first >= size
+
+            @pl.when(exactly)
+            def _():
+                use(first, size)
+
+
+def put_context_grads(grad_context, do_ref, short_do_ref, me, long):
     for h in range(do_ref.shape[1]):
-        at = slice(128 * h, 128 * h + 128)
-        piece = grad_context[:, at]
+        piece = grad_context[:, 128 * h : 128 * h + 128]
         do_ref[me, h] = piece[:long]
         short_do_ref[h] = piece[long:]
-        both = piece.astype(jnp.float32) * context[:, at].astype(jnp.float32)
-        delta = lax.dot_general(
-            picks, both, (((1,), (1,)), ((), ())), precision=lax.Precision.HIGHEST, preferred_element_type=jnp.float32
-        )
+
+
+def put_row_terms(context, lse, grad_context, aux_ref, short_aux_ref, me, long):
+    width = grad_context.shape[1]
+    rows = (width // HEAD_DIM + 15) // 16 * 16
+    lane = lax.broadcasted_iota(jnp.int32, (rows, width), 1)
+    head = lax.broadcasted_iota(jnp.int32, (rows, width), 0) * HEAD_DIM
+    picks = jnp.where((lane >= head) & (lane < head + HEAD_DIM), 1.0, 0.0).astype(jnp.bfloat16)
+    both = grad_context.astype(jnp.float32) * context[...].astype(jnp.float32)
+    high = both.astype(jnp.bfloat16)
+    delta = dot_rows(picks, high) + dot_rows(picks, (both - high.astype(jnp.float32)).astype(jnp.bfloat16))
+    for h in range(aux_ref.shape[1]):
         aux_ref[me, h, 0:2] = lse[h, :, :long]
-        aux_ref[me, h, 2:4] = delta[0:2, :long]
+        aux_ref[me, h, 2:4] = delta[2 * h : 2 * h + 2, :long]
         short_aux_ref[h, 0:2] = lse[h, :, long:]
-        short_aux_ref[h, 2:4] = delta[0:2, long:]
+        short_aux_ref[h, 2:4] = delta[2 * h : 2 * h + 2, long:]
 
 
 def attend_back_pair(n_dp, me, width, r, do_spread, aux_spread, h):
@@ -630,54 +680,60 @@
     mixed_ref = r.mixed
     long = r.kv.shape[3]
 
-    def row_of(aux, first):
-        return jnp.concatenate([aux[first : first + 1], aux[first + 1 : first + 2]], axis=1)
-
-    def score_grads(keys, values, queries, grads, aux, seen):
+    def row_of(aux):
+        return [jnp.concatenate([aux[i : i + 1], aux[i + 1 : i + 2]], axis=1) for i in (0, 2)]
+
+    def score_grads(keys, values, queries, grads, rows, seen):
         scores = dot_rows(keys, queries)
-        probs = jnp.exp(scores - row_of(aux, 0))
+        probs = jnp.exp(scores - rows[0])
         if seen is not None:
             probs = jnp.where(seen, probs, 0.0)
-        grad_scores = probs * (dot_rows(values, grads) - row_of(aux, 2))
+        grad_scores = probs * (dot_rows(values, grads) - rows[1])
         return probs.astype(jnp.bfloat16), grad_scores.astype(jnp.bfloat16)
 
     def put(third, first, value):
         at = pl.ds(pl.multiple_of(third * width + 128 * h, 128), 128)
         mixed_ref[first : first + value.shape[0], at] = value.astype(jnp.bfloat16)
 
-    seen = short_seen(r.doc_row[...], r.doc_col[...])
+    seen = short_seen(r.doc_row[...])
     queries, grads = head_pair(r.short_q[h]), head_pair(r.short_do[h])
     keys = r.short_kv[h, 0]
-    probs, grad_scores = score_grads(keys, r.short_kv[h, 1], queries, grads, r.short_aux[h], seen)
+    probs, grad_scores = score_grads(keys, r.short_kv[h, 1], queries, grads, row_of(r.short_aux[h]), seen)
     put(0, long, (pair_rows(dot_columns(keys, grad_scores)) * scale).T)
     put(1, long, dot(grad_scores, queries))
     put(2, long, dot(probs, grads))
     queries, grads = head_pair(r.q[me, h]), head_pair(r.do[me, h])
     own_keys, own_values = r.kv[me, h, 0], r.kv[me, h, 1]
-    probs, grad_scores = score_grads(own_keys, own_values, queries, grads, r.aux[me, h], causal(long, long))
+    probs, grad_scores = score_grads(own_keys, own_values, queries, grads, row_of(r.aux[me, h]), causal(long, long))
     r.dq[...] = dot_columns(own_keys, grad_scores)
     r.dk[...] = dot(grad_scores, queries)
     r.dv[...] = dot(probs, grads)
-    for block in range(n_dp - 1):
-
-        @pl.when(block < me)
-        def _():
-            keys = r.kv[block, h, 0]
-            _, grad_scores = score_grads(keys, r.kv[block, h, 1], queries, grads, r.aux[me, h], None)
-            r.dq[...] += dot_columns(keys, grad_scores)
-
+
+    def earlier(first, size):
+        at = pl.ds(first, size)
+        keys = r.kv[at, h, 0].reshape(size * long, 128)
+        values = r.kv[at, h, 1].reshape(size * long, 128)
+        _, grad_scores = score_grads(keys, values, queries, grads, row_of(r.aux[me, h]), None)
+        r.dq[...] += dot_columns(keys, grad_scores)
+
+    runs(n_dp - 1, me, earlier)
     put(0, 0, (pair_rows(r.dq[...]) * scale).T)
     do_spread.relay(h)
     aux_spread.relay(h)
 
-    def use(block):
-        queries, grads = head_pair(r.q[block, h]), head_pair(r.do[block, h])
-        probs, grad_scores = score_grads(own_keys, own_values, queries, grads, r.aux[block, h], None)
+    def later(first, size):
+        blocks = [me + 1 + first + i for i in range(size)]
+        queries = jnp.concatenate([head_pair(r.q[block, h]) for block in blocks], axis=0)
+        grads = jnp.concatenate([head_pair(r.do[block, h]) for block in blocks], axis=0)
+        rows = [row_of(r.aux[block, h]) for block in blocks]
+        rows = [jnp.concatenate([row[i] for row in rows], axis=1) for i in range(2)]
+        probs, grad_scores = score_grads(own_keys, own_values, queries, grads, rows, None)
         r.dk[...] += dot(grad_scores, queries)
         r.dv[...] += dot(probs, grads)
 
     aux_spread.each(h, lambda block: None)
-    do_spread.each(h, use)
+    do_spread.each(h, lambda block: None)
+    runs(n_dp - 1, n_dp - 1 - me, later)
     put(1, 0, r.dk[...])
     put(2, 0, r.dv[...])
 
@@ -744,7 +800,7 @@
         scratch = [pltpu.VMEM((2,) + s, jnp.bfloat16) for s in shapes]
         scratch += [pltpu.VMEM((4,) + s, jnp.bfloat16) for s in shapes]
         scratch += [pltpu.VMEM((2,) + s, jnp.float32) for s in shapes]
-        scratch += [pltpu.VMEM((len(halved) + 3, rows, width), jnp.bfloat16)]
+        scratch += [pltpu.VMEM((len(halved) + 3, rows, width) if halved else (1, 16, 128), jnp.bfloat16)]
         return scratch + [pltpu.SemaphoreType.DMA((4,)) for _ in kinds] * 2
 
     def peer(self, kind, level):
@@ -819,11 +875,10 @@
 
 
 class Reduction:
-    def __init__(self, n_dp, n_ex, rows, groups, lanes, refs):
+    def __init__(self, n_dp, n_ex, rows, groups, lanes, refs, out):
         self.n_dp, self.rows, self.groups = n_dp, rows, groups
-        refs = iter(refs)
         self.lanes = [Lane(n_dp, n_ex, rows, columns, order, refs) for columns, order in lanes]
-        self.stage_ref, self.stage_sem, self.out = next(refs), next(refs), next(refs)
+        self.stage_ref, self.stage_sem, self.out = next(refs), next(refs), out
         self.count = self.lanes[0].count
         self.chunks = sum(g[0] for g in groups)
         self.firsts = [sum(g[0] for g in groups[:i]) for i in range(len(groups))]
@@ -919,9 +974,9 @@
         buffer, sem = next(extra), next(extra)
         setattr(loads, name, pltpu.make_async_copy(getattr(r, name), buffer, sem))
         setattr(r, name, buffer)
-    w_in_ref, w_out_ref, weight_sem = (next(extra) for _ in range(3))
-    rows_ref, send_ref, grad_ref, home_ref, result_ref, result_home_ref = (next(extra) for _ in range(6))
-    rows_t_ref, back_ref, active_t_ref, hidden_ref, dispatch_ref, gate_ref = (next(extra) for _ in range(6))
+    w_in_ref, w_out_ref, weight_sem, factor_sem = (next(extra) for _ in range(4))
+    rows_ref, send_ref, grad_ref, home_ref, result_ref = (next(extra) for _ in range(5))
+    rows_t_ref, back_ref, active_t_ref, hidden_ref = (next(extra) for _ in range(4))
     dgate_ref, home_dgate_ref, stat_send, stat_recv, result_acc, grad_acc = (next(extra) for _ in range(6))
     (
         x_send_sem, x_recv_sem, grad_send_sem, grad_recv_sem, dgate_send_sem, dgate_recv_sem,
@@ -941,7 +996,6 @@
     pairs, long = r.kv.shape[1], r.kv.shape[3]
     group = min(max(4, 128 // padded), n_ex)
     groups = n_ex // group
-    exact = dict(precision=lax.Precision.HIGHEST, preferred_element_type=jnp.float32)
     hops = [(flip(d, b), e) for b in range(dp_levels)] + [(d, flip(e, b)) for b in range(ex_levels)]
 
     def column(i):
@@ -979,10 +1033,10 @@
         cot_copy.start()
 
     unit, inverse = norm_parts(r.stream[...])
-    routed = (unit * r.gain[...] + r.shift[...]).astype(jnp.bfloat16)
+    routed = (unit * r.gains[3:4] + r.shifts[3:4]).astype(jnp.bfloat16)
     assign = r.assign[...]
     dispatch = dispatch_of(assign, n_ex)
-    dispatch_ref[...] = dispatch
+    r.dispatch[...] = dispatch
     send_ref[...] = dot(dispatch, routed).astype(jnp.bfloat16).reshape(send_ref.shape)
     x_across = Across(n_ex, send_ref, rows_ref, x_send_sem, x_recv_sem)
 
@@ -1001,7 +1055,7 @@
     router = r.router[...]
     hot = chosen_rows(assign, n_ex)
     gate = jax.nn.sigmoid(jnp.sum(hot * dot_rows(router, routed), axis=0, keepdims=True))
-    gate_ref[...] = gate
+    r.gate[...] = gate
 
     def stat_copy(i):
         return pltpu.make_async_remote_copy(
@@ -1079,14 +1133,16 @@
         expert_rows(rows, cot, at, True)
         grad = grad_acc[:count].astype(jnp.bfloat16)
         result = result_acc[:count].astype(jnp.bfloat16)
-        dgate = lax.dot_general(
-            jnp.ones((8, width), jnp.float32), cot * result.astype(jnp.float32), (((1,), (1,)), ((), ())), **exact
-        )
+        both = cot * result.astype(jnp.float32)
+        high = both.astype(jnp.bfloat16)
+        rest = both - high.astype(jnp.float32)
+        ones = jnp.ones((16, width), jnp.bfloat16)
+        dgate = dot_rows(ones, high) + dot_rows(ones, rest.astype(jnp.bfloat16))
         for m, (k, i) in enumerate(members):
             j, part = sources[m], slice(m * padded, (m + 1) * padded)
             grad_ref[j] = grad[part]
             result_ref[j] = result[part]
-            dgate_ref[j, :, :padded] = dgate[:, part]
+            dgate_ref[j, :, :padded] = dgate[:8, part]
             if (k, i) == (0, 0):
                 home_ref[e] = grad_ref[e]
                 home_dgate_ref[e] = dgate_ref[e]
@@ -1125,39 +1181,52 @@
     def rows_of(ref, j, q):
         return ref[pl.ds(pl.multiple_of((q * (ref.shape[0] // width) + j) * rows, rows), rows), :]
 
-    base = 2 * links.chip if shared else 0
-    factors = [
-        (blocks, lambda j, q: rows_of(rows_t_ref, 0, base + q), lambda j: hidden_ref[:, pl.ds(pl.multiple_of(j * width, width), width)]),
-        (blocks, lambda j, q: rows_of(active_t_ref, j, base + q), lambda j: back_ref[...]),
-    ]
-    red = Reduction(2 if shared else n_dp, 1, rows, factors, [((0, width), 0)], list(extra) + [r.chunks])
-    red.tick(0, 0, 1)
-    early = 1
+    red, writes = None, []
+    if shared:
+        factors = ((rows_t_ref, r.rows_t), (back_ref, r.back), (active_t_ref, r.expert_active_t), (hidden_ref, r.expert_hidden))
+        writes = [pltpu.make_async_copy(here, there, factor_sem.at[i]) for i, (here, there) in enumerate(factors)]
+        for write in writes:
+            write.start()
+    else:
+        factors = [
+            (blocks, lambda j, q: rows_of(rows_t_ref, 0, q), lambda j: hidden_ref[:, pl.ds(pl.multiple_of(j * width, width), width)]),
+            (blocks, lambda j, q: rows_of(active_t_ref, j, q), lambda j: back_ref[...]),
+        ]
+        red = Reduction(n_dp, 1, rows, factors, [((0, width), 0)], extra, r.chunks)
+    early = 0
+    if red:
+        red.tick(0, 0, 1)
+        early = 1
     while done < len(hops):
         stat_step(done)
         done += 1
     x_across.others(x_across.wait_to)
-    red.tick(1, 1, 2)
-    early += 1
+    if red:
+        red.tick(1, 1, 2)
+        early = 2
     dgate_across.wait_all()
-    dgate = jnp.zeros((8, tokens), jnp.float32)
-    for j in range(n_ex):
-        part = dispatch_ref[j * padded : (j + 1) * padded].astype(jnp.float32)
-        dgate = dgate + jnp.dot(home_dgate_ref[j, :, :padded], part, **exact)
+    slot_grads = jnp.concatenate([home_dgate_ref[j, :, :padded] for j in range(n_ex)], axis=1)
+    dgate = dot(split(slot_grads), r.dispatch[...])
+    dgate = dgate[0:8] + dgate[8:16] + dgate[16:24]
     everyone = tokens * n_dp * n_ex
     share = jnp.sum(jnp.where(lane == 0, r.stats[...], 0.0), axis=1, keepdims=True) / everyone
     weight = balance_weight * n_ex * (share - 1.0 / n_ex) / everyone
-    gate = gate_ref[...]
+    mean_gate = jnp.sum(jnp.where(lane == 1, r.stats[...], 0.0), axis=1, keepdims=True) / everyone
+    balance = n_ex * jnp.sum((share - 1.0 / n_ex) * mean_gate, axis=0, keepdims=True)
+    r.balance[...] = jnp.broadcast_to(balance, r.balance.shape)
     grad_gate = dgate[0:1] + jnp.sum(hot * weight, axis=0, keepdims=True)
     grad_logits = hot * (grad_gate * gate * (1.0 - gate))
-    r.router_grad[...] = jnp.dot(grad_logits, routed.astype(jnp.float32), **exact)
-    grad_normed = lax.dot_general(grad_logits, router.astype(jnp.float32), (((0,), (0,)), ((), ())), **exact)
-    red.tick(2, 2, 3)
-    early += 1
+    parts = split(grad_logits)
+    product = dot(parts, routed)
+    r.router_grad[...] = product[:n_ex] + product[n_ex : 2 * n_ex] + product[2 * n_ex :]
+    grad_normed = dot_columns(parts, jnp.concatenate([router] * 3, axis=0))
+    if red:
+        red.tick(2, 2, 3)
+        early = 3
     grad_across.wait_all()
-    grad_normed = grad_normed + dot_columns(dispatch_ref[...], home_ref[...].reshape(n_ex * padded, width))
+    grad_normed = grad_normed + dot_columns(r.dispatch[...], home_ref[...].reshape(n_ex * padded, width))
     unit, inverse = norm_parts(r.stream[...])
-    up = r.cot[...].astype(jnp.float32) + norm_back(unit, inverse, r.gain[...], grad_normed)
+    up = r.cot[...].astype(jnp.float32) + norm_back(unit, inverse, r.gains[3:4], grad_normed)
     r.sums[0:1] = jnp.sum(grad_normed * unit, axis=0, keepdims=True)
     r.sums[1:2] = jnp.sum(grad_normed, axis=0, keepdims=True)
 
@@ -1168,24 +1237,26 @@
     for name in staged:
         getattr(loads, name).wait()
     grad_context = dot_rows(up_low, w_out_ref[0]).astype(jnp.bfloat16)
-    share_context(r.context, r.lse, grad_context, do_ref, aux_ref, short_do_ref, short_aux_ref, me, long)
+    put_context_grads(grad_context, do_ref, short_do_ref, me, long)
     do_spread = Spread(links, lambda b, p: do_ref.at[b, p], pairs, False, do_far, do_near, do_recv)
     aux_spread = Spread(links, lambda b, p: aux_ref.at[b, p], pairs, False, aux_far, aux_near, aux_recv)
+    put_row_terms(r.context, r.lse, grad_context, aux_ref, short_aux_ref, me, long)
     for h in range(pairs):
         do_spread.send(h)
         aux_spread.send(h)
-    result_across = Across(n_ex, result_ref, result_home_ref, result_send_sem, result_recv_sem)
+    result_across = Across(n_ex, result_ref, r.result_home, result_send_sem, result_recv_sem)
     result_across.start_all()
-    result_home_ref[e] = result_ref[e]
+    r.result_home[e] = result_ref[e]
     sequence = types.SimpleNamespace(
-        doc_row=r.doc_row, doc_col=r.doc_col, kv=r.kv, q=r.q, short_kv=r.short_kv, short_q=r.short_q,
+        doc_row=r.doc_row, kv=r.kv, q=r.q, short_kv=r.short_kv, short_q=r.short_q,
         do=do_ref, aux=aux_ref, short_do=short_do_ref, short_aux=short_aux_ref, dq=dq_ref, dk=dk_ref, dv=dv_ref,
         mixed=r.mixed,
     )
 
     def pair(h, _):
         attend_back_pair(n_dp, me, width, sequence, do_spread, aux_spread, h)
-        red.tick(early + h, early, early + pairs)
+        if red:
+            red.tick(early + h, early, early + pairs)
         return 0
 
     lax.fori_loop(0, pairs, pair, 0)
@@ -1194,20 +1265,21 @@
         in_loads[i].wait()
         grad_normed = grad_normed + dot_rows(r.mixed[:, i * width : (i + 1) * width], third[...])
     unit, inverse = norm_parts(r.attn_x[...])
-    r.up_next[...] += norm_back(unit, inverse, r.attn_gain[...], grad_normed)
+    r.up_next[...] += norm_back(unit, inverse, r.gains[2:3], grad_normed)
     r.attn_sums[0:1] = jnp.sum(grad_normed * unit, axis=0, keepdims=True)
     r.attn_sums[1:2] = jnp.sum(grad_normed, axis=0, keepdims=True)
 
-    def rest(t, _):
-        red.tick(t, early + pairs, red.ticks)
-        return 0
-
-    lax.fori_loop(early + pairs, red.ticks, rest, 0)
+    if red:
+
+        def rest(t, _):
+            red.tick(t, early + pairs, red.ticks)
+            return 0
+
+        lax.fori_loop(early + pairs, red.ticks, rest, 0)
+        red.finish()
     result_across.wait_all()
-    result = dot_columns(dispatch_ref[...], result_home_ref[...].reshape(n_ex * padded, width))
-    gate = jnp.broadcast_to(gate_ref[...], (128, tokens)).T[:, 0:1]
-    r.output[...] = (r.stream[...] + gate * result).astype(jnp.bfloat16)
-    red.finish()
+    for write in writes:
+        write.wait()
     for h in range(pairs):
         do_spread.sent(h)
         aux_spread.sent(h)
@@ -1235,23 +1307,32 @@
         attn_sums=jax.ShapeDtypeStruct((2, width), wide),
         router_grad=jax.ShapeDtypeStruct((n_ex, width), wide),
         stats=jax.ShapeDtypeStruct((n_ex, 128), wide),
-        output=jax.ShapeDtypeStruct((tokens, width), low),
-        chunks=jax.ShapeDtypeStruct((2 * blocks, rows, width), low),
+        balance=jax.ShapeDtypeStruct((1, 128), wide),
+        result_home=jax.ShapeDtypeStruct(slab, low),
+        gate=jax.ShapeDtypeStruct((1, tokens), wide),
+        dispatch=jax.ShapeDtypeStruct((slots, tokens), low),
     )
+    direct, shared = len(outs), n_dp == 4
+    known = 2 * slots if shared else slots
+    if shared:
+        outs.update(
+            rows_t=jax.ShapeDtypeStruct((width, known), low),
+            back=jax.ShapeDtypeStruct((known, width), low),
+            expert_active_t=jax.ShapeDtypeStruct((hidden, known), low),
+            expert_hidden=jax.ShapeDtypeStruct((known, hidden), low),
+        )
+    else:
+        outs.update(chunks=jax.ShapeDtypeStruct((2 * blocks, rows, width), low))
     scratch = []
     for name in staged:
         scratch += [pltpu.VMEM(arrays[name].shape, arrays[name].dtype), pltpu.SemaphoreType.DMA]
-    scratch += [pltpu.VMEM((blocks, width, width), low)] * 2 + [pltpu.SemaphoreType.DMA((2, blocks))]
-    scratch += [pltpu.VMEM(slab, low)] * 6
-    shared = n_dp == 4
-    known = 2 * slots if shared else slots
+    scratch += [pltpu.VMEM((blocks, width, width), low)] * 2 + [pltpu.SemaphoreType.DMA((2, blocks)), pltpu.SemaphoreType.DMA((4,))]
+    scratch += [pltpu.VMEM(slab, low)] * 5
     scratch += [
         pltpu.VMEM((width, known), low),
         pltpu.VMEM((known, width), low),
         pltpu.VMEM((hidden, known), low),
         pltpu.VMEM((known, hidden), low),
-        pltpu.VMEM((slots, tokens), low),
-        pltpu.VMEM((1, tokens), wide),
         pltpu.VMEM((n_ex, 8, 128), wide),
         pltpu.VMEM((n_ex, 8, 128), wide),
         pltpu.VMEM((hops, n_ex, 128), wide),
@@ -1263,17 +1344,18 @@
     scratch += back_scratch(n_dp, pairs, long, short)
     if shared:
         scratch += [pltpu.VMEM(slab, low)] * 2 + [pltpu.SemaphoreType.DMA((n_ex, 2)), pltpu.SemaphoreType.DMA((2,))]
-    scratch += Reduction.scratch(2 if shared else n_dp, 1, rows, width, [((0, width), 0)])
+    else:
+        scratch += Reduction.scratch(n_dp, 1, rows, width, [((0, width), 0)])
     vmem, anywhere = pl.BlockSpec(memory_space=pltpu.VMEM), pl.BlockSpec(memory_space=pl.ANY)
     names = tuple(arrays) + tuple(outs)
     values = pl.pallas_call(
         functools.partial(middle_kernel, n_dp, n_ex, names, tuple(staged)),
         out_shape=list(outs.values()),
         in_specs=[vmem] * len(near) + [anywhere] * (len(staged) + len(far)),
-        out_specs=[vmem] * (len(outs) - 1) + [anywhere],
+        out_specs=[vmem] * direct + [anywhere] * (len(outs) - direct),
         scratch_shapes=scratch,
         compiler_params=pltpu.CompilerParams(
-            collective_id=collective_id, has_side_effects=True, vmem_limit_bytes=61 * 1024 * 1024
+            collective_id=collective_id, has_side_effects=True, vmem_limit_bytes=62 * 1024 * 1024
         ),
         name="middle",
     )(*arrays.values())
@@ -1290,10 +1372,14 @@
         setattr(r, name, buffer)
     weights_in, weights_out, slopes, weight_sem = (next(extra) for _ in range(4))
     first_sem = next(extra)
-    up_ref, acc_ref, dense_low_ref, dense_hidden_ref, first_low_ref, mixed_ref = (next(extra) for _ in range(6))
+    acc_ref, dense_low_ref, dense_hidden_ref = (next(extra) for _ in range(3))
+    up_ref, first_low_ref, mixed_ref = acc_ref, r.second_low, r.second_mixed
     do_ref, aux_ref, short_do_ref, short_aux_ref, dq_ref, dk_ref, dv_ref = (next(extra) for _ in range(7))
     do_far, do_near, do_recv, aux_far, aux_near, aux_recv = (next(extra) for _ in range(6))
     small_send, small_recv, small_send_sem, small_recv_sem = (next(extra) for _ in range(4))
+    shared = n_dp == 4
+    if shared:
+        expert_x, expert_y, expert_sem = (next(extra) for _ in range(3))
     links = Links(n_dp)
     me = links.me
     width = up_ref.shape[1]
@@ -1343,8 +1429,33 @@
         (1, one(r.first_context_t), columns(first_low_ref)),
         (per_in, one(r.first_normed_t), columns(mixed_ref)),
     ]
-    red_refs = list(extra) + [r.chunks]
-    red = Reduction(n_dp, n_ex, rows, groups, dense_lanes(width), red_refs)
+    red = Reduction(n_dp, n_ex, rows, groups, dense_lanes(width), extra, r.chunks)
+    if shared:
+        expert_blocks = r.expert_hidden.shape[1] // width
+        base = 2 * links.chip
+
+        def expert_loads(c, act):
+            slot = lax.rem(c, 2)
+
+            def load(rows_t, at, per, factor):
+                for q in range(2):
+                    row = pl.multiple_of(((base + q) * per + at) * rows, rows)
+                    act(pltpu.make_async_copy(rows_t.at[pl.ds(row, rows), :], expert_x.at[slot, q], expert_sem.at[slot, q]))
+                act(pltpu.make_async_copy(factor, expert_y.at[slot], expert_sem.at[slot, 2]))
+
+            @pl.when(c < expert_blocks)
+            def _():
+                load(r.rows_t, 0, 1, r.expert_hidden.at[:, pl.ds(pl.multiple_of(c * width, width), width)])
+
+            @pl.when((c >= expert_blocks) & (c < 2 * expert_blocks))
+            def _():
+                load(r.expert_active_t, c - expert_blocks, expert_blocks, r.back)
+
+        def expert_part(j, q):
+            return expert_x[lax.rem(j, 2), q]
+
+        expert_groups = [(2 * expert_blocks, expert_part, lambda j: expert_y[lax.rem(j, 2)])]
+        expert_red = Reduction(2, 1, rows, expert_groups, [((0, width), 0)], extra, r.expert_chunks)
     levels = [("dp", b) for b in range(n_dp.bit_length() - 1)] + [("ex", b) for b in range(n_ex.bit_length() - 1)]
     greet([red.peer(*level) for level in levels] + (links.peers()[1:] if links.chips > 2 else []))
 
@@ -1386,9 +1497,12 @@
             getattr(loads, name).wait()
     unit, inverse = norm_parts(r.dense_x[...])
     grad_normed = acc_ref[...]
-    up = up + norm_back(unit, inverse, r.dense_gain[...], grad_normed)
+    up = up + norm_back(unit, inverse, r.gains[1:2], grad_normed)
     up_ref[...] = up
-    small_send[0] = r.small[...]
+    for first, sums in ((2, r.second_sums), (3, r.last_sums)):
+        small_send[0, first : first + 1] = sums[0:1]
+        small_send[0, first + 4 : first + 5] = sums[1:2]
+    small_send[0, 8:] = r.router_grad[...]
     small_send[0, 1:2] = jnp.sum(grad_normed * unit, axis=0, keepdims=True)
     small_send[0, 5:6] = jnp.sum(grad_normed, axis=0, keepdims=True)
     at_tick = 1 + blocks
@@ -1398,16 +1512,19 @@
     first_low_ref[...] = up_low
     out_load.wait()
     grad_context = dot_rows(up_low, weights_out[free]).astype(jnp.bfloat16)
-    share_context(r.context, r.lse, grad_context, do_ref, aux_ref, short_do_ref, short_aux_ref, me, long)
+    red.tick(at_tick, at_tick, at_tick + 1)
+    at_tick += 1
+    put_context_grads(grad_context, do_ref, short_do_ref, me, long)
     do_spread = Spread(links, lambda b, p: do_ref.at[b, p], pairs, False, do_far, do_near, do_recv)
     aux_spread = Spread(links, lambda b, p: aux_ref.at[b, p], pairs, False, aux_far, aux_near, aux_recv)
+    put_row_terms(r.context, r.lse, grad_context, aux_ref, short_aux_ref, me, long)
     for h in range(pairs):
         do_spread.send(h)
         aux_spread.send(h)
     red.tick(at_tick, at_tick, at_tick + 1)
     at_tick += 1
     sequence = types.SimpleNamespace(
-        doc_row=r.doc_row, doc_col=r.doc_col, kv=r.kv, q=r.q, short_kv=r.short_kv, short_q=r.short_q,
+        doc_row=r.doc_row, kv=r.kv, q=r.q, short_kv=r.short_kv, short_q=r.short_q,
         do=do_ref, aux=aux_ref, short_do=short_do_ref, short_aux=short_aux_ref, dq=dq_ref, dk=dk_ref, dv=dv_ref,
         mixed=mixed_ref,
     )
@@ -1425,7 +1542,7 @@
         grad_normed = grad_normed + dot_rows(mixed_ref[:, i * width : (i + 1) * width], third[...])
     unit, inverse = norm_parts(r.first_x[...].astype(jnp.float32))
     r.grad_tokens[...] = (
-        up_ref[...] + norm_back(unit, inverse, r.first_gain[...], grad_normed)
+        up_ref[...] + norm_back(unit, inverse, r.gains[0:1], grad_normed)
     ).astype(jnp.bfloat16)
     small_send[0, 0:1] = jnp.sum(grad_normed * unit, axis=0, keepdims=True)
     small_send[0, 4:5] = jnp.sum(grad_normed, axis=0, keepdims=True)
@@ -1442,8 +1559,27 @@
 
     small_copy(0).start()
 
+    if shared:
+        for c in range(2):
+            expert_loads(jnp.int32(c), lambda copy: copy.start())
+
     def rest(t, _):
         red.tick(t, at_tick, red.ticks)
+        if shared:
+            c = t - at_tick
+            expert_loads(c, lambda copy: copy.wait())
+            expert_red.tick(c, 0, red.ticks - at_tick)
+            expert_loads(c + 2, lambda copy: copy.start())
+
+        @pl.when(t == red.ticks - 2)
+        def _():
+            gate = jnp.broadcast_to(r.gate[...], (128, r.gate.shape[1])).T[:, 0:1]
+            for first in range(0, width, 256):
+                at = slice(first, first + 256)
+                home = r.result_home[:, :, at].reshape(r.dispatch.shape[0], 256)
+                result = dot_columns(r.dispatch[...], home)
+                r.output[:, at] = (r.last_x[:, at] + gate * result).astype(jnp.bfloat16)
+
         for i in range(1, len(levels) + 1):
 
             @pl.when(t == at_tick + i)
@@ -1454,11 +1590,20 @@
                     small_send[i] = value
                     small_copy(i).start()
                 else:
-                    r.small_sum[...] = value
+                    own = jnp.zeros((value.shape[0], rows), jnp.float32)
+                    for q in range(n_dp):
+                        own = own + jnp.where(me == q, value[:, q * rows : (q + 1) * rows], 0.0)
+                    r.small_sum[...] = own
 
         return 0
 
     lax.fori_loop(at_tick, red.ticks, rest, 0)
+    if shared:
+        for c in range(red.ticks - at_tick, expert_red.ticks):
+            expert_loads(jnp.int32(c), lambda copy: copy.wait())
+            expert_red.tick(jnp.int32(c), c, c + 1)
+            expert_loads(jnp.int32(c + 2), lambda copy: copy.start())
+        expert_red.finish()
     red.finish()
     for h in range(pairs):
         do_spread.sent(h)
@@ -1475,37 +1620,48 @@
     rows = width // n_dp
     long, short, pairs = LONG_DEV, tokens - LONG_DEV, width // 128
     chunks = 2 * (hidden // width) + 2 * (1 + mixed // width)
-    small = a.small.shape
+    small = (8 + a.router_grad.shape[0], width)
     outs = dict(
         grad_tokens=jax.ShapeDtypeStruct((tokens, width), low),
-        small_sum=jax.ShapeDtypeStruct(small, wide),
-        chunks=jax.ShapeDtypeStruct((chunks, rows, width), low),
+        output=jax.ShapeDtypeStruct((tokens, width), low),
+        small_sum=jax.ShapeDtypeStruct((small[0], rows), wide),
     )
+    direct, shared = len(outs), n_dp == 4
+    outs.update(chunks=jax.ShapeDtypeStruct((chunks, rows, width), low))
+    if shared:
+        slots, expert_hidden = a.expert_hidden.shape
+        outs.update(expert_chunks=jax.ShapeDtypeStruct((2 * expert_hidden // width, rows, width), low))
     scratch = []
     for name in staged:
         scratch += [pltpu.VMEM(arrays[name].shape, arrays[name].dtype), pltpu.SemaphoreType.DMA]
     scratch += [pltpu.VMEM((2, width, width), low)] * 2
     scratch += [pltpu.VMEM((2, tokens, width), low), pltpu.SemaphoreType.DMA((2, 3))]
     scratch += [pltpu.SemaphoreType.DMA((4,))]
-    scratch += [pltpu.VMEM((tokens, width), wide)] * 2
-    scratch += [pltpu.VMEM((tokens, n), low) for n in (width, hidden, width, mixed)]
+    scratch += [pltpu.VMEM((tokens, width), wide)]
+    scratch += [pltpu.VMEM((tokens, n), low) for n in (width, hidden)]
     scratch += back_scratch(n_dp, pairs, long, short)
     hops = (n_dp * n_ex).bit_length() - 1
     scratch += [pltpu.VMEM((hops,) + small, wide)] * 2 + [pltpu.SemaphoreType.DMA((hops,))] * 2
+    if shared:
+        scratch += [pltpu.VMEM((2, 2, rows, slots), low), pltpu.VMEM((2, slots, width), low)]
+        scratch += [pltpu.SemaphoreType.DMA((2, 3))]
     scratch += Reduction.scratch(n_dp, n_ex, rows, width, dense_lanes(width))
+    if shared:
+        scratch += Reduction.scratch(2, 1, rows, width, [((0, width), 0)])
     vmem, anywhere = pl.BlockSpec(memory_space=pltpu.VMEM), pl.BlockSpec(memory_space=pl.ANY)
     names = tuple(arrays) + tuple(outs)
-    return pl.pallas_call(
+    values = pl.pallas_call(
         functools.partial(tail_kernel, n_dp, n_ex, names, tuple(staged)),
         out_shape=list(outs.values()),
         in_specs=[vmem] * len(near) + [anywhere] * (len(staged) + len(far)),
-        out_specs=[vmem] * (len(outs) - 1) + [anywhere],
+        out_specs=[vmem] * direct + [anywhere] * (len(outs) - direct),
         scratch_shapes=scratch,
         compiler_params=pltpu.CompilerParams(
-            collective_id=collective_id, has_side_effects=True, vmem_limit_bytes=61 * 1024 * 1024
+            collective_id=collective_id, has_side_effects=True, vmem_limit_bytes=62 * 1024 * 1024
         ),
         name="tail",
     )(*arrays.values())
+    return types.SimpleNamespace(**dict(zip(outs, values)))
 
 
 def shards(
@@ -1525,10 +1681,11 @@
 ):
     n_dp, n_ex = lax.axis_size("dp"), lax.axis_size("expert")
     row_count = tokens.shape[1]
-    doc_ends = jnp.cumsum(doc_lengths[0, 0])
+    lengths = doc_lengths[0, 0]
+    order = jnp.arange(lengths.shape[0])
+    doc_ends = jnp.sum(jnp.where(order[:, None] <= order[None, :], lengths[:, None], 0), axis=0)
     short_place = jnp.arange(row_count - LONG_DEV, dtype=jnp.int32)
-    short_ids = jnp.sum((short_place[:, None] >= doc_ends[None, :]).astype(jnp.int32), axis=-1)
-    doc_row, doc_col = short_ids[None, :], short_ids[:, None]
+    doc_row = jnp.sum((short_place[None, :] >= doc_ends[:, None]).astype(jnp.float32), axis=0, keepdims=True)
     weights_in, weights_out = lax.optimization_barrier((attn_in.transpose(1, 0, 2), attn_out.transpose(1, 0, 2)))
     gains, shifts = ln_gain.T, ln_bias.T
     assign_row = assign[0].T
@@ -1541,7 +1698,6 @@
             gains=gains,
             shifts=shifts,
             doc_row=doc_row,
-            doc_col=doc_col,
             assign=assign_row,
             cot=cotangent[0],
         ),
@@ -1555,15 +1711,13 @@
         4,
         dict(
             stream=fore.stream2,
-            gain=gains[3:4],
-            shift=shifts[3:4],
+            gains=gains,
+            shifts=shifts,
             router=router.T,
             assign=assign_row,
             cot=cotangent[0],
             far_cot=fore.far_cot,
-            attn_gain=gains[2:3],
             doc_row=doc_row,
-            doc_col=doc_col,
             lse=fore.lse1,
         ),
         dict(
@@ -1581,31 +1735,24 @@
             attn_out=weights_out,
         ),
     )
-    everyone = row_count * n_dp * n_ex
-    stats = mid.stats
-    balance = n_ex * jnp.sum((stats[:, 0] / everyone - 1.0 / n_ex) * (stats[:, 1] / everyone))
-    output = mid.output[None]
-    second_sums, fourth_sums = mid.attn_sums, mid.sums
-
     def blocks_of(rows_t):
         return rows_t.reshape(n_dp, -1, rows, row_count)
 
-    none = jnp.zeros((2, model_width), jnp.float32)
-    small = jnp.concatenate(
-        [none, second_sums[0:1], fourth_sums[0:1], none, second_sums[1:2], fourth_sums[1:2], mid.router_grad], axis=0
-    )
-    grad_tokens, small, chunks = tail(
+    shared = n_dp == 4
+    last = tail(
         n_dp,
         n_ex,
         5,
         dict(
             up=mid.up_next,
-            dense_gain=gains[1:2],
-            first_gain=gains[0:1],
+            gains=gains,
             doc_row=doc_row,
-            doc_col=doc_col,
             lse=fore.lse0,
-            small=small,
+            second_sums=mid.attn_sums,
+            last_sums=mid.sums,
+            router_grad=mid.router_grad,
+            dispatch=mid.dispatch,
+            gate=mid.gate,
         ),
         dict(
             dense_x=fore.stream0,
@@ -1622,6 +1769,8 @@
             first_context_t=blocks_of(fore.context_t0),
             first_normed_t=blocks_of(fore.normed_t0),
             second_low=mid.up_low,
+            result_home=mid.result_home,
+            last_x=fore.stream2,
             second_mixed=mid.mixed,
         ),
         dict(
@@ -1630,33 +1779,37 @@
             slope=fore.slope,
             attn_in=weights_in,
             attn_out=weights_out,
+            **(
+                dict(
+                    rows_t=mid.rows_t,
+                    back=mid.back,
+                    expert_active_t=mid.expert_active_t,
+                    expert_hidden=mid.expert_hidden,
+                )
+                if shared
+                else {}
+            ),
         ),
     )
-    grad_tokens = grad_tokens[None]
-    attn_in_sum, attn_out_sum, ffn_in_sum, ffn_out_sum, expert_in_sum, expert_out_sum = unpack(
-        chunks, mid.chunks, attn_in.shape[2] // model_width, ffn_in.shape[1] // model_width
+    expert_chunks = last.expert_chunks if shared else mid.chunks
+    (
+        attn_in_sum, attn_out_sum, ffn_in_sum, ffn_out_sum, expert_in_sum, expert_out_sum,
+        gain_sum, shift_sum, router_sum, grad_tokens, output,
+    ) = unpack(
+        last.chunks, expert_chunks, last.small_sum, last.grad_tokens, last.output,
+        attn_in.shape[2] // model_width, ffn_in.shape[1] // model_width,
     )
-    small = lax.dynamic_slice_in_dim(small, lax.axis_index("dp") * rows, rows, 1).T
-    summed = [
+    return (
+        output[None],
+        mid.balance[0, 0],
+        grad_tokens[None],
+        gain_sum.T,
+        shift_sum.T,
         attn_in_sum,
         attn_out_sum,
         ffn_in_sum,
         ffn_out_sum.reshape(-1, model_width),
-        small[:, 8:],
-        small[:, :4],
-        small[:, 4:8],
-    ]
-    return (
-        output,
-        balance,
-        grad_tokens,
-        summed[5],
-        summed[6],
-        summed[0],
-        summed[1],
-        summed[2],
-        summed[3],
-        summed[4],
+        router_sum.T,
         expert_in_sum[None],
         expert_out_sum.reshape(1, -1, model_width),
     )

time: 332 us -> 314 us (0.946)
  local copies, waits for them, and re-layouts: 20.1 us -> 10.2 us
  Pallas kernels: 304 us -> 297 us
    pallas_call x1, Pallas kernels: 97.4 us -> 85.5 us  [middle(): pl.pallas_call(functools.partial(middle_kernel, n_dp, n_ex, names, tuple(...]
    pallas_call x1, Pallas kernels: 5.41 us -> 9.34 us  [unpack(): pl.pallas_call(functools.partial(unpack_kernel, per_in, per_ffn), grid=(r...]
    slice x5 -> x0, local copies, waits for them, and re-layouts: 3.87 us -> none  [the longest x1 1.29 us: shards(): shifts[3:4]]
    unnamed x22 -> x4, local copies, waits for them, and re-layouts: 12.6 us -> 10.2 us
where the time goes in v7:
time: 314 us; the launch traced here: 311 us
  Pallas kernels  297 us (95%)
  local copies, waits for them, and re-layouts  10.2 us (3%)
    pallas_call x1, Pallas kernels, tail(): pl.pallas_call(functools.partial(tail_kernel, n_dp, n_ex, names, tuple(st...  145 us
    pallas_call x1, Pallas kernels, middle(): pl.pallas_call(functools.partial(middle_kernel, n_dp, n_ex, names, tuple(...  85.5 us
    pallas_call x1, Pallas kernels, front(): pl.pallas_call(functools.partial(front_kernel, n_dp, n_ex, names, tuple(s...  57.7 us
    unnamed x4, local copies, waits for them, and re-layouts  10.2 us
    pallas_call x1, Pallas kernels, unpack(): pl.pallas_call(functools.partial(unpack_kernel, per_in, per_ffn), grid=(r...  9.34 us

profile of v7, /device:TPU:0, one launch (start us, length us, event | category | flops | bytes accessed | tf_op | source)
XLA Modules:
  0.0 310.8 jit_solution(16659679766495630280)
XLA Ops:
  0.6 0.7 select_reduce_fusion
  1.4 0.6 convert_reduce_fusion
  2.0 3.4 %copy.32 = bf16[768,2,768]{2,0,1:T(8,128)(2,1)} copy(bf16[768,2,768]{2,1,0:T(2,128)(2,1)} %param.19) | data formatting | bytes 4718592 | tf_op args[6]
  5.3 6.8 %copy.31 = bf16[768,2,2304]{2,0,1:T(8,128)(2,1)} copy(bf16[768,2,2304]{2,1,0:T(2,128)(2,1)} %param.18) | data formatting | bytes 14155776 | tf_op args[5]
  12.1 57.7 %front.1 = (f32[384,768]{1,0:T(8,128)}, f32[384,768]{1,0:T(8,128)}, f32[384,768]{1,0:T(8,128)}, bf16[768,384]{1,0:T(8,128)(2,1)}, bf16[384,768]{1,0:T(8,128)(2,1...) custom-call(bf16[384,768]{1,0:T(8,128)(2,1)} %bitcast.43, ...), custom_call_target="tpu_custom_call" | custom-call | tf_op jit(solution)/shard_map/front/pallas_call | solution.py:631
  69.8 85.5 %middle.1 = (f32[384,768]{1,0:T(8,128)}, bf16[384,768]{1,0:T(8,128)(2,1)}, bf16[384,2304]{1,0:T(8,128)(2,1)}, f32[2,768]{1,0:T(2,128)}, f32[2,768]{1,0:T(2,128)}...) custom-call(f32[384,768]{1,0:T(8,128)} %get-tuple-element.69.refs_0_, ...), custom_call_target="tpu_custom_call" | custom-call | tf_op jit(solution)/shard_map/middle/pallas_call | solution.py:1351
  155.3 144.7 %tail.1 = (bf16[384,768]{1,0:T(8,128)(2,1)}, bf16[384,768]{1,0:T(8,128)(2,1)}, f32[16,192]{1,0:T(8,128)}, bf16[16,192,768]{2,1,0:T(8,128)(2,1)}, bf16[8,192,768]{2,1,0:T(8,128)(2,1)}) custom-call(f32[384,768]{1,0:T(8,128)} %get-tuple-element.78.refs_0_, f32[4,768]{1,0:T(4,128)} %bitcast.52, f32[1,128]{1,0:T(1,128)} %bitcast.60, ...), custom_call_target="tpu_custom_call" | custom-call | tf_op jit(solution)/shard_map/tail/pallas_call | solution.py:1653
  300.0 0.0 copy-start
  300.0 9.3 %unpack.1 = (f32[192,2,2304]{2,1,0:T(2,128)}, f32[192,2,768]{2,1,0:T(2,128)}, f32[192,3072]{1,0:T(8,128)}, f32[4,192,768]{2,1,0:T(8,128)}, f32[192,3072]{1,0:T(8...) custom-call(bf16[16,192,768]{2,1,0:T(8,128)(2,1)} %get-tuple-element, ...), custom_call_target="tpu_custom_call" | custom-call | tf_op jit(solution)/shard_map/unpack/pallas_call | solution.py:78
  309.4 0.0 copy-done
Async XLA Ops:
  300.0 9.4 %copy-start = (f32[1,128]{1,0:T(1,128)S(1)}, f32[1,128]{1,0:T(1,128)}, u32[]{:S(2)}) copy-start(f32[1,128]{1,0:T(1,128)} %get-tuple-element.111) | copy-start | bytes 1540
